TPU v7x, 32 devices: a whole 2x2x4 slice. The times are simulated.
32 devices in a mesh: seq: 16 (over z, x, core), mp: 2 (over y).
Axes of the slice: x: 2, y: 2, z: 4, core: 2. Of those that a mesh axis runs over, the one named last changes fastest.
Arguments:
- queries: bfloat16 [8192, 4096], P(('seq', 'mp')), may hold values from -6 to 6
- memory_keys: bfloat16 [128, 4096], P('seq', 'mp'), may hold values from -6 to 6
- memory_values: bfloat16 [128, 4096], P('seq', 'mp'), may hold values from -48 to 48
- output_grad: bfloat16 [8192, 4096], P(('seq', 'mp')), may hold values from -24 to 24
Outputs:
- attended: bfloat16 [8192, 4096], P(('seq', 'mp'))
- query_grad: bfloat16 [8192, 4096], P(('seq', 'mp'))
- key_grad: bfloat16 [128, 4096], P('seq', 'mp')
- value_grad: bfloat16 [128, 4096], P('seq', 'mp')
All inputs are finite; a program needn't handle non-finite values.
Results may differ from a plain program's by a relative error of at most 0.012.
The roundings to bfloat16 on the way count: a program that leaves them out, or rounds other values in their place, can miss the bound.
Values may be sent and summed in bfloat16 or wider, within the bound.
No kernel may reach another device: no remote copies, remote signals or barrier semaphores. Data moves between devices by JAX's collectives and lax.ppermute only.
A program may use at most 64 MiB of HBM per device.

v0:
```python
import math

import jax
import jax.numpy as jnp
from jax import lax
from jax.sharding import PartitionSpec as P

DH = 128


def split_heads(matrix, head_width):
    row_count = matrix.shape[0]
    return matrix.reshape(row_count, -1, head_width).transpose(1, 0, 2)


def join_heads(stacked):
    head_count, row_count, head_width = stacked.shape
    return stacked.transpose(1, 0, 2).reshape(row_count, head_count * head_width)


def forward_head(operands):
    query_rows, key_rows, value_rows = operands
    temper = 1.0 / math.sqrt(query_rows.shape[1])
    scores = jnp.dot(query_rows, key_rows.T, preferred_element_type=jnp.float32) * temper
    peak_score = jnp.max(scores, axis=1, keepdims=True)
    log_total = peak_score + jnp.log(jnp.sum(jnp.exp(scores - peak_score), axis=1, keepdims=True))
    attention_weights = jnp.exp(scores - log_total).astype(jnp.bfloat16)
    attended = jnp.dot(attention_weights, value_rows, preferred_element_type=jnp.float32).astype(
        jnp.bfloat16
    )
    return (attended, log_total)


def score_gradient(query_rows, key_rows, value_rows, grad_rows, attended, log_total):
    temper = 1.0 / math.sqrt(query_rows.shape[1])
    scores = jnp.dot(query_rows, key_rows.T, preferred_element_type=jnp.float32) * temper
    exact_weights = jnp.exp(scores - log_total)
    row_delta = jnp.sum(
        grad_rows.astype(jnp.float32) * attended.astype(jnp.float32), axis=1, keepdims=True
    )
    prob_grad = jnp.dot(grad_rows, value_rows.T, preferred_element_type=jnp.float32)
    score_grad = (exact_weights * (prob_grad - row_delta) * temper).astype(jnp.bfloat16)
    return (exact_weights.astype(jnp.bfloat16), score_grad)


def backward_head(operands):
    query_rows, key_rows, value_rows, grad_rows, attended, log_total = operands
    attention_weights, score_grad = score_gradient(
        query_rows, key_rows, value_rows, grad_rows, attended, log_total
    )
    query_grad = jnp.dot(score_grad, key_rows, preferred_element_type=jnp.float32).astype(
        jnp.bfloat16
    )
    key_grad = jnp.dot(score_grad.T, query_rows, preferred_element_type=jnp.float32)
    value_grad = jnp.dot(attention_weights.T, grad_rows, preferred_element_type=jnp.float32)
    return (query_grad, key_grad, value_grad)


def shards(queries, memory_keys, memory_values, output_grad):
    local_queries, local_grad = (
        lax.all_to_all(queries, "mp", split_axis=1, concat_axis=0, tiled=True),
        lax.all_to_all(output_grad, "mp", split_axis=1, concat_axis=0, tiled=True),
    )
    keys_whole, values_whole = (
        lax.all_gather(memory_keys, "seq", axis=0, tiled=True),
        lax.all_gather(memory_values, "seq", axis=0, tiled=True),
    )
    query_heads = split_heads(local_queries, DH)
    grad_heads = split_heads(local_grad, DH)
    attended_heads, log_totals = lax.map(
        forward_head, (query_heads, split_heads(keys_whole, DH), split_heads(values_whole, DH))
    )
    keys_again, values_again = (
        lax.all_gather(memory_keys, "seq", axis=0, tiled=True),
        lax.all_gather(memory_values, "seq", axis=0, tiled=True),
    )
    key_heads = split_heads(keys_again, DH)
    value_heads = split_heads(values_again, DH)
    query_grad_heads, key_terms, value_terms = lax.map(
        backward_head, (query_heads, key_heads, value_heads, grad_heads, attended_heads, log_totals)
    )
    key_grad, value_grad = (
        lax.psum_scatter(join_heads(key_terms), "seq", scatter_dimension=0, tiled=True),
        lax.psum_scatter(join_heads(value_terms), "seq", scatter_dimension=0, tiled=True),
    )
    attended, query_grad = (
        lax.all_to_all(join_heads(attended_heads), "mp", split_axis=0, concat_axis=1, tiled=True),
        lax.all_to_all(join_heads(query_grad_heads), "mp", split_axis=0, concat_axis=1, tiled=True),
    )
    return (attended, query_grad, key_grad.astype(jnp.bfloat16), value_grad.astype(jnp.bfloat16))


def solution(mesh):
    return jax.shard_map(
        shards,
        mesh=mesh,
        in_specs=(P(("seq", "mp"), None), P("seq", "mp"), P("seq", "mp"), P(("seq", "mp"), None)),
        out_specs=(P(("seq", "mp"), None), P(("seq", "mp"), None), P("seq", "mp"), P("seq", "mp")),
        check_vma=False,
    )
```

profile of v0, /device:TPU:0, one launch (start us, length us, event | category | flops | bytes accessed | tf_op | source)
XLA Modules:
  0.0 361.8 jit_solution(11109517420541586765)
XLA Ops:
  7.2 3.2 copy.74
  10.3 4.4 %all-to-all-start = ((bf16[256,2,2048]{2,0,1:T(8,128)(2,1)}), bf16[256,2,2048]{2,0,1:T(8,128)(2,1)S(1)}, u32[]{:S(2)}, u32[]{:S(2)}) async-start(bf16[256,2,2048]{2,0,1:T(8,128)(2,1)} %bitcast.141), calls=%async_computation | async-start | bytes 4194304 | tf_op jit(solution)/shard_map/all_to_all | solution.py:61
  14.7 24.2 %all_gather.8 = bf16[128,2048]{1,0:T(8,128)(2,1)S(1)} all-gather(bf16[8,2048]{1,0:T(8,128)(2,1)S(1)} %copy-done.1), channel_id=1, replica_groups=mesh['seq'=16,'mp'=2] {'seq'}, dimensions={0}, use_global_device_ids=true | all-gather | bytes 557056 | tf_op jit(solution)/shard_map/all_gather | solution.py:65
  40.2 18.9 %all_gather.9 = bf16[128,2048]{1,0:T(8,128)(2,1)S(1)} all-gather(bf16[8,2048]{1,0:T(8,128)(2,1)S(1)} %copy-done.2), channel_id=1, replica_groups=mesh['seq'=16,'mp'=2] {'seq'}, dimensions={0}, use_global_device_ids=true | all-gather | bytes 557056 | tf_op jit(solution)/shard_map/all_gather | solution.py:66
  59.6 3.2 copy.73
  62.8 4.8 %all-to-all-start.2 = ((bf16[256,2,2048]{2,0,1:T(8,128)(2,1)}), bf16[256,2,2048]{2,0,1:T(8,128)(2,1)}, u32[]{:S(2)}, u32[]{:S(2)}) async-start(bf16[256,2,2048]{2,0,1:T(8,128)(2,1)} %bitcast.97), calls=%async_computation.2 | async-start | bytes 4194304 | tf_op jit(solution)/shard_map/all_to_all | solution.py:62
  68.3 1.9 copy.47
  70.6 23.5 %while.26 = (s32[]{:T(128)}, bf16[16,512,128]{2,1,0:T(8,128)(2,1)S(1)}, f32[16,512,1]{1,2,0:T(1,128)S(1)}, bf16[16,512,128]{2,1,0:T(8,128)(2,1)}, bf16[16,128,12...) while((s32[]{:T(128)}, bf16[16,512,128]{2,1,0:T(8,128)(2,1)S(1)}, ...), condition=%wide.region_3.4_spmd, body=%wide.region_0.3_spmd.sunk | while | flops 34012672 | bytes 1134673 | solution.py:70
  94.1 2.2 copy.68
  96.3 1.9 copy.55
  99.9 134.4 %while.27 = (s32[]{:T(128)}, bf16[16,512,128]{2,1,0:T(8,128)(2,1)}, f32[16,128,128]{2,1,0:T(8,128)}, f32[16,128,128]{2,1,0:T(8,128)}, bf16[16,512,128]{2,1,0:T(8...) while((s32[]{:T(128)}, bf16[16,512,128]{2,1,0:T(8,128)(2,1)}, ...), condition=%wide.region_6.7_spmd, body=%wide.region_4.6_spmd.sunk | while | flops 84672000 | bytes 2342005 | solution.py:79
  104.8 1.8 fusion.82
  106.6 1.8 fusion.83
  115.0 1.8 fusion.83
  121.6 1.8 fusion.82
  123.4 1.8 fusion.83
  131.8 1.8 fusion.83
  138.4 1.8 fusion.82
  140.2 1.8 fusion.83
  146.8 1.8 fusion.82
  148.6 1.8 fusion.83
  155.2 1.8 fusion.82
  165.4 1.8 fusion.83
  172.0 1.8 fusion.82
  173.8 1.8 fusion.83
  180.4 1.8 fusion.82
  182.1 1.8 fusion.83
  188.8 1.8 fusion.82
  198.9 1.8 fusion.83
  207.3 1.8 fusion.83
  214.0 1.8 fusion.82
  215.7 1.8 fusion.83
  230.8 1.8 fusion.82
  232.5 1.8 fusion.83
  234.3 2.3 copy_bitcast_fusion.3
  236.6 4.3 %copy.57 = bf16[512,16,128]{2,1,0:T(8,128)(2,1)} copy(bf16[512,16,128]{2,0,1:T(8,128)(2,1)} %bitcast.143) | data formatting | bytes 4194304 | tf_op jit(solution)/shard_map/transpose | solution.py:18
  240.9 4.2 %all_to_all.62 = bf16[2,256,2048]{2,1,0:T(8,128)(2,1)} reshape(bf16[512,16,128]{2,1,0:T(8,128)(2,1)} %copy.57) | data formatting | bytes 4194304 | tf_op jit(solution)/shard_map/all_to_all | solution.py:88
  245.1 5.0 %all-to-all-start.3 = ((bf16[2,256,2048]{2,1,0:T(8,128)(2,1)}), bf16[2,256,2048]{2,1,0:T(8,128)(2,1)}, u32[]{:S(2)}, u32[]{:S(2)}) async-start(bf16[2,256,2048]{2,1,0:T(8,128)(2,1)} %all_to_all.62), calls=%async_computation.3 | async-start | bytes 4194304 | tf_op jit(solution)/shard_map/all_to_all | solution.py:88
  251.2 2.7 copy.50
  253.9 4.2 %all_to_all.55 = bf16[2,256,2048]{2,1,0:T(8,128)(2,1)} reshape(bf16[512,16,128]{2,1,0:T(8,128)(2,1)} %copy.50) | data formatting | bytes 4194304 | tf_op jit(solution)/shard_map/all_to_all | solution.py:87
  258.0 17.9 %all-to-all-done.3 = bf16[2,256,2048]{2,1,0:T(8,128)(2,1)} async-done(((bf16[2,256,2048]{2,1,0:T(8,128)(2,1)}), bf16[2,256,2048]{2,1,0:T(8,128)(2,1)}, u32[]{:S(2)}, u32[]{:S(2)}) %all-to-all-start.3) | async-done | bytes 2097184 | tf_op jit(solution)/shard_map/all_to_all | solution.py:88
  276.0 3.8 %all-to-all-start.1 = ((bf16[2,256,2048]{2,1,0:T(8,128)(2,1)}), bf16[2,256,2048]{2,1,0:T(8,128)(2,1)S(1)}, u32[]{:S(2)}, u32[]{:S(2)}) async-start(bf16[2,256,2048]{2,1,0:T(8,128)(2,1)} %all_to_all.55), calls=%async_computation.1 | async-start | bytes 4194304 | tf_op jit(solution)/shard_map/all_to_all | solution.py:87
  279.7 4.0 %copy.58 = bf16[256,2,2048]{0,2,1:T(8,128)(2,1)} copy(bf16[256,2,2048]{2,0,1:T(8,128)(2,1)} %bitcast.28) | data formatting | bytes 4194304 | tf_op jit(solution)/shard_map/all_to_all | solution.py:88
  283.7 4.1 %copy.62 = bf16[256,4096]{1,0:T(8,128)(2,1)} copy(bf16[256,4096]{0,1:T(8,128)(2,1)} %bitcast.146) | data formatting | bytes 4194304
  287.8 17.0 %all-to-all-done.1 = bf16[2,256,2048]{2,1,0:T(8,128)(2,1)S(1)} async-done(((bf16[2,256,2048]{2,1,0:T(8,128)(2,1)}), bf16[2,256,2048]{2,1,0:T(8,128)(2,1)S(1)}, u32[]{:S(2)}, u32[]{:S(2)}) %all-to-all-start.1) | async-done | bytes 2097184 | tf_op jit(solution)/shard_map/all_to_all | solution.py:87
  304.8 2.5 copy.51
  307.3 4.1 %copy.61 = bf16[256,4096]{1,0:T(8,128)(2,1)} copy(bf16[256,4096]{0,1:T(8,128)(2,1)} %bitcast.147) | data formatting | bytes 4194304
  312.8 40.6 %reduce-scatter.5.cloned.1.call-done = f32[8,2048]{1,0:T(8,128)} async-done(((f32[128,2048]{1,0:T(8,128)}), f32[8,2048]{1,0:T(8,128)}) %reduce-scatter.5.cloned.1.call-update) | async-done | bytes 65552 | tf_op jit(solution)/shard_map/reduce_scatter | solution.py:84
  (195 shorter events, 125.3 us)
Async XLA Ops:
  10.3 4.4 %copy-start.1 = (bf16[8,2048]{1,0:T(8,128)(2,1)S(1)}, bf16[8,2048]{1,0:T(8,128)(2,1)}, u32[]{:S(2)}) copy-start(bf16[8,2048]{1,0:T(8,128)(2,1)} %param.9) | copy-start | bytes 98308
  10.3 52.5 %all-to-all-start = ((bf16[256,2,2048]{2,0,1:T(8,128)(2,1)}), bf16[256,2,2048]{2,0,1:T(8,128)(2,1)S(1)}, u32[]{:S(2)}, u32[]{:S(2)}) async-start(bf16[256,2,2048]{2,0,1:T(8,128)(2,1)} %bitcast.141), calls=%async_computation | async-start | bytes 4194304 | tf_op jit(solution)/shard_map/all_to_all | solution.py:61
  14.7 25.5 %copy-start.2 = (bf16[8,2048]{1,0:T(8,128)(2,1)S(1)}, bf16[8,2048]{1,0:T(8,128)(2,1)}, u32[]{:S(2)}) copy-start(bf16[8,2048]{1,0:T(8,128)(2,1)} %param.10) | copy-start | bytes 98308
  62.8 31.3 %all-to-all-start.2 = ((bf16[256,2,2048]{2,0,1:T(8,128)(2,1)}), bf16[256,2,2048]{2,0,1:T(8,128)(2,1)}, u32[]{:S(2)}, u32[]{:S(2)}) async-start(bf16[256,2,2048]{2,0,1:T(8,128)(2,1)} %bitcast.97), calls=%async_computation.2 | async-start | bytes 4194304 | tf_op jit(solution)/shard_map/all_to_all | solution.py:62
  67.6 243.7 %reduce-scatter.3.cloned.1.call-start = ((), (), s32[]{:S(2)}) async-start(), calls=%async_computation.6 | async-start | bytes 1114112 | tf_op jit(solution)/shard_map/reduce_scatter | solution.py:83
  245.1 5.0 %copy-start = (f32[16,128,128]{2,1,0:T(8,128)S(1)}, f32[16,128,128]{2,1,0:T(8,128)}, u32[]{:S(2)}) copy-start(f32[16,128,128]{2,1,0:T(8,128)} %get-tuple-element.95) | copy-start | bytes 3145732
  245.1 30.9 %all-to-all-start.3 = ((bf16[2,256,2048]{2,1,0:T(8,128)(2,1)}), bf16[2,256,2048]{2,1,0:T(8,128)(2,1)}, u32[]{:S(2)}, u32[]{:S(2)}) async-start(bf16[2,256,2048]{2,1,0:T(8,128)(2,1)} %all_to_all.62), calls=%async_computation.3 | async-start | bytes 4194304 | tf_op jit(solution)/shard_map/all_to_all | solution.py:88
  250.0 103.4 %reduce-scatter.5.cloned.1.call-start = ((), (), s32[]{:S(2)}) async-start(), calls=%async_computation.7 | async-start | bytes 1114112 | tf_op jit(solution)/shard_map/reduce_scatter | solution.py:84
  276.0 28.8 %all-to-all-start.1 = ((bf16[2,256,2048]{2,1,0:T(8,128)(2,1)}), bf16[2,256,2048]{2,1,0:T(8,128)(2,1)S(1)}, u32[]{:S(2)}, u32[]{:S(2)}) async-start(bf16[2,256,2048]{2,1,0:T(8,128)(2,1)} %all_to_all.55), calls=%async_computation.1 | async-start | bytes 4194304 | tf_op jit(solution)/shard_map/all_to_all | solution.py:87
Sparse Core Ops, SparseCore 0:
  236.8 56.2 reduce-scatter.2
  297.1 56.3 reduce-scatter.4
where the time goes:
time: 366 us; the launch traced here: 362 us
  matrix products  139 us (38%)
  waiting for transfers between devices  75.6 us (21%)
  local copies, waits for them, and re-layouts  50.5 us (14%)
  blocking collectives  43 us (12%)
  other arithmetic  21 us (6%)
  starting transfers between devices  18 us (5%)
  between operations  14.1 us (4%)
    reduce_scatter x1, waiting for transfers between devices, shards(): lax.psum_scatter(join_heads(value_terms), 'seq', scatter_dimension=0, til...  40.6 us
    dot_general x16, matrix products, backward_head(): jnp.dot(attention_weights.T, grad_rows, preferred_element_type=jnp.float32)  28.1 us
    dot_general x16, matrix products, backward_head(): jnp.dot(score_grad.T, query_rows, preferred_element_type=jnp.float32)  28 us
    dot_general x16, matrix products, backward_head(): jnp.dot(score_grad, key_rows, preferred_element_type=jnp.float32)  25.5 us
    all_gather x1, blocking collectives, shards(): lax.all_gather(memory_keys, 'seq', axis=0, tiled=True)  24.2 us
    all_gather x1, blocking collectives, shards(): lax.all_gather(memory_values, 'seq', axis=0, tiled=True)  18.9 us
    all_to_all x1, waiting for transfers between devices, shards(): lax.all_to_all(join_heads(query_grad_heads), 'mp', split_axis=0, concat_a...  17.9 us
    dot_general x16, matrix products, forward_head(): jnp.dot(query_rows, key_rows.T, preferred_element_type=jnp.float32) * temper  17.8 us
  transfers between devices with their start and end apart: 6, of which 3 were waited for; matrix products, arithmetic and copies ran while one was open for 15% of the time, Pallas kernels for 0%

commit v1 on v0

v1 whole, which is shorter than its diff:
```python
import functools
import math

import jax
import jax.numpy as jnp
from jax import lax
from jax.experimental import pallas as pl
from jax.experimental.pallas import tpu as pltpu
from jax.sharding import PartitionSpec as P

DH = 128

NT = (((1,), (1,)), ((), ()))
NN = (((1,), (0,)), ((), ()))

bf16, f32 = jnp.bfloat16, jnp.float32


def dot(a, b, dims):
    return lax.dot_general(a, b, dims, preferred_element_type=f32)


def softmax_part(raw, prob_grad):
    temper = 1.0 / math.sqrt(DH)
    peak = jnp.max(raw, axis=0, keepdims=True)
    powers = jnp.exp2((raw - peak) * (temper * math.log2(math.e)))
    inverse = 1.0 / jnp.sum(powers, axis=0, keepdims=True)
    delta = jnp.sum(powers * prob_grad, axis=0, keepdims=True) * inverse
    weights = (powers * inverse).astype(bf16)
    score_grad = (powers * (inverse * temper) * (prob_grad - delta)).astype(bf16)
    return score_grad, weights


def columns(n_mp, blocks, block, width, of_sibling):
    core, my = lax.axis_index("seq") & 1, lax.axis_index("mp")
    core = 1 - core if of_sibling else core
    return lambda r: pl.multiple_of((((my ^ r) * 2 + core) * blocks + block) * width, width)


def attention_kernel(n_mp, blocks, block, rs, n_memory, q_ref, g_ref, sq_ref, sg_ref, *refs):
    memory_refs, refs = refs[:n_memory], refs[-10 - n_memory :]
    (attended_ref, query_grad_ref, sibling_ref), term_refs = refs[:3], refs[3:-7]
    token_buf, result_buf, raw_ref, prob_ref, grad_ref, weight_ref, sems = refs[-7:]
    count, width = q_ref.shape[0], term_refs[0].shape[1] // 2
    heads, group = width // DH, min(2 * DH, width)
    parts = width // group
    size = memory_refs[0].shape[0] // len(rs)
    column = columns(n_mp, blocks, block, width, False)
    step = min(DH, 2 * count)
    cols = [slice(n * DH, (n + 1) * DH) for n in range(heads)]
    targets = [[slice(m * width + n * DH, m * width + (n + 1) * DH) for n in range(heads)] for m in (0, 1)]

    def inputs(k, part):
        begin = part * group
        where = pl.ds(pl.multiple_of(column(rs[0] + k) + begin, group), group)
        return [
            pltpu.make_async_copy(
                array.at[:, where],
                token_buf.at[k, m, pl.ds(n * count, count), pl.ds(begin, group)],
                sems.at[0, k, part, m, n],
            )
            for m, pair in enumerate(((q_ref, sq_ref), (g_ref, sg_ref)))
            for n, array in enumerate(pair)
        ]

    def outputs(k, part):
        begin = part * group
        copies = []
        for m, own in enumerate((query_grad_ref, attended_ref)):
            starts = (column(rs[0] + k), (2 * (rs[0] + k) + m) * width)
            for n, (array, start) in enumerate(zip((own, sibling_ref), starts)):
                copies.append(
                    pltpu.make_async_copy(
                        result_buf.at[k, m, pl.ds(n * count, count), pl.ds(begin, group)],
                        array.at[:, pl.ds(pl.multiple_of(start + begin, group), group)],
                        sems.at[1, k, part, m, n],
                    )
                )
        return copies

    def every(action):
        def at(k, _):
            for part in range(parts):
                for copy in action(k, part):
                    copy()

        repeat(at)

    def repeat(body):
        if len(rs) == 1:
            body(0, None)
        else:
            lax.fori_loop(0, len(rs), body, None)

    def work(k, _):
        rows = pl.ds(pl.multiple_of(k * size, size), size)
        memory = [[jnp.concatenate([ref[rows, t] for ref in memory_refs], axis=0) for t in row] for row in targets]
        for n in range(heads):
            if n * DH % group == 0:
                for copy in inputs(k, n * DH // group):
                    copy.wait()
            raw_ref[n] = dot(memory[0][n], token_buf[k, 0, :, cols[n]], NT)
            prob_ref[n] = dot(memory[1][n], token_buf[k, 1, :, cols[n]], NT)
        for n in range(heads):
            for begin in range(0, 2 * count, step):
                part = slice(begin, begin + step)
                grad_ref[n, :, part], weight_ref[n, :, part] = softmax_part(raw_ref[n, :, part], prob_ref[n, :, part])
        for n in range(heads):
            for m, pair_ref in enumerate((grad_ref, weight_ref)):
                result_buf[k, m, :, cols[n]] = dot(memory[m][n].T, pair_ref[n], NN).astype(bf16).T
            if (n + 1) * DH % group == 0:
                for copy in outputs(k, n * DH // group):
                    copy.start()
        for n in range(heads):
            for m, pair_ref in enumerate((grad_ref, weight_ref)):
                term = dot(pair_ref[n], token_buf[k, m, :, cols[n]], NN)
                for i, term_ref in enumerate(term_refs):
                    term_ref[rows, targets[m][n]] = term[i * size : (i + 1) * size].astype(term_ref.dtype)

    every(lambda k, part: [copy.start for copy in inputs(k, part)])
    repeat(work)
    every(lambda k, part: [copy.wait for copy in outputs(k, part)])


def pinned(space, *arrays):
    return [pltpu.with_memory_space_constraint(array, space) for array in arrays]


HBM, VMEM = pl.BlockSpec(memory_space=pltpu.HBM), pl.BlockSpec(memory_space=pltpu.VMEM)


def attention(n_mp, blocks, block, rs, tokens, memory, types, outputs, sent):
    rows, whole = tokens[0].shape
    width = memory[0].shape[1] // 2
    count = sum(m.shape[0] for m in memory) // len(rs)
    group = min(2 * DH, width)
    scratch = (width // DH, count, 2 * rows)
    earlier = [*outputs] + ([] if sent is None else [sent])
    first = 4 + len(memory)
    return pl.pallas_call(
        functools.partial(attention_kernel, n_mp, blocks, block, rs, len(memory)),
        in_specs=[HBM] * 4 + [VMEM] * len(memory) + [HBM] * len(earlier),
        out_specs=[HBM] * 3 + [VMEM] * len(memory),
        out_shape=[jax.ShapeDtypeStruct((rows, whole), bf16)] * 2
        + [jax.ShapeDtypeStruct((rows, whole // blocks), bf16)]
        + [pltpu.VMEM(m.shape, t) for m, t in zip(memory, types)],
        scratch_shapes=[pltpu.VMEM((len(rs), 2, 2 * rows, width), bf16)] * 2
        + [pltpu.VMEM(scratch, t) for t in (f32, f32, bf16, bf16)]
        + [pltpu.SemaphoreType.DMA((2, len(rs), width // group, 2, 2))],
        input_output_aliases={first + n: n for n in range(len(earlier))},
        compiler_params=pltpu.CompilerParams(vmem_limit_bytes=32 * 1024 * 1024),
        cost_estimate=pl.CostEstimate(
            flops=24 * rows * count * width * len(rs),
            bytes_accessed=16 * rows * width * len(rs),
            transcendentals=2 * rows * count * width * len(rs) // DH,
        ),
    )(*pinned(pltpu.HBM, *tokens[:2]), *tokens[2:], *pinned(pltpu.VMEM, *memory), *earlier)


def placing_kernel(n_mp, blocks, *refs):
    returned_refs, (attended_ref, query_grad_ref, sems) = refs[:blocks], refs[-3:]
    width = returned_refs[0].shape[1] // (2 * n_mp)
    copies = []
    for block, returned_ref in enumerate(returned_refs):
        column = columns(n_mp, blocks, block, width, True)
        for r in range(n_mp):
            for m, target in enumerate((query_grad_ref, attended_ref)):
                start = (2 * r + m) * width
                copies.append(
                    pltpu.make_async_copy(
                        returned_ref.at[:, start : start + width],
                        target.at[:, pl.ds(column(r), width)],
                        sems.at[len(copies)],
                    )
                )
    for copy in copies:
        copy.start()
    for copy in copies:
        copy.wait()


def placing(n_mp, returned, attended, query_grad):
    blocks = len(returned)
    return pl.pallas_call(
        functools.partial(placing_kernel, n_mp, blocks),
        in_specs=[VMEM] * blocks + [HBM] * 2,
        out_specs=[HBM] * 2,
        out_shape=[jax.ShapeDtypeStruct(attended.shape, bf16)] * 2,
        scratch_shapes=[pltpu.SemaphoreType.DMA((2 * blocks * n_mp,))],
        input_output_aliases={blocks: 0, blocks + 1: 1},
    )(*pinned(pltpu.VMEM, *returned), attended, query_grad)


def together(*values):
    return lax.optimization_barrier(values)


def shards(n_seq, n_mp, queries, memory_keys, memory_values, output_grad):
    def swap(array, axis, bits):
        size = n_seq if axis == "seq" else n_mp
        return lax.ppermute(array, axis, [(i, i ^ bits) for i in range(size)])

    core_bit, x_bit = 1, 2
    z_bits = range(4, n_seq, 4)
    y_bits = [1 << b for b in range(n_mp.bit_length() - 1)]
    rows, part = memory_keys.shape
    share, blocks = part // 2, 2
    block = share // blocks
    core = lax.axis_index("seq") & 1

    def packed(c):
        both = [lax.dynamic_slice_in_dim(array, c * share, share, axis=1) for array in (memory_keys, memory_values)]
        return jnp.concatenate([b[:, n * block : (n + 1) * block] for n in range(blocks) for b in both], axis=1)

    base = jnp.concatenate([packed(core), swap(packed(1 - core), "seq", core_bit)])
    base, queries_out, grad_out = together(base, queries, output_grad)
    sibling_queries, sibling_grad = swap(queries_out, "seq", core_bit), swap(grad_out, "seq", core_bit)
    tokens = (queries, output_grad, sibling_queries, sibling_grad)

    got = [base] + [swap(base, "seq", bits) for bits in z_bits]
    first, second = (jnp.concatenate([g[:, n * 2 * block : (n + 1) * 2 * block] for g in got]) for n in (0, 1))

    def wider(held, got):
        return jnp.concatenate([held, got])

    first_got, second_got = together(swap(first, "seq", x_bit), swap(second, "mp", y_bits[0]))
    first, second = wider(first, first_got), wider(second, second_got)
    for bits in y_bits[:-1]:
        first = wider(first, swap(first, "mp", bits))
    for bits in y_bits[1:]:
        second = wider(second, swap(second, "mp", bits))
    first_got, second_got = swap(first, "mp", y_bits[-1]), swap(second, "seq", x_bit)

    half = n_mp // 2
    *outputs, out, first_keep = attention(n_mp, blocks, 0, range(half), tokens, [first], [f32], [], None)
    *outputs, out_first, give = attention(
        n_mp, blocks, 0, range(half, n_mp), tokens, [first_got], [bf16], outputs, out
    )
    first_got = swap(give, "mp", y_bits[-1])
    *outputs, out_second, second_keep, give = attention(
        n_mp, blocks, 1, range(n_mp), tokens, [second, second_got], [f32, bf16], outputs, None
    )
    second_got = swap(give, "seq", x_bit)
    first, second = together(first_keep + first_got.astype(f32), second_keep + second_got.astype(f32))

    def fold(total, axis, bits):
        middle = total.shape[0] // 2
        return total[:middle] + swap(total[middle:].astype(bf16), axis, bits).astype(f32)

    for bits in y_bits[-2::-1]:
        first = fold(first, "mp", bits)
    for bits in y_bits[:0:-1]:
        second = fold(second, "mp", bits)
    first, second = fold(first, "seq", x_bit), fold(second, "mp", y_bits[0])
    returned = [swap(out, "seq", core_bit) for out in (out_first, out_second)]
    first, second, returned = together(first, second, returned)
    total = jnp.concatenate([first, second], axis=1)
    outputs = placing(n_mp, returned, *outputs)
    count, give = 2 * rows, total.astype(bf16)
    got = [swap(give[n * count : (n + 1) * count], "seq", bits) for n, bits in enumerate(z_bits, 1)]
    got, outputs = together(got, outputs)
    total = (total[:count] + sum(g.astype(f32) for g in got)).astype(bf16)
    mine, other = total[:rows], swap(total[rows:], "seq", core_bit)

    def joined(m):
        a, b = (
            jnp.concatenate([t[:, (2 * n + m) * block : (2 * n + m + 1) * block] for n in range(blocks)], axis=1)
            for t in (mine, other)
        )
        whole = lax.dynamic_update_slice_in_dim(jnp.zeros((rows, part), bf16), a, core * share, axis=1)
        return lax.dynamic_update_slice_in_dim(whole, b, (1 - core) * share, axis=1)

    return (*outputs, joined(0), joined(1))


def solution(mesh):
    body = functools.partial(shards, mesh.shape["seq"], mesh.shape["mp"])
    return jax.shard_map(
        body,
        mesh=mesh,
        in_specs=(P(("seq", "mp"), None), P("seq", "mp"), P("seq", "mp"), P(("seq", "mp"), None)),
        out_specs=(P(("seq", "mp"), None), P(("seq", "mp"), None), P("seq", "mp"), P("seq", "mp")),
        check_vma=False,
    )
```

time: 366 us -> 65.3 us (0.18); the launches traced: 362 us -> 65.1 us
  matrix products: 139 us -> 0 us
  waiting for transfers between devices: 75.6 us -> 26.6 us
  local copies, waits for them, and re-layouts: 50.5 us -> 2.21 us
  blocking collectives: 43 us -> 0 us
  other arithmetic: 21 us -> 0.29 us
  Pallas kernels: 0 us -> 13.9 us
  between operations: 14.1 us -> 0.89 us
    dot_general x112 -> x0, matrix products: 139 us -> none  [the longest x16 28.1 us: backward_head(): jnp.dot(attention_weights.T, grad_rows, preferred_element_type=jnp.float32)]
    all_gather x2 -> x0, blocking collectives: 43 us -> none  [the longest x1 24.2 us: shards(): lax.all_gather(memory_keys, 'seq', axis=0, tiled=True)]
    reduce_scatter x2 -> x0, waiting for transfers between devices: 40.6 us -> none  [the longest x1 40.6 us: shards(): lax.psum_scatter(join_heads(value_terms), 'seq', scatter_dimension=0, til...]
    all_to_all x4 -> x0, waiting for transfers between devices: 34.9 us -> none  [the longest x1 17.9 us: shards(): lax.all_to_all(join_heads(query_grad_heads), 'mp', split_axis=0, concat_a...]
    ppermute x0 -> x20, waiting for transfers between devices: none -> 26.6 us  [swap(): return lax.ppermute(array, axis, [(i, i ^ bits) for i in range(size)])]
    ppermute x0 -> x20, starting transfers between devices: none -> 21.2 us  [swap(): return lax.ppermute(array, axis, [(i, i ^ bits) for i in range(size)])]
    all_to_all x6 -> x0, local copies, waits for them, and re-layouts: 21.2 us -> none  [the longest x2 8.16 us: shards(): lax.all_to_all(join_heads(query_grad_heads), 'mp', split_axis=0, concat_a...]
    reduce_sum x32 -> x0, other arithmetic: 18 us -> none  [the longest x16 16.9 us: score_gradient(): jnp.sum(grad_rows.astype(jnp.float32) * attended.astype(jnp.float32), axi...]
  transfers between devices with their start and end apart: 6 -> 20, of which waited for: 3 -> 11; matrix products, arithmetic and copies ran while one was open for 15% -> 0% of each run, Pallas kernels for 0% -> 21%
where the time goes in v1:
time: 65.3 us; the launch traced here: 65.1 us
  waiting for transfers between devices  26.6 us (41%)
  starting transfers between devices  21.2 us (32%)
  Pallas kernels  13.9 us (21%)
  local copies, waits for them, and re-layouts  2.21 us (3%)
  between operations  0.89 us (1%)
    ppermute x20, waiting for transfers between devices, swap(): return lax.ppermute(array, axis, [(i, i ^ bits) for i in range(size)])  26.6 us
    ppermute x20, starting transfers between devices, swap(): return lax.ppermute(array, axis, [(i, i ^ bits) for i in range(size)])  21.2 us
    pallas_call x3, Pallas kernels, attention(): pl.pallas_call(functools.partial(attention_kernel, n_mp, blocks, block, r...  12.5 us
    pallas_call x1, Pallas kernels, placing(): pl.pallas_call(functools.partial(placing_kernel, n_mp, blocks), in_specs=...  1.37 us
  transfers between devices with their start and end apart: 20, of which 11 were waited for; matrix products, arithmetic and copies ran while one was open for 0% of the time, Pallas kernels for 21%

profile of v1, /device:TPU:0, one launch (start us, length us, event | category | flops | bytes accessed | tf_op | source)
XLA Modules:
  0.0 65.1 jit_solution(10054289432873115577)
XLA Ops:
  0.6 0.8 %constant_dynamic-slice_fusion.2 = (bf16[8,512]{1,0:T(8,128)(2,1)S(1)}, bf16[8,512]{1,0:T(8,128)(2,1)S(1)}, bf16[8,512]{1,0:T(8,128)(2,1)S(1)}, bf16[8,512]{1,0:...) fusion(bf16[8,2048]{1,0:T(8,128)(2,1)} %param.6, ...), kind=kLoop, calls=%fused_computation.30 | loop fusion | bytes 131088 | tf_op jit(solution)/shard_map/slice | solution.py:213
  1.5 0.5 collective-permute-start
  2.0 0.9 %collective-permute-done = bf16[8,2048]{1,0:T(8,128)(2,1)S(1)} collective-permute-done((bf16[8,2048]{1,0:T(8,128)(2,1)S(1)}, bf16[8,2048]{1,0:T(8,128)(2,1)S(1)}, u32[]{:S(2)}, u32[]{:S(2)}) %collective-permute-start) | collective-permute-done | bytes 32800 | tf_op jit(solution)/shard_map/ppermute | solution.py:201
  2.9 0.3 collective-permute-start.1
  3.2 0.2 collective-permute-start.2
  3.4 2.9 %collective-permute-start.3 = (bf16[16,2048]{1,0:T(8,128)(2,1)S(1)}, bf16[16,2048]{1,0:T(8,128)(2,1)S(1)}, u32[]{:S(2)}, u32[]{:S(2)}) collective-permute-start(bf16[16,2048]{1,0:T(8,128)(2,1)S(1)} %pad_maximum_fusion.2), channel_id=1, source_target_pairs={{0,8},{2,10},{4,12},{6,14},{8,0},{10,2},{12,4},{14,6},{16,24},{18,... | collective-permute-start | bytes 196616 | tf_op jit(solution)/shard_map/ppermute | solution.py:201
  6.3 2.7 %collective-permute-start.4 = (bf16[16,2048]{1,0:T(8,128)(2,1)S(1)}, bf16[16,2048]{1,0:T(8,128)(2,1)S(1)}, u32[]{:S(2)}, u32[]{:S(2)}) collective-permute-start(bf16[16,2048]{1,0:T(8,128)(2,1)S(1)} %pad_maximum_fusion.2), channel_id=1, source_target_pairs={{0,16},{2,18},{4,20},{6,22},{8,24},{10,26},{12,28},{14,30},{16,0},... | collective-permute-start | bytes 196616 | tf_op jit(solution)/shard_map/ppermute | solution.py:201
  9.0 0.0 collective-permute-start.5
  9.0 0.0 collective-permute-done.3
  9.0 4.9 %collective-permute-done.4 = bf16[16,2048]{1,0:T(8,128)(2,1)S(1)} collective-permute-done((bf16[16,2048]{1,0:T(8,128)(2,1)S(1)}, bf16[16,2048]{1,0:T(8,128)(2,1)S(1)}, u32[]{:S(2)}, u32[]{:S(2)}) %collective-permute-start.4) | collective-permute-done | bytes 65568 | tf_op jit(solution)/shard_map/ppermute | solution.py:201
  13.9 1.2 %collective-permute-done.5 = bf16[16,2048]{1,0:T(8,128)(2,1)S(1)} collective-permute-done((bf16[16,2048]{1,0:T(8,128)(2,1)S(1)}, bf16[16,2048]{1,0:T(8,128)(2,1)S(1)}, u32[]{:S(2)}, u32[]{:S(2)}) %collective-permute-start.5) | collective-permute-done | bytes 65568 | tf_op jit(solution)/shard_map/ppermute | solution.py:201
  15.2 1.6 %collective-permute-start.6 = (bf16[64,1024]{1,0:T(8,128)(2,1)S(1)}, bf16[64,1024]{1,0:T(8,128)(2,1)S(1)}, u32[]{:S(2)}, u32[]{:S(2)}) collective-permute-start(bf16[64,1024]{1,0:T(8,128)(2,1)S(1)} %pad_maximum_fusion), channel_id=1, source_target_pairs={{0,4},{2,6},{4,0},{6,2},{8,12},{10,14},{12,8},{14,10},{16,20},{18,... | collective-permute-start | bytes 393224 | tf_op jit(solution)/shard_map/ppermute | solution.py:201
  16.7 1.6 %collective-permute-start.7 = (bf16[64,1024]{1,0:T(8,128)(2,1)S(1)}, bf16[64,1024]{1,0:T(8,128)(2,1)S(1)}, u32[]{:S(2)}, u32[]{:S(2)}) collective-permute-start(bf16[64,1024]{1,0:T(8,128)(2,1)S(1)} %pad_maximum_fusion.1), channel_id=1, source_target_pairs={{0,1},{1,0},{2,3},{3,2},{4,5},{5,4},{6,7},{7,6},{8,9},{9,8},{10,11... | collective-permute-start | bytes 393224 | tf_op jit(solution)/shard_map/ppermute | solution.py:201
  18.3 1.9 %collective-permute-done.6 = bf16[64,1024]{1,0:T(8,128)(2,1)S(1)} collective-permute-done((bf16[64,1024]{1,0:T(8,128)(2,1)S(1)}, bf16[64,1024]{1,0:T(8,128)(2,1)S(1)}, u32[]{:S(2)}, u32[]{:S(2)}) %collective-permute-start.6) | collective-permute-done | bytes 131104 | tf_op jit(solution)/shard_map/ppermute | solution.py:201
  20.2 1.6 %collective-permute-done.7 = bf16[64,1024]{1,0:T(8,128)(2,1)S(1)} collective-permute-done((bf16[64,1024]{1,0:T(8,128)(2,1)S(1)}, bf16[64,1024]{1,0:T(8,128)(2,1)S(1)}, u32[]{:S(2)}, u32[]{:S(2)}) %collective-permute-start.7) | collective-permute-done | bytes 131104 | tf_op jit(solution)/shard_map/ppermute | solution.py:201
  21.8 1.6 %collective-permute-start.8 = (bf16[128,1024]{1,0:T(8,128)(2,1)S(1)}, bf16[128,1024]{1,0:T(8,128)(2,1)S(1)}, u32[]{:S(2)}, u32[]{:S(2)}) collective-permute-start(bf16[128,1024]{1,0:T(8,128)(2,1)S(1)} %constant_dynamic-update-slice_fusion.refs_0_), channel_id=1, source_target_pairs={{0,1},{1,0},{2,3},{3,2},{4,5},{5,4},{6,7},{7,6},{8,9},{9,8},{10,11... | collective-permute-start | bytes 786440 | tf_op jit(solution)/shard_map/ppermute | solution.py:201
  23.4 0.9 %collective-permute-start.10 = (bf16[128,1024]{1,0:T(8,128)(2,1)S(1)}, bf16[128,1024]{1,0:T(8,128)(2,1)S(1)}, u32[]{:S(2)}, u32[]{:S(2)}) collective-permute-start(bf16[128,1024]{1,0:T(8,128)(2,1)S(1)} %constant_dynamic-update-slice_fusion.5.refs_0_), channel_id=1, source_target_pairs={{0,4},{2,6},{4,0},{6,2},{8,12},{10,14},{12,8},{14,10},{16,20},{18,... | collective-permute-start | bytes 786440 | tf_op jit(solution)/shard_map/ppermute | solution.py:201
  24.3 0.0 collective-permute-done.1.sq_ref
  24.3 0.0 collective-permute-done.2.sg_ref
  24.3 3.4 %shard_map.75 = (bf16[256,4096]{1,0:T(8,128)(2,1)}, bf16[256,4096]{1,0:T(8,128)(2,1)}, bf16[256,2048]{1,0:T(8,128)(2,1)S(1)}, f32[128,1024]{1,0:T(8,128)S(1)}) custom-call(bf16[256,4096]{1,0:T(8,128)(2,1)} %q_ref.5, bf16[256,4096]{1,0:T(8,128)(2,1)} %g_ref.5, bf16[256,4096]{1,0:T(8,128)(2,1)S(1)} %collective-permute-done.1.sq_ref, ...), custom_call_target="tpu_custom_call" | custom-call | flops 402653184 | bytes 2097152 | tf_op jit(solution)/shard_map/pallas_call | solution.py:140
  27.7 0.5 collective-permute-done.8.refs_0_
  28.2 3.4 %shard_map.76 = (bf16[256,4096]{1,0:T(8,128)(2,1)}, bf16[256,4096]{1,0:T(8,128)(2,1)}, bf16[256,2048]{1,0:T(8,128)(2,1)S(1)}, bf16[128,1024]{1,0:T(8,128)(2,1)S(1)}) custom-call(bf16[256,4096]{1,0:T(8,128)(2,1)} %q_ref.5, bf16[256,4096]{1,0:T(8,128)(2,1)} %g_ref.5, ...), custom_call_target="tpu_custom_call", output_to_operand_aliasing={{0}: (5, {}), {1}: (6, {}), {2}: (7, {})} | custom-call | flops 402653184 | bytes 2097152 | tf_op jit(solution)/shard_map/pallas_call | solution.py:140
  31.7 1.6 %collective-permute-start.9 = (bf16[128,1024]{1,0:T(8,128)(2,1)S(1)}, bf16[128,1024]{1,0:T(8,128)(2,1)S(1)}, u32[]{:S(2)}, u32[]{:S(2)}) collective-permute-start(bf16[128,1024]{1,0:T(8,128)(2,1)S(1)} %get-tuple-element.43), channel_id=1, source_target_pairs={{0,1},{1,0},{2,3},{3,2},{4,5},{5,4},{6,7},{7,6},{8,9},{9,8},{10,11... | collective-permute-start | bytes 786440 | tf_op jit(solution)/shard_map/ppermute | solution.py:201
  33.2 0.0 collective-permute-done.10.refs_1_
  33.3 5.7 %shard_map.77 = (bf16[256,4096]{1,0:T(8,128)(2,1)}, bf16[256,4096]{1,0:T(8,128)(2,1)}, bf16[256,2048]{1,0:T(8,128)(2,1)S(1)}, f32[128,1024]{1,0:T(8,128)S(1)}, bf16[128,1024]{1,0:T(8,128)(2,1)S(1)}) custom-call(bf16[256,4096]{1,0:T(8,128)(2,1)} %q_ref.5, bf16[256,4096]{1,0:T(8,128)(2,1)} %g_ref.5, ...), custom_call_target="tpu_custom_call", output_to_operand_aliasing={{0}: (6, {}), {1}: (7, {})} | custom-call | flops 805306368 | bytes 4194304 | tf_op jit(solution)/shard_map/pallas_call | solution.py:140
  38.9 0.9 %collective-permute-start.11 = (bf16[128,1024]{1,0:T(8,128)(2,1)S(1)}, bf16[128,1024]{1,0:T(8,128)(2,1)S(1)}, u32[]{:S(2)}, u32[]{:S(2)}) collective-permute-start(bf16[128,1024]{1,0:T(8,128)(2,1)S(1)} %get-tuple-element.48), channel_id=1, source_target_pairs={{0,4},{2,6},{4,0},{6,2},{8,12},{10,14},{12,8},{14,10},{16,20},{18,... | collective-permute-start | bytes 786440 | tf_op jit(solution)/shard_map/ppermute | solution.py:201
  39.8 0.0 collective-permute-start.14
  39.8 0.5 collective-permute-start.15
  40.3 0.0 collective-permute-done.9
  40.3 0.1 convert_add_fusion.1
  40.4 6.4 %collective-permute-done.11 = bf16[128,1024]{1,0:T(8,128)(2,1)S(1)} collective-permute-done((bf16[128,1024]{1,0:T(8,128)(2,1)S(1)}, bf16[128,1024]{1,0:T(8,128)(2,1)S(1)}, u32[]{:S(2)}, u32[]{:S(2)}) %collective-permute-start.11) | collective-permute-done | bytes 262176 | tf_op jit(solution)/shard_map/ppermute | solution.py:201
  46.8 0.1 convert_add_fusion
  46.9 0.9 %collective-permute-start.12 = (bf16[64,1024]{1,0:T(8,128)(2,1)S(1)}, bf16[64,1024]{1,0:T(8,128)(2,1)S(1)}, u32[]{:S(2)}, u32[]{:S(2)}) collective-permute-start(bf16[64,1024]{1,0:T(8,128)(2,1)S(1)} %slice.176), channel_id=1, source_target_pairs={{0,4},{2,6},{4,0},{6,2},{8,12},{10,14},{12,8},{14,10},{16,20},{18,... | collective-permute-start | bytes 393224 | tf_op jit(solution)/shard_map/ppermute | solution.py:201
  47.8 0.6 collective-permute-start.13
  48.3 3.5 %collective-permute-done.12 = bf16[64,1024]{1,0:T(8,128)(2,1)S(1)} collective-permute-done((bf16[64,1024]{1,0:T(8,128)(2,1)S(1)}, bf16[64,1024]{1,0:T(8,128)(2,1)S(1)}, u32[]{:S(2)}, u32[]{:S(2)}) %collective-permute-start.12) | collective-permute-done | bytes 131104 | tf_op jit(solution)/shard_map/ppermute | solution.py:201
  51.9 0.9 %collective-permute-done.13 = bf16[64,1024]{1,0:T(8,128)(2,1)S(1)} collective-permute-done((bf16[64,1024]{1,0:T(8,128)(2,1)S(1)}, bf16[64,1024]{1,0:T(8,128)(2,1)S(1)}, u32[]{:S(2)}, u32[]{:S(2)}) %collective-permute-start.13) | collective-permute-done | bytes 131104 | tf_op jit(solution)/shard_map/ppermute | solution.py:201
  52.8 0.0 collective-permute-done.14.refs_0_
  52.8 0.0 collective-permute-done.15.refs_1_
  53.0 0.6 collective-permute-start.16
  53.6 2.9 %collective-permute-start.17 = (bf16[16,2048]{1,0:T(8,128)(2,1)S(1)}, bf16[16,2048]{1,0:T(8,128)(2,1)S(1)}, u32[]{:S(2)}, u32[]{:S(2)}) collective-permute-start(bf16[16,2048]{1,0:T(8,128)(2,1)S(1)} %get-tuple-element.67), channel_id=1, source_target_pairs={{0,16},{2,18},{4,20},{6,22},{8,24},{10,26},{12,28},{14,30},{16,0},... | collective-permute-start | bytes 196616 | tf_op jit(solution)/shard_map/ppermute | solution.py:201
  56.4 1.0 %collective-permute-start.18 = (bf16[16,2048]{1,0:T(8,128)(2,1)S(1)}, bf16[16,2048]{1,0:T(8,128)(2,1)S(1)}, u32[]{:S(2)}, u32[]{:S(2)}) collective-permute-start(bf16[16,2048]{1,0:T(8,128)(2,1)S(1)} %get-tuple-element.66), channel_id=1, source_target_pairs={{0,24},{2,26},{4,28},{6,30},{8,16},{10,18},{12,20},{14,22},{16,8},... | collective-permute-start | bytes 196616 | tf_op jit(solution)/shard_map/ppermute | solution.py:201
  57.4 1.4 %shard_map.78 = (bf16[256,4096]{1,0:T(8,128)(2,1)}, bf16[256,4096]{1,0:T(8,128)(2,1)}) custom-call(bf16[256,2048]{1,0:T(8,128)(2,1)S(1)} %collective-permute-done.14.refs_0_, bf16[256,2048]{1,0:T(8,128)(2,1)S(1)} %collective-permute-done.15.refs_1_, bf16[256,4096]{1,0:T(8,128)(2,1)} %get-tuple-element.57.refs_2_, ...), custom_call_target="tpu_custom_call", output_to_operand_aliasing={{0}: (2, {}), {1}: (3, {})} | custom-call | tf_op jit(solution)/shard_map/pallas_call | solution.py:184
  58.8 0.0 collective-permute-done.16
  58.8 3.7 %collective-permute-done.18 = bf16[16,2048]{1,0:T(8,128)(2,1)S(1)} collective-permute-done((bf16[16,2048]{1,0:T(8,128)(2,1)S(1)}, bf16[16,2048]{1,0:T(8,128)(2,1)S(1)}, u32[]{:S(2)}, u32[]{:S(2)}) %collective-permute-start.18) | collective-permute-done | bytes 65568 | tf_op jit(solution)/shard_map/ppermute | solution.py:201
  62.6 0.1 collective-permute-start.19
  62.7 1.1 %collective-permute-done.19 = bf16[8,2048]{1,0:T(8,128)(2,1)S(1)} collective-permute-done((bf16[8,2048]{1,0:T(8,128)(2,1)S(1)}, bf16[8,2048]{1,0:T(8,128)(2,1)S(1)}, u32[]{:S(2)}, u32[]{:S(2)}) %collective-permute-start.19) | collective-permute-done | bytes 32800 | tf_op jit(solution)/shard_map/ppermute | solution.py:201
  63.9 0.6 copy-done.1
  64.5 0.6 copy-done
  (31 shorter events, 0.4 us)
Async XLA Ops:
  1.5 1.4 %collective-permute-start = (bf16[8,2048]{1,0:T(8,128)(2,1)S(1)}, bf16[8,2048]{1,0:T(8,128)(2,1)S(1)}, u32[]{:S(2)}, u32[]{:S(2)}) collective-permute-start(bf16[8,2048]{1,0:T(8,128)(2,1)S(1)} %pad_maximum_fusion.3), channel_id=1, source_target_pairs={{0,2},{2,0},{4,6},{6,4},{8,10},{10,8},{12,14},{14,12},{16,18},{18,... | collective-permute-start | bytes 98312 | tf_op jit(solution)/shard_map/ppermute | solution.py:201
  2.9 21.4 %collective-permute-start.1 = (bf16[256,4096]{1,0:T(8,128)(2,1)}, bf16[256,4096]{1,0:T(8,128)(2,1)S(1)}, u32[]{:S(2)}, u32[]{:S(2)}) collective-permute-start(bf16[256,4096]{1,0:T(8,128)(2,1)} %q_ref.5), channel_id=1, source_target_pairs={{0,2},{2,0},{4,6},{6,4},{8,10},{10,8},{12,14},{14,12},{16,18},{18,... | collective-permute-start | bytes 6291464 | tf_op jit(solution)/shard_map/ppermute | solution.py:201
  3.2 21.1 %collective-permute-start.2 = (bf16[256,4096]{1,0:T(8,128)(2,1)}, bf16[256,4096]{1,0:T(8,128)(2,1)S(1)}, u32[]{:S(2)}, u32[]{:S(2)}) collective-permute-start(bf16[256,4096]{1,0:T(8,128)(2,1)} %g_ref.5), channel_id=1, source_target_pairs={{0,2},{2,0},{4,6},{6,4},{8,10},{10,8},{12,14},{14,12},{16,18},{18,... | collective-permute-start | bytes 6291464 | tf_op jit(solution)/shard_map/ppermute | solution.py:201
  3.4 5.6 %collective-permute-start.3 = (bf16[16,2048]{1,0:T(8,128)(2,1)S(1)}, bf16[16,2048]{1,0:T(8,128)(2,1)S(1)}, u32[]{:S(2)}, u32[]{:S(2)}) collective-permute-start(bf16[16,2048]{1,0:T(8,128)(2,1)S(1)} %pad_maximum_fusion.2), channel_id=1, source_target_pairs={{0,8},{2,10},{4,12},{6,14},{8,0},{10,2},{12,4},{14,6},{16,24},{18,... | collective-permute-start | bytes 196616 | tf_op jit(solution)/shard_map/ppermute | solution.py:201
  6.3 7.6 %collective-permute-start.4 = (bf16[16,2048]{1,0:T(8,128)(2,1)S(1)}, bf16[16,2048]{1,0:T(8,128)(2,1)S(1)}, u32[]{:S(2)}, u32[]{:S(2)}) collective-permute-start(bf16[16,2048]{1,0:T(8,128)(2,1)S(1)} %pad_maximum_fusion.2), channel_id=1, source_target_pairs={{0,16},{2,18},{4,20},{6,22},{8,24},{10,26},{12,28},{14,30},{16,0},... | collective-permute-start | bytes 196616 | tf_op jit(solution)/shard_map/ppermute | solution.py:201
  9.0 6.2 %collective-permute-start.5 = (bf16[16,2048]{1,0:T(8,128)(2,1)S(1)}, bf16[16,2048]{1,0:T(8,128)(2,1)S(1)}, u32[]{:S(2)}, u32[]{:S(2)}) collective-permute-start(bf16[16,2048]{1,0:T(8,128)(2,1)S(1)} %pad_maximum_fusion.2), channel_id=1, source_target_pairs={{0,24},{2,26},{4,28},{6,30},{8,16},{10,18},{12,20},{14,22},{16,8},... | collective-permute-start | bytes 196616 | tf_op jit(solution)/shard_map/ppermute | solution.py:201
  15.2 5.0 %collective-permute-start.6 = (bf16[64,1024]{1,0:T(8,128)(2,1)S(1)}, bf16[64,1024]{1,0:T(8,128)(2,1)S(1)}, u32[]{:S(2)}, u32[]{:S(2)}) collective-permute-start(bf16[64,1024]{1,0:T(8,128)(2,1)S(1)} %pad_maximum_fusion), channel_id=1, source_target_pairs={{0,4},{2,6},{4,0},{6,2},{8,12},{10,14},{12,8},{14,10},{16,20},{18,... | collective-permute-start | bytes 393224 | tf_op jit(solution)/shard_map/ppermute | solution.py:201
  16.7 5.0 %collective-permute-start.7 = (bf16[64,1024]{1,0:T(8,128)(2,1)S(1)}, bf16[64,1024]{1,0:T(8,128)(2,1)S(1)}, u32[]{:S(2)}, u32[]{:S(2)}) collective-permute-start(bf16[64,1024]{1,0:T(8,128)(2,1)S(1)} %pad_maximum_fusion.1), channel_id=1, source_target_pairs={{0,1},{1,0},{2,3},{3,2},{4,5},{5,4},{6,7},{7,6},{8,9},{9,8},{10,11... | collective-permute-start | bytes 393224 | tf_op jit(solution)/shard_map/ppermute | solution.py:201
  21.8 6.4 %collective-permute-start.8 = (bf16[128,1024]{1,0:T(8,128)(2,1)S(1)}, bf16[128,1024]{1,0:T(8,128)(2,1)S(1)}, u32[]{:S(2)}, u32[]{:S(2)}) collective-permute-start(bf16[128,1024]{1,0:T(8,128)(2,1)S(1)} %constant_dynamic-update-slice_fusion.refs_0_), channel_id=1, source_target_pairs={{0,1},{1,0},{2,3},{3,2},{4,5},{5,4},{6,7},{7,6},{8,9},{9,8},{10,11... | collective-permute-start | bytes 786440 | tf_op jit(solution)/shard_map/ppermute | solution.py:201
  23.4 9.9 %collective-permute-start.10 = (bf16[128,1024]{1,0:T(8,128)(2,1)S(1)}, bf16[128,1024]{1,0:T(8,128)(2,1)S(1)}, u32[]{:S(2)}, u32[]{:S(2)}) collective-permute-start(bf16[128,1024]{1,0:T(8,128)(2,1)S(1)} %constant_dynamic-update-slice_fusion.5.refs_0_), channel_id=1, source_target_pairs={{0,4},{2,6},{4,0},{6,2},{8,12},{10,14},{12,8},{14,10},{16,20},{18,... | collective-permute-start | bytes 786440 | tf_op jit(solution)/shard_map/ppermute | solution.py:201
  31.7 8.7 %collective-permute-start.9 = (bf16[128,1024]{1,0:T(8,128)(2,1)S(1)}, bf16[128,1024]{1,0:T(8,128)(2,1)S(1)}, u32[]{:S(2)}, u32[]{:S(2)}) collective-permute-start(bf16[128,1024]{1,0:T(8,128)(2,1)S(1)} %get-tuple-element.43), channel_id=1, source_target_pairs={{0,1},{1,0},{2,3},{3,2},{4,5},{5,4},{6,7},{7,6},{8,9},{9,8},{10,11... | collective-permute-start | bytes 786440 | tf_op jit(solution)/shard_map/ppermute | solution.py:201
  38.9 7.8 %collective-permute-start.11 = (bf16[128,1024]{1,0:T(8,128)(2,1)S(1)}, bf16[128,1024]{1,0:T(8,128)(2,1)S(1)}, u32[]{:S(2)}, u32[]{:S(2)}) collective-permute-start(bf16[128,1024]{1,0:T(8,128)(2,1)S(1)} %get-tuple-element.48), channel_id=1, source_target_pairs={{0,4},{2,6},{4,0},{6,2},{8,12},{10,14},{12,8},{14,10},{16,20},{18,... | collective-permute-start | bytes 786440 | tf_op jit(solution)/shard_map/ppermute | solution.py:201
  39.8 13.0 %collective-permute-start.14 = (bf16[256,2048]{1,0:T(8,128)(2,1)S(1)}, bf16[256,2048]{1,0:T(8,128)(2,1)S(1)}, u32[]{:S(2)}, u32[]{:S(2)}) collective-permute-start(bf16[256,2048]{1,0:T(8,128)(2,1)S(1)} %get-tuple-element.51), channel_id=1, source_target_pairs={{0,2},{2,0},{4,6},{6,4},{8,10},{10,8},{12,14},{14,12},{16,18},{18,... | collective-permute-start | bytes 3145736 | tf_op jit(solution)/shard_map/ppermute | solution.py:201
  39.8 13.0 %collective-permute-start.15 = (bf16[256,2048]{1,0:T(8,128)(2,1)S(1)}, bf16[256,2048]{1,0:T(8,128)(2,1)S(1)}, u32[]{:S(2)}, u32[]{:S(2)}) collective-permute-start(bf16[256,2048]{1,0:T(8,128)(2,1)S(1)} %get-tuple-element.52), channel_id=1, source_target_pairs={{0,2},{2,0},{4,6},{6,4},{8,10},{10,8},{12,14},{14,12},{16,18},{18,... | collective-permute-start | bytes 3145736 | tf_op jit(solution)/shard_map/ppermute | solution.py:201
  46.9 5.0 %collective-permute-start.12 = (bf16[64,1024]{1,0:T(8,128)(2,1)S(1)}, bf16[64,1024]{1,0:T(8,128)(2,1)S(1)}, u32[]{:S(2)}, u32[]{:S(2)}) collective-permute-start(bf16[64,1024]{1,0:T(8,128)(2,1)S(1)} %slice.176), channel_id=1, source_target_pairs={{0,4},{2,6},{4,0},{6,2},{8,12},{10,14},{12,8},{14,10},{16,20},{18,... | collective-permute-start | bytes 393224 | tf_op jit(solution)/shard_map/ppermute | solution.py:201
  47.8 5.0 %collective-permute-start.13 = (bf16[64,1024]{1,0:T(8,128)(2,1)S(1)}, bf16[64,1024]{1,0:T(8,128)(2,1)S(1)}, u32[]{:S(2)}, u32[]{:S(2)}) collective-permute-start(bf16[64,1024]{1,0:T(8,128)(2,1)S(1)} %slice.175), channel_id=1, source_target_pairs={{0,1},{1,0},{2,3},{3,2},{4,5},{5,4},{6,7},{7,6},{8,9},{9,8},{10,11... | collective-permute-start | bytes 393224 | tf_op jit(solution)/shard_map/ppermute | solution.py:201
  53.0 5.8 %collective-permute-start.16 = (bf16[16,2048]{1,0:T(8,128)(2,1)S(1)}, bf16[16,2048]{1,0:T(8,128)(2,1)S(1)}, u32[]{:S(2)}, u32[]{:S(2)}) collective-permute-start(bf16[16,2048]{1,0:T(8,128)(2,1)S(1)} %get-tuple-element.68), channel_id=1, source_target_pairs={{0,8},{2,10},{4,12},{6,14},{8,0},{10,2},{12,4},{14,6},{16,24},{18,... | collective-permute-start | bytes 196616 | tf_op jit(solution)/shard_map/ppermute | solution.py:201
  53.6 5.2 %collective-permute-start.17 = (bf16[16,2048]{1,0:T(8,128)(2,1)S(1)}, bf16[16,2048]{1,0:T(8,128)(2,1)S(1)}, u32[]{:S(2)}, u32[]{:S(2)}) collective-permute-start(bf16[16,2048]{1,0:T(8,128)(2,1)S(1)} %get-tuple-element.67), channel_id=1, source_target_pairs={{0,16},{2,18},{4,20},{6,22},{8,24},{10,26},{12,28},{14,30},{16,0},... | collective-permute-start | bytes 196616 | tf_op jit(solution)/shard_map/ppermute | solution.py:201
  56.4 6.1 %collective-permute-start.18 = (bf16[16,2048]{1,0:T(8,128)(2,1)S(1)}, bf16[16,2048]{1,0:T(8,128)(2,1)S(1)}, u32[]{:S(2)}, u32[]{:S(2)}) collective-permute-start(bf16[16,2048]{1,0:T(8,128)(2,1)S(1)} %get-tuple-element.66), channel_id=1, source_target_pairs={{0,24},{2,26},{4,28},{6,30},{8,16},{10,18},{12,20},{14,22},{16,8},... | collective-permute-start | bytes 196616 | tf_op jit(solution)/shard_map/ppermute | solution.py:201
  62.6 1.3 %collective-permute-start.19 = (bf16[8,2048]{1,0:T(8,128)(2,1)S(1)}, bf16[8,2048]{1,0:T(8,128)(2,1)S(1)}, u32[]{:S(2)}, u32[]{:S(2)}) collective-permute-start(bf16[8,2048]{1,0:T(8,128)(2,1)S(1)} %slice.153), channel_id=1, source_target_pairs={{0,2},{2,0},{4,6},{6,4},{8,10},{10,8},{12,14},{14,12},{16,18},{18,... | collective-permute-start | bytes 98312 | tf_op jit(solution)/shard_map/ppermute | solution.py:201
  63.9 0.6 copy-start.1
  64.5 0.6 copy-start

commit v2 on v1

--- a/solution.py
+++ b/solution.py
@@ -52,10 +52,10 @@
 
     def inputs(k, part):
         begin = part * group
-        where = pl.ds(pl.multiple_of(column(rs[0] + k) + begin, group), group)
+        starts = (column(rs[0] + k) + begin, (block * n_mp + rs[0] + k) * width + begin)
         return [
             pltpu.make_async_copy(
-                array.at[:, where],
+                array.at[:, pl.ds(pl.multiple_of(starts[n], group), group)],
                 token_buf.at[k, m, pl.ds(n * count, count), pl.ds(begin, group)],
                 sems.at[0, k, part, m, n],
             )
@@ -157,6 +157,37 @@
     )(*pinned(pltpu.HBM, *tokens[:2]), *tokens[2:], *pinned(pltpu.VMEM, *memory), *earlier)
 
 
+def packing_kernel(n_mp, blocks, q_ref, g_ref, packed_q_ref, packed_g_ref, sems):
+    width = packed_q_ref.shape[1] // (blocks * n_mp)
+    copies = []
+    for block in range(blocks):
+        column = columns(n_mp, blocks, block, width, True)
+        for r in range(n_mp):
+            where = pl.ds((block * n_mp + r) * width, width)
+            for array, packed in ((q_ref, packed_q_ref), (g_ref, packed_g_ref)):
+                copies.append(
+                    pltpu.make_async_copy(
+                        array.at[:, pl.ds(column(r), width)], packed.at[:, where], sems.at[len(copies)]
+                    )
+                )
+    for copy in copies:
+        copy.start()
+    for copy in copies:
+        copy.wait()
+
+
+def packing(n_mp, blocks, queries, grad):
+    rows, whole = queries.shape
+    return pl.pallas_call(
+        functools.partial(packing_kernel, n_mp, blocks),
+        in_specs=[HBM] * 2,
+        out_specs=[VMEM] * 2,
+        out_shape=[pltpu.VMEM((rows, whole // 2), bf16)] * 2,
+        scratch_shapes=[pltpu.SemaphoreType.DMA((2 * blocks * n_mp,))],
+        cost_estimate=pl.CostEstimate(flops=0, bytes_accessed=4 * rows * whole, transcendentals=0),
+    )(*pinned(pltpu.HBM, queries, grad))
+
+
 def placing_kernel(n_mp, blocks, *refs):
     returned_refs, (attended_ref, query_grad_ref, sems) = refs[:blocks], refs[-3:]
     width = returned_refs[0].shape[1] // (2 * n_mp)
@@ -213,11 +244,12 @@
         return jnp.concatenate([b[:, n * block : (n + 1) * block] for n in range(blocks) for b in both], axis=1)
 
     base = jnp.concatenate([packed(core), swap(packed(1 - core), "seq", core_bit)])
-    base, queries_out, grad_out = together(base, queries, output_grad)
-    sibling_queries, sibling_grad = swap(queries_out, "seq", core_bit), swap(grad_out, "seq", core_bit)
-    tokens = (queries, output_grad, sibling_queries, sibling_grad)
-
-    got = [base] + [swap(base, "seq", bits) for bits in z_bits]
+
+    got = [swap(base, "seq", bits) for bits in z_bits]
+    got[0], queries_out, grad_out = together(got[0], queries, output_grad)
+    tokens = (queries, output_grad)
+    tokens += tuple(swap(array, "seq", core_bit) for array in packing(n_mp, blocks, queries_out, grad_out))
+    got = [base] + got
     first, second = (jnp.concatenate([g[:, n * 2 * block : (n + 1) * 2 * block] for g in got]) for n in (0, 1))
 
     def wider(held, got):
@@ -252,13 +284,14 @@
     for bits in y_bits[:0:-1]:
         second = fold(second, "mp", bits)
     first, second = fold(first, "seq", x_bit), fold(second, "mp", y_bits[0])
+    first, second, out_first, out_second = together(first, second, out_first, out_second)
     returned = [swap(out, "seq", core_bit) for out in (out_first, out_second)]
-    first, second, returned = together(first, second, returned)
     total = jnp.concatenate([first, second], axis=1)
-    outputs = placing(n_mp, returned, *outputs)
     count, give = 2 * rows, total.astype(bf16)
     got = [swap(give[n * count : (n + 1) * count], "seq", bits) for n, bits in enumerate(z_bits, 1)]
-    got, outputs = together(got, outputs)
+    got[0], returned = together(got[0], returned)
+    outputs = placing(n_mp, returned, *outputs)
+    got[-1], outputs = together(got[-1], outputs)
     total = (total[:count] + sum(g.astype(f32) for g in got)).astype(bf16)
     mine, other = total[:rows], swap(total[rows:], "seq", core_bit)
 

time: 65.3 us -> 66.6 us (1.020)
  Pallas kernels: 13.9 us -> 15.5 us
  other arithmetic: 0.29 us -> 1.2 us
  starting transfers between devices: 21.2 us -> 20.4 us
    pallas_call x0 -> x1, Pallas kernels: none -> 1.59 us  [packing(): pl.pallas_call(functools.partial(packing_kernel, n_mp, blocks), in_specs=...]
    convert_element_type x1, other arithmetic: 0.03 us -> 0.94 us  [shards(): total = (total[:count] + sum((g.astype(f32) for g in got))).astype(bf16)]
    ppermute x20, starting transfers between devices: 21.2 us -> 20.4 us  [swap(): return lax.ppermute(array, axis, [(i, i ^ bits) for i in range(size)])]
  transfers between devices with their start and end apart: 20 -> 20, of which waited for: 11 -> 13; matrix products, arithmetic and copies ran while one was open for 0% -> 0% of each run, Pallas kernels for 21% -> 23%
where the time goes in v2:
time: 66.6 us; the launch traced here: 66.3 us
  waiting for transfers between devices  26.1 us (39%)
  starting transfers between devices  20.4 us (31%)
  Pallas kernels  15.5 us (23%)
  local copies, waits for them, and re-layouts  2.21 us (3%)
  other arithmetic  1.2 us (2%)
  between operations  0.89 us (1%)
    ppermute x20, waiting for transfers between devices, swap(): return lax.ppermute(array, axis, [(i, i ^ bits) for i in range(size)])  26.1 us
    ppermute x20, starting transfers between devices, swap(): return lax.ppermute(array, axis, [(i, i ^ bits) for i in range(size)])  20.4 us
    pallas_call x3, Pallas kernels, attention(): pl.pallas_call(functools.partial(attention_kernel, n_mp, blocks, block, r...  12.5 us
    pallas_call x1, Pallas kernels, packing(): pl.pallas_call(functools.partial(packing_kernel, n_mp, blocks), in_specs=...  1.59 us
    pallas_call x1, Pallas kernels, placing(): pl.pallas_call(functools.partial(placing_kernel, n_mp, blocks), in_specs=...  1.39 us
  transfers between devices with their start and end apart: 20, of which 13 were waited for; matrix products, arithmetic and copies ran while one was open for 0% of the time, Pallas kernels for 23%

profile of v2, /device:TPU:0, one launch (start us, length us, event | category | flops | bytes accessed | tf_op | source)
XLA Modules:
  0.0 66.3 jit_solution(9433823065958628507)
XLA Ops:
  0.6 0.8 %constant_dynamic-slice_fusion.2 = (bf16[8,512]{1,0:T(8,128)(2,1)S(1)}, bf16[8,512]{1,0:T(8,128)(2,1)S(1)}, bf16[8,512]{1,0:T(8,128)(2,1)S(1)}, bf16[8,512]{1,0:...) fusion(bf16[8,2048]{1,0:T(8,128)(2,1)} %param.6, ...), kind=kLoop, calls=%fused_computation.30 | loop fusion | bytes 131088 | tf_op jit(solution)/shard_map/slice | solution.py:244
  1.5 0.5 collective-permute-start
  2.0 0.9 %collective-permute-done = bf16[8,2048]{1,0:T(8,128)(2,1)S(1)} collective-permute-done((bf16[8,2048]{1,0:T(8,128)(2,1)S(1)}, bf16[8,2048]{1,0:T(8,128)(2,1)S(1)}, u32[]{:S(2)}, u32[]{:S(2)}) %collective-permute-start) | collective-permute-done | bytes 32800 | tf_op jit(solution)/shard_map/ppermute | solution.py:232
  2.9 2.9 %collective-permute-start.1 = (bf16[16,2048]{1,0:T(8,128)(2,1)S(1)}, bf16[16,2048]{1,0:T(8,128)(2,1)S(1)}, u32[]{:S(2)}, u32[]{:S(2)}) collective-permute-start(bf16[16,2048]{1,0:T(8,128)(2,1)S(1)} %pad_maximum_fusion.2), channel_id=1, source_target_pairs={{0,8},{2,10},{4,12},{6,14},{8,0},{10,2},{12,4},{14,6},{16,24},{18,... | collective-permute-start | bytes 196616 | tf_op jit(solution)/shard_map/ppermute | solution.py:232
  5.8 2.7 %collective-permute-start.4 = (bf16[16,2048]{1,0:T(8,128)(2,1)S(1)}, bf16[16,2048]{1,0:T(8,128)(2,1)S(1)}, u32[]{:S(2)}, u32[]{:S(2)}) collective-permute-start(bf16[16,2048]{1,0:T(8,128)(2,1)S(1)} %pad_maximum_fusion.2), channel_id=1, source_target_pairs={{0,16},{2,18},{4,20},{6,22},{8,24},{10,26},{12,28},{14,30},{16,0},... | collective-permute-start | bytes 196616 | tf_op jit(solution)/shard_map/ppermute | solution.py:232
  8.4 0.0 collective-permute-start.5
  8.5 0.0 collective-permute-done.1
  8.5 1.6 %shard_map.75 = (bf16[256,2048]{1,0:T(8,128)(2,1)S(1)}, bf16[256,2048]{1,0:T(8,128)(2,1)S(1)}) custom-call(bf16[256,4096]{1,0:T(8,128)(2,1)} %q_ref.6, bf16[256,4096]{1,0:T(8,128)(2,1)} %g_ref.6), custom_call_target="tpu_custom_call" | custom-call | bytes 4194304 | tf_op jit(solution)/shard_map/pallas_call | solution.py:181
  10.0 0.1 collective-permute-start.2
  10.1 0.5 collective-permute-start.3
  10.6 2.7 %collective-permute-done.4 = bf16[16,2048]{1,0:T(8,128)(2,1)S(1)} collective-permute-done((bf16[16,2048]{1,0:T(8,128)(2,1)S(1)}, bf16[16,2048]{1,0:T(8,128)(2,1)S(1)}, u32[]{:S(2)}, u32[]{:S(2)}) %collective-permute-start.4) | collective-permute-done | bytes 65568 | tf_op jit(solution)/shard_map/ppermute | solution.py:232
  13.4 1.2 %collective-permute-done.5 = bf16[16,2048]{1,0:T(8,128)(2,1)S(1)} collective-permute-done((bf16[16,2048]{1,0:T(8,128)(2,1)S(1)}, bf16[16,2048]{1,0:T(8,128)(2,1)S(1)}, u32[]{:S(2)}, u32[]{:S(2)}) %collective-permute-start.5) | collective-permute-done | bytes 65568 | tf_op jit(solution)/shard_map/ppermute | solution.py:232
  14.7 1.6 %collective-permute-start.6 = (bf16[64,1024]{1,0:T(8,128)(2,1)S(1)}, bf16[64,1024]{1,0:T(8,128)(2,1)S(1)}, u32[]{:S(2)}, u32[]{:S(2)}) collective-permute-start(bf16[64,1024]{1,0:T(8,128)(2,1)S(1)} %pad_maximum_fusion), channel_id=1, source_target_pairs={{0,4},{2,6},{4,0},{6,2},{8,12},{10,14},{12,8},{14,10},{16,20},{18,... | collective-permute-start | bytes 393224 | tf_op jit(solution)/shard_map/ppermute | solution.py:232
  16.2 1.6 %collective-permute-start.7 = (bf16[64,1024]{1,0:T(8,128)(2,1)S(1)}, bf16[64,1024]{1,0:T(8,128)(2,1)S(1)}, u32[]{:S(2)}, u32[]{:S(2)}) collective-permute-start(bf16[64,1024]{1,0:T(8,128)(2,1)S(1)} %pad_maximum_fusion.1), channel_id=1, source_target_pairs={{0,1},{1,0},{2,3},{3,2},{4,5},{5,4},{6,7},{7,6},{8,9},{9,8},{10,11... | collective-permute-start | bytes 393224 | tf_op jit(solution)/shard_map/ppermute | solution.py:232
  17.8 1.9 %collective-permute-done.6 = bf16[64,1024]{1,0:T(8,128)(2,1)S(1)} collective-permute-done((bf16[64,1024]{1,0:T(8,128)(2,1)S(1)}, bf16[64,1024]{1,0:T(8,128)(2,1)S(1)}, u32[]{:S(2)}, u32[]{:S(2)}) %collective-permute-start.6) | collective-permute-done | bytes 131104 | tf_op jit(solution)/shard_map/ppermute | solution.py:232
  19.7 1.6 %collective-permute-done.7 = bf16[64,1024]{1,0:T(8,128)(2,1)S(1)} collective-permute-done((bf16[64,1024]{1,0:T(8,128)(2,1)S(1)}, bf16[64,1024]{1,0:T(8,128)(2,1)S(1)}, u32[]{:S(2)}, u32[]{:S(2)}) %collective-permute-start.7) | collective-permute-done | bytes 131104 | tf_op jit(solution)/shard_map/ppermute | solution.py:232
  21.3 1.6 %collective-permute-start.8 = (bf16[128,1024]{1,0:T(8,128)(2,1)S(1)}, bf16[128,1024]{1,0:T(8,128)(2,1)S(1)}, u32[]{:S(2)}, u32[]{:S(2)}) collective-permute-start(bf16[128,1024]{1,0:T(8,128)(2,1)S(1)} %constant_dynamic-update-slice_fusion.refs_0_), channel_id=1, source_target_pairs={{0,1},{1,0},{2,3},{3,2},{4,5},{5,4},{6,7},{7,6},{8,9},{9,8},{10,11... | collective-permute-start | bytes 786440 | tf_op jit(solution)/shard_map/ppermute | solution.py:232
  22.9 0.9 %collective-permute-start.10 = (bf16[128,1024]{1,0:T(8,128)(2,1)S(1)}, bf16[128,1024]{1,0:T(8,128)(2,1)S(1)}, u32[]{:S(2)}, u32[]{:S(2)}) collective-permute-start(bf16[128,1024]{1,0:T(8,128)(2,1)S(1)} %constant_dynamic-update-slice_fusion.5.refs_0_), channel_id=1, source_target_pairs={{0,4},{2,6},{4,0},{6,2},{8,12},{10,14},{12,8},{14,10},{16,20},{18,... | collective-permute-start | bytes 786440 | tf_op jit(solution)/shard_map/ppermute | solution.py:232
  23.8 0.0 collective-permute-done.2.sq_ref
  23.8 0.0 collective-permute-done.3.sg_ref
  23.8 3.4 %shard_map.76 = (bf16[256,4096]{1,0:T(8,128)(2,1)}, bf16[256,4096]{1,0:T(8,128)(2,1)}, bf16[256,2048]{1,0:T(8,128)(2,1)S(1)}, f32[128,1024]{1,0:T(8,128)S(1)}) custom-call(bf16[256,4096]{1,0:T(8,128)(2,1)} %q_ref.6, bf16[256,4096]{1,0:T(8,128)(2,1)} %g_ref.6, bf16[256,2048]{1,0:T(8,128)(2,1)S(1)} %collective-permute-done.2.sq_ref, ...), custom_call_target="tpu_custom_call" | custom-call | flops 402653184 | bytes 2097152 | tf_op jit(solution)/shard_map/pallas_call | solution.py:140
  27.2 0.5 collective-permute-done.8.refs_0_
  27.7 3.4 %shard_map.77 = (bf16[256,4096]{1,0:T(8,128)(2,1)}, bf16[256,4096]{1,0:T(8,128)(2,1)}, bf16[256,2048]{1,0:T(8,128)(2,1)S(1)}, bf16[128,1024]{1,0:T(8,128)(2,1)S(1)}) custom-call(bf16[256,4096]{1,0:T(8,128)(2,1)} %q_ref.6, bf16[256,4096]{1,0:T(8,128)(2,1)} %g_ref.6, ...), custom_call_target="tpu_custom_call", output_to_operand_aliasing={{0}: (5, {}), {1}: (6, {}), {2}: (7, {})} | custom-call | flops 402653184 | bytes 2097152 | tf_op jit(solution)/shard_map/pallas_call | solution.py:140
  31.1 1.6 %collective-permute-start.9 = (bf16[128,1024]{1,0:T(8,128)(2,1)S(1)}, bf16[128,1024]{1,0:T(8,128)(2,1)S(1)}, u32[]{:S(2)}, u32[]{:S(2)}) collective-permute-start(bf16[128,1024]{1,0:T(8,128)(2,1)S(1)} %get-tuple-element.48), channel_id=1, source_target_pairs={{0,1},{1,0},{2,3},{3,2},{4,5},{5,4},{6,7},{7,6},{8,9},{9,8},{10,11... | collective-permute-start | bytes 786440 | tf_op jit(solution)/shard_map/ppermute | solution.py:232
  32.7 5.7 %shard_map.78 = (bf16[256,4096]{1,0:T(8,128)(2,1)}, bf16[256,4096]{1,0:T(8,128)(2,1)}, bf16[256,2048]{1,0:T(8,128)(2,1)S(1)}, f32[128,1024]{1,0:T(8,128)S(1)}, bf16[128,1024]{1,0:T(8,128)(2,1)S(1)}) custom-call(bf16[256,4096]{1,0:T(8,128)(2,1)} %q_ref.6, bf16[256,4096]{1,0:T(8,128)(2,1)} %g_ref.6, ...), custom_call_target="tpu_custom_call", output_to_operand_aliasing={{0}: (6, {}), {1}: (7, {})} | custom-call | flops 805306368 | bytes 4194304 | tf_op jit(solution)/shard_map/pallas_call | solution.py:140
  38.4 0.9 %collective-permute-start.11 = (bf16[128,1024]{1,0:T(8,128)(2,1)S(1)}, bf16[128,1024]{1,0:T(8,128)(2,1)S(1)}, u32[]{:S(2)}, u32[]{:S(2)}) collective-permute-start(bf16[128,1024]{1,0:T(8,128)(2,1)S(1)} %get-tuple-element.53), channel_id=1, source_target_pairs={{0,4},{2,6},{4,0},{6,2},{8,12},{10,14},{12,8},{14,10},{16,20},{18,... | collective-permute-start | bytes 786440 | tf_op jit(solution)/shard_map/ppermute | solution.py:232
  39.3 0.1 convert_add_fusion.1
  39.4 6.9 %collective-permute-done.11 = bf16[128,1024]{1,0:T(8,128)(2,1)S(1)} collective-permute-done((bf16[128,1024]{1,0:T(8,128)(2,1)S(1)}, bf16[128,1024]{1,0:T(8,128)(2,1)S(1)}, u32[]{:S(2)}, u32[]{:S(2)}) %collective-permute-start.11) | collective-permute-done | bytes 262176 | tf_op jit(solution)/shard_map/ppermute | solution.py:232
  46.3 0.1 convert_add_fusion
  46.3 0.9 %collective-permute-start.12 = (bf16[64,1024]{1,0:T(8,128)(2,1)S(1)}, bf16[64,1024]{1,0:T(8,128)(2,1)S(1)}, u32[]{:S(2)}, u32[]{:S(2)}) collective-permute-start(bf16[64,1024]{1,0:T(8,128)(2,1)S(1)} %slice.176), channel_id=1, source_target_pairs={{0,4},{2,6},{4,0},{6,2},{8,12},{10,14},{12,8},{14,10},{16,20},{18,... | collective-permute-start | bytes 393224 | tf_op jit(solution)/shard_map/ppermute | solution.py:232
  47.2 0.6 collective-permute-start.13
  47.8 3.5 %collective-permute-done.12 = bf16[64,1024]{1,0:T(8,128)(2,1)S(1)} collective-permute-done((bf16[64,1024]{1,0:T(8,128)(2,1)S(1)}, bf16[64,1024]{1,0:T(8,128)(2,1)S(1)}, u32[]{:S(2)}, u32[]{:S(2)}) %collective-permute-start.12) | collective-permute-done | bytes 131104 | tf_op jit(solution)/shard_map/ppermute | solution.py:232
  51.4 0.9 %collective-permute-done.13 = bf16[64,1024]{1,0:T(8,128)(2,1)S(1)} collective-permute-done((bf16[64,1024]{1,0:T(8,128)(2,1)S(1)}, bf16[64,1024]{1,0:T(8,128)(2,1)S(1)}, u32[]{:S(2)}, u32[]{:S(2)}) %collective-permute-start.13) | collective-permute-done | bytes 131104 | tf_op jit(solution)/shard_map/ppermute | solution.py:232
  52.3 0.1 collective-permute-start.16
  52.4 0.5 collective-permute-start.17
  53.0 0.6 collective-permute-start.15
  53.6 2.4 %collective-permute-start.14 = (bf16[16,2048]{1,0:T(8,128)(2,1)S(1)}, bf16[16,2048]{1,0:T(8,128)(2,1)S(1)}, u32[]{:S(2)}, u32[]{:S(2)}) collective-permute-start(bf16[16,2048]{1,0:T(8,128)(2,1)S(1)} %get-tuple-element.74), channel_id=1, source_target_pairs={{0,24},{2,26},{4,28},{6,30},{8,16},{10,18},{12,20},{14,22},{16,8},... | collective-permute-start | bytes 196616 | tf_op jit(solution)/shard_map/ppermute | solution.py:232
  56.1 0.5 collective-permute-start.18
  56.6 0.8 %collective-permute-done.15 = bf16[16,2048]{1,0:T(8,128)(2,1)S(1)} collective-permute-done((bf16[16,2048]{1,0:T(8,128)(2,1)S(1)}, bf16[16,2048]{1,0:T(8,128)(2,1)S(1)}, u32[]{:S(2)}, u32[]{:S(2)}) %collective-permute-start.15) | collective-permute-done | bytes 65568 | tf_op jit(solution)/shard_map/ppermute | solution.py:232
  57.3 0.0 collective-permute-done.17.refs_1_
  57.4 1.4 %shard_map.79 = (bf16[256,4096]{1,0:T(8,128)(2,1)}, bf16[256,4096]{1,0:T(8,128)(2,1)}) custom-call(bf16[256,2048]{1,0:T(8,128)(2,1)S(1)} %collective-permute-done.16.refs_0_, bf16[256,2048]{1,0:T(8,128)(2,1)S(1)} %collective-permute-done.17.refs_1_, bf16[256,4096]{1,0:T(8,128)(2,1)} %get-tuple-element.64.refs_2_, ...), custom_call_target="tpu_custom_call", output_to_operand_aliasing={{0}: (2, {}), {1}: (3, {})} | custom-call | tf_op jit(solution)/shard_map/pallas_call | solution.py:215
  58.8 1.7 %collective-permute-done.14 = bf16[16,2048]{1,0:T(8,128)(2,1)S(1)} collective-permute-done((bf16[16,2048]{1,0:T(8,128)(2,1)S(1)}, bf16[16,2048]{1,0:T(8,128)(2,1)S(1)}, u32[]{:S(2)}, u32[]{:S(2)}) %collective-permute-start.14) | collective-permute-done | bytes 65568 | tf_op jit(solution)/shard_map/ppermute | solution.py:232
  60.5 2.4 %collective-permute-done.18 = bf16[16,2048]{1,0:T(8,128)(2,1)S(1)} collective-permute-done((bf16[16,2048]{1,0:T(8,128)(2,1)S(1)}, bf16[16,2048]{1,0:T(8,128)(2,1)S(1)}, u32[]{:S(2)}, u32[]{:S(2)}) %collective-permute-start.18) | collective-permute-done | bytes 65568 | tf_op jit(solution)/shard_map/ppermute | solution.py:232
  62.9 0.9 %fusion = bf16[16,2048]{1,0:T(8,128)(2,1)S(1)} fusion(f32[64,2048]{1,0:T(8,128)} %copy-done, bf16[16,2048]{1,0:T(8,128)(2,1)S(1)} %collective-permute-done.14, bf16[16,2048]{1,0:T(8,128)(2,1)S(1)} %collective-permute-done.18, bf16[16,2048]{1,0:T(8,128)(2,1)S(1)} %collective-permute-done.15), kind=kLoop, calls=%fused_computation.7 | loop fusion | flops 229376 | bytes 393216 | tf_op jit(solution)/shard_map/convert_element_type | solution.py:295
  63.8 0.1 collective-permute-start.19
  64.0 1.1 %collective-permute-done.19 = bf16[8,2048]{1,0:T(8,128)(2,1)S(1)} collective-permute-done((bf16[8,2048]{1,0:T(8,128)(2,1)S(1)}, bf16[8,2048]{1,0:T(8,128)(2,1)S(1)}, u32[]{:S(2)}, u32[]{:S(2)}) %collective-permute-start.19) | collective-permute-done | bytes 32800 | tf_op jit(solution)/shard_map/ppermute | solution.py:232
  65.1 0.6 copy-done.2
  65.7 0.6 copy-done.1
  (34 shorter events, 0.3 us)
Async XLA Ops:
  1.5 1.4 %collective-permute-start = (bf16[8,2048]{1,0:T(8,128)(2,1)S(1)}, bf16[8,2048]{1,0:T(8,128)(2,1)S(1)}, u32[]{:S(2)}, u32[]{:S(2)}) collective-permute-start(bf16[8,2048]{1,0:T(8,128)(2,1)S(1)} %pad_maximum_fusion.3), channel_id=1, source_target_pairs={{0,2},{2,0},{4,6},{6,4},{8,10},{10,8},{12,14},{14,12},{16,18},{18,... | collective-permute-start | bytes 98312 | tf_op jit(solution)/shard_map/ppermute | solution.py:232
  2.9 5.6 %collective-permute-start.1 = (bf16[16,2048]{1,0:T(8,128)(2,1)S(1)}, bf16[16,2048]{1,0:T(8,128)(2,1)S(1)}, u32[]{:S(2)}, u32[]{:S(2)}) collective-permute-start(bf16[16,2048]{1,0:T(8,128)(2,1)S(1)} %pad_maximum_fusion.2), channel_id=1, source_target_pairs={{0,8},{2,10},{4,12},{6,14},{8,0},{10,2},{12,4},{14,6},{16,24},{18,... | collective-permute-start | bytes 196616 | tf_op jit(solution)/shard_map/ppermute | solution.py:232
  5.8 7.6 %collective-permute-start.4 = (bf16[16,2048]{1,0:T(8,128)(2,1)S(1)}, bf16[16,2048]{1,0:T(8,128)(2,1)S(1)}, u32[]{:S(2)}, u32[]{:S(2)}) collective-permute-start(bf16[16,2048]{1,0:T(8,128)(2,1)S(1)} %pad_maximum_fusion.2), channel_id=1, source_target_pairs={{0,16},{2,18},{4,20},{6,22},{8,24},{10,26},{12,28},{14,30},{16,0},... | collective-permute-start | bytes 196616 | tf_op jit(solution)/shard_map/ppermute | solution.py:232
  8.4 6.2 %collective-permute-start.5 = (bf16[16,2048]{1,0:T(8,128)(2,1)S(1)}, bf16[16,2048]{1,0:T(8,128)(2,1)S(1)}, u32[]{:S(2)}, u32[]{:S(2)}) collective-permute-start(bf16[16,2048]{1,0:T(8,128)(2,1)S(1)} %pad_maximum_fusion.2), channel_id=1, source_target_pairs={{0,24},{2,26},{4,28},{6,30},{8,16},{10,18},{12,20},{14,22},{16,8},... | collective-permute-start | bytes 196616 | tf_op jit(solution)/shard_map/ppermute | solution.py:232
  10.0 13.7 %collective-permute-start.2 = (bf16[256,2048]{1,0:T(8,128)(2,1)S(1)}, bf16[256,2048]{1,0:T(8,128)(2,1)S(1)}, u32[]{:S(2)}, u32[]{:S(2)}) collective-permute-start(bf16[256,2048]{1,0:T(8,128)(2,1)S(1)} %get-tuple-element.40), channel_id=1, source_target_pairs={{0,2},{2,0},{4,6},{6,4},{8,10},{10,8},{12,14},{14,12},{16,18},{18,... | collective-permute-start | bytes 3145736 | tf_op jit(solution)/shard_map/ppermute | solution.py:232
  10.1 13.6 %collective-permute-start.3 = (bf16[256,2048]{1,0:T(8,128)(2,1)S(1)}, bf16[256,2048]{1,0:T(8,128)(2,1)S(1)}, u32[]{:S(2)}, u32[]{:S(2)}) collective-permute-start(bf16[256,2048]{1,0:T(8,128)(2,1)S(1)} %get-tuple-element.41), channel_id=1, source_target_pairs={{0,2},{2,0},{4,6},{6,4},{8,10},{10,8},{12,14},{14,12},{16,18},{18,... | collective-permute-start | bytes 3145736 | tf_op jit(solution)/shard_map/ppermute | solution.py:232
  14.7 5.0 %collective-permute-start.6 = (bf16[64,1024]{1,0:T(8,128)(2,1)S(1)}, bf16[64,1024]{1,0:T(8,128)(2,1)S(1)}, u32[]{:S(2)}, u32[]{:S(2)}) collective-permute-start(bf16[64,1024]{1,0:T(8,128)(2,1)S(1)} %pad_maximum_fusion), channel_id=1, source_target_pairs={{0,4},{2,6},{4,0},{6,2},{8,12},{10,14},{12,8},{14,10},{16,20},{18,... | collective-permute-start | bytes 393224 | tf_op jit(solution)/shard_map/ppermute | solution.py:232
  16.2 5.0 %collective-permute-start.7 = (bf16[64,1024]{1,0:T(8,128)(2,1)S(1)}, bf16[64,1024]{1,0:T(8,128)(2,1)S(1)}, u32[]{:S(2)}, u32[]{:S(2)}) collective-permute-start(bf16[64,1024]{1,0:T(8,128)(2,1)S(1)} %pad_maximum_fusion.1), channel_id=1, source_target_pairs={{0,1},{1,0},{2,3},{3,2},{4,5},{5,4},{6,7},{7,6},{8,9},{9,8},{10,11... | collective-permute-start | bytes 393224 | tf_op jit(solution)/shard_map/ppermute | solution.py:232
  21.3 6.4 %collective-permute-start.8 = (bf16[128,1024]{1,0:T(8,128)(2,1)S(1)}, bf16[128,1024]{1,0:T(8,128)(2,1)S(1)}, u32[]{:S(2)}, u32[]{:S(2)}) collective-permute-start(bf16[128,1024]{1,0:T(8,128)(2,1)S(1)} %constant_dynamic-update-slice_fusion.refs_0_), channel_id=1, source_target_pairs={{0,1},{1,0},{2,3},{3,2},{4,5},{5,4},{6,7},{7,6},{8,9},{9,8},{10,11... | collective-permute-start | bytes 786440 | tf_op jit(solution)/shard_map/ppermute | solution.py:232
  22.9 9.9 %collective-permute-start.10 = (bf16[128,1024]{1,0:T(8,128)(2,1)S(1)}, bf16[128,1024]{1,0:T(8,128)(2,1)S(1)}, u32[]{:S(2)}, u32[]{:S(2)}) collective-permute-start(bf16[128,1024]{1,0:T(8,128)(2,1)S(1)} %constant_dynamic-update-slice_fusion.5.refs_0_), channel_id=1, source_target_pairs={{0,4},{2,6},{4,0},{6,2},{8,12},{10,14},{12,8},{14,10},{16,20},{18,... | collective-permute-start | bytes 786440 | tf_op jit(solution)/shard_map/ppermute | solution.py:232
  31.1 8.2 %collective-permute-start.9 = (bf16[128,1024]{1,0:T(8,128)(2,1)S(1)}, bf16[128,1024]{1,0:T(8,128)(2,1)S(1)}, u32[]{:S(2)}, u32[]{:S(2)}) collective-permute-start(bf16[128,1024]{1,0:T(8,128)(2,1)S(1)} %get-tuple-element.48), channel_id=1, source_target_pairs={{0,1},{1,0},{2,3},{3,2},{4,5},{5,4},{6,7},{7,6},{8,9},{9,8},{10,11... | collective-permute-start | bytes 786440 | tf_op jit(solution)/shard_map/ppermute | solution.py:232
  38.4 7.8 %collective-permute-start.11 = (bf16[128,1024]{1,0:T(8,128)(2,1)S(1)}, bf16[128,1024]{1,0:T(8,128)(2,1)S(1)}, u32[]{:S(2)}, u32[]{:S(2)}) collective-permute-start(bf16[128,1024]{1,0:T(8,128)(2,1)S(1)} %get-tuple-element.53), channel_id=1, source_target_pairs={{0,4},{2,6},{4,0},{6,2},{8,12},{10,14},{12,8},{14,10},{16,20},{18,... | collective-permute-start | bytes 786440 | tf_op jit(solution)/shard_map/ppermute | solution.py:232
  46.3 5.0 %collective-permute-start.12 = (bf16[64,1024]{1,0:T(8,128)(2,1)S(1)}, bf16[64,1024]{1,0:T(8,128)(2,1)S(1)}, u32[]{:S(2)}, u32[]{:S(2)}) collective-permute-start(bf16[64,1024]{1,0:T(8,128)(2,1)S(1)} %slice.176), channel_id=1, source_target_pairs={{0,4},{2,6},{4,0},{6,2},{8,12},{10,14},{12,8},{14,10},{16,20},{18,... | collective-permute-start | bytes 393224 | tf_op jit(solution)/shard_map/ppermute | solution.py:232
  47.2 5.0 %collective-permute-start.13 = (bf16[64,1024]{1,0:T(8,128)(2,1)S(1)}, bf16[64,1024]{1,0:T(8,128)(2,1)S(1)}, u32[]{:S(2)}, u32[]{:S(2)}) collective-permute-start(bf16[64,1024]{1,0:T(8,128)(2,1)S(1)} %slice.175), channel_id=1, source_target_pairs={{0,1},{1,0},{2,3},{3,2},{4,5},{5,4},{6,7},{7,6},{8,9},{9,8},{10,11... | collective-permute-start | bytes 393224 | tf_op jit(solution)/shard_map/ppermute | solution.py:232
  52.3 5.0 %collective-permute-start.16 = (bf16[256,2048]{1,0:T(8,128)(2,1)S(1)}, bf16[256,2048]{1,0:T(8,128)(2,1)S(1)}, u32[]{:S(2)}, u32[]{:S(2)}) collective-permute-start(bf16[256,2048]{1,0:T(8,128)(2,1)S(1)} %get-tuple-element.60), channel_id=1, source_target_pairs={{0,2},{2,0},{4,6},{6,4},{8,10},{10,8},{12,14},{14,12},{16,18},{18,... | collective-permute-start | bytes 3145736 | tf_op jit(solution)/shard_map/ppermute | solution.py:232
  52.4 5.0 %collective-permute-start.17 = (bf16[256,2048]{1,0:T(8,128)(2,1)S(1)}, bf16[256,2048]{1,0:T(8,128)(2,1)S(1)}, u32[]{:S(2)}, u32[]{:S(2)}) collective-permute-start(bf16[256,2048]{1,0:T(8,128)(2,1)S(1)} %get-tuple-element.61), channel_id=1, source_target_pairs={{0,2},{2,0},{4,6},{6,4},{8,10},{10,8},{12,14},{14,12},{16,18},{18,... | collective-permute-start | bytes 3145736 | tf_op jit(solution)/shard_map/ppermute | solution.py:232
  52.9 4.4 %copy-start = (f32[64,2048]{1,0:T(8,128)}, f32[64,2048]{1,0:T(8,128)S(1)}, u32[]{:S(2)}) copy-start(f32[64,2048]{1,0:T(8,128)S(1)} %constant_dynamic-update-slice_fusion.10) | copy-start | bytes 1572868
  53.0 4.3 %collective-permute-start.15 = (bf16[16,2048]{1,0:T(8,128)(2,1)S(1)}, bf16[16,2048]{1,0:T(8,128)(2,1)S(1)}, u32[]{:S(2)}, u32[]{:S(2)}) collective-permute-start(bf16[16,2048]{1,0:T(8,128)(2,1)S(1)} %get-tuple-element.73), channel_id=1, source_target_pairs={{0,8},{2,10},{4,12},{6,14},{8,0},{10,2},{12,4},{14,6},{16,24},{18,... | collective-permute-start | bytes 196616 | tf_op jit(solution)/shard_map/ppermute | solution.py:232
  53.6 6.9 %collective-permute-start.14 = (bf16[16,2048]{1,0:T(8,128)(2,1)S(1)}, bf16[16,2048]{1,0:T(8,128)(2,1)S(1)}, u32[]{:S(2)}, u32[]{:S(2)}) collective-permute-start(bf16[16,2048]{1,0:T(8,128)(2,1)S(1)} %get-tuple-element.74), channel_id=1, source_target_pairs={{0,24},{2,26},{4,28},{6,30},{8,16},{10,18},{12,20},{14,22},{16,8},... | collective-permute-start | bytes 196616 | tf_op jit(solution)/shard_map/ppermute | solution.py:232
  56.1 6.8 %collective-permute-start.18 = (bf16[16,2048]{1,0:T(8,128)(2,1)S(1)}, bf16[16,2048]{1,0:T(8,128)(2,1)S(1)}, u32[]{:S(2)}, u32[]{:S(2)}) collective-permute-start(bf16[16,2048]{1,0:T(8,128)(2,1)S(1)} %get-tuple-element.72), channel_id=1, source_target_pairs={{0,16},{2,18},{4,20},{6,22},{8,24},{10,26},{12,28},{14,30},{16,0},... | collective-permute-start | bytes 196616 | tf_op jit(solution)/shard_map/ppermute | solution.py:232
  63.8 1.3 %collective-permute-start.19 = (bf16[8,2048]{1,0:T(8,128)(2,1)S(1)}, bf16[8,2048]{1,0:T(8,128)(2,1)S(1)}, u32[]{:S(2)}, u32[]{:S(2)}) collective-permute-start(bf16[8,2048]{1,0:T(8,128)(2,1)S(1)} %slice.153), channel_id=1, source_target_pairs={{0,2},{2,0},{4,6},{6,4},{8,10},{10,8},{12,14},{14,12},{16,18},{18,... | collective-permute-start | bytes 98312 | tf_op jit(solution)/shard_map/ppermute | solution.py:232
  65.1 0.6 copy-start.2
  65.7 0.6 copy-start.1

commit v3 on v1

--- a/solution.py
+++ b/solution.py
@@ -42,49 +42,37 @@
     (attended_ref, query_grad_ref, sibling_ref), term_refs = refs[:3], refs[3:-7]
     token_buf, result_buf, raw_ref, prob_ref, grad_ref, weight_ref, sems = refs[-7:]
     count, width = q_ref.shape[0], term_refs[0].shape[1] // 2
-    heads, group = width // DH, min(2 * DH, width)
-    parts = width // group
+    heads = width // DH
     size = memory_refs[0].shape[0] // len(rs)
     column = columns(n_mp, blocks, block, width, False)
     step = min(DH, 2 * count)
     cols = [slice(n * DH, (n + 1) * DH) for n in range(heads)]
     targets = [[slice(m * width + n * DH, m * width + (n + 1) * DH) for n in range(heads)] for m in (0, 1)]
 
-    def inputs(k, part):
-        begin = part * group
-        where = pl.ds(pl.multiple_of(column(rs[0] + k) + begin, group), group)
+    def inputs(k):
         return [
             pltpu.make_async_copy(
-                array.at[:, where],
-                token_buf.at[k, m, pl.ds(n * count, count), pl.ds(begin, group)],
-                sems.at[0, k, part, m, n],
+                array.at[:, pl.ds(column(rs[0] + k), width)],
+                token_buf.at[k, m, pl.ds(n * count, count)],
+                sems.at[0, k, m, n],
             )
             for m, pair in enumerate(((q_ref, sq_ref), (g_ref, sg_ref)))
             for n, array in enumerate(pair)
         ]
 
-    def outputs(k, part):
-        begin = part * group
+    def outputs(k):
         copies = []
         for m, own in enumerate((query_grad_ref, attended_ref)):
-            starts = (column(rs[0] + k), (2 * (rs[0] + k) + m) * width)
+            starts = (column(rs[0] + k), pl.multiple_of((2 * (rs[0] + k) + m) * width, width))
             for n, (array, start) in enumerate(zip((own, sibling_ref), starts)):
                 copies.append(
                     pltpu.make_async_copy(
-                        result_buf.at[k, m, pl.ds(n * count, count), pl.ds(begin, group)],
-                        array.at[:, pl.ds(pl.multiple_of(start + begin, group), group)],
-                        sems.at[1, k, part, m, n],
+                        result_buf.at[k, m, pl.ds(n * count, count)],
+                        array.at[:, pl.ds(start, width)],
+                        sems.at[1, k, m, n],
                     )
                 )
         return copies
-
-    def every(action):
-        def at(k, _):
-            for part in range(parts):
-                for copy in action(k, part):
-                    copy()
-
-        repeat(at)
 
     def repeat(body):
         if len(rs) == 1:
@@ -92,34 +80,55 @@
         else:
             lax.fori_loop(0, len(rs), body, None)
 
+    def start_inputs(k, _):
+        for copy in inputs(k):
+            copy.start()
+
+    def wait_outputs(k, _):
+        for copy in outputs(k):
+            copy.wait()
+
     def work(k, _):
         rows = pl.ds(pl.multiple_of(k * size, size), size)
         memory = [[jnp.concatenate([ref[rows, t] for ref in memory_refs], axis=0) for t in row] for row in targets]
-        for n in range(heads):
-            if n * DH % group == 0:
-                for copy in inputs(k, n * DH // group):
-                    copy.wait()
+
+        def scores(n):
             raw_ref[n] = dot(memory[0][n], token_buf[k, 0, :, cols[n]], NT)
             prob_ref[n] = dot(memory[1][n], token_buf[k, 1, :, cols[n]], NT)
-        for n in range(heads):
+
+        def softmax(n):
             for begin in range(0, 2 * count, step):
                 part = slice(begin, begin + step)
                 grad_ref[n, :, part], weight_ref[n, :, part] = softmax_part(raw_ref[n, :, part], prob_ref[n, :, part])
-        for n in range(heads):
+
+        def results(n):
             for m, pair_ref in enumerate((grad_ref, weight_ref)):
                 result_buf[k, m, :, cols[n]] = dot(memory[m][n].T, pair_ref[n], NN).astype(bf16).T
-            if (n + 1) * DH % group == 0:
-                for copy in outputs(k, n * DH // group):
-                    copy.start()
-        for n in range(heads):
+
+        def terms(n):
             for m, pair_ref in enumerate((grad_ref, weight_ref)):
                 term = dot(pair_ref[n], token_buf[k, m, :, cols[n]], NN)
                 for i, term_ref in enumerate(term_refs):
                     term_ref[rows, targets[m][n]] = term[i * size : (i + 1) * size].astype(term_ref.dtype)
 
-    every(lambda k, part: [copy.start for copy in inputs(k, part)])
+        for copy in inputs(k):
+            copy.wait()
+        for n in range(heads + 2):
+            if n < heads:
+                scores(n)
+            if 1 <= n <= heads:
+                softmax(n - 1)
+            if n >= 2:
+                results(n - 2)
+                if n <= heads:
+                    terms(n - 2)
+        for copy in outputs(k):
+            copy.start()
+        terms(heads - 1)
+
+    repeat(start_inputs)
     repeat(work)
-    every(lambda k, part: [copy.wait for copy in outputs(k, part)])
+    repeat(wait_outputs)
 
 
 def pinned(space, *arrays):
@@ -133,7 +142,6 @@
     rows, whole = tokens[0].shape
     width = memory[0].shape[1] // 2
     count = sum(m.shape[0] for m in memory) // len(rs)
-    group = min(2 * DH, width)
     scratch = (width // DH, count, 2 * rows)
     earlier = [*outputs] + ([] if sent is None else [sent])
     first = 4 + len(memory)
@@ -146,7 +154,7 @@
         + [pltpu.VMEM(m.shape, t) for m, t in zip(memory, types)],
         scratch_shapes=[pltpu.VMEM((len(rs), 2, 2 * rows, width), bf16)] * 2
         + [pltpu.VMEM(scratch, t) for t in (f32, f32, bf16, bf16)]
-        + [pltpu.SemaphoreType.DMA((2, len(rs), width // group, 2, 2))],
+        + [pltpu.SemaphoreType.DMA((2, len(rs), 2, 2))],
         input_output_aliases={first + n: n for n in range(len(earlier))},
         compiler_params=pltpu.CompilerParams(vmem_limit_bytes=32 * 1024 * 1024),
         cost_estimate=pl.CostEstimate(
@@ -241,7 +249,9 @@
         n_mp, blocks, 1, range(n_mp), tokens, [second, second_got], [f32, bf16], outputs, None
     )
     second_got = swap(give, "seq", x_bit)
-    first, second = together(first_keep + first_got.astype(f32), second_keep + second_got.astype(f32))
+    first, second, out_first, out_second = together(
+        first_keep + first_got.astype(f32), second_keep + second_got.astype(f32), out_first, out_second
+    )
 
     def fold(total, axis, bits):
         middle = total.shape[0] // 2

time: 65.3 us -> 63.5 us (0.972)
  Pallas kernels: 13.9 us -> 12.3 us
    pallas_call x3, Pallas kernels: 12.5 us -> 11 us  [attention(): pl.pallas_call(functools.partial(attention_kernel, n_mp, blocks, block, r...]
  transfers between devices with their start and end apart: 20 -> 20, of which waited for: 11 -> 11; matrix products, arithmetic and copies ran while one was open for 0% -> 0% of each run, Pallas kernels for 21% -> 20%
where the time goes in v3:
time: 63.5 us; the launch traced here: 63.2 us
  waiting for transfers between devices  26.2 us (41%)
  starting transfers between devices  21.3 us (34%)
  Pallas kernels  12.3 us (19%)
  local copies, waits for them, and re-layouts  2.21 us (3%)
  between operations  0.89 us (1%)
    ppermute x20, waiting for transfers between devices, swap(): return lax.ppermute(array, axis, [(i, i ^ bits) for i in range(size)])  26.2 us
    ppermute x20, starting transfers between devices, swap(): return lax.ppermute(array, axis, [(i, i ^ bits) for i in range(size)])  21.3 us
    pallas_call x3, Pallas kernels, attention(): pl.pallas_call(functools.partial(attention_kernel, n_mp, blocks, block, r...  11 us
    pallas_call x1, Pallas kernels, placing(): pl.pallas_call(functools.partial(placing_kernel, n_mp, blocks), in_specs=...  1.37 us
  transfers between devices with their start and end apart: 20, of which 11 were waited for; matrix products, arithmetic and copies ran while one was open for 0% of the time, Pallas kernels for 20%

profile of v3, /device:TPU:0, one launch (start us, length us, event | category | flops | bytes accessed | tf_op | source)
XLA Modules:
  0.0 63.2 jit_solution(16553039952563324593)
XLA Ops:
  0.6 0.8 %constant_dynamic-slice_fusion.2 = (bf16[8,512]{1,0:T(8,128)(2,1)S(1)}, bf16[8,512]{1,0:T(8,128)(2,1)S(1)}, bf16[8,512]{1,0:T(8,128)(2,1)S(1)}, bf16[8,512]{1,0:...) fusion(bf16[8,2048]{1,0:T(8,128)(2,1)} %param.6, ...), kind=kLoop, calls=%fused_computation.30 | loop fusion | bytes 131088 | tf_op jit(solution)/shard_map/slice | solution.py:221
  1.5 0.5 collective-permute-start
  2.0 0.9 %collective-permute-done = bf16[8,2048]{1,0:T(8,128)(2,1)S(1)} collective-permute-done((bf16[8,2048]{1,0:T(8,128)(2,1)S(1)}, bf16[8,2048]{1,0:T(8,128)(2,1)S(1)}, u32[]{:S(2)}, u32[]{:S(2)}) %collective-permute-start) | collective-permute-done | bytes 32800 | tf_op jit(solution)/shard_map/ppermute | solution.py:209
  2.9 0.3 collective-permute-start.1
  3.2 0.2 collective-permute-start.2
  3.4 2.9 %collective-permute-start.3 = (bf16[16,2048]{1,0:T(8,128)(2,1)S(1)}, bf16[16,2048]{1,0:T(8,128)(2,1)S(1)}, u32[]{:S(2)}, u32[]{:S(2)}) collective-permute-start(bf16[16,2048]{1,0:T(8,128)(2,1)S(1)} %pad_maximum_fusion.2), channel_id=1, source_target_pairs={{0,8},{2,10},{4,12},{6,14},{8,0},{10,2},{12,4},{14,6},{16,24},{18,... | collective-permute-start | bytes 196616 | tf_op jit(solution)/shard_map/ppermute | solution.py:209
  6.3 2.7 %collective-permute-start.4 = (bf16[16,2048]{1,0:T(8,128)(2,1)S(1)}, bf16[16,2048]{1,0:T(8,128)(2,1)S(1)}, u32[]{:S(2)}, u32[]{:S(2)}) collective-permute-start(bf16[16,2048]{1,0:T(8,128)(2,1)S(1)} %pad_maximum_fusion.2), channel_id=1, source_target_pairs={{0,16},{2,18},{4,20},{6,22},{8,24},{10,26},{12,28},{14,30},{16,0},... | collective-permute-start | bytes 196616 | tf_op jit(solution)/shard_map/ppermute | solution.py:209
  9.0 0.0 collective-permute-start.5
  9.0 0.0 collective-permute-done.3
  9.0 4.9 %collective-permute-done.4 = bf16[16,2048]{1,0:T(8,128)(2,1)S(1)} collective-permute-done((bf16[16,2048]{1,0:T(8,128)(2,1)S(1)}, bf16[16,2048]{1,0:T(8,128)(2,1)S(1)}, u32[]{:S(2)}, u32[]{:S(2)}) %collective-permute-start.4) | collective-permute-done | bytes 65568 | tf_op jit(solution)/shard_map/ppermute | solution.py:209
  13.9 1.2 %collective-permute-done.5 = bf16[16,2048]{1,0:T(8,128)(2,1)S(1)} collective-permute-done((bf16[16,2048]{1,0:T(8,128)(2,1)S(1)}, bf16[16,2048]{1,0:T(8,128)(2,1)S(1)}, u32[]{:S(2)}, u32[]{:S(2)}) %collective-permute-start.5) | collective-permute-done | bytes 65568 | tf_op jit(solution)/shard_map/ppermute | solution.py:209
  15.2 1.6 %collective-permute-start.6 = (bf16[64,1024]{1,0:T(8,128)(2,1)S(1)}, bf16[64,1024]{1,0:T(8,128)(2,1)S(1)}, u32[]{:S(2)}, u32[]{:S(2)}) collective-permute-start(bf16[64,1024]{1,0:T(8,128)(2,1)S(1)} %pad_maximum_fusion), channel_id=1, source_target_pairs={{0,4},{2,6},{4,0},{6,2},{8,12},{10,14},{12,8},{14,10},{16,20},{18,... | collective-permute-start | bytes 393224 | tf_op jit(solution)/shard_map/ppermute | solution.py:209
  16.7 1.6 %collective-permute-start.7 = (bf16[64,1024]{1,0:T(8,128)(2,1)S(1)}, bf16[64,1024]{1,0:T(8,128)(2,1)S(1)}, u32[]{:S(2)}, u32[]{:S(2)}) collective-permute-start(bf16[64,1024]{1,0:T(8,128)(2,1)S(1)} %pad_maximum_fusion.1), channel_id=1, source_target_pairs={{0,1},{1,0},{2,3},{3,2},{4,5},{5,4},{6,7},{7,6},{8,9},{9,8},{10,11... | collective-permute-start | bytes 393224 | tf_op jit(solution)/shard_map/ppermute | solution.py:209
  18.3 1.9 %collective-permute-done.6 = bf16[64,1024]{1,0:T(8,128)(2,1)S(1)} collective-permute-done((bf16[64,1024]{1,0:T(8,128)(2,1)S(1)}, bf16[64,1024]{1,0:T(8,128)(2,1)S(1)}, u32[]{:S(2)}, u32[]{:S(2)}) %collective-permute-start.6) | collective-permute-done | bytes 131104 | tf_op jit(solution)/shard_map/ppermute | solution.py:209
  20.2 1.6 %collective-permute-done.7 = bf16[64,1024]{1,0:T(8,128)(2,1)S(1)} collective-permute-done((bf16[64,1024]{1,0:T(8,128)(2,1)S(1)}, bf16[64,1024]{1,0:T(8,128)(2,1)S(1)}, u32[]{:S(2)}, u32[]{:S(2)}) %collective-permute-start.7) | collective-permute-done | bytes 131104 | tf_op jit(solution)/shard_map/ppermute | solution.py:209
  21.8 1.6 %collective-permute-start.8 = (bf16[128,1024]{1,0:T(8,128)(2,1)S(1)}, bf16[128,1024]{1,0:T(8,128)(2,1)S(1)}, u32[]{:S(2)}, u32[]{:S(2)}) collective-permute-start(bf16[128,1024]{1,0:T(8,128)(2,1)S(1)} %constant_dynamic-update-slice_fusion.refs_0_), channel_id=1, source_target_pairs={{0,1},{1,0},{2,3},{3,2},{4,5},{5,4},{6,7},{7,6},{8,9},{9,8},{10,11... | collective-permute-start | bytes 786440 | tf_op jit(solution)/shard_map/ppermute | solution.py:209
  23.4 0.9 %collective-permute-start.10 = (bf16[128,1024]{1,0:T(8,128)(2,1)S(1)}, bf16[128,1024]{1,0:T(8,128)(2,1)S(1)}, u32[]{:S(2)}, u32[]{:S(2)}) collective-permute-start(bf16[128,1024]{1,0:T(8,128)(2,1)S(1)} %constant_dynamic-update-slice_fusion.5.refs_0_), channel_id=1, source_target_pairs={{0,4},{2,6},{4,0},{6,2},{8,12},{10,14},{12,8},{14,10},{16,20},{18,... | collective-permute-start | bytes 786440 | tf_op jit(solution)/shard_map/ppermute | solution.py:209
  24.3 0.0 collective-permute-done.1.sq_ref
  24.3 0.0 collective-permute-done.2.sg_ref
  24.3 3.1 %shard_map.75 = (bf16[256,4096]{1,0:T(8,128)(2,1)}, bf16[256,4096]{1,0:T(8,128)(2,1)}, bf16[256,2048]{1,0:T(8,128)(2,1)S(1)}, f32[128,1024]{1,0:T(8,128)S(1)}) custom-call(bf16[256,4096]{1,0:T(8,128)(2,1)} %q_ref.5, bf16[256,4096]{1,0:T(8,128)(2,1)} %g_ref.5, bf16[256,4096]{1,0:T(8,128)(2,1)S(1)} %collective-permute-done.1.sq_ref, ...), custom_call_target="tpu_custom_call" | custom-call | flops 402653184 | bytes 2097152 | tf_op jit(solution)/shard_map/pallas_call | solution.py:148
  27.4 0.8 %collective-permute-done.8.refs_0_ = bf16[128,1024]{1,0:T(8,128)(2,1)S(1)} collective-permute-done((bf16[128,1024]{1,0:T(8,128)(2,1)S(1)}, bf16[128,1024]{1,0:T(8,128)(2,1)S(1)}, u32[]{:S(2)}, u32[]{:S(2)}) %collective-permute-start.8) | collective-permute-done | bytes 262176 | tf_op jit(solution)/shard_map/ppermute | solution.py:209
  28.2 3.1 %shard_map.76 = (bf16[256,4096]{1,0:T(8,128)(2,1)}, bf16[256,4096]{1,0:T(8,128)(2,1)}, bf16[256,2048]{1,0:T(8,128)(2,1)S(1)}, bf16[128,1024]{1,0:T(8,128)(2,1)S(1)}) custom-call(bf16[256,4096]{1,0:T(8,128)(2,1)} %q_ref.5, bf16[256,4096]{1,0:T(8,128)(2,1)} %g_ref.5, ...), custom_call_target="tpu_custom_call", output_to_operand_aliasing={{0}: (5, {}), {1}: (6, {}), {2}: (7, {})} | custom-call | flops 402653184 | bytes 2097152 | tf_op jit(solution)/shard_map/pallas_call | solution.py:148
  31.4 1.6 %collective-permute-start.9 = (bf16[128,1024]{1,0:T(8,128)(2,1)S(1)}, bf16[128,1024]{1,0:T(8,128)(2,1)S(1)}, u32[]{:S(2)}, u32[]{:S(2)}) collective-permute-start(bf16[128,1024]{1,0:T(8,128)(2,1)S(1)} %get-tuple-element.45), channel_id=1, source_target_pairs={{0,1},{1,0},{2,3},{3,2},{4,5},{5,4},{6,7},{7,6},{8,9},{9,8},{10,11... | collective-permute-start | bytes 786440 | tf_op jit(solution)/shard_map/ppermute | solution.py:209
  33.0 0.0 collective-permute-done.10.refs_1_
  33.0 4.7 %shard_map.77 = (bf16[256,4096]{1,0:T(8,128)(2,1)}, bf16[256,4096]{1,0:T(8,128)(2,1)}, bf16[256,2048]{1,0:T(8,128)(2,1)S(1)}, f32[128,1024]{1,0:T(8,128)S(1)}, bf16[128,1024]{1,0:T(8,128)(2,1)S(1)}) custom-call(bf16[256,4096]{1,0:T(8,128)(2,1)} %q_ref.5, bf16[256,4096]{1,0:T(8,128)(2,1)} %g_ref.5, ...), custom_call_target="tpu_custom_call", output_to_operand_aliasing={{0}: (6, {}), {1}: (7, {})} | custom-call | flops 805306368 | bytes 4194304 | tf_op jit(solution)/shard_map/pallas_call | solution.py:148
  37.7 0.9 %collective-permute-start.11 = (bf16[128,1024]{1,0:T(8,128)(2,1)S(1)}, bf16[128,1024]{1,0:T(8,128)(2,1)S(1)}, u32[]{:S(2)}, u32[]{:S(2)}) collective-permute-start(bf16[128,1024]{1,0:T(8,128)(2,1)S(1)} %get-tuple-element.50), channel_id=1, source_target_pairs={{0,4},{2,6},{4,0},{6,2},{8,12},{10,14},{12,8},{14,10},{16,20},{18,... | collective-permute-start | bytes 786440 | tf_op jit(solution)/shard_map/ppermute | solution.py:209
  38.5 0.0 collective-permute-done.9
  38.6 0.1 convert_add_fusion.1
  38.6 5.5 %collective-permute-done.11 = bf16[128,1024]{1,0:T(8,128)(2,1)S(1)} collective-permute-done((bf16[128,1024]{1,0:T(8,128)(2,1)S(1)}, bf16[128,1024]{1,0:T(8,128)(2,1)S(1)}, u32[]{:S(2)}, u32[]{:S(2)}) %collective-permute-start.11) | collective-permute-done | bytes 262176 | tf_op jit(solution)/shard_map/ppermute | solution.py:209
  44.1 0.1 convert_add_fusion
  44.2 0.1 collective-permute-start.14
  44.2 0.5 collective-permute-start.15
  44.8 0.9 %collective-permute-start.12 = (bf16[64,1024]{1,0:T(8,128)(2,1)S(1)}, bf16[64,1024]{1,0:T(8,128)(2,1)S(1)}, u32[]{:S(2)}, u32[]{:S(2)}) collective-permute-start(bf16[64,1024]{1,0:T(8,128)(2,1)S(1)} %slice.176), channel_id=1, source_target_pairs={{0,4},{2,6},{4,0},{6,2},{8,12},{10,14},{12,8},{14,10},{16,20},{18,... | collective-permute-start | bytes 393224 | tf_op jit(solution)/shard_map/ppermute | solution.py:209
  45.7 0.6 collective-permute-start.13
  46.2 4.1 %collective-permute-done.12 = bf16[64,1024]{1,0:T(8,128)(2,1)S(1)} collective-permute-done((bf16[64,1024]{1,0:T(8,128)(2,1)S(1)}, bf16[64,1024]{1,0:T(8,128)(2,1)S(1)}, u32[]{:S(2)}, u32[]{:S(2)}) %collective-permute-start.12) | collective-permute-done | bytes 131104 | tf_op jit(solution)/shard_map/ppermute | solution.py:209
  50.3 0.6 collective-permute-done.13
  51.0 0.0 collective-permute-done.14.refs_0_
  51.0 0.0 collective-permute-done.15.refs_1_
  51.1 0.6 collective-permute-start.16
  51.7 2.9 %collective-permute-start.17 = (bf16[16,2048]{1,0:T(8,128)(2,1)S(1)}, bf16[16,2048]{1,0:T(8,128)(2,1)S(1)}, u32[]{:S(2)}, u32[]{:S(2)}) collective-permute-start(bf16[16,2048]{1,0:T(8,128)(2,1)S(1)} %get-tuple-element.71), channel_id=1, source_target_pairs={{0,16},{2,18},{4,20},{6,22},{8,24},{10,26},{12,28},{14,30},{16,0},... | collective-permute-start | bytes 196616 | tf_op jit(solution)/shard_map/ppermute | solution.py:209
  54.6 1.0 %collective-permute-start.18 = (bf16[16,2048]{1,0:T(8,128)(2,1)S(1)}, bf16[16,2048]{1,0:T(8,128)(2,1)S(1)}, u32[]{:S(2)}, u32[]{:S(2)}) collective-permute-start(bf16[16,2048]{1,0:T(8,128)(2,1)S(1)} %get-tuple-element.70), channel_id=1, source_target_pairs={{0,24},{2,26},{4,28},{6,30},{8,16},{10,18},{12,20},{14,22},{16,8},... | collective-permute-start | bytes 196616 | tf_op jit(solution)/shard_map/ppermute | solution.py:209
  55.5 1.4 %shard_map.78 = (bf16[256,4096]{1,0:T(8,128)(2,1)}, bf16[256,4096]{1,0:T(8,128)(2,1)}) custom-call(bf16[256,2048]{1,0:T(8,128)(2,1)S(1)} %collective-permute-done.14.refs_0_, bf16[256,2048]{1,0:T(8,128)(2,1)S(1)} %collective-permute-done.15.refs_1_, bf16[256,4096]{1,0:T(8,128)(2,1)} %get-tuple-element.61.refs_2_, ...), custom_call_target="tpu_custom_call", output_to_operand_aliasing={{0}: (2, {}), {1}: (3, {})} | custom-call | tf_op jit(solution)/shard_map/pallas_call | solution.py:192
  56.9 0.0 collective-permute-done.16
  56.9 3.7 %collective-permute-done.18 = bf16[16,2048]{1,0:T(8,128)(2,1)S(1)} collective-permute-done((bf16[16,2048]{1,0:T(8,128)(2,1)S(1)}, bf16[16,2048]{1,0:T(8,128)(2,1)S(1)}, u32[]{:S(2)}, u32[]{:S(2)}) %collective-permute-start.18) | collective-permute-done | bytes 65568 | tf_op jit(solution)/shard_map/ppermute | solution.py:209
  60.7 0.1 collective-permute-start.19
  60.8 1.1 %collective-permute-done.19 = bf16[8,2048]{1,0:T(8,128)(2,1)S(1)} collective-permute-done((bf16[8,2048]{1,0:T(8,128)(2,1)S(1)}, bf16[8,2048]{1,0:T(8,128)(2,1)S(1)}, u32[]{:S(2)}, u32[]{:S(2)}) %collective-permute-start.19) | collective-permute-done | bytes 32800 | tf_op jit(solution)/shard_map/ppermute | solution.py:209
  62.0 0.6 copy-done.1
  62.6 0.6 copy-done
  (31 shorter events, 0.4 us)
Async XLA Ops:
  1.5 1.4 %collective-permute-start = (bf16[8,2048]{1,0:T(8,128)(2,1)S(1)}, bf16[8,2048]{1,0:T(8,128)(2,1)S(1)}, u32[]{:S(2)}, u32[]{:S(2)}) collective-permute-start(bf16[8,2048]{1,0:T(8,128)(2,1)S(1)} %pad_maximum_fusion.3), channel_id=1, source_target_pairs={{0,2},{2,0},{4,6},{6,4},{8,10},{10,8},{12,14},{14,12},{16,18},{18,... | collective-permute-start | bytes 98312 | tf_op jit(solution)/shard_map/ppermute | solution.py:209
  2.9 21.4 %collective-permute-start.1 = (bf16[256,4096]{1,0:T(8,128)(2,1)}, bf16[256,4096]{1,0:T(8,128)(2,1)S(1)}, u32[]{:S(2)}, u32[]{:S(2)}) collective-permute-start(bf16[256,4096]{1,0:T(8,128)(2,1)} %q_ref.5), channel_id=1, source_target_pairs={{0,2},{2,0},{4,6},{6,4},{8,10},{10,8},{12,14},{14,12},{16,18},{18,... | collective-permute-start | bytes 6291464 | tf_op jit(solution)/shard_map/ppermute | solution.py:209
  3.2 21.1 %collective-permute-start.2 = (bf16[256,4096]{1,0:T(8,128)(2,1)}, bf16[256,4096]{1,0:T(8,128)(2,1)S(1)}, u32[]{:S(2)}, u32[]{:S(2)}) collective-permute-start(bf16[256,4096]{1,0:T(8,128)(2,1)} %g_ref.5), channel_id=1, source_target_pairs={{0,2},{2,0},{4,6},{6,4},{8,10},{10,8},{12,14},{14,12},{16,18},{18,... | collective-permute-start | bytes 6291464 | tf_op jit(solution)/shard_map/ppermute | solution.py:209
  3.4 5.6 %collective-permute-start.3 = (bf16[16,2048]{1,0:T(8,128)(2,1)S(1)}, bf16[16,2048]{1,0:T(8,128)(2,1)S(1)}, u32[]{:S(2)}, u32[]{:S(2)}) collective-permute-start(bf16[16,2048]{1,0:T(8,128)(2,1)S(1)} %pad_maximum_fusion.2), channel_id=1, source_target_pairs={{0,8},{2,10},{4,12},{6,14},{8,0},{10,2},{12,4},{14,6},{16,24},{18,... | collective-permute-start | bytes 196616 | tf_op jit(solution)/shard_map/ppermute | solution.py:209
  6.3 7.6 %collective-permute-start.4 = (bf16[16,2048]{1,0:T(8,128)(2,1)S(1)}, bf16[16,2048]{1,0:T(8,128)(2,1)S(1)}, u32[]{:S(2)}, u32[]{:S(2)}) collective-permute-start(bf16[16,2048]{1,0:T(8,128)(2,1)S(1)} %pad_maximum_fusion.2), channel_id=1, source_target_pairs={{0,16},{2,18},{4,20},{6,22},{8,24},{10,26},{12,28},{14,30},{16,0},... | collective-permute-start | bytes 196616 | tf_op jit(solution)/shard_map/ppermute | solution.py:209
  9.0 6.2 %collective-permute-start.5 = (bf16[16,2048]{1,0:T(8,128)(2,1)S(1)}, bf16[16,2048]{1,0:T(8,128)(2,1)S(1)}, u32[]{:S(2)}, u32[]{:S(2)}) collective-permute-start(bf16[16,2048]{1,0:T(8,128)(2,1)S(1)} %pad_maximum_fusion.2), channel_id=1, source_target_pairs={{0,24},{2,26},{4,28},{6,30},{8,16},{10,18},{12,20},{14,22},{16,8},... | collective-permute-start | bytes 196616 | tf_op jit(solution)/shard_map/ppermute | solution.py:209
  15.2 5.0 %collective-permute-start.6 = (bf16[64,1024]{1,0:T(8,128)(2,1)S(1)}, bf16[64,1024]{1,0:T(8,128)(2,1)S(1)}, u32[]{:S(2)}, u32[]{:S(2)}) collective-permute-start(bf16[64,1024]{1,0:T(8,128)(2,1)S(1)} %pad_maximum_fusion), channel_id=1, source_target_pairs={{0,4},{2,6},{4,0},{6,2},{8,12},{10,14},{12,8},{14,10},{16,20},{18,... | collective-permute-start | bytes 393224 | tf_op jit(solution)/shard_map/ppermute | solution.py:209
  16.7 5.0 %collective-permute-start.7 = (bf16[64,1024]{1,0:T(8,128)(2,1)S(1)}, bf16[64,1024]{1,0:T(8,128)(2,1)S(1)}, u32[]{:S(2)}, u32[]{:S(2)}) collective-permute-start(bf16[64,1024]{1,0:T(8,128)(2,1)S(1)} %pad_maximum_fusion.1), channel_id=1, source_target_pairs={{0,1},{1,0},{2,3},{3,2},{4,5},{5,4},{6,7},{7,6},{8,9},{9,8},{10,11... | collective-permute-start | bytes 393224 | tf_op jit(solution)/shard_map/ppermute | solution.py:209
  21.8 6.4 %collective-permute-start.8 = (bf16[128,1024]{1,0:T(8,128)(2,1)S(1)}, bf16[128,1024]{1,0:T(8,128)(2,1)S(1)}, u32[]{:S(2)}, u32[]{:S(2)}) collective-permute-start(bf16[128,1024]{1,0:T(8,128)(2,1)S(1)} %constant_dynamic-update-slice_fusion.refs_0_), channel_id=1, source_target_pairs={{0,1},{1,0},{2,3},{3,2},{4,5},{5,4},{6,7},{7,6},{8,9},{9,8},{10,11... | collective-permute-start | bytes 786440 | tf_op jit(solution)/shard_map/ppermute | solution.py:209
  23.4 9.6 %collective-permute-start.10 = (bf16[128,1024]{1,0:T(8,128)(2,1)S(1)}, bf16[128,1024]{1,0:T(8,128)(2,1)S(1)}, u32[]{:S(2)}, u32[]{:S(2)}) collective-permute-start(bf16[128,1024]{1,0:T(8,128)(2,1)S(1)} %constant_dynamic-update-slice_fusion.5.refs_0_), channel_id=1, source_target_pairs={{0,4},{2,6},{4,0},{6,2},{8,12},{10,14},{12,8},{14,10},{16,20},{18,... | collective-permute-start | bytes 786440 | tf_op jit(solution)/shard_map/ppermute | solution.py:209
  31.4 7.2 %collective-permute-start.9 = (bf16[128,1024]{1,0:T(8,128)(2,1)S(1)}, bf16[128,1024]{1,0:T(8,128)(2,1)S(1)}, u32[]{:S(2)}, u32[]{:S(2)}) collective-permute-start(bf16[128,1024]{1,0:T(8,128)(2,1)S(1)} %get-tuple-element.45), channel_id=1, source_target_pairs={{0,1},{1,0},{2,3},{3,2},{4,5},{5,4},{6,7},{7,6},{8,9},{9,8},{10,11... | collective-permute-start | bytes 786440 | tf_op jit(solution)/shard_map/ppermute | solution.py:209
  37.7 6.4 %collective-permute-start.11 = (bf16[128,1024]{1,0:T(8,128)(2,1)S(1)}, bf16[128,1024]{1,0:T(8,128)(2,1)S(1)}, u32[]{:S(2)}, u32[]{:S(2)}) collective-permute-start(bf16[128,1024]{1,0:T(8,128)(2,1)S(1)} %get-tuple-element.50), channel_id=1, source_target_pairs={{0,4},{2,6},{4,0},{6,2},{8,12},{10,14},{12,8},{14,10},{16,20},{18,... | collective-permute-start | bytes 786440 | tf_op jit(solution)/shard_map/ppermute | solution.py:209
  44.2 6.8 %collective-permute-start.14 = (bf16[256,2048]{1,0:T(8,128)(2,1)S(1)}, bf16[256,2048]{1,0:T(8,128)(2,1)S(1)}, u32[]{:S(2)}, u32[]{:S(2)}) collective-permute-start(bf16[256,2048]{1,0:T(8,128)(2,1)S(1)} %get-tuple-element.55), channel_id=1, source_target_pairs={{0,2},{2,0},{4,6},{6,4},{8,10},{10,8},{12,14},{14,12},{16,18},{18,... | collective-permute-start | bytes 3145736 | tf_op jit(solution)/shard_map/ppermute | solution.py:209
  44.2 6.7 %collective-permute-start.15 = (bf16[256,2048]{1,0:T(8,128)(2,1)S(1)}, bf16[256,2048]{1,0:T(8,128)(2,1)S(1)}, u32[]{:S(2)}, u32[]{:S(2)}) collective-permute-start(bf16[256,2048]{1,0:T(8,128)(2,1)S(1)} %get-tuple-element.56), channel_id=1, source_target_pairs={{0,2},{2,0},{4,6},{6,4},{8,10},{10,8},{12,14},{14,12},{16,18},{18,... | collective-permute-start | bytes 3145736 | tf_op jit(solution)/shard_map/ppermute | solution.py:209
  44.8 5.5 %collective-permute-start.12 = (bf16[64,1024]{1,0:T(8,128)(2,1)S(1)}, bf16[64,1024]{1,0:T(8,128)(2,1)S(1)}, u32[]{:S(2)}, u32[]{:S(2)}) collective-permute-start(bf16[64,1024]{1,0:T(8,128)(2,1)S(1)} %slice.176), channel_id=1, source_target_pairs={{0,4},{2,6},{4,0},{6,2},{8,12},{10,14},{12,8},{14,10},{16,20},{18,... | collective-permute-start | bytes 393224 | tf_op jit(solution)/shard_map/ppermute | solution.py:209
  45.7 5.3 %collective-permute-start.13 = (bf16[64,1024]{1,0:T(8,128)(2,1)S(1)}, bf16[64,1024]{1,0:T(8,128)(2,1)S(1)}, u32[]{:S(2)}, u32[]{:S(2)}) collective-permute-start(bf16[64,1024]{1,0:T(8,128)(2,1)S(1)} %slice.175), channel_id=1, source_target_pairs={{0,1},{1,0},{2,3},{3,2},{4,5},{5,4},{6,7},{7,6},{8,9},{9,8},{10,11... | collective-permute-start | bytes 393224 | tf_op jit(solution)/shard_map/ppermute | solution.py:209
  51.1 5.8 %collective-permute-start.16 = (bf16[16,2048]{1,0:T(8,128)(2,1)S(1)}, bf16[16,2048]{1,0:T(8,128)(2,1)S(1)}, u32[]{:S(2)}, u32[]{:S(2)}) collective-permute-start(bf16[16,2048]{1,0:T(8,128)(2,1)S(1)} %get-tuple-element.72), channel_id=1, source_target_pairs={{0,8},{2,10},{4,12},{6,14},{8,0},{10,2},{12,4},{14,6},{16,24},{18,... | collective-permute-start | bytes 196616 | tf_op jit(solution)/shard_map/ppermute | solution.py:209
  51.7 5.2 %collective-permute-start.17 = (bf16[16,2048]{1,0:T(8,128)(2,1)S(1)}, bf16[16,2048]{1,0:T(8,128)(2,1)S(1)}, u32[]{:S(2)}, u32[]{:S(2)}) collective-permute-start(bf16[16,2048]{1,0:T(8,128)(2,1)S(1)} %get-tuple-element.71), channel_id=1, source_target_pairs={{0,16},{2,18},{4,20},{6,22},{8,24},{10,26},{12,28},{14,30},{16,0},... | collective-permute-start | bytes 196616 | tf_op jit(solution)/shard_map/ppermute | solution.py:209
  54.6 6.1 %collective-permute-start.18 = (bf16[16,2048]{1,0:T(8,128)(2,1)S(1)}, bf16[16,2048]{1,0:T(8,128)(2,1)S(1)}, u32[]{:S(2)}, u32[]{:S(2)}) collective-permute-start(bf16[16,2048]{1,0:T(8,128)(2,1)S(1)} %get-tuple-element.70), channel_id=1, source_target_pairs={{0,24},{2,26},{4,28},{6,30},{8,16},{10,18},{12,20},{14,22},{16,8},... | collective-permute-start | bytes 196616 | tf_op jit(solution)/shard_map/ppermute | solution.py:209
  60.7 1.3 %collective-permute-start.19 = (bf16[8,2048]{1,0:T(8,128)(2,1)S(1)}, bf16[8,2048]{1,0:T(8,128)(2,1)S(1)}, u32[]{:S(2)}, u32[]{:S(2)}) collective-permute-start(bf16[8,2048]{1,0:T(8,128)(2,1)S(1)} %slice.153), channel_id=1, source_target_pairs={{0,2},{2,0},{4,6},{6,4},{8,10},{10,8},{12,14},{14,12},{16,18},{18,... | collective-permute-start | bytes 98312 | tf_op jit(solution)/shard_map/ppermute | solution.py:209
  62.0 0.6 copy-start.1
  62.6 0.6 copy-start

commit v4 on v1

--- a/solution.py
+++ b/solution.py
@@ -37,89 +37,91 @@
     return lambda r: pl.multiple_of((((my ^ r) * 2 + core) * blocks + block) * width, width)
 
 
-def attention_kernel(n_mp, blocks, block, rs, n_memory, q_ref, g_ref, sq_ref, sg_ref, *refs):
-    memory_refs, refs = refs[:n_memory], refs[-10 - n_memory :]
-    (attended_ref, query_grad_ref, sibling_ref), term_refs = refs[:3], refs[3:-7]
+def attention_kernel(n_mp, blocks, jobs, n_memory, q_ref, g_ref, sq_ref, sg_ref, *refs):
+    used = sorted({block for block, *_ in jobs})
+    memory_refs, refs = refs[:n_memory], refs[n_memory:]
     token_buf, result_buf, raw_ref, prob_ref, grad_ref, weight_ref, sems = refs[-7:]
-    count, width = q_ref.shape[0], term_refs[0].shape[1] // 2
-    heads, group = width // DH, min(2 * DH, width)
-    parts = width // group
-    size = memory_refs[0].shape[0] // len(rs)
-    column = columns(n_mp, blocks, block, width, False)
+    n_terms = 1 + max(i for *_, terms in jobs for i, _ in terms)
+    term_refs, refs = refs[-7 - n_terms : -7], refs[: -7 - n_terms]
+    attended_ref, query_grad_ref, *sent_refs = refs[-2 - len(used) :]
+    count, width = q_ref.shape[0], memory_refs[0].shape[1] // 2
+    heads, slots = width // DH, raw_ref.shape[0]
     step = min(DH, 2 * count)
     cols = [slice(n * DH, (n + 1) * DH) for n in range(heads)]
     targets = [[slice(m * width + n * DH, m * width + (n + 1) * DH) for n in range(heads)] for m in (0, 1)]
 
-    def inputs(k, part):
-        begin = part * group
-        where = pl.ds(pl.multiple_of(column(rs[0] + k) + begin, group), group)
+    def inputs(j):
+        where = pl.ds(columns(n_mp, blocks, jobs[j][0], width, False)(jobs[j][1]), width)
         return [
             pltpu.make_async_copy(
-                array.at[:, where],
-                token_buf.at[k, m, pl.ds(n * count, count), pl.ds(begin, group)],
-                sems.at[0, k, part, m, n],
+                array.at[:, where], token_buf.at[j, m, pl.ds(n * count, count)], sems.at[0, j, m, n]
             )
             for m, pair in enumerate(((q_ref, sq_ref), (g_ref, sg_ref)))
             for n, array in enumerate(pair)
         ]
 
-    def outputs(k, part):
-        begin = part * group
-        copies = []
+    def outputs(j):
+        block, r = jobs[j][:2]
+        where = pl.ds(columns(n_mp, blocks, block, width, False)(r), width)
+        sent_ref, copies = sent_refs[used.index(block)], []
         for m, own in enumerate((query_grad_ref, attended_ref)):
-            starts = (column(rs[0] + k), (2 * (rs[0] + k) + m) * width)
-            for n, (array, start) in enumerate(zip((own, sibling_ref), starts)):
+            sent = sent_ref.at[:, pl.ds((2 * r + m) * width, width)]
+            for n, target in enumerate((own.at[:, where], sent)):
                 copies.append(
-                    pltpu.make_async_copy(
-                        result_buf.at[k, m, pl.ds(n * count, count), pl.ds(begin, group)],
-                        array.at[:, pl.ds(pl.multiple_of(start + begin, group), group)],
-                        sems.at[1, k, part, m, n],
-                    )
+                    pltpu.make_async_copy(result_buf.at[j, m, pl.ds(n * count, count)], target, sems.at[1, j, m, n])
                 )
         return copies
 
-    def every(action):
-        def at(k, _):
-            for part in range(parts):
-                for copy in action(k, part):
-                    copy()
-
-        repeat(at)
-
-    def repeat(body):
-        if len(rs) == 1:
-            body(0, None)
-        else:
-            lax.fori_loop(0, len(rs), body, None)
-
-    def work(k, _):
-        rows = pl.ds(pl.multiple_of(k * size, size), size)
-        memory = [[jnp.concatenate([ref[rows, t] for ref in memory_refs], axis=0) for t in row] for row in targets]
-        for n in range(heads):
-            if n * DH % group == 0:
-                for copy in inputs(k, n * DH // group):
+    def memory_of(j, m, n):
+        return jnp.concatenate(
+            [memory_refs[i][start : start + size, targets[m][n]] for i, start, size in jobs[j][2]], axis=0
+        )
+
+    def scores(j, n, slot):
+        raw_ref[slot] = dot(memory_of(j, 0, n), token_buf[j, 0, :, cols[n]], NT)
+        prob_ref[slot] = dot(memory_of(j, 1, n), token_buf[j, 1, :, cols[n]], NT)
+
+    def softmax(slot):
+        for begin in range(0, 2 * count, step):
+            part = slice(begin, begin + step)
+            grad_ref[slot, :, part], weight_ref[slot, :, part] = softmax_part(
+                raw_ref[slot, :, part], prob_ref[slot, :, part]
+            )
+
+    def results(j, n, slot):
+        for m, pair_ref in enumerate((grad_ref, weight_ref)):
+            result_buf[j, m, :, cols[n]] = dot(memory_of(j, m, n).T, pair_ref[slot], NN).astype(bf16).T
+
+    def terms(j, n, slot):
+        for m, pair_ref in enumerate((grad_ref, weight_ref)):
+            term, row = dot(pair_ref[slot], token_buf[j, m, :, cols[n]], NN), 0
+            for (_, _, size), (i, start) in zip(*jobs[j][2:]):
+                term_refs[i][start : start + size, targets[m][n]] = term[row : row + size].astype(term_refs[i].dtype)
+                row += size
+
+    for j in range(len(jobs)):
+        for copy in inputs(j):
+            copy.start()
+    items = [(j, n) for j in range(len(jobs)) for n in range(heads)]
+    for i in range(len(items) + 2):
+        if i < len(items):
+            j, n = items[i]
+            if n == 0:
+                for copy in inputs(j):
                     copy.wait()
-            raw_ref[n] = dot(memory[0][n], token_buf[k, 0, :, cols[n]], NT)
-            prob_ref[n] = dot(memory[1][n], token_buf[k, 1, :, cols[n]], NT)
-        for n in range(heads):
-            for begin in range(0, 2 * count, step):
-                part = slice(begin, begin + step)
-                grad_ref[n, :, part], weight_ref[n, :, part] = softmax_part(raw_ref[n, :, part], prob_ref[n, :, part])
-        for n in range(heads):
-            for m, pair_ref in enumerate((grad_ref, weight_ref)):
-                result_buf[k, m, :, cols[n]] = dot(memory[m][n].T, pair_ref[n], NN).astype(bf16).T
-            if (n + 1) * DH % group == 0:
-                for copy in outputs(k, n * DH // group):
+            scores(j, n, i % slots)
+        if 1 <= i <= len(items):
+            softmax((i - 1) % slots)
+        if i >= 2:
+            j, n = items[i - 2]
+            results(j, n, (i - 2) % slots)
+            if n == heads - 1:
+                for copy in outputs(j):
                     copy.start()
-        for n in range(heads):
-            for m, pair_ref in enumerate((grad_ref, weight_ref)):
-                term = dot(pair_ref[n], token_buf[k, m, :, cols[n]], NN)
-                for i, term_ref in enumerate(term_refs):
-                    term_ref[rows, targets[m][n]] = term[i * size : (i + 1) * size].astype(term_ref.dtype)
-
-    every(lambda k, part: [copy.start for copy in inputs(k, part)])
-    repeat(work)
-    every(lambda k, part: [copy.wait for copy in outputs(k, part)])
+            terms(j, n, (i - 2) % slots)
+    for j in range(len(jobs)):
+        for copy in outputs(j):
+            copy.wait()
 
 
 def pinned(space, *arrays):
@@ -129,32 +131,34 @@
 HBM, VMEM = pl.BlockSpec(memory_space=pltpu.HBM), pl.BlockSpec(memory_space=pltpu.VMEM)
 
 
-def attention(n_mp, blocks, block, rs, tokens, memory, types, outputs, sent):
+def attention(n_mp, blocks, jobs, tokens, memory, terms, outputs, sent):
     rows, whole = tokens[0].shape
     width = memory[0].shape[1] // 2
-    count = sum(m.shape[0] for m in memory) // len(rs)
-    group = min(2 * DH, width)
-    scratch = (width // DH, count, 2 * rows)
-    earlier = [*outputs] + ([] if sent is None else [sent])
+    count = sum(size for _, _, size in jobs[0][2])
+    used = sorted({block for block, *_ in jobs})
+    scratch = (min(4, len(jobs) * width // DH), count, 2 * rows)
+    earlier = [*outputs] + [sent[block] for block in used if block in sent]
     first = 4 + len(memory)
-    return pl.pallas_call(
-        functools.partial(attention_kernel, n_mp, blocks, block, rs, len(memory)),
+    results = pl.pallas_call(
+        functools.partial(attention_kernel, n_mp, blocks, jobs, len(memory)),
         in_specs=[HBM] * 4 + [VMEM] * len(memory) + [HBM] * len(earlier),
-        out_specs=[HBM] * 3 + [VMEM] * len(memory),
+        out_specs=[HBM] * (2 + len(used)) + [VMEM] * len(terms),
         out_shape=[jax.ShapeDtypeStruct((rows, whole), bf16)] * 2
-        + [jax.ShapeDtypeStruct((rows, whole // blocks), bf16)]
-        + [pltpu.VMEM(m.shape, t) for m, t in zip(memory, types)],
-        scratch_shapes=[pltpu.VMEM((len(rs), 2, 2 * rows, width), bf16)] * 2
+        + [jax.ShapeDtypeStruct((rows, whole // blocks), bf16)] * len(used)
+        + [pltpu.VMEM(memory[0].shape, t) for t in terms],
+        scratch_shapes=[pltpu.VMEM((len(jobs), 2, 2 * rows, width), bf16)] * 2
         + [pltpu.VMEM(scratch, t) for t in (f32, f32, bf16, bf16)]
-        + [pltpu.SemaphoreType.DMA((2, len(rs), width // group, 2, 2))],
+        + [pltpu.SemaphoreType.DMA((2, len(jobs), 2, 2))],
         input_output_aliases={first + n: n for n in range(len(earlier))},
         compiler_params=pltpu.CompilerParams(vmem_limit_bytes=32 * 1024 * 1024),
         cost_estimate=pl.CostEstimate(
-            flops=24 * rows * count * width * len(rs),
-            bytes_accessed=16 * rows * width * len(rs),
-            transcendentals=2 * rows * count * width * len(rs) // DH,
+            flops=24 * rows * count * width * len(jobs),
+            bytes_accessed=16 * rows * width * len(jobs),
+            transcendentals=2 * rows * count * width * len(jobs) // DH,
         ),
     )(*pinned(pltpu.HBM, *tokens[:2]), *tokens[2:], *pinned(pltpu.VMEM, *memory), *earlier)
+    sent = {**sent, **dict(zip(used, results[2:]))}
+    return results[:2], sent, results[2 + len(used) :]
 
 
 def placing_kernel(n_mp, blocks, *refs):
@@ -231,17 +235,32 @@
         second = wider(second, swap(second, "mp", bits))
     first_got, second_got = swap(first, "mp", y_bits[-1]), swap(second, "seq", x_bit)
 
-    half = n_mp // 2
-    *outputs, out, first_keep = attention(n_mp, blocks, 0, range(half), tokens, [first], [f32], [], None)
-    *outputs, out_first, give = attention(
-        n_mp, blocks, 0, range(half, n_mp), tokens, [first_got], [bf16], outputs, out
+    half, size = n_mp // 2, second.shape[0] // n_mp
+
+    def of_first(r, memory, term):
+        start = (r % half) * 2 * size
+        return (0, r, ((memory, start, 2 * size),), ((term, start),))
+
+    def of_second(r, held, got, keep, give):
+        return (1, r, ((held, r * size, size), (got, r * size, size)), ((keep, r * size), (give, r * size)))
+
+    outputs, sent, (first_keep,) = attention(
+        n_mp, blocks, [of_first(r, 0, 0) for r in range(half)], tokens, [first], [f32], [], {}
     )
-    first_got = swap(give, "mp", y_bits[-1])
-    *outputs, out_second, second_keep, give = attention(
-        n_mp, blocks, 1, range(n_mp), tokens, [second, second_got], [f32, bf16], outputs, None
+    outputs, sent, (first_give, second_keep, second_give) = attention(
+        n_mp,
+        blocks,
+        [of_first(r, 0, 0) for r in range(half, n_mp)] + [of_second(r, 1, 2, 1, 2) for r in range(n_mp)],
+        tokens,
+        [first_got, second, second_got],
+        [bf16, f32, bf16],
+        outputs,
+        sent,
     )
-    second_got = swap(give, "seq", x_bit)
-    first, second = together(first_keep + first_got.astype(f32), second_keep + second_got.astype(f32))
+    first_got, second_got = swap(first_give, "mp", y_bits[-1]), swap(second_give, "seq", x_bit)
+    first, second, sent = together(
+        first_keep + first_got.astype(f32), second_keep + second_got.astype(f32), sent
+    )
 
     def fold(total, axis, bits):
         middle = total.shape[0] // 2
@@ -252,7 +271,7 @@
     for bits in y_bits[:0:-1]:
         second = fold(second, "mp", bits)
     first, second = fold(first, "seq", x_bit), fold(second, "mp", y_bits[0])
-    returned = [swap(out, "seq", core_bit) for out in (out_first, out_second)]
+    returned = [swap(sent[block], "seq", core_bit) for block in range(blocks)]
     first, second, returned = together(first, second, returned)
     total = jnp.concatenate([first, second], axis=1)
     outputs = placing(n_mp, returned, *outputs)

time: 65.3 us -> 62.9 us (0.963)
  Pallas kernels: 13.9 us -> 11.3 us
    pallas_call x3 -> x2, Pallas kernels: 12.5 us -> 9.9 us  [attention(): pl.pallas_call(functools.partial(attention_kernel, n_mp, blocks, jobs, le...]
  transfers between devices with their start and end apart: 20 -> 20, of which waited for: 11 -> 13; matrix products, arithmetic and copies ran while one was open for 0% -> 0% of each run, Pallas kernels for 21% -> 7%
where the time goes in v4:
time: 62.9 us; the launch traced here: 62.6 us
  waiting for transfers between devices  26.8 us (43%)
  starting transfers between devices  21.2 us (34%)
  Pallas kernels  11.3 us (18%)
  local copies, waits for them, and re-layouts  2.21 us (4%)
  between operations  0.89 us (1%)
    ppermute x20, waiting for transfers between devices, swap(): return lax.ppermute(array, axis, [(i, i ^ bits) for i in range(size)])  26.8 us
    ppermute x20, starting transfers between devices, swap(): return lax.ppermute(array, axis, [(i, i ^ bits) for i in range(size)])  21.2 us
    pallas_call x2, Pallas kernels, attention(): pl.pallas_call(functools.partial(attention_kernel, n_mp, blocks, jobs, le...  9.9 us
    pallas_call x1, Pallas kernels, placing(): pl.pallas_call(functools.partial(placing_kernel, n_mp, blocks), in_specs=...  1.37 us
    unnamed x9, local copies, waits for them, and re-layouts  1.27 us
  transfers between devices with their start and end apart: 20, of which 13 were waited for; matrix products, arithmetic and copies ran while one was open for 0% of the time, Pallas kernels for 7%

profile of v4, /device:TPU:0, one launch (start us, length us, event | category | flops | bytes accessed | tf_op | source)
XLA Modules:
  0.0 62.6 jit_solution(3263989420406908621)
XLA Ops:
  0.6 0.8 %constant_dynamic-slice_fusion.2 = (bf16[8,512]{1,0:T(8,128)(2,1)S(1)}, bf16[8,512]{1,0:T(8,128)(2,1)S(1)}, bf16[8,512]{1,0:T(8,128)(2,1)S(1)}, bf16[8,512]{1,0:...) fusion(bf16[8,2048]{1,0:T(8,128)(2,1)} %param.6, ...), kind=kLoop, calls=%fused_computation.30 | loop fusion | bytes 131088 | tf_op jit(solution)/shard_map/slice | solution.py:217
  1.5 0.5 collective-permute-start
  2.0 0.9 %collective-permute-done = bf16[8,2048]{1,0:T(8,128)(2,1)S(1)} collective-permute-done((bf16[8,2048]{1,0:T(8,128)(2,1)S(1)}, bf16[8,2048]{1,0:T(8,128)(2,1)S(1)}, u32[]{:S(2)}, u32[]{:S(2)}) %collective-permute-start) | collective-permute-done | bytes 32800 | tf_op jit(solution)/shard_map/ppermute | solution.py:205
  2.9 0.3 collective-permute-start.1
  3.2 0.2 collective-permute-start.2
  3.4 2.9 %collective-permute-start.3 = (bf16[16,2048]{1,0:T(8,128)(2,1)S(1)}, bf16[16,2048]{1,0:T(8,128)(2,1)S(1)}, u32[]{:S(2)}, u32[]{:S(2)}) collective-permute-start(bf16[16,2048]{1,0:T(8,128)(2,1)S(1)} %pad_maximum_fusion.2), channel_id=1, source_target_pairs={{0,8},{2,10},{4,12},{6,14},{8,0},{10,2},{12,4},{14,6},{16,24},{18,... | collective-permute-start | bytes 196616 | tf_op jit(solution)/shard_map/ppermute | solution.py:205
  6.3 2.7 %collective-permute-start.4 = (bf16[16,2048]{1,0:T(8,128)(2,1)S(1)}, bf16[16,2048]{1,0:T(8,128)(2,1)S(1)}, u32[]{:S(2)}, u32[]{:S(2)}) collective-permute-start(bf16[16,2048]{1,0:T(8,128)(2,1)S(1)} %pad_maximum_fusion.2), channel_id=1, source_target_pairs={{0,16},{2,18},{4,20},{6,22},{8,24},{10,26},{12,28},{14,30},{16,0},... | collective-permute-start | bytes 196616 | tf_op jit(solution)/shard_map/ppermute | solution.py:205
  9.0 0.0 collective-permute-start.5
  9.0 0.0 collective-permute-done.3
  9.0 4.9 %collective-permute-done.4 = bf16[16,2048]{1,0:T(8,128)(2,1)S(1)} collective-permute-done((bf16[16,2048]{1,0:T(8,128)(2,1)S(1)}, bf16[16,2048]{1,0:T(8,128)(2,1)S(1)}, u32[]{:S(2)}, u32[]{:S(2)}) %collective-permute-start.4) | collective-permute-done | bytes 65568 | tf_op jit(solution)/shard_map/ppermute | solution.py:205
  13.9 1.2 %collective-permute-done.5 = bf16[16,2048]{1,0:T(8,128)(2,1)S(1)} collective-permute-done((bf16[16,2048]{1,0:T(8,128)(2,1)S(1)}, bf16[16,2048]{1,0:T(8,128)(2,1)S(1)}, u32[]{:S(2)}, u32[]{:S(2)}) %collective-permute-start.5) | collective-permute-done | bytes 65568 | tf_op jit(solution)/shard_map/ppermute | solution.py:205
  15.2 1.6 %collective-permute-start.6 = (bf16[64,1024]{1,0:T(8,128)(2,1)S(1)}, bf16[64,1024]{1,0:T(8,128)(2,1)S(1)}, u32[]{:S(2)}, u32[]{:S(2)}) collective-permute-start(bf16[64,1024]{1,0:T(8,128)(2,1)S(1)} %pad_maximum_fusion), channel_id=1, source_target_pairs={{0,4},{2,6},{4,0},{6,2},{8,12},{10,14},{12,8},{14,10},{16,20},{18,... | collective-permute-start | bytes 393224 | tf_op jit(solution)/shard_map/ppermute | solution.py:205
  16.7 1.6 %collective-permute-start.7 = (bf16[64,1024]{1,0:T(8,128)(2,1)S(1)}, bf16[64,1024]{1,0:T(8,128)(2,1)S(1)}, u32[]{:S(2)}, u32[]{:S(2)}) collective-permute-start(bf16[64,1024]{1,0:T(8,128)(2,1)S(1)} %pad_maximum_fusion.1), channel_id=1, source_target_pairs={{0,1},{1,0},{2,3},{3,2},{4,5},{5,4},{6,7},{7,6},{8,9},{9,8},{10,11... | collective-permute-start | bytes 393224 | tf_op jit(solution)/shard_map/ppermute | solution.py:205
  18.3 1.9 %collective-permute-done.6 = bf16[64,1024]{1,0:T(8,128)(2,1)S(1)} collective-permute-done((bf16[64,1024]{1,0:T(8,128)(2,1)S(1)}, bf16[64,1024]{1,0:T(8,128)(2,1)S(1)}, u32[]{:S(2)}, u32[]{:S(2)}) %collective-permute-start.6) | collective-permute-done | bytes 131104 | tf_op jit(solution)/shard_map/ppermute | solution.py:205
  20.2 1.6 %collective-permute-done.7 = bf16[64,1024]{1,0:T(8,128)(2,1)S(1)} collective-permute-done((bf16[64,1024]{1,0:T(8,128)(2,1)S(1)}, bf16[64,1024]{1,0:T(8,128)(2,1)S(1)}, u32[]{:S(2)}, u32[]{:S(2)}) %collective-permute-start.7) | collective-permute-done | bytes 131104 | tf_op jit(solution)/shard_map/ppermute | solution.py:205
  21.8 1.6 %collective-permute-start.8 = (bf16[128,1024]{1,0:T(8,128)(2,1)S(1)}, bf16[128,1024]{1,0:T(8,128)(2,1)S(1)}, u32[]{:S(2)}, u32[]{:S(2)}) collective-permute-start(bf16[128,1024]{1,0:T(8,128)(2,1)S(1)} %constant_dynamic-update-slice_fusion.refs_0_), channel_id=1, source_target_pairs={{0,1},{1,0},{2,3},{3,2},{4,5},{5,4},{6,7},{7,6},{8,9},{9,8},{10,11... | collective-permute-start | bytes 786440 | tf_op jit(solution)/shard_map/ppermute | solution.py:205
  23.4 0.9 %collective-permute-start.9 = (bf16[128,1024]{1,0:T(8,128)(2,1)S(1)}, bf16[128,1024]{1,0:T(8,128)(2,1)S(1)}, u32[]{:S(2)}, u32[]{:S(2)}) collective-permute-start(bf16[128,1024]{1,0:T(8,128)(2,1)S(1)} %constant_dynamic-update-slice_fusion.5.refs_1_), channel_id=1, source_target_pairs={{0,4},{2,6},{4,0},{6,2},{8,12},{10,14},{12,8},{14,10},{16,20},{18,... | collective-permute-start | bytes 786440 | tf_op jit(solution)/shard_map/ppermute | solution.py:205
  24.3 0.0 collective-permute-done.1.sq_ref
  24.3 0.0 collective-permute-done.2.sg_ref
  24.3 3.2 %shard_map.75 = (bf16[256,4096]{1,0:T(8,128)(2,1)}, bf16[256,4096]{1,0:T(8,128)(2,1)}, bf16[256,2048]{1,0:T(8,128)(2,1)S(1)}, f32[128,1024]{1,0:T(8,128)S(1)}) custom-call(bf16[256,4096]{1,0:T(8,128)(2,1)} %q_ref.3, bf16[256,4096]{1,0:T(8,128)(2,1)} %g_ref.3, bf16[256,4096]{1,0:T(8,128)(2,1)S(1)} %collective-permute-done.1.sq_ref, ...), custom_call_target="tpu_custom_call" | custom-call | flops 402653184 | bytes 2097152 | tf_op jit(solution)/shard_map/pallas_call | solution.py:142
  27.4 0.8 %collective-permute-done.8.refs_0_ = bf16[128,1024]{1,0:T(8,128)(2,1)S(1)} collective-permute-done((bf16[128,1024]{1,0:T(8,128)(2,1)S(1)}, bf16[128,1024]{1,0:T(8,128)(2,1)S(1)}, u32[]{:S(2)}, u32[]{:S(2)}) %collective-permute-start.8) | collective-permute-done | bytes 262176 | tf_op jit(solution)/shard_map/ppermute | solution.py:205
  28.2 1.6 %collective-permute-done.9.refs_2_ = bf16[128,1024]{1,0:T(8,128)(2,1)S(1)} collective-permute-done((bf16[128,1024]{1,0:T(8,128)(2,1)S(1)}, bf16[128,1024]{1,0:T(8,128)(2,1)S(1)}, u32[]{:S(2)}, u32[]{:S(2)}) %collective-permute-start.9) | collective-permute-done | bytes 262176 | tf_op jit(solution)/shard_map/ppermute | solution.py:205
  29.8 6.7 %shard_map.76 = (bf16[256,4096]{1,0:T(8,128)(2,1)}, bf16[256,4096]{1,0:T(8,128)(2,1)}, bf16[256,2048]{1,0:T(8,128)(2,1)S(1)}, bf16[256,2048]{1,0:T(8,128)(2,1)S(...) custom-call(bf16[256,4096]{1,0:T(8,128)(2,1)} %q_ref.3, ...), custom_call_target="tpu_custom_call", output_to_operand_aliasing={{0}: (7, {}), {1}: (8, {}), {2}: (9, {})} | custom-call | flops 1207959552 | bytes 6291456 | tf_op jit(solution)/shard_map/pallas_call | solution.py:142
  36.6 0.6 collective-permute-start.10
  37.1 0.8 %collective-permute-start.11 = (bf16[128,1024]{1,0:T(8,128)(2,1)S(1)}, bf16[128,1024]{1,0:T(8,128)(2,1)S(1)}, u32[]{:S(2)}, u32[]{:S(2)}) collective-permute-start(bf16[128,1024]{1,0:T(8,128)(2,1)S(1)} %get-tuple-element.46), channel_id=1, source_target_pairs={{0,4},{2,6},{4,0},{6,2},{8,12},{10,14},{12,8},{14,10},{16,20},{18,... | collective-permute-start | bytes 786440 | tf_op jit(solution)/shard_map/ppermute | solution.py:205
  38.0 5.0 %collective-permute-done.10 = bf16[128,1024]{1,0:T(8,128)(2,1)S(1)} collective-permute-done((bf16[128,1024]{1,0:T(8,128)(2,1)S(1)}, bf16[128,1024]{1,0:T(8,128)(2,1)S(1)}, u32[]{:S(2)}, u32[]{:S(2)}) %collective-permute-start.10) | collective-permute-done | bytes 262176 | tf_op jit(solution)/shard_map/ppermute | solution.py:205
  43.0 0.1 convert_add_fusion.1
  43.1 0.4 collective-permute-done.11
  43.5 0.1 convert_add_fusion
  43.6 0.1 collective-permute-start.14
  43.7 0.5 collective-permute-start.15
  44.2 0.9 %collective-permute-start.12 = (bf16[64,1024]{1,0:T(8,128)(2,1)S(1)}, bf16[64,1024]{1,0:T(8,128)(2,1)S(1)}, u32[]{:S(2)}, u32[]{:S(2)}) collective-permute-start(bf16[64,1024]{1,0:T(8,128)(2,1)S(1)} %slice.176), channel_id=1, source_target_pairs={{0,4},{2,6},{4,0},{6,2},{8,12},{10,14},{12,8},{14,10},{16,20},{18,... | collective-permute-start | bytes 393224 | tf_op jit(solution)/shard_map/ppermute | solution.py:205
  45.1 1.6 %collective-permute-start.13 = (bf16[64,1024]{1,0:T(8,128)(2,1)S(1)}, bf16[64,1024]{1,0:T(8,128)(2,1)S(1)}, u32[]{:S(2)}, u32[]{:S(2)}) collective-permute-start(bf16[64,1024]{1,0:T(8,128)(2,1)S(1)} %slice.175), channel_id=1, source_target_pairs={{0,1},{1,0},{2,3},{3,2},{4,5},{5,4},{6,7},{7,6},{8,9},{9,8},{10,11... | collective-permute-start | bytes 393224 | tf_op jit(solution)/shard_map/ppermute | solution.py:205
  46.7 3.0 %collective-permute-done.12 = bf16[64,1024]{1,0:T(8,128)(2,1)S(1)} collective-permute-done((bf16[64,1024]{1,0:T(8,128)(2,1)S(1)}, bf16[64,1024]{1,0:T(8,128)(2,1)S(1)}, u32[]{:S(2)}, u32[]{:S(2)}) %collective-permute-start.12) | collective-permute-done | bytes 131104 | tf_op jit(solution)/shard_map/ppermute | solution.py:205
  49.8 0.6 collective-permute-done.13
  50.4 0.0 collective-permute-done.14.refs_0_
  50.4 0.0 collective-permute-done.15.refs_1_
  50.5 0.6 collective-permute-start.16
  51.1 2.9 %collective-permute-start.17 = (bf16[16,2048]{1,0:T(8,128)(2,1)S(1)}, bf16[16,2048]{1,0:T(8,128)(2,1)S(1)}, u32[]{:S(2)}, u32[]{:S(2)}) collective-permute-start(bf16[16,2048]{1,0:T(8,128)(2,1)S(1)} %get-tuple-element.67), channel_id=1, source_target_pairs={{0,16},{2,18},{4,20},{6,22},{8,24},{10,26},{12,28},{14,30},{16,0},... | collective-permute-start | bytes 196616 | tf_op jit(solution)/shard_map/ppermute | solution.py:205
  54.0 1.0 %collective-permute-start.18 = (bf16[16,2048]{1,0:T(8,128)(2,1)S(1)}, bf16[16,2048]{1,0:T(8,128)(2,1)S(1)}, u32[]{:S(2)}, u32[]{:S(2)}) collective-permute-start(bf16[16,2048]{1,0:T(8,128)(2,1)S(1)} %get-tuple-element.66), channel_id=1, source_target_pairs={{0,24},{2,26},{4,28},{6,30},{8,16},{10,18},{12,20},{14,22},{16,8},... | collective-permute-start | bytes 196616 | tf_op jit(solution)/shard_map/ppermute | solution.py:205
  55.0 1.4 %shard_map.77 = (bf16[256,4096]{1,0:T(8,128)(2,1)}, bf16[256,4096]{1,0:T(8,128)(2,1)}) custom-call(bf16[256,2048]{1,0:T(8,128)(2,1)S(1)} %collective-permute-done.14.refs_0_, bf16[256,2048]{1,0:T(8,128)(2,1)S(1)} %collective-permute-done.15.refs_1_, bf16[256,4096]{1,0:T(8,128)(2,1)} %get-tuple-element.57.refs_2_, ...), custom_call_target="tpu_custom_call", output_to_operand_aliasing={{0}: (2, {}), {1}: (3, {})} | custom-call | tf_op jit(solution)/shard_map/pallas_call | solution.py:188
  56.4 0.0 collective-permute-done.16
  56.4 0.0 collective-permute-done.17
  56.4 3.7 %collective-permute-done.18 = bf16[16,2048]{1,0:T(8,128)(2,1)S(1)} collective-permute-done((bf16[16,2048]{1,0:T(8,128)(2,1)S(1)}, bf16[16,2048]{1,0:T(8,128)(2,1)S(1)}, u32[]{:S(2)}, u32[]{:S(2)}) %collective-permute-start.18) | collective-permute-done | bytes 65568 | tf_op jit(solution)/shard_map/ppermute | solution.py:205
  60.1 0.1 collective-permute-start.19
  60.3 1.1 %collective-permute-done.19 = bf16[8,2048]{1,0:T(8,128)(2,1)S(1)} collective-permute-done((bf16[8,2048]{1,0:T(8,128)(2,1)S(1)}, bf16[8,2048]{1,0:T(8,128)(2,1)S(1)}, u32[]{:S(2)}, u32[]{:S(2)}) %collective-permute-start.19) | collective-permute-done | bytes 32800 | tf_op jit(solution)/shard_map/ppermute | solution.py:205
  61.4 0.6 copy-done.1
  62.0 0.6 copy-done
  (30 shorter events, 0.4 us)
Async XLA Ops:
  1.5 1.4 %collective-permute-start = (bf16[8,2048]{1,0:T(8,128)(2,1)S(1)}, bf16[8,2048]{1,0:T(8,128)(2,1)S(1)}, u32[]{:S(2)}, u32[]{:S(2)}) collective-permute-start(bf16[8,2048]{1,0:T(8,128)(2,1)S(1)} %pad_maximum_fusion.3), channel_id=1, source_target_pairs={{0,2},{2,0},{4,6},{6,4},{8,10},{10,8},{12,14},{14,12},{16,18},{18,... | collective-permute-start | bytes 98312 | tf_op jit(solution)/shard_map/ppermute | solution.py:205
  2.9 21.4 %collective-permute-start.1 = (bf16[256,4096]{1,0:T(8,128)(2,1)}, bf16[256,4096]{1,0:T(8,128)(2,1)S(1)}, u32[]{:S(2)}, u32[]{:S(2)}) collective-permute-start(bf16[256,4096]{1,0:T(8,128)(2,1)} %q_ref.3), channel_id=1, source_target_pairs={{0,2},{2,0},{4,6},{6,4},{8,10},{10,8},{12,14},{14,12},{16,18},{18,... | collective-permute-start | bytes 6291464 | tf_op jit(solution)/shard_map/ppermute | solution.py:205
  3.2 21.1 %collective-permute-start.2 = (bf16[256,4096]{1,0:T(8,128)(2,1)}, bf16[256,4096]{1,0:T(8,128)(2,1)S(1)}, u32[]{:S(2)}, u32[]{:S(2)}) collective-permute-start(bf16[256,4096]{1,0:T(8,128)(2,1)} %g_ref.3), channel_id=1, source_target_pairs={{0,2},{2,0},{4,6},{6,4},{8,10},{10,8},{12,14},{14,12},{16,18},{18,... | collective-permute-start | bytes 6291464 | tf_op jit(solution)/shard_map/ppermute | solution.py:205
  3.4 5.6 %collective-permute-start.3 = (bf16[16,2048]{1,0:T(8,128)(2,1)S(1)}, bf16[16,2048]{1,0:T(8,128)(2,1)S(1)}, u32[]{:S(2)}, u32[]{:S(2)}) collective-permute-start(bf16[16,2048]{1,0:T(8,128)(2,1)S(1)} %pad_maximum_fusion.2), channel_id=1, source_target_pairs={{0,8},{2,10},{4,12},{6,14},{8,0},{10,2},{12,4},{14,6},{16,24},{18,... | collective-permute-start | bytes 196616 | tf_op jit(solution)/shard_map/ppermute | solution.py:205
  6.3 7.6 %collective-permute-start.4 = (bf16[16,2048]{1,0:T(8,128)(2,1)S(1)}, bf16[16,2048]{1,0:T(8,128)(2,1)S(1)}, u32[]{:S(2)}, u32[]{:S(2)}) collective-permute-start(bf16[16,2048]{1,0:T(8,128)(2,1)S(1)} %pad_maximum_fusion.2), channel_id=1, source_target_pairs={{0,16},{2,18},{4,20},{6,22},{8,24},{10,26},{12,28},{14,30},{16,0},... | collective-permute-start | bytes 196616 | tf_op jit(solution)/shard_map/ppermute | solution.py:205
  9.0 6.2 %collective-permute-start.5 = (bf16[16,2048]{1,0:T(8,128)(2,1)S(1)}, bf16[16,2048]{1,0:T(8,128)(2,1)S(1)}, u32[]{:S(2)}, u32[]{:S(2)}) collective-permute-start(bf16[16,2048]{1,0:T(8,128)(2,1)S(1)} %pad_maximum_fusion.2), channel_id=1, source_target_pairs={{0,24},{2,26},{4,28},{6,30},{8,16},{10,18},{12,20},{14,22},{16,8},... | collective-permute-start | bytes 196616 | tf_op jit(solution)/shard_map/ppermute | solution.py:205
  15.2 5.0 %collective-permute-start.6 = (bf16[64,1024]{1,0:T(8,128)(2,1)S(1)}, bf16[64,1024]{1,0:T(8,128)(2,1)S(1)}, u32[]{:S(2)}, u32[]{:S(2)}) collective-permute-start(bf16[64,1024]{1,0:T(8,128)(2,1)S(1)} %pad_maximum_fusion), channel_id=1, source_target_pairs={{0,4},{2,6},{4,0},{6,2},{8,12},{10,14},{12,8},{14,10},{16,20},{18,... | collective-permute-start | bytes 393224 | tf_op jit(solution)/shard_map/ppermute | solution.py:205
  16.7 5.0 %collective-permute-start.7 = (bf16[64,1024]{1,0:T(8,128)(2,1)S(1)}, bf16[64,1024]{1,0:T(8,128)(2,1)S(1)}, u32[]{:S(2)}, u32[]{:S(2)}) collective-permute-start(bf16[64,1024]{1,0:T(8,128)(2,1)S(1)} %pad_maximum_fusion.1), channel_id=1, source_target_pairs={{0,1},{1,0},{2,3},{3,2},{4,5},{5,4},{6,7},{7,6},{8,9},{9,8},{10,11... | collective-permute-start | bytes 393224 | tf_op jit(solution)/shard_map/ppermute | solution.py:205
  21.8 6.4 %collective-permute-start.8 = (bf16[128,1024]{1,0:T(8,128)(2,1)S(1)}, bf16[128,1024]{1,0:T(8,128)(2,1)S(1)}, u32[]{:S(2)}, u32[]{:S(2)}) collective-permute-start(bf16[128,1024]{1,0:T(8,128)(2,1)S(1)} %constant_dynamic-update-slice_fusion.refs_0_), channel_id=1, source_target_pairs={{0,1},{1,0},{2,3},{3,2},{4,5},{5,4},{6,7},{7,6},{8,9},{9,8},{10,11... | collective-permute-start | bytes 786440 | tf_op jit(solution)/shard_map/ppermute | solution.py:205
  23.4 6.4 %collective-permute-start.9 = (bf16[128,1024]{1,0:T(8,128)(2,1)S(1)}, bf16[128,1024]{1,0:T(8,128)(2,1)S(1)}, u32[]{:S(2)}, u32[]{:S(2)}) collective-permute-start(bf16[128,1024]{1,0:T(8,128)(2,1)S(1)} %constant_dynamic-update-slice_fusion.5.refs_1_), channel_id=1, source_target_pairs={{0,4},{2,6},{4,0},{6,2},{8,12},{10,14},{12,8},{14,10},{16,20},{18,... | collective-permute-start | bytes 786440 | tf_op jit(solution)/shard_map/ppermute | solution.py:205
  36.6 6.4 %collective-permute-start.10 = (bf16[128,1024]{1,0:T(8,128)(2,1)S(1)}, bf16[128,1024]{1,0:T(8,128)(2,1)S(1)}, u32[]{:S(2)}, u32[]{:S(2)}) collective-permute-start(bf16[128,1024]{1,0:T(8,128)(2,1)S(1)} %get-tuple-element.44), channel_id=1, source_target_pairs={{0,1},{1,0},{2,3},{3,2},{4,5},{5,4},{6,7},{7,6},{8,9},{9,8},{10,11... | collective-permute-start | bytes 786440 | tf_op jit(solution)/shard_map/ppermute | solution.py:205
  37.1 6.4 %collective-permute-start.11 = (bf16[128,1024]{1,0:T(8,128)(2,1)S(1)}, bf16[128,1024]{1,0:T(8,128)(2,1)S(1)}, u32[]{:S(2)}, u32[]{:S(2)}) collective-permute-start(bf16[128,1024]{1,0:T(8,128)(2,1)S(1)} %get-tuple-element.46), channel_id=1, source_target_pairs={{0,4},{2,6},{4,0},{6,2},{8,12},{10,14},{12,8},{14,10},{16,20},{18,... | collective-permute-start | bytes 786440 | tf_op jit(solution)/shard_map/ppermute | solution.py:205
  43.6 6.8 %collective-permute-start.14 = (bf16[256,2048]{1,0:T(8,128)(2,1)S(1)}, bf16[256,2048]{1,0:T(8,128)(2,1)S(1)}, u32[]{:S(2)}, u32[]{:S(2)}) collective-permute-start(bf16[256,2048]{1,0:T(8,128)(2,1)S(1)} %get-tuple-element.51), channel_id=1, source_target_pairs={{0,2},{2,0},{4,6},{6,4},{8,10},{10,8},{12,14},{14,12},{16,18},{18,... | collective-permute-start | bytes 3145736 | tf_op jit(solution)/shard_map/ppermute | solution.py:205
  43.7 6.7 %collective-permute-start.15 = (bf16[256,2048]{1,0:T(8,128)(2,1)S(1)}, bf16[256,2048]{1,0:T(8,128)(2,1)S(1)}, u32[]{:S(2)}, u32[]{:S(2)}) collective-permute-start(bf16[256,2048]{1,0:T(8,128)(2,1)S(1)} %get-tuple-element.52), channel_id=1, source_target_pairs={{0,2},{2,0},{4,6},{6,4},{8,10},{10,8},{12,14},{14,12},{16,18},{18,... | collective-permute-start | bytes 3145736 | tf_op jit(solution)/shard_map/ppermute | solution.py:205
  44.2 5.5 %collective-permute-start.12 = (bf16[64,1024]{1,0:T(8,128)(2,1)S(1)}, bf16[64,1024]{1,0:T(8,128)(2,1)S(1)}, u32[]{:S(2)}, u32[]{:S(2)}) collective-permute-start(bf16[64,1024]{1,0:T(8,128)(2,1)S(1)} %slice.176), channel_id=1, source_target_pairs={{0,4},{2,6},{4,0},{6,2},{8,12},{10,14},{12,8},{14,10},{16,20},{18,... | collective-permute-start | bytes 393224 | tf_op jit(solution)/shard_map/ppermute | solution.py:205
  45.1 5.3 %collective-permute-start.13 = (bf16[64,1024]{1,0:T(8,128)(2,1)S(1)}, bf16[64,1024]{1,0:T(8,128)(2,1)S(1)}, u32[]{:S(2)}, u32[]{:S(2)}) collective-permute-start(bf16[64,1024]{1,0:T(8,128)(2,1)S(1)} %slice.175), channel_id=1, source_target_pairs={{0,1},{1,0},{2,3},{3,2},{4,5},{5,4},{6,7},{7,6},{8,9},{9,8},{10,11... | collective-permute-start | bytes 393224 | tf_op jit(solution)/shard_map/ppermute | solution.py:205
  50.5 5.8 %collective-permute-start.16 = (bf16[16,2048]{1,0:T(8,128)(2,1)S(1)}, bf16[16,2048]{1,0:T(8,128)(2,1)S(1)}, u32[]{:S(2)}, u32[]{:S(2)}) collective-permute-start(bf16[16,2048]{1,0:T(8,128)(2,1)S(1)} %get-tuple-element.68), channel_id=1, source_target_pairs={{0,8},{2,10},{4,12},{6,14},{8,0},{10,2},{12,4},{14,6},{16,24},{18,... | collective-permute-start | bytes 196616 | tf_op jit(solution)/shard_map/ppermute | solution.py:205
  51.1 5.3 %collective-permute-start.17 = (bf16[16,2048]{1,0:T(8,128)(2,1)S(1)}, bf16[16,2048]{1,0:T(8,128)(2,1)S(1)}, u32[]{:S(2)}, u32[]{:S(2)}) collective-permute-start(bf16[16,2048]{1,0:T(8,128)(2,1)S(1)} %get-tuple-element.67), channel_id=1, source_target_pairs={{0,16},{2,18},{4,20},{6,22},{8,24},{10,26},{12,28},{14,30},{16,0},... | collective-permute-start | bytes 196616 | tf_op jit(solution)/shard_map/ppermute | solution.py:205
  54.0 6.1 %collective-permute-start.18 = (bf16[16,2048]{1,0:T(8,128)(2,1)S(1)}, bf16[16,2048]{1,0:T(8,128)(2,1)S(1)}, u32[]{:S(2)}, u32[]{:S(2)}) collective-permute-start(bf16[16,2048]{1,0:T(8,128)(2,1)S(1)} %get-tuple-element.66), channel_id=1, source_target_pairs={{0,24},{2,26},{4,28},{6,30},{8,16},{10,18},{12,20},{14,22},{16,8},... | collective-permute-start | bytes 196616 | tf_op jit(solution)/shard_map/ppermute | solution.py:205
  60.1 1.3 %collective-permute-start.19 = (bf16[8,2048]{1,0:T(8,128)(2,1)S(1)}, bf16[8,2048]{1,0:T(8,128)(2,1)S(1)}, u32[]{:S(2)}, u32[]{:S(2)}) collective-permute-start(bf16[8,2048]{1,0:T(8,128)(2,1)S(1)} %slice.153), channel_id=1, source_target_pairs={{0,2},{2,0},{4,6},{6,4},{8,10},{10,8},{12,14},{14,12},{16,18},{18,... | collective-permute-start | bytes 98312 | tf_op jit(solution)/shard_map/ppermute | solution.py:205
  61.4 0.6 copy-start.1
  62.0 0.6 copy-start

commit v5 on v4

--- a/solution.py
+++ b/solution.py
@@ -23,7 +23,7 @@
 def softmax_part(raw, prob_grad):
     temper = 1.0 / math.sqrt(DH)
     peak = jnp.max(raw, axis=0, keepdims=True)
-    powers = jnp.exp2((raw - peak) * (temper * math.log2(math.e)))
+    powers = jnp.exp((raw - peak) * temper)
     inverse = 1.0 / jnp.sum(powers, axis=0, keepdims=True)
     delta = jnp.sum(powers * prob_grad, axis=0, keepdims=True) * inverse
     weights = (powers * inverse).astype(bf16)
@@ -51,10 +51,11 @@
     targets = [[slice(m * width + n * DH, m * width + (n + 1) * DH) for n in range(heads)] for m in (0, 1)]
 
     def inputs(j):
-        where = pl.ds(columns(n_mp, blocks, jobs[j][0], width, False)(jobs[j][1]), width)
+        block, r = jobs[j][:2]
+        starts = (columns(n_mp, blocks, block, width, False)(r), (block * n_mp + r) * width)
         return [
             pltpu.make_async_copy(
-                array.at[:, where], token_buf.at[j, m, pl.ds(n * count, count)], sems.at[0, j, m, n]
+                array.at[:, pl.ds(starts[n], width)], token_buf.at[j, m, pl.ds(n * count, count)], sems.at[0, j, m, n]
             )
             for m, pair in enumerate(((q_ref, sq_ref), (g_ref, sg_ref)))
             for n, array in enumerate(pair)
@@ -77,9 +78,12 @@
             [memory_refs[i][start : start + size, targets[m][n]] for i, start, size in jobs[j][2]], axis=0
         )
 
+    memory = {}
+
     def scores(j, n, slot):
-        raw_ref[slot] = dot(memory_of(j, 0, n), token_buf[j, 0, :, cols[n]], NT)
-        prob_ref[slot] = dot(memory_of(j, 1, n), token_buf[j, 1, :, cols[n]], NT)
+        memory[j, n] = [memory_of(j, m, n) for m in (0, 1)]
+        raw_ref[slot] = dot(memory[j, n][0], token_buf[j, 0, :, cols[n]], NT)
+        prob_ref[slot] = dot(memory[j, n][1], token_buf[j, 1, :, cols[n]], NT)
 
     def softmax(slot):
         for begin in range(0, 2 * count, step):
@@ -90,7 +94,7 @@
 
     def results(j, n, slot):
         for m, pair_ref in enumerate((grad_ref, weight_ref)):
-            result_buf[j, m, :, cols[n]] = dot(memory_of(j, m, n).T, pair_ref[slot], NN).astype(bf16).T
+            result_buf[j, m, :, cols[n]] = dot(memory[j, n][m].T, pair_ref[slot], NN).astype(bf16).T
 
     def terms(j, n, slot):
         for m, pair_ref in enumerate((grad_ref, weight_ref)):
@@ -161,6 +165,63 @@
     return results[:2], sent, results[2 + len(used) :]
 
 
+def packing_kernel(n_mp, blocks, q_ref, g_ref, packed_q_ref, packed_g_ref, sems):
+    width = packed_q_ref.shape[1] // (blocks * n_mp)
+    copies = []
+    for block in range(blocks):
+        column = columns(n_mp, blocks, block, width, True)
+        for r in range(n_mp):
+            where = pl.ds((block * n_mp + r) * width, width)
+            for array, packed in ((q_ref, packed_q_ref), (g_ref, packed_g_ref)):
+                copies.append(
+                    pltpu.make_async_copy(
+                        array.at[:, pl.ds(column(r), width)], packed.at[:, where], sems.at[len(copies)]
+                    )
+                )
+    for copy in copies:
+        copy.start()
+    for copy in copies:
+        copy.wait()
+
+
+def packing(n_mp, blocks, queries, grad):
+    rows, whole = queries.shape
+    return pl.pallas_call(
+        functools.partial(packing_kernel, n_mp, blocks),
+        in_specs=[HBM] * 2,
+        out_specs=[VMEM] * 2,
+        out_shape=[pltpu.VMEM((rows, whole // 2), bf16)] * 2,
+        scratch_shapes=[pltpu.SemaphoreType.DMA((2 * blocks * n_mp,))],
+        cost_estimate=pl.CostEstimate(flops=0, bytes_accessed=4 * rows * whole, transcendentals=0),
+    )(*pinned(pltpu.HBM, queries, grad))
+
+
+def joining_kernel(blocks, mine_ref, other_ref, key_ref, value_ref, sems):
+    core, block = lax.axis_index("seq") & 1, mine_ref.shape[1] // (2 * blocks)
+    copies = []
+    for place, source in ((core, mine_ref), (1 - core, other_ref)):
+        for n in range(blocks):
+            where = pl.ds(pl.multiple_of((place * blocks + n) * block, block), block)
+            for m, target in enumerate((key_ref, value_ref)):
+                part = source.at[:, pl.ds((2 * n + m) * block, block)]
+                copies.append(pltpu.make_async_copy(part, target.at[:, where], sems.at[len(copies)]))
+    for copy in copies:
+        copy.start()
+    for copy in copies:
+        copy.wait()
+
+
+def joining(blocks, mine, other):
+    rows, width = mine.shape
+    return pl.pallas_call(
+        functools.partial(joining_kernel, blocks),
+        in_specs=[VMEM] * 2,
+        out_specs=[HBM] * 2,
+        out_shape=[jax.ShapeDtypeStruct((rows, width), bf16)] * 2,
+        scratch_shapes=[pltpu.SemaphoreType.DMA((4 * blocks,))],
+    )(*pinned(pltpu.VMEM, mine, other))
+
+
 def placing_kernel(n_mp, blocks, *refs):
     returned_refs, (attended_ref, query_grad_ref, sems) = refs[:blocks], refs[-3:]
     width = returned_refs[0].shape[1] // (2 * n_mp)
@@ -205,7 +266,7 @@
         return lax.ppermute(array, axis, [(i, i ^ bits) for i in range(size)])
 
     core_bit, x_bit = 1, 2
-    z_bits = range(4, n_seq, 4)
+    z_bits = range(n_seq - 4, 0, -4)
     y_bits = [1 << b for b in range(n_mp.bit_length() - 1)]
     rows, part = memory_keys.shape
     share, blocks = part // 2, 2
@@ -217,11 +278,12 @@
         return jnp.concatenate([b[:, n * block : (n + 1) * block] for n in range(blocks) for b in both], axis=1)
 
     base = jnp.concatenate([packed(core), swap(packed(1 - core), "seq", core_bit)])
-    base, queries_out, grad_out = together(base, queries, output_grad)
-    sibling_queries, sibling_grad = swap(queries_out, "seq", core_bit), swap(grad_out, "seq", core_bit)
-    tokens = (queries, output_grad, sibling_queries, sibling_grad)
-
-    got = [base] + [swap(base, "seq", bits) for bits in z_bits]
+
+    got = [swap(base, "seq", bits) for bits in z_bits]
+    got[-1], queries_out, grad_out = together(got[-1], queries, output_grad)
+    tokens = (queries, output_grad)
+    tokens += tuple(swap(array, "seq", core_bit) for array in packing(n_mp, blocks, queries_out, grad_out))
+    got = [base] + got
     first, second = (jnp.concatenate([g[:, n * 2 * block : (n + 1) * 2 * block] for g in got]) for n in (0, 1))
 
     def wider(held, got):
@@ -281,15 +343,7 @@
     total = (total[:count] + sum(g.astype(f32) for g in got)).astype(bf16)
     mine, other = total[:rows], swap(total[rows:], "seq", core_bit)
 
-    def joined(m):
-        a, b = (
-            jnp.concatenate([t[:, (2 * n + m) * block : (2 * n + m + 1) * block] for n in range(blocks)], axis=1)
-            for t in (mine, other)
-        )
-        whole = lax.dynamic_update_slice_in_dim(jnp.zeros((rows, part), bf16), a, core * share, axis=1)
-        return lax.dynamic_update_slice_in_dim(whole, b, (1 - core) * share, axis=1)
-
-    return (*outputs, joined(0), joined(1))
+    return (*outputs, *joining(blocks, mine, other))
 
 
 def solution(mesh):

time: 62.9 us -> 63.9 us (1.016)
  Pallas kernels: 11.3 us -> 13.8 us
  waiting for transfers between devices: 26.8 us -> 25.4 us
  local copies, waits for them, and re-layouts: 2.21 us -> 0.98 us
  starting transfers between devices: 21.2 us -> 22.4 us
    pallas_call x0 -> x2, Pallas kernels: none -> 2.28 us  [the longest x1 1.58 us: packing(): pl.pallas_call(functools.partial(packing_kernel, n_mp, blocks), in_specs=...]
    ppermute x20, waiting for transfers between devices: 26.8 us -> 25.4 us  [swap(): return lax.ppermute(array, axis, [(i, i ^ bits) for i in range(size)])]
    unnamed x9 -> x5, local copies, waits for them, and re-layouts: 1.27 us -> 0.06 us
    ppermute x20, starting transfers between devices: 21.2 us -> 22.4 us  [swap(): return lax.ppermute(array, axis, [(i, i ^ bits) for i in range(size)])]
  transfers between devices with their start and end apart: 20 -> 20, of which waited for: 13 -> 13; matrix products, arithmetic and copies ran while one was open for 0% -> 0% of each run, Pallas kernels for 7% -> 10%
where the time goes in v5:
time: 63.9 us; the launch traced here: 63.6 us
  waiting for transfers between devices  25.4 us (40%)
  starting transfers between devices  22.4 us (35%)
  Pallas kernels  13.8 us (22%)
  local copies, waits for them, and re-layouts  0.98 us (2%)
  between operations  0.86 us (1%)
    ppermute x20, waiting for transfers between devices, swap(): return lax.ppermute(array, axis, [(i, i ^ bits) for i in range(size)])  25.4 us
    ppermute x20, starting transfers between devices, swap(): return lax.ppermute(array, axis, [(i, i ^ bits) for i in range(size)])  22.4 us
    pallas_call x2, Pallas kernels, attention(): pl.pallas_call(functools.partial(attention_kernel, n_mp, blocks, jobs, le...  10.1 us
    pallas_call x1, Pallas kernels, packing(): pl.pallas_call(functools.partial(packing_kernel, n_mp, blocks), in_specs=...  1.58 us
    pallas_call x1, Pallas kernels, placing(): pl.pallas_call(functools.partial(placing_kernel, n_mp, blocks), in_specs=...  1.37 us
  transfers between devices with their start and end apart: 20, of which 13 were waited for; matrix products, arithmetic and copies ran while one was open for 0% of the time, Pallas kernels for 10%

profile of v5, /device:TPU:0, one launch (start us, length us, event | category | flops | bytes accessed | tf_op | source)
XLA Modules:
  0.0 63.6 jit_solution(10605860640800222312)
XLA Ops:
  0.6 0.8 %constant_dynamic-slice_fusion.2 = (bf16[8,512]{1,0:T(8,128)(2,1)S(1)}, bf16[8,512]{1,0:T(8,128)(2,1)S(1)}, bf16[8,512]{1,0:T(8,128)(2,1)S(1)}, bf16[8,512]{1,0:...) fusion(bf16[8,2048]{1,0:T(8,128)(2,1)} %param.6, ...), kind=kLoop, calls=%fused_computation.26 | loop fusion | bytes 131088 | tf_op jit(solution)/shard_map/slice | solution.py:278
  1.5 0.5 collective-permute-start
  2.0 0.9 %collective-permute-done = bf16[8,2048]{1,0:T(8,128)(2,1)S(1)} collective-permute-done((bf16[8,2048]{1,0:T(8,128)(2,1)S(1)}, bf16[8,2048]{1,0:T(8,128)(2,1)S(1)}, u32[]{:S(2)}, u32[]{:S(2)}) %collective-permute-start) | collective-permute-done | bytes 32800 | tf_op jit(solution)/shard_map/ppermute | solution.py:266
  2.9 3.9 %collective-permute-start.5 = (bf16[16,2048]{1,0:T(8,128)(2,1)S(1)}, bf16[16,2048]{1,0:T(8,128)(2,1)S(1)}, u32[]{:S(2)}, u32[]{:S(2)}) collective-permute-start(bf16[16,2048]{1,0:T(8,128)(2,1)S(1)} %pad_maximum_fusion.2), channel_id=1, source_target_pairs={{0,16},{2,18},{4,20},{6,22},{8,24},{10,26},{12,28},{14,30},{16,0},... | collective-permute-start | bytes 196616 | tf_op jit(solution)/shard_map/ppermute | solution.py:266
  6.8 1.3 %collective-permute-start.4 = (bf16[16,2048]{1,0:T(8,128)(2,1)S(1)}, bf16[16,2048]{1,0:T(8,128)(2,1)S(1)}, u32[]{:S(2)}, u32[]{:S(2)}) collective-permute-start(bf16[16,2048]{1,0:T(8,128)(2,1)S(1)} %pad_maximum_fusion.2), channel_id=1, source_target_pairs={{0,24},{2,26},{4,28},{6,30},{8,16},{10,18},{12,20},{14,22},{16,8},... | collective-permute-start | bytes 196616 | tf_op jit(solution)/shard_map/ppermute | solution.py:266
  8.1 0.2 collective-permute-start.1
  8.4 5.0 %collective-permute-done.1 = bf16[16,2048]{1,0:T(8,128)(2,1)S(1)} collective-permute-done((bf16[16,2048]{1,0:T(8,128)(2,1)S(1)}, bf16[16,2048]{1,0:T(8,128)(2,1)S(1)}, u32[]{:S(2)}, u32[]{:S(2)}) %collective-permute-start.1) | collective-permute-done | bytes 65568 | tf_op jit(solution)/shard_map/ppermute | solution.py:266
  13.4 1.6 %shard_map.75 = (bf16[256,2048]{1,0:T(8,128)(2,1)S(1)}, bf16[256,2048]{1,0:T(8,128)(2,1)S(1)}) custom-call(bf16[256,4096]{1,0:T(8,128)(2,1)} %q_ref.4, bf16[256,4096]{1,0:T(8,128)(2,1)} %g_ref.4), custom_call_target="tpu_custom_call" | custom-call | bytes 4194304 | tf_op jit(solution)/shard_map/pallas_call | solution.py:189
  15.0 0.1 collective-permute-start.2
  15.1 0.5 collective-permute-start.3
  15.6 0.0 collective-permute-done.4
  15.6 0.0 collective-permute-done.5
  15.6 1.7 %collective-permute-start.6 = (bf16[64,1024]{1,0:T(8,128)(2,1)S(1)}, bf16[64,1024]{1,0:T(8,128)(2,1)S(1)}, u32[]{:S(2)}, u32[]{:S(2)}) collective-permute-start(bf16[64,1024]{1,0:T(8,128)(2,1)S(1)} %pad_maximum_fusion), channel_id=1, source_target_pairs={{0,4},{2,6},{4,0},{6,2},{8,12},{10,14},{12,8},{14,10},{16,20},{18,... | collective-permute-start | bytes 393224 | tf_op jit(solution)/shard_map/ppermute | solution.py:266
  17.4 1.6 %collective-permute-start.7 = (bf16[64,1024]{1,0:T(8,128)(2,1)S(1)}, bf16[64,1024]{1,0:T(8,128)(2,1)S(1)}, u32[]{:S(2)}, u32[]{:S(2)}) collective-permute-start(bf16[64,1024]{1,0:T(8,128)(2,1)S(1)} %pad_maximum_fusion.1), channel_id=1, source_target_pairs={{0,1},{1,0},{2,3},{3,2},{4,5},{5,4},{6,7},{7,6},{8,9},{9,8},{10,11... | collective-permute-start | bytes 393224 | tf_op jit(solution)/shard_map/ppermute | solution.py:266
  19.0 2.2 %collective-permute-done.6 = bf16[64,1024]{1,0:T(8,128)(2,1)S(1)} collective-permute-done((bf16[64,1024]{1,0:T(8,128)(2,1)S(1)}, bf16[64,1024]{1,0:T(8,128)(2,1)S(1)}, u32[]{:S(2)}, u32[]{:S(2)}) %collective-permute-start.6) | collective-permute-done | bytes 131104 | tf_op jit(solution)/shard_map/ppermute | solution.py:266
  21.2 1.4 %collective-permute-done.7 = bf16[64,1024]{1,0:T(8,128)(2,1)S(1)} collective-permute-done((bf16[64,1024]{1,0:T(8,128)(2,1)S(1)}, bf16[64,1024]{1,0:T(8,128)(2,1)S(1)}, u32[]{:S(2)}, u32[]{:S(2)}) %collective-permute-start.7) | collective-permute-done | bytes 131104 | tf_op jit(solution)/shard_map/ppermute | solution.py:266
  22.7 0.4 collective-permute-start.9
  23.1 1.7 %collective-permute-start.8 = (bf16[128,1024]{1,0:T(8,128)(2,1)S(1)}, bf16[128,1024]{1,0:T(8,128)(2,1)S(1)}, u32[]{:S(2)}, u32[]{:S(2)}) collective-permute-start(bf16[128,1024]{1,0:T(8,128)(2,1)S(1)} %constant_dynamic-update-slice_fusion.refs_0_), channel_id=1, source_target_pairs={{0,1},{1,0},{2,3},{3,2},{4,5},{5,4},{6,7},{7,6},{8,9},{9,8},{10,11... | collective-permute-start | bytes 786440 | tf_op jit(solution)/shard_map/ppermute | solution.py:266
  24.9 0.0 collective-permute-done.2.sq_ref
  24.9 0.0 collective-permute-done.3.sg_ref
  24.9 3.2 %shard_map.76 = (bf16[256,4096]{1,0:T(8,128)(2,1)}, bf16[256,4096]{1,0:T(8,128)(2,1)}, bf16[256,2048]{1,0:T(8,128)(2,1)S(1)}, f32[128,1024]{1,0:T(8,128)S(1)}) custom-call(bf16[256,4096]{1,0:T(8,128)(2,1)} %q_ref.4, bf16[256,4096]{1,0:T(8,128)(2,1)} %g_ref.4, bf16[256,2048]{1,0:T(8,128)(2,1)S(1)} %collective-permute-done.2.sq_ref, ...), custom_call_target="tpu_custom_call" | custom-call | flops 402653184 | bytes 2097152 | tf_op jit(solution)/shard_map/pallas_call | solution.py:146
  28.1 1.8 %collective-permute-done.9.refs_2_ = bf16[128,1024]{1,0:T(8,128)(2,1)S(1)} collective-permute-done((bf16[128,1024]{1,0:T(8,128)(2,1)S(1)}, bf16[128,1024]{1,0:T(8,128)(2,1)S(1)}, u32[]{:S(2)}, u32[]{:S(2)}) %collective-permute-start.9) | collective-permute-done | bytes 262176 | tf_op jit(solution)/shard_map/ppermute | solution.py:266
  29.8 0.3 collective-permute-done.8.refs_0_
  30.2 6.9 %shard_map.77 = (bf16[256,4096]{1,0:T(8,128)(2,1)}, bf16[256,4096]{1,0:T(8,128)(2,1)}, bf16[256,2048]{1,0:T(8,128)(2,1)S(1)}, bf16[256,2048]{1,0:T(8,128)(2,1)S(...) custom-call(bf16[256,4096]{1,0:T(8,128)(2,1)} %q_ref.4, ...), custom_call_target="tpu_custom_call", output_to_operand_aliasing={{0}: (7, {}), {1}: (8, {}), {2}: (9, {})} | custom-call | flops 1207959552 | bytes 6291456 | tf_op jit(solution)/shard_map/pallas_call | solution.py:146
  37.1 1.6 %collective-permute-start.10 = (bf16[128,1024]{1,0:T(8,128)(2,1)S(1)}, bf16[128,1024]{1,0:T(8,128)(2,1)S(1)}, u32[]{:S(2)}, u32[]{:S(2)}) collective-permute-start(bf16[128,1024]{1,0:T(8,128)(2,1)S(1)} %get-tuple-element.50), channel_id=1, source_target_pairs={{0,1},{1,0},{2,3},{3,2},{4,5},{5,4},{6,7},{7,6},{8,9},{9,8},{10,11... | collective-permute-start | bytes 786440 | tf_op jit(solution)/shard_map/ppermute | solution.py:266
  38.7 1.5 %collective-permute-start.11 = (bf16[128,1024]{1,0:T(8,128)(2,1)S(1)}, bf16[128,1024]{1,0:T(8,128)(2,1)S(1)}, u32[]{:S(2)}, u32[]{:S(2)}) collective-permute-start(bf16[128,1024]{1,0:T(8,128)(2,1)S(1)} %get-tuple-element.52), channel_id=1, source_target_pairs={{0,4},{2,6},{4,0},{6,2},{8,12},{10,14},{12,8},{14,10},{16,20},{18,... | collective-permute-start | bytes 786440 | tf_op jit(solution)/shard_map/ppermute | solution.py:266
  40.2 3.3 %collective-permute-done.10 = bf16[128,1024]{1,0:T(8,128)(2,1)S(1)} collective-permute-done((bf16[128,1024]{1,0:T(8,128)(2,1)S(1)}, bf16[128,1024]{1,0:T(8,128)(2,1)S(1)}, u32[]{:S(2)}, u32[]{:S(2)}) %collective-permute-start.10) | collective-permute-done | bytes 262176 | tf_op jit(solution)/shard_map/ppermute | solution.py:266
  43.5 0.1 convert_add_fusion.1
  43.6 1.5 %collective-permute-done.11 = bf16[128,1024]{1,0:T(8,128)(2,1)S(1)} collective-permute-done((bf16[128,1024]{1,0:T(8,128)(2,1)S(1)}, bf16[128,1024]{1,0:T(8,128)(2,1)S(1)}, u32[]{:S(2)}, u32[]{:S(2)}) %collective-permute-start.11) | collective-permute-done | bytes 262176 | tf_op jit(solution)/shard_map/ppermute | solution.py:266
  45.1 0.1 convert_add_fusion
  45.1 0.1 collective-permute-start.14
  45.2 0.5 collective-permute-start.15
  45.7 0.6 collective-permute-start.13
  46.3 1.6 %collective-permute-start.12 = (bf16[64,1024]{1,0:T(8,128)(2,1)S(1)}, bf16[64,1024]{1,0:T(8,128)(2,1)S(1)}, u32[]{:S(2)}, u32[]{:S(2)}) collective-permute-start(bf16[64,1024]{1,0:T(8,128)(2,1)S(1)} %slice.136), channel_id=1, source_target_pairs={{0,4},{2,6},{4,0},{6,2},{8,12},{10,14},{12,8},{14,10},{16,20},{18,... | collective-permute-start | bytes 393224 | tf_op jit(solution)/shard_map/ppermute | solution.py:266
  47.9 3.4 %collective-permute-done.13 = bf16[64,1024]{1,0:T(8,128)(2,1)S(1)} collective-permute-done((bf16[64,1024]{1,0:T(8,128)(2,1)S(1)}, bf16[64,1024]{1,0:T(8,128)(2,1)S(1)}, u32[]{:S(2)}, u32[]{:S(2)}) %collective-permute-start.13) | collective-permute-done | bytes 131104 | tf_op jit(solution)/shard_map/ppermute | solution.py:266
  51.3 0.3 collective-permute-done.12
  51.6 0.0 collective-permute-done.14.refs_0_
  51.6 0.0 collective-permute-done.15.refs_1_
  51.7 0.4 collective-permute-start.18
  52.1 3.4 %collective-permute-start.17 = (bf16[16,2048]{1,0:T(8,128)(2,1)S(1)}, bf16[16,2048]{1,0:T(8,128)(2,1)S(1)}, u32[]{:S(2)}, u32[]{:S(2)}) collective-permute-start(bf16[16,2048]{1,0:T(8,128)(2,1)S(1)} %get-tuple-element.75), channel_id=1, source_target_pairs={{0,16},{2,18},{4,20},{6,22},{8,24},{10,26},{12,28},{14,30},{16,0},... | collective-permute-start | bytes 196616 | tf_op jit(solution)/shard_map/ppermute | solution.py:266
  55.6 0.6 collective-permute-start.16
  56.2 1.4 %shard_map.78 = (bf16[256,4096]{1,0:T(8,128)(2,1)}, bf16[256,4096]{1,0:T(8,128)(2,1)}) custom-call(bf16[256,2048]{1,0:T(8,128)(2,1)S(1)} %collective-permute-done.14.refs_0_, bf16[256,2048]{1,0:T(8,128)(2,1)S(1)} %collective-permute-done.15.refs_1_, bf16[256,4096]{1,0:T(8,128)(2,1)} %get-tuple-element.63.refs_2_, ...), custom_call_target="tpu_custom_call", output_to_operand_aliasing={{0}: (2, {}), {1}: (3, {})} | custom-call | tf_op jit(solution)/shard_map/pallas_call | solution.py:249
  57.6 0.0 collective-permute-done.18
  57.6 1.7 %collective-permute-done.17 = bf16[16,2048]{1,0:T(8,128)(2,1)S(1)} collective-permute-done((bf16[16,2048]{1,0:T(8,128)(2,1)S(1)}, bf16[16,2048]{1,0:T(8,128)(2,1)S(1)}, u32[]{:S(2)}, u32[]{:S(2)}) %collective-permute-start.17) | collective-permute-done | bytes 65568 | tf_op jit(solution)/shard_map/ppermute | solution.py:266
  59.3 2.3 %collective-permute-done.16 = bf16[16,2048]{1,0:T(8,128)(2,1)S(1)} collective-permute-done((bf16[16,2048]{1,0:T(8,128)(2,1)S(1)}, bf16[16,2048]{1,0:T(8,128)(2,1)S(1)}, u32[]{:S(2)}, u32[]{:S(2)}) %collective-permute-start.16) | collective-permute-done | bytes 65568 | tf_op jit(solution)/shard_map/ppermute | solution.py:266
  61.7 0.1 collective-permute-start.19
  61.8 1.2 %collective-permute-done.19.other_ref = bf16[8,2048]{1,0:T(8,128)(2,1)S(1)} collective-permute-done((bf16[8,2048]{1,0:T(8,128)(2,1)S(1)}, bf16[8,2048]{1,0:T(8,128)(2,1)S(1)}, u32[]{:S(2)}, u32[]{:S(2)}) %collective-permute-start.19) | collective-permute-done | bytes 32800 | tf_op jit(solution)/shard_map/ppermute | solution.py:266
  62.9 0.7 %shard_map.79 = (bf16[8,2048]{1,0:T(8,128)(2,1)}, bf16[8,2048]{1,0:T(8,128)(2,1)}) custom-call(bf16[8,2048]{1,0:T(8,128)(2,1)S(1)} %get-tuple-element.78.mine_ref, bf16[8,2048]{1,0:T(8,128)(2,1)S(1)} %collective-permute-done.19.other_ref), custom_call_target="tpu_custom_call" | custom-call | tf_op jit(solution)/shard_map/pallas_call | solution.py:216
  (20 shorter events, 0.3 us)
Async XLA Ops:
  1.5 1.4 %collective-permute-start = (bf16[8,2048]{1,0:T(8,128)(2,1)S(1)}, bf16[8,2048]{1,0:T(8,128)(2,1)S(1)}, u32[]{:S(2)}, u32[]{:S(2)}) collective-permute-start(bf16[8,2048]{1,0:T(8,128)(2,1)S(1)} %pad_maximum_fusion.3), channel_id=1, source_target_pairs={{0,2},{2,0},{4,6},{6,4},{8,10},{10,8},{12,14},{14,12},{16,18},{18,... | collective-permute-start | bytes 98312 | tf_op jit(solution)/shard_map/ppermute | solution.py:266
  2.9 12.7 %collective-permute-start.5 = (bf16[16,2048]{1,0:T(8,128)(2,1)S(1)}, bf16[16,2048]{1,0:T(8,128)(2,1)S(1)}, u32[]{:S(2)}, u32[]{:S(2)}) collective-permute-start(bf16[16,2048]{1,0:T(8,128)(2,1)S(1)} %pad_maximum_fusion.2), channel_id=1, source_target_pairs={{0,16},{2,18},{4,20},{6,22},{8,24},{10,26},{12,28},{14,30},{16,0},... | collective-permute-start | bytes 196616 | tf_op jit(solution)/shard_map/ppermute | solution.py:266
  6.8 8.8 %collective-permute-start.4 = (bf16[16,2048]{1,0:T(8,128)(2,1)S(1)}, bf16[16,2048]{1,0:T(8,128)(2,1)S(1)}, u32[]{:S(2)}, u32[]{:S(2)}) collective-permute-start(bf16[16,2048]{1,0:T(8,128)(2,1)S(1)} %pad_maximum_fusion.2), channel_id=1, source_target_pairs={{0,24},{2,26},{4,28},{6,30},{8,16},{10,18},{12,20},{14,22},{16,8},... | collective-permute-start | bytes 196616 | tf_op jit(solution)/shard_map/ppermute | solution.py:266
  8.1 5.2 %collective-permute-start.1 = (bf16[16,2048]{1,0:T(8,128)(2,1)S(1)}, bf16[16,2048]{1,0:T(8,128)(2,1)S(1)}, u32[]{:S(2)}, u32[]{:S(2)}) collective-permute-start(bf16[16,2048]{1,0:T(8,128)(2,1)S(1)} %pad_maximum_fusion.2), channel_id=1, source_target_pairs={{0,8},{2,10},{4,12},{6,14},{8,0},{10,2},{12,4},{14,6},{16,24},{18,... | collective-permute-start | bytes 196616 | tf_op jit(solution)/shard_map/ppermute | solution.py:266
  15.0 9.9 %collective-permute-start.2 = (bf16[256,2048]{1,0:T(8,128)(2,1)S(1)}, bf16[256,2048]{1,0:T(8,128)(2,1)S(1)}, u32[]{:S(2)}, u32[]{:S(2)}) collective-permute-start(bf16[256,2048]{1,0:T(8,128)(2,1)S(1)} %get-tuple-element.41), channel_id=1, source_target_pairs={{0,2},{2,0},{4,6},{6,4},{8,10},{10,8},{12,14},{14,12},{16,18},{18,... | collective-permute-start | bytes 3145736 | tf_op jit(solution)/shard_map/ppermute | solution.py:266
  15.1 9.8 %collective-permute-start.3 = (bf16[256,2048]{1,0:T(8,128)(2,1)S(1)}, bf16[256,2048]{1,0:T(8,128)(2,1)S(1)}, u32[]{:S(2)}, u32[]{:S(2)}) collective-permute-start(bf16[256,2048]{1,0:T(8,128)(2,1)S(1)} %get-tuple-element.42), channel_id=1, source_target_pairs={{0,2},{2,0},{4,6},{6,4},{8,10},{10,8},{12,14},{14,12},{16,18},{18,... | collective-permute-start | bytes 3145736 | tf_op jit(solution)/shard_map/ppermute | solution.py:266
  15.6 5.5 %collective-permute-start.6 = (bf16[64,1024]{1,0:T(8,128)(2,1)S(1)}, bf16[64,1024]{1,0:T(8,128)(2,1)S(1)}, u32[]{:S(2)}, u32[]{:S(2)}) collective-permute-start(bf16[64,1024]{1,0:T(8,128)(2,1)S(1)} %pad_maximum_fusion), channel_id=1, source_target_pairs={{0,4},{2,6},{4,0},{6,2},{8,12},{10,14},{12,8},{14,10},{16,20},{18,... | collective-permute-start | bytes 393224 | tf_op jit(solution)/shard_map/ppermute | solution.py:266
  17.4 5.3 %collective-permute-start.7 = (bf16[64,1024]{1,0:T(8,128)(2,1)S(1)}, bf16[64,1024]{1,0:T(8,128)(2,1)S(1)}, u32[]{:S(2)}, u32[]{:S(2)}) collective-permute-start(bf16[64,1024]{1,0:T(8,128)(2,1)S(1)} %pad_maximum_fusion.1), channel_id=1, source_target_pairs={{0,1},{1,0},{2,3},{3,2},{4,5},{5,4},{6,7},{7,6},{8,9},{9,8},{10,11... | collective-permute-start | bytes 393224 | tf_op jit(solution)/shard_map/ppermute | solution.py:266
  22.7 7.2 %collective-permute-start.9 = (bf16[128,1024]{1,0:T(8,128)(2,1)S(1)}, bf16[128,1024]{1,0:T(8,128)(2,1)S(1)}, u32[]{:S(2)}, u32[]{:S(2)}) collective-permute-start(bf16[128,1024]{1,0:T(8,128)(2,1)S(1)} %constant_dynamic-update-slice_fusion.5.refs_1_), channel_id=1, source_target_pairs={{0,4},{2,6},{4,0},{6,2},{8,12},{10,14},{12,8},{14,10},{16,20},{18,... | collective-permute-start | bytes 786440 | tf_op jit(solution)/shard_map/ppermute | solution.py:266
  23.1 7.1 %collective-permute-start.8 = (bf16[128,1024]{1,0:T(8,128)(2,1)S(1)}, bf16[128,1024]{1,0:T(8,128)(2,1)S(1)}, u32[]{:S(2)}, u32[]{:S(2)}) collective-permute-start(bf16[128,1024]{1,0:T(8,128)(2,1)S(1)} %constant_dynamic-update-slice_fusion.refs_0_), channel_id=1, source_target_pairs={{0,1},{1,0},{2,3},{3,2},{4,5},{5,4},{6,7},{7,6},{8,9},{9,8},{10,11... | collective-permute-start | bytes 786440 | tf_op jit(solution)/shard_map/ppermute | solution.py:266
  37.1 6.4 %collective-permute-start.10 = (bf16[128,1024]{1,0:T(8,128)(2,1)S(1)}, bf16[128,1024]{1,0:T(8,128)(2,1)S(1)}, u32[]{:S(2)}, u32[]{:S(2)}) collective-permute-start(bf16[128,1024]{1,0:T(8,128)(2,1)S(1)} %get-tuple-element.50), channel_id=1, source_target_pairs={{0,1},{1,0},{2,3},{3,2},{4,5},{5,4},{6,7},{7,6},{8,9},{9,8},{10,11... | collective-permute-start | bytes 786440 | tf_op jit(solution)/shard_map/ppermute | solution.py:266
  38.7 6.4 %collective-permute-start.11 = (bf16[128,1024]{1,0:T(8,128)(2,1)S(1)}, bf16[128,1024]{1,0:T(8,128)(2,1)S(1)}, u32[]{:S(2)}, u32[]{:S(2)}) collective-permute-start(bf16[128,1024]{1,0:T(8,128)(2,1)S(1)} %get-tuple-element.52), channel_id=1, source_target_pairs={{0,4},{2,6},{4,0},{6,2},{8,12},{10,14},{12,8},{14,10},{16,20},{18,... | collective-permute-start | bytes 786440 | tf_op jit(solution)/shard_map/ppermute | solution.py:266
  45.1 6.5 %collective-permute-start.14 = (bf16[256,2048]{1,0:T(8,128)(2,1)S(1)}, bf16[256,2048]{1,0:T(8,128)(2,1)S(1)}, u32[]{:S(2)}, u32[]{:S(2)}) collective-permute-start(bf16[256,2048]{1,0:T(8,128)(2,1)S(1)} %get-tuple-element.57), channel_id=1, source_target_pairs={{0,2},{2,0},{4,6},{6,4},{8,10},{10,8},{12,14},{14,12},{16,18},{18,... | collective-permute-start | bytes 3145736 | tf_op jit(solution)/shard_map/ppermute | solution.py:266
  45.2 6.4 %collective-permute-start.15 = (bf16[256,2048]{1,0:T(8,128)(2,1)S(1)}, bf16[256,2048]{1,0:T(8,128)(2,1)S(1)}, u32[]{:S(2)}, u32[]{:S(2)}) collective-permute-start(bf16[256,2048]{1,0:T(8,128)(2,1)S(1)} %get-tuple-element.58), channel_id=1, source_target_pairs={{0,2},{2,0},{4,6},{6,4},{8,10},{10,8},{12,14},{14,12},{16,18},{18,... | collective-permute-start | bytes 3145736 | tf_op jit(solution)/shard_map/ppermute | solution.py:266
  45.7 5.5 %collective-permute-start.13 = (bf16[64,1024]{1,0:T(8,128)(2,1)S(1)}, bf16[64,1024]{1,0:T(8,128)(2,1)S(1)}, u32[]{:S(2)}, u32[]{:S(2)}) collective-permute-start(bf16[64,1024]{1,0:T(8,128)(2,1)S(1)} %slice.135), channel_id=1, source_target_pairs={{0,1},{1,0},{2,3},{3,2},{4,5},{5,4},{6,7},{7,6},{8,9},{9,8},{10,11... | collective-permute-start | bytes 393224 | tf_op jit(solution)/shard_map/ppermute | solution.py:266
  46.3 5.3 %collective-permute-start.12 = (bf16[64,1024]{1,0:T(8,128)(2,1)S(1)}, bf16[64,1024]{1,0:T(8,128)(2,1)S(1)}, u32[]{:S(2)}, u32[]{:S(2)}) collective-permute-start(bf16[64,1024]{1,0:T(8,128)(2,1)S(1)} %slice.136), channel_id=1, source_target_pairs={{0,4},{2,6},{4,0},{6,2},{8,12},{10,14},{12,8},{14,10},{16,20},{18,... | collective-permute-start | bytes 393224 | tf_op jit(solution)/shard_map/ppermute | solution.py:266
  51.7 5.8 %collective-permute-start.18 = (bf16[16,2048]{1,0:T(8,128)(2,1)S(1)}, bf16[16,2048]{1,0:T(8,128)(2,1)S(1)}, u32[]{:S(2)}, u32[]{:S(2)}) collective-permute-start(bf16[16,2048]{1,0:T(8,128)(2,1)S(1)} %get-tuple-element.74), channel_id=1, source_target_pairs={{0,8},{2,10},{4,12},{6,14},{8,0},{10,2},{12,4},{14,6},{16,24},{18,... | collective-permute-start | bytes 196616 | tf_op jit(solution)/shard_map/ppermute | solution.py:266
  52.1 7.2 %collective-permute-start.17 = (bf16[16,2048]{1,0:T(8,128)(2,1)S(1)}, bf16[16,2048]{1,0:T(8,128)(2,1)S(1)}, u32[]{:S(2)}, u32[]{:S(2)}) collective-permute-start(bf16[16,2048]{1,0:T(8,128)(2,1)S(1)} %get-tuple-element.75), channel_id=1, source_target_pairs={{0,16},{2,18},{4,20},{6,22},{8,24},{10,26},{12,28},{14,30},{16,0},... | collective-permute-start | bytes 196616 | tf_op jit(solution)/shard_map/ppermute | solution.py:266
  55.6 6.1 %collective-permute-start.16 = (bf16[16,2048]{1,0:T(8,128)(2,1)S(1)}, bf16[16,2048]{1,0:T(8,128)(2,1)S(1)}, u32[]{:S(2)}, u32[]{:S(2)}) collective-permute-start(bf16[16,2048]{1,0:T(8,128)(2,1)S(1)} %get-tuple-element.76), channel_id=1, source_target_pairs={{0,24},{2,26},{4,28},{6,30},{8,16},{10,18},{12,20},{14,22},{16,8},... | collective-permute-start | bytes 196616 | tf_op jit(solution)/shard_map/ppermute | solution.py:266
  61.7 1.3 %collective-permute-start.19 = (bf16[8,2048]{1,0:T(8,128)(2,1)S(1)}, bf16[8,2048]{1,0:T(8,128)(2,1)S(1)}, u32[]{:S(2)}, u32[]{:S(2)}) collective-permute-start(bf16[8,2048]{1,0:T(8,128)(2,1)S(1)} %get-tuple-element.77), channel_id=1, source_target_pairs={{0,2},{2,0},{4,6},{6,4},{8,10},{10,8},{12,14},{14,12},{16,18},{18,... | collective-permute-start | bytes 98312 | tf_op jit(solution)/shard_map/ppermute | solution.py:266

commit v6 on v5

--- a/solution.py
+++ b/solution.py
@@ -37,95 +37,119 @@
     return lambda r: pl.multiple_of((((my ^ r) * 2 + core) * blocks + block) * width, width)
 
 
-def attention_kernel(n_mp, blocks, jobs, n_memory, q_ref, g_ref, sq_ref, sg_ref, *refs):
-    used = sorted({block for block, *_ in jobs})
+def attention_kernel(n_mp, blocks, groups, n_memory, q_ref, g_ref, sq_ref, sg_ref, *refs):
+    used = sorted({block for block, *_ in groups})
     memory_refs, refs = refs[:n_memory], refs[n_memory:]
     token_buf, result_buf, raw_ref, prob_ref, grad_ref, weight_ref, sems = refs[-7:]
-    n_terms = 1 + max(i for *_, terms in jobs for i, _ in terms)
+    n_terms = 1 + max(max(terms) for *_, terms in groups)
     term_refs, refs = refs[-7 - n_terms : -7], refs[: -7 - n_terms]
     attended_ref, query_grad_ref, *sent_refs = refs[-2 - len(used) :]
     count, width = q_ref.shape[0], memory_refs[0].shape[1] // 2
-    heads, slots = width // DH, raw_ref.shape[0]
+    heads = width // DH
     step = min(DH, 2 * count)
     cols = [slice(n * DH, (n + 1) * DH) for n in range(heads)]
     targets = [[slice(m * width + n * DH, m * width + (n + 1) * DH) for n in range(heads)] for m in (0, 1)]
 
-    def inputs(j):
-        block, r = jobs[j][:2]
-        starts = (columns(n_mp, blocks, block, width, False)(r), (block * n_mp + r) * width)
-        return [
-            pltpu.make_async_copy(
-                array.at[:, pl.ds(starts[n], width)], token_buf.at[j, m, pl.ds(n * count, count)], sems.at[0, j, m, n]
-            )
-            for m, pair in enumerate(((q_ref, sq_ref), (g_ref, sg_ref)))
-            for n, array in enumerate(pair)
-        ]
-
-    def outputs(j):
-        block, r = jobs[j][:2]
-        where = pl.ds(columns(n_mp, blocks, block, width, False)(r), width)
-        sent_ref, copies = sent_refs[used.index(block)], []
-        for m, own in enumerate((query_grad_ref, attended_ref)):
-            sent = sent_ref.at[:, pl.ds((2 * r + m) * width, width)]
-            for n, target in enumerate((own.at[:, where], sent)):
-                copies.append(
-                    pltpu.make_async_copy(result_buf.at[j, m, pl.ds(n * count, count)], target, sems.at[1, j, m, n])
+    def of_group(block, r0, number, memories, terms, slot0):
+        column = columns(n_mp, blocks, block, width, False)
+        size = memory_refs[memories[0]].shape[0] // number
+        sent_ref = sent_refs[used.index(block)]
+
+        def inputs(k):
+            starts = (column(r0 + k), pl.multiple_of((block * n_mp + r0 + k) * width, width))
+            return [
+                pltpu.make_async_copy(
+                    array.at[:, pl.ds(start, width)],
+                    token_buf.at[slot0 + k, m, pl.ds(n * count, count)],
+                    sems.at[0, slot0 + k, m, n],
                 )
-        return copies
-
-    def memory_of(j, m, n):
-        return jnp.concatenate(
-            [memory_refs[i][start : start + size, targets[m][n]] for i, start, size in jobs[j][2]], axis=0
-        )
-
-    memory = {}
-
-    def scores(j, n, slot):
-        memory[j, n] = [memory_of(j, m, n) for m in (0, 1)]
-        raw_ref[slot] = dot(memory[j, n][0], token_buf[j, 0, :, cols[n]], NT)
-        prob_ref[slot] = dot(memory[j, n][1], token_buf[j, 1, :, cols[n]], NT)
-
-    def softmax(slot):
-        for begin in range(0, 2 * count, step):
-            part = slice(begin, begin + step)
-            grad_ref[slot, :, part], weight_ref[slot, :, part] = softmax_part(
-                raw_ref[slot, :, part], prob_ref[slot, :, part]
-            )
-
-    def results(j, n, slot):
-        for m, pair_ref in enumerate((grad_ref, weight_ref)):
-            result_buf[j, m, :, cols[n]] = dot(memory[j, n][m].T, pair_ref[slot], NN).astype(bf16).T
-
-    def terms(j, n, slot):
-        for m, pair_ref in enumerate((grad_ref, weight_ref)):
-            term, row = dot(pair_ref[slot], token_buf[j, m, :, cols[n]], NN), 0
-            for (_, _, size), (i, start) in zip(*jobs[j][2:]):
-                term_refs[i][start : start + size, targets[m][n]] = term[row : row + size].astype(term_refs[i].dtype)
-                row += size
-
-    for j in range(len(jobs)):
-        for copy in inputs(j):
-            copy.start()
-    items = [(j, n) for j in range(len(jobs)) for n in range(heads)]
-    for i in range(len(items) + 2):
-        if i < len(items):
-            j, n = items[i]
-            if n == 0:
-                for copy in inputs(j):
-                    copy.wait()
-            scores(j, n, i % slots)
-        if 1 <= i <= len(items):
-            softmax((i - 1) % slots)
-        if i >= 2:
-            j, n = items[i - 2]
-            results(j, n, (i - 2) % slots)
-            if n == heads - 1:
-                for copy in outputs(j):
-                    copy.start()
-            terms(j, n, (i - 2) % slots)
-    for j in range(len(jobs)):
-        for copy in outputs(j):
-            copy.wait()
+                for m, pair in enumerate(((q_ref, sq_ref), (g_ref, sg_ref)))
+                for n, (array, start) in enumerate(zip(pair, starts))
+            ]
+
+        def outputs(k):
+            copies = []
+            for m, own in enumerate((query_grad_ref, attended_ref)):
+                starts = (column(r0 + k), pl.multiple_of((2 * (r0 + k) + m) * width, width))
+                for n, (array, start) in enumerate(zip((own, sent_ref), starts)):
+                    copies.append(
+                        pltpu.make_async_copy(
+                            result_buf.at[slot0 + k, m, pl.ds(n * count, count)],
+                            array.at[:, pl.ds(start, width)],
+                            sems.at[1, slot0 + k, m, n],
+                        )
+                    )
+            return copies
+
+        def repeat(body):
+            if number == 1:
+                body(0, None)
+            else:
+                lax.fori_loop(0, number, body, None)
+
+        def start_inputs(k, _):
+            for copy in inputs(k):
+                copy.start()
+
+        def wait_outputs(k, _):
+            for copy in outputs(k):
+                copy.wait()
+
+        def work(k, _):
+            rows = pl.ds(pl.multiple_of(k * size, size), size)
+            memory = [
+                [jnp.concatenate([memory_refs[i][rows, t] for i in memories], axis=0) for t in row] for row in targets
+            ]
+
+            def tokens(m, n):
+                return token_buf[slot0 + k, m, :, cols[n]]
+
+            def scores(n):
+                raw_ref[n] = dot(memory[0][n], tokens(0, n), NT)
+                prob_ref[n] = dot(memory[1][n], tokens(1, n), NT)
+
+            def softmax(n):
+                for begin in range(0, 2 * count, step):
+                    part = slice(begin, begin + step)
+                    grad_ref[n, :, part], weight_ref[n, :, part] = softmax_part(
+                        raw_ref[n, :, part], prob_ref[n, :, part]
+                    )
+
+            def results(n):
+                for m, pair_ref in enumerate((grad_ref, weight_ref)):
+                    result = dot(memory[m][n].T, pair_ref[n], NN).astype(bf16)
+                    result_buf[slot0 + k, m, :, cols[n]] = result.T
+
+            def gradients(n):
+                for m, pair_ref in enumerate((grad_ref, weight_ref)):
+                    term = dot(pair_ref[n], tokens(m, n), NN)
+                    for i, t in enumerate(terms):
+                        term_refs[t][rows, targets[m][n]] = term[i * size : (i + 1) * size].astype(term_refs[t].dtype)
+
+            for copy in inputs(k):
+                copy.wait()
+            for n in range(heads + 2):
+                if n < heads:
+                    scores(n)
+                if 1 <= n <= heads:
+                    softmax(n - 1)
+                if n >= 2:
+                    results(n - 2)
+                    if n <= heads:
+                        gradients(n - 2)
+            for copy in outputs(k):
+                copy.start()
+            gradients(heads - 1)
+
+        return [functools.partial(repeat, body) for body in (start_inputs, work, wait_outputs)]
+
+    slot0, phases = 0, []
+    for group in groups:
+        phases.append(of_group(*group, slot0))
+        slot0 += group[2]
+    for phase in zip(*phases):
+        for run in phase:
+            run()
 
 
 def pinned(space, *arrays):
@@ -135,30 +159,31 @@
 HBM, VMEM = pl.BlockSpec(memory_space=pltpu.HBM), pl.BlockSpec(memory_space=pltpu.VMEM)
 
 
-def attention(n_mp, blocks, jobs, tokens, memory, terms, outputs, sent):
+def attention(n_mp, blocks, groups, tokens, memory, terms, outputs, sent):
     rows, whole = tokens[0].shape
     width = memory[0].shape[1] // 2
-    count = sum(size for _, _, size in jobs[0][2])
-    used = sorted({block for block, *_ in jobs})
-    scratch = (min(4, len(jobs) * width // DH), count, 2 * rows)
+    number = sum(n for _, _, n, *_ in groups)
+    count = len(groups[0][3]) * memory[0].shape[0] // groups[0][2]
+    used = sorted({block for block, *_ in groups})
+    scratch = (width // DH, count, 2 * rows)
     earlier = [*outputs] + [sent[block] for block in used if block in sent]
     first = 4 + len(memory)
     results = pl.pallas_call(
-        functools.partial(attention_kernel, n_mp, blocks, jobs, len(memory)),
+        functools.partial(attention_kernel, n_mp, blocks, groups, len(memory)),
         in_specs=[HBM] * 4 + [VMEM] * len(memory) + [HBM] * len(earlier),
         out_specs=[HBM] * (2 + len(used)) + [VMEM] * len(terms),
         out_shape=[jax.ShapeDtypeStruct((rows, whole), bf16)] * 2
         + [jax.ShapeDtypeStruct((rows, whole // blocks), bf16)] * len(used)
         + [pltpu.VMEM(memory[0].shape, t) for t in terms],
-        scratch_shapes=[pltpu.VMEM((len(jobs), 2, 2 * rows, width), bf16)] * 2
+        scratch_shapes=[pltpu.VMEM((number, 2, 2 * rows, width), bf16)] * 2
         + [pltpu.VMEM(scratch, t) for t in (f32, f32, bf16, bf16)]
-        + [pltpu.SemaphoreType.DMA((2, len(jobs), 2, 2))],
+        + [pltpu.SemaphoreType.DMA((2, number, 2, 2))],
         input_output_aliases={first + n: n for n in range(len(earlier))},
         compiler_params=pltpu.CompilerParams(vmem_limit_bytes=32 * 1024 * 1024),
         cost_estimate=pl.CostEstimate(
-            flops=24 * rows * count * width * len(jobs),
-            bytes_accessed=16 * rows * width * len(jobs),
-            transcendentals=2 * rows * count * width * len(jobs) // DH,
+            flops=24 * rows * count * width * number,
+            bytes_accessed=16 * rows * width * number,
+            transcendentals=2 * rows * count * width * number // DH,
         ),
     )(*pinned(pltpu.HBM, *tokens[:2]), *tokens[2:], *pinned(pltpu.VMEM, *memory), *earlier)
     sent = {**sent, **dict(zip(used, results[2:]))}
@@ -266,7 +291,7 @@
         return lax.ppermute(array, axis, [(i, i ^ bits) for i in range(size)])
 
     core_bit, x_bit = 1, 2
-    z_bits = range(n_seq - 4, 0, -4)
+    z_bits = [4, *range(n_seq - 4, 4, -4)]
     y_bits = [1 << b for b in range(n_mp.bit_length() - 1)]
     rows, part = memory_keys.shape
     share, blocks = part // 2, 2
@@ -279,8 +304,8 @@
 
     base = jnp.concatenate([packed(core), swap(packed(1 - core), "seq", core_bit)])
 
+    base, queries_out, grad_out = together(base, queries, output_grad)
     got = [swap(base, "seq", bits) for bits in z_bits]
-    got[-1], queries_out, grad_out = together(got[-1], queries, output_grad)
     tokens = (queries, output_grad)
     tokens += tuple(swap(array, "seq", core_bit) for array in packing(n_mp, blocks, queries_out, grad_out))
     got = [base] + got
@@ -297,22 +322,14 @@
         second = wider(second, swap(second, "mp", bits))
     first_got, second_got = swap(first, "mp", y_bits[-1]), swap(second, "seq", x_bit)
 
-    half, size = n_mp // 2, second.shape[0] // n_mp
-
-    def of_first(r, memory, term):
-        start = (r % half) * 2 * size
-        return (0, r, ((memory, start, 2 * size),), ((term, start),))
-
-    def of_second(r, held, got, keep, give):
-        return (1, r, ((held, r * size, size), (got, r * size, size)), ((keep, r * size), (give, r * size)))
-
+    half = n_mp // 2
     outputs, sent, (first_keep,) = attention(
-        n_mp, blocks, [of_first(r, 0, 0) for r in range(half)], tokens, [first], [f32], [], {}
+        n_mp, blocks, [(0, 0, half, (0,), (0,))], tokens, [first], [f32], [], {}
     )
     outputs, sent, (first_give, second_keep, second_give) = attention(
         n_mp,
         blocks,
-        [of_first(r, 0, 0) for r in range(half, n_mp)] + [of_second(r, 1, 2, 1, 2) for r in range(n_mp)],
+        [(0, half, n_mp - half, (0,), (0,)), (1, 0, n_mp, (1, 2), (1, 2))],
         tokens,
         [first_got, second, second_got],
         [bf16, f32, bf16],

time: 63.9 us -> 60 us (0.939)
  waiting for transfers between devices: 25.4 us -> 22 us
    ppermute x20, waiting for transfers between devices: 25.4 us -> 22 us  [swap(): return lax.ppermute(array, axis, [(i, i ^ bits) for i in range(size)])]
where the time goes in v6:
time: 60 us; the launch traced here: 59.7 us
  starting transfers between devices  22.3 us (37%)
  waiting for transfers between devices  22 us (37%)
  Pallas kernels  13.4 us (22%)
  local copies, waits for them, and re-layouts  0.98 us (2%)
  between operations  0.86 us (1%)
    ppermute x20, starting transfers between devices, swap(): return lax.ppermute(array, axis, [(i, i ^ bits) for i in range(size)])  22.3 us
    ppermute x20, waiting for transfers between devices, swap(): return lax.ppermute(array, axis, [(i, i ^ bits) for i in range(size)])  22 us
    pallas_call x2, Pallas kernels, attention(): pl.pallas_call(functools.partial(attention_kernel, n_mp, blocks, groups,...  9.71 us
    pallas_call x1, Pallas kernels, packing(): pl.pallas_call(functools.partial(packing_kernel, n_mp, blocks), in_specs=...  1.6 us
    pallas_call x1, Pallas kernels, placing(): pl.pallas_call(functools.partial(placing_kernel, n_mp, blocks), in_specs=...  1.37 us
  transfers between devices with their start and end apart: 20, of which 13 were waited for; matrix products, arithmetic and copies ran while one was open for 0% of the time, Pallas kernels for 10%

profile of v6, /device:TPU:0, one launch (start us, length us, event | category | flops | bytes accessed | tf_op | source)
XLA Modules:
  0.0 59.7 jit_solution(5628645374969531429)
XLA Ops:
  0.6 0.8 %constant_dynamic-slice_fusion.2 = (bf16[8,512]{1,0:T(8,128)(2,1)S(1)}, bf16[8,512]{1,0:T(8,128)(2,1)S(1)}, bf16[8,512]{1,0:T(8,128)(2,1)S(1)}, bf16[8,512]{1,0:...) fusion(bf16[8,2048]{1,0:T(8,128)(2,1)} %param.6, ...), kind=kLoop, calls=%fused_computation.26 | loop fusion | bytes 131088 | tf_op jit(solution)/shard_map/slice | solution.py:303
  1.5 0.5 collective-permute-start
  2.0 0.9 %collective-permute-done = bf16[8,2048]{1,0:T(8,128)(2,1)S(1)} collective-permute-done((bf16[8,2048]{1,0:T(8,128)(2,1)S(1)}, bf16[8,2048]{1,0:T(8,128)(2,1)S(1)}, u32[]{:S(2)}, u32[]{:S(2)}) %collective-permute-start) | collective-permute-done | bytes 32800 | tf_op jit(solution)/shard_map/ppermute | solution.py:291
  2.9 3.9 %collective-permute-start.5 = (bf16[16,2048]{1,0:T(8,128)(2,1)S(1)}, bf16[16,2048]{1,0:T(8,128)(2,1)S(1)}, u32[]{:S(2)}, u32[]{:S(2)}) collective-permute-start(bf16[16,2048]{1,0:T(8,128)(2,1)S(1)} %pad_maximum_fusion.2), channel_id=1, source_target_pairs={{0,16},{2,18},{4,20},{6,22},{8,24},{10,26},{12,28},{14,30},{16,0},... | collective-permute-start | bytes 196616 | tf_op jit(solution)/shard_map/ppermute | solution.py:291
  6.8 1.3 %collective-permute-start.4 = (bf16[16,2048]{1,0:T(8,128)(2,1)S(1)}, bf16[16,2048]{1,0:T(8,128)(2,1)S(1)}, u32[]{:S(2)}, u32[]{:S(2)}) collective-permute-start(bf16[16,2048]{1,0:T(8,128)(2,1)S(1)} %pad_maximum_fusion.2), channel_id=1, source_target_pairs={{0,24},{2,26},{4,28},{6,30},{8,16},{10,18},{12,20},{14,22},{16,8},... | collective-permute-start | bytes 196616 | tf_op jit(solution)/shard_map/ppermute | solution.py:291
  8.1 0.2 collective-permute-start.3
  8.4 1.6 %shard_map.75 = (bf16[256,2048]{1,0:T(8,128)(2,1)S(1)}, bf16[256,2048]{1,0:T(8,128)(2,1)S(1)}) custom-call(bf16[256,4096]{1,0:T(8,128)(2,1)} %q_ref.4, bf16[256,4096]{1,0:T(8,128)(2,1)} %g_ref.4), custom_call_target="tpu_custom_call" | custom-call | bytes 4194304 | tf_op jit(solution)/shard_map/pallas_call | solution.py:214
  10.0 0.1 collective-permute-start.1
  10.1 0.5 collective-permute-start.2
  10.6 2.8 %collective-permute-done.3 = bf16[16,2048]{1,0:T(8,128)(2,1)S(1)} collective-permute-done((bf16[16,2048]{1,0:T(8,128)(2,1)S(1)}, bf16[16,2048]{1,0:T(8,128)(2,1)S(1)}, u32[]{:S(2)}, u32[]{:S(2)}) %collective-permute-start.3) | collective-permute-done | bytes 65568 | tf_op jit(solution)/shard_map/ppermute | solution.py:291
  13.4 0.0 collective-permute-done.4
  13.4 0.0 collective-permute-done.5
  13.5 1.7 %collective-permute-start.6 = (bf16[64,1024]{1,0:T(8,128)(2,1)S(1)}, bf16[64,1024]{1,0:T(8,128)(2,1)S(1)}, u32[]{:S(2)}, u32[]{:S(2)}) collective-permute-start(bf16[64,1024]{1,0:T(8,128)(2,1)S(1)} %pad_maximum_fusion), channel_id=1, source_target_pairs={{0,4},{2,6},{4,0},{6,2},{8,12},{10,14},{12,8},{14,10},{16,20},{18,... | collective-permute-start | bytes 393224 | tf_op jit(solution)/shard_map/ppermute | solution.py:291
  15.2 1.6 %collective-permute-start.7 = (bf16[64,1024]{1,0:T(8,128)(2,1)S(1)}, bf16[64,1024]{1,0:T(8,128)(2,1)S(1)}, u32[]{:S(2)}, u32[]{:S(2)}) collective-permute-start(bf16[64,1024]{1,0:T(8,128)(2,1)S(1)} %pad_maximum_fusion.1), channel_id=1, source_target_pairs={{0,1},{1,0},{2,3},{3,2},{4,5},{5,4},{6,7},{7,6},{8,9},{9,8},{10,11... | collective-permute-start | bytes 393224 | tf_op jit(solution)/shard_map/ppermute | solution.py:291
  16.8 1.7 %collective-permute-done.6 = bf16[64,1024]{1,0:T(8,128)(2,1)S(1)} collective-permute-done((bf16[64,1024]{1,0:T(8,128)(2,1)S(1)}, bf16[64,1024]{1,0:T(8,128)(2,1)S(1)}, u32[]{:S(2)}, u32[]{:S(2)}) %collective-permute-start.6) | collective-permute-done | bytes 131104 | tf_op jit(solution)/shard_map/ppermute | solution.py:291
  18.5 1.7 %collective-permute-done.7 = bf16[64,1024]{1,0:T(8,128)(2,1)S(1)} collective-permute-done((bf16[64,1024]{1,0:T(8,128)(2,1)S(1)}, bf16[64,1024]{1,0:T(8,128)(2,1)S(1)}, u32[]{:S(2)}, u32[]{:S(2)}) %collective-permute-start.7) | collective-permute-done | bytes 131104 | tf_op jit(solution)/shard_map/ppermute | solution.py:291
  20.3 0.4 collective-permute-start.9
  20.7 1.7 %collective-permute-start.8 = (bf16[128,1024]{1,0:T(8,128)(2,1)S(1)}, bf16[128,1024]{1,0:T(8,128)(2,1)S(1)}, u32[]{:S(2)}, u32[]{:S(2)}) collective-permute-start(bf16[128,1024]{1,0:T(8,128)(2,1)S(1)} %constant_dynamic-update-slice_fusion.refs_0_), channel_id=1, source_target_pairs={{0,1},{1,0},{2,3},{3,2},{4,5},{5,4},{6,7},{7,6},{8,9},{9,8},{10,11... | collective-permute-start | bytes 786440 | tf_op jit(solution)/shard_map/ppermute | solution.py:291
  22.5 0.0 collective-permute-done.1.sq_ref
  22.5 0.0 collective-permute-done.2.sg_ref
  22.5 3.2 %shard_map.76 = (bf16[256,4096]{1,0:T(8,128)(2,1)}, bf16[256,4096]{1,0:T(8,128)(2,1)}, bf16[256,2048]{1,0:T(8,128)(2,1)S(1)}, f32[128,1024]{1,0:T(8,128)S(1)}) custom-call(bf16[256,4096]{1,0:T(8,128)(2,1)} %q_ref.4, bf16[256,4096]{1,0:T(8,128)(2,1)} %g_ref.4, bf16[256,2048]{1,0:T(8,128)(2,1)S(1)} %collective-permute-done.1.sq_ref, ...), custom_call_target="tpu_custom_call" | custom-call | flops 402653184 | bytes 2097152 | tf_op jit(solution)/shard_map/pallas_call | solution.py:171
  25.7 1.0 %collective-permute-done.9.refs_2_ = bf16[128,1024]{1,0:T(8,128)(2,1)S(1)} collective-permute-done((bf16[128,1024]{1,0:T(8,128)(2,1)S(1)}, bf16[128,1024]{1,0:T(8,128)(2,1)S(1)}, u32[]{:S(2)}, u32[]{:S(2)}) %collective-permute-start.9) | collective-permute-done | bytes 262176 | tf_op jit(solution)/shard_map/ppermute | solution.py:291
  26.7 0.5 collective-permute-done.8.refs_0_
  27.2 6.5 %shard_map.77 = (bf16[256,4096]{1,0:T(8,128)(2,1)}, bf16[256,4096]{1,0:T(8,128)(2,1)}, bf16[256,2048]{1,0:T(8,128)(2,1)S(1)}, bf16[256,2048]{1,0:T(8,128)(2,1)S(...) custom-call(bf16[256,4096]{1,0:T(8,128)(2,1)} %q_ref.4, ...), custom_call_target="tpu_custom_call", output_to_operand_aliasing={{0}: (7, {}), {1}: (8, {}), {2}: (9, {})} | custom-call | flops 1207959552 | bytes 6291456 | tf_op jit(solution)/shard_map/pallas_call | solution.py:171
  33.7 1.7 %collective-permute-start.10 = (bf16[128,1024]{1,0:T(8,128)(2,1)S(1)}, bf16[128,1024]{1,0:T(8,128)(2,1)S(1)}, u32[]{:S(2)}, u32[]{:S(2)}) collective-permute-start(bf16[128,1024]{1,0:T(8,128)(2,1)S(1)} %get-tuple-element.50), channel_id=1, source_target_pairs={{0,1},{1,0},{2,3},{3,2},{4,5},{5,4},{6,7},{7,6},{8,9},{9,8},{10,11... | collective-permute-start | bytes 786440 | tf_op jit(solution)/shard_map/ppermute | solution.py:291
  35.4 1.5 %collective-permute-start.11 = (bf16[128,1024]{1,0:T(8,128)(2,1)S(1)}, bf16[128,1024]{1,0:T(8,128)(2,1)S(1)}, u32[]{:S(2)}, u32[]{:S(2)}) collective-permute-start(bf16[128,1024]{1,0:T(8,128)(2,1)S(1)} %get-tuple-element.52), channel_id=1, source_target_pairs={{0,4},{2,6},{4,0},{6,2},{8,12},{10,14},{12,8},{14,10},{16,20},{18,... | collective-permute-start | bytes 786440 | tf_op jit(solution)/shard_map/ppermute | solution.py:291
  36.9 3.2 %collective-permute-done.10 = bf16[128,1024]{1,0:T(8,128)(2,1)S(1)} collective-permute-done((bf16[128,1024]{1,0:T(8,128)(2,1)S(1)}, bf16[128,1024]{1,0:T(8,128)(2,1)S(1)}, u32[]{:S(2)}, u32[]{:S(2)}) %collective-permute-start.10) | collective-permute-done | bytes 262176 | tf_op jit(solution)/shard_map/ppermute | solution.py:291
  40.1 0.1 convert_add_fusion.1
  40.2 1.6 %collective-permute-done.11 = bf16[128,1024]{1,0:T(8,128)(2,1)S(1)} collective-permute-done((bf16[128,1024]{1,0:T(8,128)(2,1)S(1)}, bf16[128,1024]{1,0:T(8,128)(2,1)S(1)}, u32[]{:S(2)}, u32[]{:S(2)}) %collective-permute-start.11) | collective-permute-done | bytes 262176 | tf_op jit(solution)/shard_map/ppermute | solution.py:291
  41.8 0.1 convert_add_fusion
  41.9 0.1 collective-permute-start.14
  41.9 0.5 collective-permute-start.15
  42.5 0.4 collective-permute-start.13
  42.9 1.7 %collective-permute-start.12 = (bf16[64,1024]{1,0:T(8,128)(2,1)S(1)}, bf16[64,1024]{1,0:T(8,128)(2,1)S(1)}, u32[]{:S(2)}, u32[]{:S(2)}) collective-permute-start(bf16[64,1024]{1,0:T(8,128)(2,1)S(1)} %slice.136), channel_id=1, source_target_pairs={{0,4},{2,6},{4,0},{6,2},{8,12},{10,14},{12,8},{14,10},{16,20},{18,... | collective-permute-start | bytes 393224 | tf_op jit(solution)/shard_map/ppermute | solution.py:291
  44.6 3.4 %collective-permute-done.13 = bf16[64,1024]{1,0:T(8,128)(2,1)S(1)} collective-permute-done((bf16[64,1024]{1,0:T(8,128)(2,1)S(1)}, bf16[64,1024]{1,0:T(8,128)(2,1)S(1)}, u32[]{:S(2)}, u32[]{:S(2)}) %collective-permute-start.13) | collective-permute-done | bytes 131104 | tf_op jit(solution)/shard_map/ppermute | solution.py:291
  48.0 0.1 collective-permute-done.12
  48.2 0.0 collective-permute-done.14.refs_0_
  48.2 0.0 collective-permute-done.15.refs_1_
  48.3 3.3 %collective-permute-start.18 = (bf16[16,2048]{1,0:T(8,128)(2,1)S(1)}, bf16[16,2048]{1,0:T(8,128)(2,1)S(1)}, u32[]{:S(2)}, u32[]{:S(2)}) collective-permute-start(bf16[16,2048]{1,0:T(8,128)(2,1)S(1)} %get-tuple-element.74), channel_id=1, source_target_pairs={{0,16},{2,18},{4,20},{6,22},{8,24},{10,26},{12,28},{14,30},{16,0},... | collective-permute-start | bytes 196616 | tf_op jit(solution)/shard_map/ppermute | solution.py:291
  51.6 0.4 collective-permute-start.17
  52.1 0.4 collective-permute-start.16
  52.5 1.4 %shard_map.78 = (bf16[256,4096]{1,0:T(8,128)(2,1)}, bf16[256,4096]{1,0:T(8,128)(2,1)}) custom-call(bf16[256,2048]{1,0:T(8,128)(2,1)S(1)} %collective-permute-done.14.refs_0_, bf16[256,2048]{1,0:T(8,128)(2,1)S(1)} %collective-permute-done.15.refs_1_, bf16[256,4096]{1,0:T(8,128)(2,1)} %get-tuple-element.63.refs_2_, ...), custom_call_target="tpu_custom_call", output_to_operand_aliasing={{0}: (2, {}), {1}: (3, {})} | custom-call | tf_op jit(solution)/shard_map/pallas_call | solution.py:274
  53.9 2.0 %collective-permute-done.18 = bf16[16,2048]{1,0:T(8,128)(2,1)S(1)} collective-permute-done((bf16[16,2048]{1,0:T(8,128)(2,1)S(1)}, bf16[16,2048]{1,0:T(8,128)(2,1)S(1)}, u32[]{:S(2)}, u32[]{:S(2)}) %collective-permute-start.18) | collective-permute-done | bytes 65568 | tf_op jit(solution)/shard_map/ppermute | solution.py:291
  55.9 1.8 %collective-permute-done.17 = bf16[16,2048]{1,0:T(8,128)(2,1)S(1)} collective-permute-done((bf16[16,2048]{1,0:T(8,128)(2,1)S(1)}, bf16[16,2048]{1,0:T(8,128)(2,1)S(1)}, u32[]{:S(2)}, u32[]{:S(2)}) %collective-permute-start.17) | collective-permute-done | bytes 65568 | tf_op jit(solution)/shard_map/ppermute | solution.py:291
  57.7 0.0 collective-permute-done.16
  57.7 0.1 collective-permute-start.19
  57.8 1.2 %collective-permute-done.19.other_ref = bf16[8,2048]{1,0:T(8,128)(2,1)S(1)} collective-permute-done((bf16[8,2048]{1,0:T(8,128)(2,1)S(1)}, bf16[8,2048]{1,0:T(8,128)(2,1)S(1)}, u32[]{:S(2)}, u32[]{:S(2)}) %collective-permute-start.19) | collective-permute-done | bytes 32800 | tf_op jit(solution)/shard_map/ppermute | solution.py:291
  59.0 0.7 %shard_map.79 = (bf16[8,2048]{1,0:T(8,128)(2,1)}, bf16[8,2048]{1,0:T(8,128)(2,1)}) custom-call(bf16[8,2048]{1,0:T(8,128)(2,1)S(1)} %get-tuple-element.78.mine_ref, bf16[8,2048]{1,0:T(8,128)(2,1)S(1)} %collective-permute-done.19.other_ref), custom_call_target="tpu_custom_call" | custom-call | tf_op jit(solution)/shard_map/pallas_call | solution.py:241
  (20 shorter events, 0.3 us)
Async XLA Ops:
  1.5 1.4 %collective-permute-start = (bf16[8,2048]{1,0:T(8,128)(2,1)S(1)}, bf16[8,2048]{1,0:T(8,128)(2,1)S(1)}, u32[]{:S(2)}, u32[]{:S(2)}) collective-permute-start(bf16[8,2048]{1,0:T(8,128)(2,1)S(1)} %pad_maximum_fusion.3), channel_id=1, source_target_pairs={{0,2},{2,0},{4,6},{6,4},{8,10},{10,8},{12,14},{14,12},{16,18},{18,... | collective-permute-start | bytes 98312 | tf_op jit(solution)/shard_map/ppermute | solution.py:291
  2.9 10.6 %collective-permute-start.5 = (bf16[16,2048]{1,0:T(8,128)(2,1)S(1)}, bf16[16,2048]{1,0:T(8,128)(2,1)S(1)}, u32[]{:S(2)}, u32[]{:S(2)}) collective-permute-start(bf16[16,2048]{1,0:T(8,128)(2,1)S(1)} %pad_maximum_fusion.2), channel_id=1, source_target_pairs={{0,16},{2,18},{4,20},{6,22},{8,24},{10,26},{12,28},{14,30},{16,0},... | collective-permute-start | bytes 196616 | tf_op jit(solution)/shard_map/ppermute | solution.py:291
  6.8 6.6 %collective-permute-start.4 = (bf16[16,2048]{1,0:T(8,128)(2,1)S(1)}, bf16[16,2048]{1,0:T(8,128)(2,1)S(1)}, u32[]{:S(2)}, u32[]{:S(2)}) collective-permute-start(bf16[16,2048]{1,0:T(8,128)(2,1)S(1)} %pad_maximum_fusion.2), channel_id=1, source_target_pairs={{0,24},{2,26},{4,28},{6,30},{8,16},{10,18},{12,20},{14,22},{16,8},... | collective-permute-start | bytes 196616 | tf_op jit(solution)/shard_map/ppermute | solution.py:291
  8.1 5.2 %collective-permute-start.3 = (bf16[16,2048]{1,0:T(8,128)(2,1)S(1)}, bf16[16,2048]{1,0:T(8,128)(2,1)S(1)}, u32[]{:S(2)}, u32[]{:S(2)}) collective-permute-start(bf16[16,2048]{1,0:T(8,128)(2,1)S(1)} %pad_maximum_fusion.2), channel_id=1, source_target_pairs={{0,8},{2,10},{4,12},{6,14},{8,0},{10,2},{12,4},{14,6},{16,24},{18,... | collective-permute-start | bytes 196616 | tf_op jit(solution)/shard_map/ppermute | solution.py:291
  10.0 12.5 %collective-permute-start.1 = (bf16[256,2048]{1,0:T(8,128)(2,1)S(1)}, bf16[256,2048]{1,0:T(8,128)(2,1)S(1)}, u32[]{:S(2)}, u32[]{:S(2)}) collective-permute-start(bf16[256,2048]{1,0:T(8,128)(2,1)S(1)} %get-tuple-element.41), channel_id=1, source_target_pairs={{0,2},{2,0},{4,6},{6,4},{8,10},{10,8},{12,14},{14,12},{16,18},{18,... | collective-permute-start | bytes 3145736 | tf_op jit(solution)/shard_map/ppermute | solution.py:291
  10.1 12.4 %collective-permute-start.2 = (bf16[256,2048]{1,0:T(8,128)(2,1)S(1)}, bf16[256,2048]{1,0:T(8,128)(2,1)S(1)}, u32[]{:S(2)}, u32[]{:S(2)}) collective-permute-start(bf16[256,2048]{1,0:T(8,128)(2,1)S(1)} %get-tuple-element.42), channel_id=1, source_target_pairs={{0,2},{2,0},{4,6},{6,4},{8,10},{10,8},{12,14},{14,12},{16,18},{18,... | collective-permute-start | bytes 3145736 | tf_op jit(solution)/shard_map/ppermute | solution.py:291
  13.5 5.0 %collective-permute-start.6 = (bf16[64,1024]{1,0:T(8,128)(2,1)S(1)}, bf16[64,1024]{1,0:T(8,128)(2,1)S(1)}, u32[]{:S(2)}, u32[]{:S(2)}) collective-permute-start(bf16[64,1024]{1,0:T(8,128)(2,1)S(1)} %pad_maximum_fusion), channel_id=1, source_target_pairs={{0,4},{2,6},{4,0},{6,2},{8,12},{10,14},{12,8},{14,10},{16,20},{18,... | collective-permute-start | bytes 393224 | tf_op jit(solution)/shard_map/ppermute | solution.py:291
  15.2 5.0 %collective-permute-start.7 = (bf16[64,1024]{1,0:T(8,128)(2,1)S(1)}, bf16[64,1024]{1,0:T(8,128)(2,1)S(1)}, u32[]{:S(2)}, u32[]{:S(2)}) collective-permute-start(bf16[64,1024]{1,0:T(8,128)(2,1)S(1)} %pad_maximum_fusion.1), channel_id=1, source_target_pairs={{0,1},{1,0},{2,3},{3,2},{4,5},{5,4},{6,7},{7,6},{8,9},{9,8},{10,11... | collective-permute-start | bytes 393224 | tf_op jit(solution)/shard_map/ppermute | solution.py:291
  20.3 6.4 %collective-permute-start.9 = (bf16[128,1024]{1,0:T(8,128)(2,1)S(1)}, bf16[128,1024]{1,0:T(8,128)(2,1)S(1)}, u32[]{:S(2)}, u32[]{:S(2)}) collective-permute-start(bf16[128,1024]{1,0:T(8,128)(2,1)S(1)} %constant_dynamic-update-slice_fusion.5.refs_1_), channel_id=1, source_target_pairs={{0,4},{2,6},{4,0},{6,2},{8,12},{10,14},{12,8},{14,10},{16,20},{18,... | collective-permute-start | bytes 786440 | tf_op jit(solution)/shard_map/ppermute | solution.py:291
  20.7 6.4 %collective-permute-start.8 = (bf16[128,1024]{1,0:T(8,128)(2,1)S(1)}, bf16[128,1024]{1,0:T(8,128)(2,1)S(1)}, u32[]{:S(2)}, u32[]{:S(2)}) collective-permute-start(bf16[128,1024]{1,0:T(8,128)(2,1)S(1)} %constant_dynamic-update-slice_fusion.refs_0_), channel_id=1, source_target_pairs={{0,1},{1,0},{2,3},{3,2},{4,5},{5,4},{6,7},{7,6},{8,9},{9,8},{10,11... | collective-permute-start | bytes 786440 | tf_op jit(solution)/shard_map/ppermute | solution.py:291
  33.7 6.4 %collective-permute-start.10 = (bf16[128,1024]{1,0:T(8,128)(2,1)S(1)}, bf16[128,1024]{1,0:T(8,128)(2,1)S(1)}, u32[]{:S(2)}, u32[]{:S(2)}) collective-permute-start(bf16[128,1024]{1,0:T(8,128)(2,1)S(1)} %get-tuple-element.50), channel_id=1, source_target_pairs={{0,1},{1,0},{2,3},{3,2},{4,5},{5,4},{6,7},{7,6},{8,9},{9,8},{10,11... | collective-permute-start | bytes 786440 | tf_op jit(solution)/shard_map/ppermute | solution.py:291
  35.4 6.4 %collective-permute-start.11 = (bf16[128,1024]{1,0:T(8,128)(2,1)S(1)}, bf16[128,1024]{1,0:T(8,128)(2,1)S(1)}, u32[]{:S(2)}, u32[]{:S(2)}) collective-permute-start(bf16[128,1024]{1,0:T(8,128)(2,1)S(1)} %get-tuple-element.52), channel_id=1, source_target_pairs={{0,4},{2,6},{4,0},{6,2},{8,12},{10,14},{12,8},{14,10},{16,20},{18,... | collective-permute-start | bytes 786440 | tf_op jit(solution)/shard_map/ppermute | solution.py:291
  41.9 6.3 %collective-permute-start.14 = (bf16[256,2048]{1,0:T(8,128)(2,1)S(1)}, bf16[256,2048]{1,0:T(8,128)(2,1)S(1)}, u32[]{:S(2)}, u32[]{:S(2)}) collective-permute-start(bf16[256,2048]{1,0:T(8,128)(2,1)S(1)} %get-tuple-element.57), channel_id=1, source_target_pairs={{0,2},{2,0},{4,6},{6,4},{8,10},{10,8},{12,14},{14,12},{16,18},{18,... | collective-permute-start | bytes 3145736 | tf_op jit(solution)/shard_map/ppermute | solution.py:291
  41.9 6.3 %collective-permute-start.15 = (bf16[256,2048]{1,0:T(8,128)(2,1)S(1)}, bf16[256,2048]{1,0:T(8,128)(2,1)S(1)}, u32[]{:S(2)}, u32[]{:S(2)}) collective-permute-start(bf16[256,2048]{1,0:T(8,128)(2,1)S(1)} %get-tuple-element.58), channel_id=1, source_target_pairs={{0,2},{2,0},{4,6},{6,4},{8,10},{10,8},{12,14},{14,12},{16,18},{18,... | collective-permute-start | bytes 3145736 | tf_op jit(solution)/shard_map/ppermute | solution.py:291
  42.5 5.5 %collective-permute-start.13 = (bf16[64,1024]{1,0:T(8,128)(2,1)S(1)}, bf16[64,1024]{1,0:T(8,128)(2,1)S(1)}, u32[]{:S(2)}, u32[]{:S(2)}) collective-permute-start(bf16[64,1024]{1,0:T(8,128)(2,1)S(1)} %slice.135), channel_id=1, source_target_pairs={{0,1},{1,0},{2,3},{3,2},{4,5},{5,4},{6,7},{7,6},{8,9},{9,8},{10,11... | collective-permute-start | bytes 393224 | tf_op jit(solution)/shard_map/ppermute | solution.py:291
  42.9 5.3 %collective-permute-start.12 = (bf16[64,1024]{1,0:T(8,128)(2,1)S(1)}, bf16[64,1024]{1,0:T(8,128)(2,1)S(1)}, u32[]{:S(2)}, u32[]{:S(2)}) collective-permute-start(bf16[64,1024]{1,0:T(8,128)(2,1)S(1)} %slice.136), channel_id=1, source_target_pairs={{0,4},{2,6},{4,0},{6,2},{8,12},{10,14},{12,8},{14,10},{16,20},{18,... | collective-permute-start | bytes 393224 | tf_op jit(solution)/shard_map/ppermute | solution.py:291
  48.3 7.6 %collective-permute-start.18 = (bf16[16,2048]{1,0:T(8,128)(2,1)S(1)}, bf16[16,2048]{1,0:T(8,128)(2,1)S(1)}, u32[]{:S(2)}, u32[]{:S(2)}) collective-permute-start(bf16[16,2048]{1,0:T(8,128)(2,1)S(1)} %get-tuple-element.74), channel_id=1, source_target_pairs={{0,16},{2,18},{4,20},{6,22},{8,24},{10,26},{12,28},{14,30},{16,0},... | collective-permute-start | bytes 196616 | tf_op jit(solution)/shard_map/ppermute | solution.py:291
  51.6 6.1 %collective-permute-start.17 = (bf16[16,2048]{1,0:T(8,128)(2,1)S(1)}, bf16[16,2048]{1,0:T(8,128)(2,1)S(1)}, u32[]{:S(2)}, u32[]{:S(2)}) collective-permute-start(bf16[16,2048]{1,0:T(8,128)(2,1)S(1)} %get-tuple-element.75), channel_id=1, source_target_pairs={{0,24},{2,26},{4,28},{6,30},{8,16},{10,18},{12,20},{14,22},{16,8},... | collective-permute-start | bytes 196616 | tf_op jit(solution)/shard_map/ppermute | solution.py:291
  52.1 5.6 %collective-permute-start.16 = (bf16[16,2048]{1,0:T(8,128)(2,1)S(1)}, bf16[16,2048]{1,0:T(8,128)(2,1)S(1)}, u32[]{:S(2)}, u32[]{:S(2)}) collective-permute-start(bf16[16,2048]{1,0:T(8,128)(2,1)S(1)} %get-tuple-element.76), channel_id=1, source_target_pairs={{0,8},{2,10},{4,12},{6,14},{8,0},{10,2},{12,4},{14,6},{16,24},{18,... | collective-permute-start | bytes 196616 | tf_op jit(solution)/shard_map/ppermute | solution.py:291
  57.7 1.3 %collective-permute-start.19 = (bf16[8,2048]{1,0:T(8,128)(2,1)S(1)}, bf16[8,2048]{1,0:T(8,128)(2,1)S(1)}, u32[]{:S(2)}, u32[]{:S(2)}) collective-permute-start(bf16[8,2048]{1,0:T(8,128)(2,1)S(1)} %get-tuple-element.77), channel_id=1, source_target_pairs={{0,2},{2,0},{4,6},{6,4},{8,10},{10,8},{12,14},{14,12},{16,18},{18,... | collective-permute-start | bytes 98312 | tf_op jit(solution)/shard_map/ppermute | solution.py:291

commit v7 on v6

--- a/solution.py
+++ b/solution.py
@@ -106,6 +106,9 @@
 
             def scores(n):
                 raw_ref[n] = dot(memory[0][n], tokens(0, n), NT)
+                if n == 0:
+                    for copy in inputs(k)[2:]:
+                        copy.wait()
                 prob_ref[n] = dot(memory[1][n], tokens(1, n), NT)
 
             def softmax(n):
@@ -126,7 +129,7 @@
                     for i, t in enumerate(terms):
                         term_refs[t][rows, targets[m][n]] = term[i * size : (i + 1) * size].astype(term_refs[t].dtype)
 
-            for copy in inputs(k):
+            for copy in inputs(k)[:2]:
                 copy.wait()
             for n in range(heads + 2):
                 if n < heads:
@@ -291,19 +294,19 @@
         return lax.ppermute(array, axis, [(i, i ^ bits) for i in range(size)])
 
     core_bit, x_bit = 1, 2
-    z_bits = [4, *range(n_seq - 4, 4, -4)]
+    z_bits = range(4, n_seq, 4)
     y_bits = [1 << b for b in range(n_mp.bit_length() - 1)]
     rows, part = memory_keys.shape
     share, blocks = part // 2, 2
     block = share // blocks
     core = lax.axis_index("seq") & 1
 
-    def packed(c):
-        both = [lax.dynamic_slice_in_dim(array, c * share, share, axis=1) for array in (memory_keys, memory_values)]
+    def packed(keys, values):
+        both = [lax.dynamic_slice_in_dim(array, core * share, share, axis=1) for array in (keys, values)]
         return jnp.concatenate([b[:, n * block : (n + 1) * block] for n in range(blocks) for b in both], axis=1)
 
-    base = jnp.concatenate([packed(core), swap(packed(1 - core), "seq", core_bit)])
-
+    other = [swap(array, "seq", core_bit) for array in (memory_keys, memory_values)]
+    base = jnp.concatenate([packed(memory_keys, memory_values), packed(*other)])
     base, queries_out, grad_out = together(base, queries, output_grad)
     got = [swap(base, "seq", bits) for bits in z_bits]
     tokens = (queries, output_grad)

time: 60 us -> 59.3 us (0.988)
  waiting for transfers between devices: 22 us -> 21.1 us
    ppermute x20 -> x21, waiting for transfers between devices: 22 us -> 21.1 us  [swap(): return lax.ppermute(array, axis, [(i, i ^ bits) for i in range(size)])]
    ppermute x20 -> x21, starting transfers between devices: 22.3 us -> 22.3 us  [swap(): return lax.ppermute(array, axis, [(i, i ^ bits) for i in range(size)])]
  transfers between devices with their start and end apart: 20 -> 21, of which waited for: 13 -> 15; matrix products, arithmetic and copies ran while one was open for 0% -> 2% of each run, Pallas kernels for 10% -> 11%
where the time goes in v7:
time: 59.3 us; the launch traced here: 59.1 us
  starting transfers between devices  22.3 us (38%)
  waiting for transfers between devices  21.1 us (36%)
  Pallas kernels  13.7 us (23%)
  local copies, waits for them, and re-layouts  0.9 us (2%)
  between operations  0.84 us (1%)
    ppermute x21, starting transfers between devices, swap(): return lax.ppermute(array, axis, [(i, i ^ bits) for i in range(size)])  22.3 us
    ppermute x21, waiting for transfers between devices, swap(): return lax.ppermute(array, axis, [(i, i ^ bits) for i in range(size)])  21.1 us
    pallas_call x2, Pallas kernels, attention(): pl.pallas_call(functools.partial(attention_kernel, n_mp, blocks, groups,...  10.1 us
    pallas_call x1, Pallas kernels, packing(): pl.pallas_call(functools.partial(packing_kernel, n_mp, blocks), in_specs=...  1.6 us
    pallas_call x1, Pallas kernels, placing(): pl.pallas_call(functools.partial(placing_kernel, n_mp, blocks), in_specs=...  1.37 us
  transfers between devices with their start and end apart: 21, of which 15 were waited for; matrix products, arithmetic and copies ran while one was open for 2% of the time, Pallas kernels for 11%

profile of v7, /device:TPU:0, one launch (start us, length us, event | category | flops | bytes accessed | tf_op | source)
XLA Modules:
  0.0 59.1 jit_solution(8001765497167560371)
XLA Ops:
  0.6 0.5 collective-permute-start
  1.1 0.1 collective-permute-start.1
  1.2 0.7 %constant_dynamic-slice_fusion.2 = (bf16[8,512]{1,0:T(8,128)(2,1)S(1)}, bf16[8,512]{1,0:T(8,128)(2,1)S(1)}, bf16[8,512]{1,0:T(8,128)(2,1)S(1)}, bf16[8,512]{1,0:T(8,128)(2,1)S(1)}) fusion(bf16[8,2048]{1,0:T(8,128)(2,1)} %param.6, s32[]{:T(128)S(6)} %select_n.2, s32[]{:T(128)S(6)} %add.35, bf16[8,2048]{1,0:T(8,128)(2,1)} %param.5), kind=kLoop, calls=%fused_computation.25 | loop fusion | bytes 65544 | tf_op jit(solution)/shard_map/slice | solution.py:306
  2.0 0.2 collective-permute-done
  2.2 0.3 collective-permute-done.1
  2.6 4.8 %collective-permute-start.6 = (bf16[16,2048]{1,0:T(8,128)(2,1)S(1)}, bf16[16,2048]{1,0:T(8,128)(2,1)S(1)}, u32[]{:S(2)}, u32[]{:S(2)}) collective-permute-start(bf16[16,2048]{1,0:T(8,128)(2,1)S(1)} %maximum_maximum_fusion), channel_id=1, source_target_pairs={{0,24},{2,26},{4,28},{6,30},{8,16},{10,18},{12,20},{14,22},{16,8},... | collective-permute-start | bytes 196616 | tf_op jit(solution)/shard_map/ppermute | solution.py:294
  7.4 0.0 collective-permute-start.5
  7.4 0.6 %collective-permute-start.4 = (bf16[16,2048]{1,0:T(8,128)(2,1)S(1)}, bf16[16,2048]{1,0:T(8,128)(2,1)S(1)}, u32[]{:S(2)}, u32[]{:S(2)}) collective-permute-start(bf16[16,2048]{1,0:T(8,128)(2,1)S(1)} %maximum_maximum_fusion), channel_id=1, source_target_pairs={{0,8},{2,10},{4,12},{6,14},{8,0},{10,2},{12,4},{14,6},{16,24},{18,... | collective-permute-start | bytes 196616 | tf_op jit(solution)/shard_map/ppermute | solution.py:294
  8.1 1.6 %shard_map.75 = (bf16[256,2048]{1,0:T(8,128)(2,1)S(1)}, bf16[256,2048]{1,0:T(8,128)(2,1)S(1)}) custom-call(bf16[256,4096]{1,0:T(8,128)(2,1)} %q_ref.4, bf16[256,4096]{1,0:T(8,128)(2,1)} %g_ref.4), custom_call_target="tpu_custom_call" | custom-call | bytes 4194304 | tf_op jit(solution)/shard_map/pallas_call | solution.py:217
  9.7 0.1 collective-permute-start.2
  9.7 0.5 collective-permute-start.3
  10.2 1.9 %collective-permute-done.4 = bf16[16,2048]{1,0:T(8,128)(2,1)S(1)} collective-permute-done((bf16[16,2048]{1,0:T(8,128)(2,1)S(1)}, bf16[16,2048]{1,0:T(8,128)(2,1)S(1)}, u32[]{:S(2)}, u32[]{:S(2)}) %collective-permute-start.4) | collective-permute-done | bytes 65568 | tf_op jit(solution)/shard_map/ppermute | solution.py:294
  12.1 1.2 %collective-permute-done.5 = bf16[16,2048]{1,0:T(8,128)(2,1)S(1)} collective-permute-done((bf16[16,2048]{1,0:T(8,128)(2,1)S(1)}, bf16[16,2048]{1,0:T(8,128)(2,1)S(1)}, u32[]{:S(2)}, u32[]{:S(2)}) %collective-permute-start.5) | collective-permute-done | bytes 65568 | tf_op jit(solution)/shard_map/ppermute | solution.py:294
  13.4 0.0 collective-permute-done.6
  13.4 1.6 %collective-permute-start.7 = (bf16[64,1024]{1,0:T(8,128)(2,1)S(1)}, bf16[64,1024]{1,0:T(8,128)(2,1)S(1)}, u32[]{:S(2)}, u32[]{:S(2)}) collective-permute-start(bf16[64,1024]{1,0:T(8,128)(2,1)S(1)} %pad_maximum_fusion), channel_id=1, source_target_pairs={{0,4},{2,6},{4,0},{6,2},{8,12},{10,14},{12,8},{14,10},{16,20},{18,... | collective-permute-start | bytes 393224 | tf_op jit(solution)/shard_map/ppermute | solution.py:294
  15.0 1.6 %collective-permute-start.8 = (bf16[64,1024]{1,0:T(8,128)(2,1)S(1)}, bf16[64,1024]{1,0:T(8,128)(2,1)S(1)}, u32[]{:S(2)}, u32[]{:S(2)}) collective-permute-start(bf16[64,1024]{1,0:T(8,128)(2,1)S(1)} %pad_maximum_fusion.1), channel_id=1, source_target_pairs={{0,1},{1,0},{2,3},{3,2},{4,5},{5,4},{6,7},{7,6},{8,9},{9,8},{10,11... | collective-permute-start | bytes 393224 | tf_op jit(solution)/shard_map/ppermute | solution.py:294
  16.6 2.0 %collective-permute-done.7 = bf16[64,1024]{1,0:T(8,128)(2,1)S(1)} collective-permute-done((bf16[64,1024]{1,0:T(8,128)(2,1)S(1)}, bf16[64,1024]{1,0:T(8,128)(2,1)S(1)}, u32[]{:S(2)}, u32[]{:S(2)}) %collective-permute-start.7) | collective-permute-done | bytes 131104 | tf_op jit(solution)/shard_map/ppermute | solution.py:294
  18.6 1.4 %collective-permute-done.8 = bf16[64,1024]{1,0:T(8,128)(2,1)S(1)} collective-permute-done((bf16[64,1024]{1,0:T(8,128)(2,1)S(1)}, bf16[64,1024]{1,0:T(8,128)(2,1)S(1)}, u32[]{:S(2)}, u32[]{:S(2)}) %collective-permute-start.8) | collective-permute-done | bytes 131104 | tf_op jit(solution)/shard_map/ppermute | solution.py:294
  20.1 0.6 %collective-permute-start.10 = (bf16[128,1024]{1,0:T(8,128)(2,1)S(1)}, bf16[128,1024]{1,0:T(8,128)(2,1)S(1)}, u32[]{:S(2)}, u32[]{:S(2)}) collective-permute-start(bf16[128,1024]{1,0:T(8,128)(2,1)S(1)} %constant_dynamic-update-slice_fusion.5.refs_1_), channel_id=1, source_target_pairs={{0,4},{2,6},{4,0},{6,2},{8,12},{10,14},{12,8},{14,10},{16,20},{18,... | collective-permute-start | bytes 786440 | tf_op jit(solution)/shard_map/ppermute | solution.py:294
  20.7 1.6 %collective-permute-start.9 = (bf16[128,1024]{1,0:T(8,128)(2,1)S(1)}, bf16[128,1024]{1,0:T(8,128)(2,1)S(1)}, u32[]{:S(2)}, u32[]{:S(2)}) collective-permute-start(bf16[128,1024]{1,0:T(8,128)(2,1)S(1)} %constant_dynamic-update-slice_fusion.refs_0_), channel_id=1, source_target_pairs={{0,1},{1,0},{2,3},{3,2},{4,5},{5,4},{6,7},{7,6},{8,9},{9,8},{10,11... | collective-permute-start | bytes 786440 | tf_op jit(solution)/shard_map/ppermute | solution.py:294
  22.3 0.0 collective-permute-done.2.sq_ref
  22.3 0.0 collective-permute-done.3.sg_ref
  22.3 3.2 %shard_map.76 = (bf16[256,4096]{1,0:T(8,128)(2,1)}, bf16[256,4096]{1,0:T(8,128)(2,1)}, bf16[256,2048]{1,0:T(8,128)(2,1)S(1)}, f32[128,1024]{1,0:T(8,128)S(1)}) custom-call(bf16[256,4096]{1,0:T(8,128)(2,1)} %q_ref.4, bf16[256,4096]{1,0:T(8,128)(2,1)} %g_ref.4, bf16[256,2048]{1,0:T(8,128)(2,1)S(1)} %collective-permute-done.2.sq_ref, ...), custom_call_target="tpu_custom_call" | custom-call | flops 402653184 | bytes 2097152 | tf_op jit(solution)/shard_map/pallas_call | solution.py:174
  25.5 1.4 %collective-permute-done.10.refs_2_ = bf16[128,1024]{1,0:T(8,128)(2,1)S(1)} collective-permute-done((bf16[128,1024]{1,0:T(8,128)(2,1)S(1)}, bf16[128,1024]{1,0:T(8,128)(2,1)S(1)}, u32[]{:S(2)}, u32[]{:S(2)}) %collective-permute-start.10) | collective-permute-done | bytes 262176 | tf_op jit(solution)/shard_map/ppermute | solution.py:294
  26.9 0.3 collective-permute-done.9.refs_0_
  27.2 6.8 %shard_map.77 = (bf16[256,4096]{1,0:T(8,128)(2,1)}, bf16[256,4096]{1,0:T(8,128)(2,1)}, bf16[256,2048]{1,0:T(8,128)(2,1)S(1)}, bf16[256,2048]{1,0:T(8,128)(2,1)S(...) custom-call(bf16[256,4096]{1,0:T(8,128)(2,1)} %q_ref.4, ...), custom_call_target="tpu_custom_call", output_to_operand_aliasing={{0}: (7, {}), {1}: (8, {}), {2}: (9, {})} | custom-call | flops 1207959552 | bytes 6291456 | tf_op jit(solution)/shard_map/pallas_call | solution.py:174
  34.1 1.6 %collective-permute-start.11 = (bf16[128,1024]{1,0:T(8,128)(2,1)S(1)}, bf16[128,1024]{1,0:T(8,128)(2,1)S(1)}, u32[]{:S(2)}, u32[]{:S(2)}) collective-permute-start(bf16[128,1024]{1,0:T(8,128)(2,1)S(1)} %get-tuple-element.50), channel_id=1, source_target_pairs={{0,1},{1,0},{2,3},{3,2},{4,5},{5,4},{6,7},{7,6},{8,9},{9,8},{10,11... | collective-permute-start | bytes 786440 | tf_op jit(solution)/shard_map/ppermute | solution.py:294
  35.7 1.5 %collective-permute-start.12 = (bf16[128,1024]{1,0:T(8,128)(2,1)S(1)}, bf16[128,1024]{1,0:T(8,128)(2,1)S(1)}, u32[]{:S(2)}, u32[]{:S(2)}) collective-permute-start(bf16[128,1024]{1,0:T(8,128)(2,1)S(1)} %get-tuple-element.52), channel_id=1, source_target_pairs={{0,4},{2,6},{4,0},{6,2},{8,12},{10,14},{12,8},{14,10},{16,20},{18,... | collective-permute-start | bytes 786440 | tf_op jit(solution)/shard_map/ppermute | solution.py:294
  37.1 3.4 %collective-permute-done.11 = bf16[128,1024]{1,0:T(8,128)(2,1)S(1)} collective-permute-done((bf16[128,1024]{1,0:T(8,128)(2,1)S(1)}, bf16[128,1024]{1,0:T(8,128)(2,1)S(1)}, u32[]{:S(2)}, u32[]{:S(2)}) %collective-permute-start.11) | collective-permute-done | bytes 262176 | tf_op jit(solution)/shard_map/ppermute | solution.py:294
  40.5 0.1 convert_add_fusion.1
  40.6 1.5 %collective-permute-done.12 = bf16[128,1024]{1,0:T(8,128)(2,1)S(1)} collective-permute-done((bf16[128,1024]{1,0:T(8,128)(2,1)S(1)}, bf16[128,1024]{1,0:T(8,128)(2,1)S(1)}, u32[]{:S(2)}, u32[]{:S(2)}) %collective-permute-start.12) | collective-permute-done | bytes 262176 | tf_op jit(solution)/shard_map/ppermute | solution.py:294
  42.0 0.1 convert_add_fusion
  42.1 0.1 collective-permute-start.15
  42.2 0.5 collective-permute-start.16
  42.7 0.6 collective-permute-start.14
  43.3 1.6 %collective-permute-start.13 = (bf16[64,1024]{1,0:T(8,128)(2,1)S(1)}, bf16[64,1024]{1,0:T(8,128)(2,1)S(1)}, u32[]{:S(2)}, u32[]{:S(2)}) collective-permute-start(bf16[64,1024]{1,0:T(8,128)(2,1)S(1)} %slice.136), channel_id=1, source_target_pairs={{0,4},{2,6},{4,0},{6,2},{8,12},{10,14},{12,8},{14,10},{16,20},{18,... | collective-permute-start | bytes 393224 | tf_op jit(solution)/shard_map/ppermute | solution.py:294
  44.8 3.4 %collective-permute-done.14 = bf16[64,1024]{1,0:T(8,128)(2,1)S(1)} collective-permute-done((bf16[64,1024]{1,0:T(8,128)(2,1)S(1)}, bf16[64,1024]{1,0:T(8,128)(2,1)S(1)}, u32[]{:S(2)}, u32[]{:S(2)}) %collective-permute-start.14) | collective-permute-done | bytes 131104 | tf_op jit(solution)/shard_map/ppermute | solution.py:294
  48.3 0.3 collective-permute-done.13
  48.6 0.0 collective-permute-done.15.refs_0_
  48.7 2.5 %collective-permute-start.19 = (bf16[16,2048]{1,0:T(8,128)(2,1)S(1)}, bf16[16,2048]{1,0:T(8,128)(2,1)S(1)}, u32[]{:S(2)}, u32[]{:S(2)}) collective-permute-start(bf16[16,2048]{1,0:T(8,128)(2,1)S(1)} %get-tuple-element.74), channel_id=1, source_target_pairs={{0,24},{2,26},{4,28},{6,30},{8,16},{10,18},{12,20},{14,22},{16,8},... | collective-permute-start | bytes 196616 | tf_op jit(solution)/shard_map/ppermute | solution.py:294
  51.2 0.2 collective-permute-start.18
  51.4 1.8 %collective-permute-start.17 = (bf16[16,2048]{1,0:T(8,128)(2,1)S(1)}, bf16[16,2048]{1,0:T(8,128)(2,1)S(1)}, u32[]{:S(2)}, u32[]{:S(2)}) collective-permute-start(bf16[16,2048]{1,0:T(8,128)(2,1)S(1)} %get-tuple-element.76), channel_id=1, source_target_pairs={{0,8},{2,10},{4,12},{6,14},{8,0},{10,2},{12,4},{14,6},{16,24},{18,... | collective-permute-start | bytes 196616 | tf_op jit(solution)/shard_map/ppermute | solution.py:294
  53.2 1.4 %shard_map.78 = (bf16[256,4096]{1,0:T(8,128)(2,1)}, bf16[256,4096]{1,0:T(8,128)(2,1)}) custom-call(bf16[256,2048]{1,0:T(8,128)(2,1)S(1)} %collective-permute-done.15.refs_0_, bf16[256,2048]{1,0:T(8,128)(2,1)S(1)} %collective-permute-done.16.refs_1_, bf16[256,4096]{1,0:T(8,128)(2,1)} %get-tuple-element.63.refs_2_, ...), custom_call_target="tpu_custom_call", output_to_operand_aliasing={{0}: (2, {}), {1}: (3, {})} | custom-call | tf_op jit(solution)/shard_map/pallas_call | solution.py:277
  54.5 0.7 %collective-permute-done.19 = bf16[16,2048]{1,0:T(8,128)(2,1)S(1)} collective-permute-done((bf16[16,2048]{1,0:T(8,128)(2,1)S(1)}, bf16[16,2048]{1,0:T(8,128)(2,1)S(1)}, u32[]{:S(2)}, u32[]{:S(2)}) %collective-permute-start.19) | collective-permute-done | bytes 65568 | tf_op jit(solution)/shard_map/ppermute | solution.py:294
  55.3 1.8 %collective-permute-done.18 = bf16[16,2048]{1,0:T(8,128)(2,1)S(1)} collective-permute-done((bf16[16,2048]{1,0:T(8,128)(2,1)S(1)}, bf16[16,2048]{1,0:T(8,128)(2,1)S(1)}, u32[]{:S(2)}, u32[]{:S(2)}) %collective-permute-start.18) | collective-permute-done | bytes 65568 | tf_op jit(solution)/shard_map/ppermute | solution.py:294
  57.1 0.1 collective-permute-start.20
  57.2 1.2 %collective-permute-done.20.other_ref = bf16[8,2048]{1,0:T(8,128)(2,1)S(1)} collective-permute-done((bf16[8,2048]{1,0:T(8,128)(2,1)S(1)}, bf16[8,2048]{1,0:T(8,128)(2,1)S(1)}, u32[]{:S(2)}, u32[]{:S(2)}) %collective-permute-start.20) | collective-permute-done | bytes 32800 | tf_op jit(solution)/shard_map/ppermute | solution.py:294
  58.4 0.7 %shard_map.79 = (bf16[8,2048]{1,0:T(8,128)(2,1)}, bf16[8,2048]{1,0:T(8,128)(2,1)}) custom-call(bf16[8,2048]{1,0:T(8,128)(2,1)S(1)} %get-tuple-element.78.mine_ref, bf16[8,2048]{1,0:T(8,128)(2,1)S(1)} %collective-permute-done.20.other_ref), custom_call_target="tpu_custom_call" | custom-call | tf_op jit(solution)/shard_map/pallas_call | solution.py:244
  (23 shorter events, 0.3 us)
Async XLA Ops:
  0.6 1.6 %collective-permute-start = (bf16[8,2048]{1,0:T(8,128)(2,1)}, bf16[8,2048]{1,0:T(8,128)(2,1)S(1)}, u32[]{:S(2)}, u32[]{:S(2)}) collective-permute-start(bf16[8,2048]{1,0:T(8,128)(2,1)} %param.5), channel_id=1, source_target_pairs={{0,2},{2,0},{4,6},{6,4},{8,10},{10,8},{12,14},{14,12},{16,18},{18,... | collective-permute-start | bytes 98312 | tf_op jit(solution)/shard_map/ppermute | solution.py:294
  1.1 1.4 %collective-permute-start.1 = (bf16[8,2048]{1,0:T(8,128)(2,1)}, bf16[8,2048]{1,0:T(8,128)(2,1)S(1)}, u32[]{:S(2)}, u32[]{:S(2)}) collective-permute-start(bf16[8,2048]{1,0:T(8,128)(2,1)} %param.6), channel_id=1, source_target_pairs={{0,2},{2,0},{4,6},{6,4},{8,10},{10,8},{12,14},{14,12},{16,18},{18,... | collective-permute-start | bytes 98312 | tf_op jit(solution)/shard_map/ppermute | solution.py:294
  2.6 10.8 %collective-permute-start.6 = (bf16[16,2048]{1,0:T(8,128)(2,1)S(1)}, bf16[16,2048]{1,0:T(8,128)(2,1)S(1)}, u32[]{:S(2)}, u32[]{:S(2)}) collective-permute-start(bf16[16,2048]{1,0:T(8,128)(2,1)S(1)} %maximum_maximum_fusion), channel_id=1, source_target_pairs={{0,24},{2,26},{4,28},{6,30},{8,16},{10,18},{12,20},{14,22},{16,8},... | collective-permute-start | bytes 196616 | tf_op jit(solution)/shard_map/ppermute | solution.py:294
  7.4 6.0 %collective-permute-start.5 = (bf16[16,2048]{1,0:T(8,128)(2,1)S(1)}, bf16[16,2048]{1,0:T(8,128)(2,1)S(1)}, u32[]{:S(2)}, u32[]{:S(2)}) collective-permute-start(bf16[16,2048]{1,0:T(8,128)(2,1)S(1)} %maximum_maximum_fusion), channel_id=1, source_target_pairs={{0,16},{2,18},{4,20},{6,22},{8,24},{10,26},{12,28},{14,30},{16,0},... | collective-permute-start | bytes 196616 | tf_op jit(solution)/shard_map/ppermute | solution.py:294
  7.4 4.7 %collective-permute-start.4 = (bf16[16,2048]{1,0:T(8,128)(2,1)S(1)}, bf16[16,2048]{1,0:T(8,128)(2,1)S(1)}, u32[]{:S(2)}, u32[]{:S(2)}) collective-permute-start(bf16[16,2048]{1,0:T(8,128)(2,1)S(1)} %maximum_maximum_fusion), channel_id=1, source_target_pairs={{0,8},{2,10},{4,12},{6,14},{8,0},{10,2},{12,4},{14,6},{16,24},{18,... | collective-permute-start | bytes 196616 | tf_op jit(solution)/shard_map/ppermute | solution.py:294
  9.7 12.6 %collective-permute-start.2 = (bf16[256,2048]{1,0:T(8,128)(2,1)S(1)}, bf16[256,2048]{1,0:T(8,128)(2,1)S(1)}, u32[]{:S(2)}, u32[]{:S(2)}) collective-permute-start(bf16[256,2048]{1,0:T(8,128)(2,1)S(1)} %get-tuple-element.41), channel_id=1, source_target_pairs={{0,2},{2,0},{4,6},{6,4},{8,10},{10,8},{12,14},{14,12},{16,18},{18,... | collective-permute-start | bytes 3145736 | tf_op jit(solution)/shard_map/ppermute | solution.py:294
  9.7 12.5 %collective-permute-start.3 = (bf16[256,2048]{1,0:T(8,128)(2,1)S(1)}, bf16[256,2048]{1,0:T(8,128)(2,1)S(1)}, u32[]{:S(2)}, u32[]{:S(2)}) collective-permute-start(bf16[256,2048]{1,0:T(8,128)(2,1)S(1)} %get-tuple-element.42), channel_id=1, source_target_pairs={{0,2},{2,0},{4,6},{6,4},{8,10},{10,8},{12,14},{14,12},{16,18},{18,... | collective-permute-start | bytes 3145736 | tf_op jit(solution)/shard_map/ppermute | solution.py:294
  13.4 5.2 %collective-permute-start.7 = (bf16[64,1024]{1,0:T(8,128)(2,1)S(1)}, bf16[64,1024]{1,0:T(8,128)(2,1)S(1)}, u32[]{:S(2)}, u32[]{:S(2)}) collective-permute-start(bf16[64,1024]{1,0:T(8,128)(2,1)S(1)} %pad_maximum_fusion), channel_id=1, source_target_pairs={{0,4},{2,6},{4,0},{6,2},{8,12},{10,14},{12,8},{14,10},{16,20},{18,... | collective-permute-start | bytes 393224 | tf_op jit(solution)/shard_map/ppermute | solution.py:294
  15.0 5.0 %collective-permute-start.8 = (bf16[64,1024]{1,0:T(8,128)(2,1)S(1)}, bf16[64,1024]{1,0:T(8,128)(2,1)S(1)}, u32[]{:S(2)}, u32[]{:S(2)}) collective-permute-start(bf16[64,1024]{1,0:T(8,128)(2,1)S(1)} %pad_maximum_fusion.1), channel_id=1, source_target_pairs={{0,1},{1,0},{2,3},{3,2},{4,5},{5,4},{6,7},{7,6},{8,9},{9,8},{10,11... | collective-permute-start | bytes 393224 | tf_op jit(solution)/shard_map/ppermute | solution.py:294
  20.1 6.8 %collective-permute-start.10 = (bf16[128,1024]{1,0:T(8,128)(2,1)S(1)}, bf16[128,1024]{1,0:T(8,128)(2,1)S(1)}, u32[]{:S(2)}, u32[]{:S(2)}) collective-permute-start(bf16[128,1024]{1,0:T(8,128)(2,1)S(1)} %constant_dynamic-update-slice_fusion.5.refs_1_), channel_id=1, source_target_pairs={{0,4},{2,6},{4,0},{6,2},{8,12},{10,14},{12,8},{14,10},{16,20},{18,... | collective-permute-start | bytes 786440 | tf_op jit(solution)/shard_map/ppermute | solution.py:294
  20.7 6.6 %collective-permute-start.9 = (bf16[128,1024]{1,0:T(8,128)(2,1)S(1)}, bf16[128,1024]{1,0:T(8,128)(2,1)S(1)}, u32[]{:S(2)}, u32[]{:S(2)}) collective-permute-start(bf16[128,1024]{1,0:T(8,128)(2,1)S(1)} %constant_dynamic-update-slice_fusion.refs_0_), channel_id=1, source_target_pairs={{0,1},{1,0},{2,3},{3,2},{4,5},{5,4},{6,7},{7,6},{8,9},{9,8},{10,11... | collective-permute-start | bytes 786440 | tf_op jit(solution)/shard_map/ppermute | solution.py:294
  34.1 6.4 %collective-permute-start.11 = (bf16[128,1024]{1,0:T(8,128)(2,1)S(1)}, bf16[128,1024]{1,0:T(8,128)(2,1)S(1)}, u32[]{:S(2)}, u32[]{:S(2)}) collective-permute-start(bf16[128,1024]{1,0:T(8,128)(2,1)S(1)} %get-tuple-element.50), channel_id=1, source_target_pairs={{0,1},{1,0},{2,3},{3,2},{4,5},{5,4},{6,7},{7,6},{8,9},{9,8},{10,11... | collective-permute-start | bytes 786440 | tf_op jit(solution)/shard_map/ppermute | solution.py:294
  35.7 6.4 %collective-permute-start.12 = (bf16[128,1024]{1,0:T(8,128)(2,1)S(1)}, bf16[128,1024]{1,0:T(8,128)(2,1)S(1)}, u32[]{:S(2)}, u32[]{:S(2)}) collective-permute-start(bf16[128,1024]{1,0:T(8,128)(2,1)S(1)} %get-tuple-element.52), channel_id=1, source_target_pairs={{0,4},{2,6},{4,0},{6,2},{8,12},{10,14},{12,8},{14,10},{16,20},{18,... | collective-permute-start | bytes 786440 | tf_op jit(solution)/shard_map/ppermute | solution.py:294
  42.1 6.5 %collective-permute-start.15 = (bf16[256,2048]{1,0:T(8,128)(2,1)S(1)}, bf16[256,2048]{1,0:T(8,128)(2,1)S(1)}, u32[]{:S(2)}, u32[]{:S(2)}) collective-permute-start(bf16[256,2048]{1,0:T(8,128)(2,1)S(1)} %get-tuple-element.57), channel_id=1, source_target_pairs={{0,2},{2,0},{4,6},{6,4},{8,10},{10,8},{12,14},{14,12},{16,18},{18,... | collective-permute-start | bytes 3145736 | tf_op jit(solution)/shard_map/ppermute | solution.py:294
  42.2 6.4 %collective-permute-start.16 = (bf16[256,2048]{1,0:T(8,128)(2,1)S(1)}, bf16[256,2048]{1,0:T(8,128)(2,1)S(1)}, u32[]{:S(2)}, u32[]{:S(2)}) collective-permute-start(bf16[256,2048]{1,0:T(8,128)(2,1)S(1)} %get-tuple-element.58), channel_id=1, source_target_pairs={{0,2},{2,0},{4,6},{6,4},{8,10},{10,8},{12,14},{14,12},{16,18},{18,... | collective-permute-start | bytes 3145736 | tf_op jit(solution)/shard_map/ppermute | solution.py:294
  42.7 5.5 %collective-permute-start.14 = (bf16[64,1024]{1,0:T(8,128)(2,1)S(1)}, bf16[64,1024]{1,0:T(8,128)(2,1)S(1)}, u32[]{:S(2)}, u32[]{:S(2)}) collective-permute-start(bf16[64,1024]{1,0:T(8,128)(2,1)S(1)} %slice.135), channel_id=1, source_target_pairs={{0,1},{1,0},{2,3},{3,2},{4,5},{5,4},{6,7},{7,6},{8,9},{9,8},{10,11... | collective-permute-start | bytes 393224 | tf_op jit(solution)/shard_map/ppermute | solution.py:294
  43.3 5.3 %collective-permute-start.13 = (bf16[64,1024]{1,0:T(8,128)(2,1)S(1)}, bf16[64,1024]{1,0:T(8,128)(2,1)S(1)}, u32[]{:S(2)}, u32[]{:S(2)}) collective-permute-start(bf16[64,1024]{1,0:T(8,128)(2,1)S(1)} %slice.136), channel_id=1, source_target_pairs={{0,4},{2,6},{4,0},{6,2},{8,12},{10,14},{12,8},{14,10},{16,20},{18,... | collective-permute-start | bytes 393224 | tf_op jit(solution)/shard_map/ppermute | solution.py:294
  48.7 6.6 %collective-permute-start.19 = (bf16[16,2048]{1,0:T(8,128)(2,1)S(1)}, bf16[16,2048]{1,0:T(8,128)(2,1)S(1)}, u32[]{:S(2)}, u32[]{:S(2)}) collective-permute-start(bf16[16,2048]{1,0:T(8,128)(2,1)S(1)} %get-tuple-element.74), channel_id=1, source_target_pairs={{0,24},{2,26},{4,28},{6,30},{8,16},{10,18},{12,20},{14,22},{16,8},... | collective-permute-start | bytes 196616 | tf_op jit(solution)/shard_map/ppermute | solution.py:294
  51.2 5.9 %collective-permute-start.18 = (bf16[16,2048]{1,0:T(8,128)(2,1)S(1)}, bf16[16,2048]{1,0:T(8,128)(2,1)S(1)}, u32[]{:S(2)}, u32[]{:S(2)}) collective-permute-start(bf16[16,2048]{1,0:T(8,128)(2,1)S(1)} %get-tuple-element.75), channel_id=1, source_target_pairs={{0,16},{2,18},{4,20},{6,22},{8,24},{10,26},{12,28},{14,30},{16,0},... | collective-permute-start | bytes 196616 | tf_op jit(solution)/shard_map/ppermute | solution.py:294
  51.4 5.7 %collective-permute-start.17 = (bf16[16,2048]{1,0:T(8,128)(2,1)S(1)}, bf16[16,2048]{1,0:T(8,128)(2,1)S(1)}, u32[]{:S(2)}, u32[]{:S(2)}) collective-permute-start(bf16[16,2048]{1,0:T(8,128)(2,1)S(1)} %get-tuple-element.76), channel_id=1, source_target_pairs={{0,8},{2,10},{4,12},{6,14},{8,0},{10,2},{12,4},{14,6},{16,24},{18,... | collective-permute-start | bytes 196616 | tf_op jit(solution)/shard_map/ppermute | solution.py:294
  57.1 1.3 %collective-permute-start.20 = (bf16[8,2048]{1,0:T(8,128)(2,1)S(1)}, bf16[8,2048]{1,0:T(8,128)(2,1)S(1)}, u32[]{:S(2)}, u32[]{:S(2)}) collective-permute-start(bf16[8,2048]{1,0:T(8,128)(2,1)S(1)} %get-tuple-element.77), channel_id=1, source_target_pairs={{0,2},{2,0},{4,6},{6,4},{8,10},{10,8},{12,14},{14,12},{16,18},{18,... | collective-permute-start | bytes 98312 | tf_op jit(solution)/shard_map/ppermute | solution.py:294

commit v8 on v7

--- a/solution.py
+++ b/solution.py
@@ -38,12 +38,11 @@
 
 
 def attention_kernel(n_mp, blocks, groups, n_memory, q_ref, g_ref, sq_ref, sg_ref, *refs):
-    used = sorted({block for block, *_ in groups})
     memory_refs, refs = refs[:n_memory], refs[n_memory:]
     token_buf, result_buf, raw_ref, prob_ref, grad_ref, weight_ref, sems = refs[-7:]
     n_terms = 1 + max(max(terms) for *_, terms in groups)
     term_refs, refs = refs[-7 - n_terms : -7], refs[: -7 - n_terms]
-    attended_ref, query_grad_ref, *sent_refs = refs[-2 - len(used) :]
+    attended_ref, query_grad_ref, sent_ref = refs[-3:]
     count, width = q_ref.shape[0], memory_refs[0].shape[1] // 2
     heads = width // DH
     step = min(DH, 2 * count)
@@ -53,7 +52,6 @@
     def of_group(block, r0, number, memories, terms, slot0):
         column = columns(n_mp, blocks, block, width, False)
         size = memory_refs[memories[0]].shape[0] // number
-        sent_ref = sent_refs[used.index(block)]
 
         def inputs(k):
             starts = (column(r0 + k), pl.multiple_of((block * n_mp + r0 + k) * width, width))
@@ -70,7 +68,7 @@
         def outputs(k):
             copies = []
             for m, own in enumerate((query_grad_ref, attended_ref)):
-                starts = (column(r0 + k), pl.multiple_of((2 * (r0 + k) + m) * width, width))
+                starts = (column(r0 + k), pl.multiple_of((2 * (block * n_mp + r0 + k) + m) * width, width))
                 for n, (array, start) in enumerate(zip((own, sent_ref), starts)):
                     copies.append(
                         pltpu.make_async_copy(
@@ -106,9 +104,6 @@
 
             def scores(n):
                 raw_ref[n] = dot(memory[0][n], tokens(0, n), NT)
-                if n == 0:
-                    for copy in inputs(k)[2:]:
-                        copy.wait()
                 prob_ref[n] = dot(memory[1][n], tokens(1, n), NT)
 
             def softmax(n):
@@ -129,7 +124,7 @@
                     for i, t in enumerate(terms):
                         term_refs[t][rows, targets[m][n]] = term[i * size : (i + 1) * size].astype(term_refs[t].dtype)
 
-            for copy in inputs(k)[:2]:
+            for copy in inputs(k):
                 copy.wait()
             for n in range(heads + 2):
                 if n < heads:
@@ -162,35 +157,31 @@
 HBM, VMEM = pl.BlockSpec(memory_space=pltpu.HBM), pl.BlockSpec(memory_space=pltpu.VMEM)
 
 
-def attention(n_mp, blocks, groups, tokens, memory, terms, outputs, sent):
+def attention(n_mp, blocks, groups, tokens, memory, terms, outputs):
     rows, whole = tokens[0].shape
     width = memory[0].shape[1] // 2
     number = sum(n for _, _, n, *_ in groups)
     count = len(groups[0][3]) * memory[0].shape[0] // groups[0][2]
-    used = sorted({block for block, *_ in groups})
     scratch = (width // DH, count, 2 * rows)
-    earlier = [*outputs] + [sent[block] for block in used if block in sent]
     first = 4 + len(memory)
     results = pl.pallas_call(
         functools.partial(attention_kernel, n_mp, blocks, groups, len(memory)),
-        in_specs=[HBM] * 4 + [VMEM] * len(memory) + [HBM] * len(earlier),
-        out_specs=[HBM] * (2 + len(used)) + [VMEM] * len(terms),
-        out_shape=[jax.ShapeDtypeStruct((rows, whole), bf16)] * 2
-        + [jax.ShapeDtypeStruct((rows, whole // blocks), bf16)] * len(used)
+        in_specs=[HBM] * 4 + [VMEM] * len(memory) + [HBM] * len(outputs),
+        out_specs=[HBM] * 3 + [VMEM] * len(terms),
+        out_shape=[jax.ShapeDtypeStruct((rows, whole), bf16)] * 3
         + [pltpu.VMEM(memory[0].shape, t) for t in terms],
         scratch_shapes=[pltpu.VMEM((number, 2, 2 * rows, width), bf16)] * 2
         + [pltpu.VMEM(scratch, t) for t in (f32, f32, bf16, bf16)]
         + [pltpu.SemaphoreType.DMA((2, number, 2, 2))],
-        input_output_aliases={first + n: n for n in range(len(earlier))},
-        compiler_params=pltpu.CompilerParams(vmem_limit_bytes=32 * 1024 * 1024),
+        input_output_aliases={first + n: n for n in range(len(outputs))},
+        compiler_params=pltpu.CompilerParams(vmem_limit_bytes=16 * 1024 * 1024),
         cost_estimate=pl.CostEstimate(
             flops=24 * rows * count * width * number,
             bytes_accessed=16 * rows * width * number,
             transcendentals=2 * rows * count * width * number // DH,
         ),
-    )(*pinned(pltpu.HBM, *tokens[:2]), *tokens[2:], *pinned(pltpu.VMEM, *memory), *earlier)
-    sent = {**sent, **dict(zip(used, results[2:]))}
-    return results[:2], sent, results[2 + len(used) :]
+    )(*pinned(pltpu.HBM, *tokens[:2]), *tokens[2:], *pinned(pltpu.VMEM, *memory), *outputs)
+    return results[:3], results[3:]
 
 
 def packing_kernel(n_mp, blocks, q_ref, g_ref, packed_q_ref, packed_g_ref, sems):
@@ -250,21 +241,16 @@
     )(*pinned(pltpu.VMEM, mine, other))
 
 
-def placing_kernel(n_mp, blocks, *refs):
-    returned_refs, (attended_ref, query_grad_ref, sems) = refs[:blocks], refs[-3:]
-    width = returned_refs[0].shape[1] // (2 * n_mp)
+def placing_kernel(n_mp, blocks, returned_ref, _attended, _query_grad, attended_ref, query_grad_ref, sems):
+    width = returned_ref.shape[1] // (2 * blocks * n_mp)
     copies = []
-    for block, returned_ref in enumerate(returned_refs):
+    for block in range(blocks):
         column = columns(n_mp, blocks, block, width, True)
         for r in range(n_mp):
             for m, target in enumerate((query_grad_ref, attended_ref)):
-                start = (2 * r + m) * width
+                part = returned_ref.at[:, pl.ds((2 * (block * n_mp + r) + m) * width, width)]
                 copies.append(
-                    pltpu.make_async_copy(
-                        returned_ref.at[:, start : start + width],
-                        target.at[:, pl.ds(column(r), width)],
-                        sems.at[len(copies)],
-                    )
+                    pltpu.make_async_copy(part, target.at[:, pl.ds(column(r), width)], sems.at[len(copies)])
                 )
     for copy in copies:
         copy.start()
@@ -272,16 +258,15 @@
         copy.wait()
 
 
-def placing(n_mp, returned, attended, query_grad):
-    blocks = len(returned)
+def placing(n_mp, blocks, returned, attended, query_grad):
     return pl.pallas_call(
         functools.partial(placing_kernel, n_mp, blocks),
-        in_specs=[VMEM] * blocks + [HBM] * 2,
+        in_specs=[VMEM] + [HBM] * 2,
         out_specs=[HBM] * 2,
         out_shape=[jax.ShapeDtypeStruct(attended.shape, bf16)] * 2,
         scratch_shapes=[pltpu.SemaphoreType.DMA((2 * blocks * n_mp,))],
-        input_output_aliases={blocks: 0, blocks + 1: 1},
-    )(*pinned(pltpu.VMEM, *returned), attended, query_grad)
+        input_output_aliases={1: 0, 2: 1},
+    )(*pinned(pltpu.VMEM, returned), attended, query_grad)
 
 
 def together(*values):
@@ -326,10 +311,8 @@
     first_got, second_got = swap(first, "mp", y_bits[-1]), swap(second, "seq", x_bit)
 
     half = n_mp // 2
-    outputs, sent, (first_keep,) = attention(
-        n_mp, blocks, [(0, 0, half, (0,), (0,))], tokens, [first], [f32], [], {}
-    )
-    outputs, sent, (first_give, second_keep, second_give) = attention(
+    outputs, (first_keep,) = attention(n_mp, blocks, [(0, 0, half, (0,), (0,))], tokens, [first], [f32], [])
+    (*outputs, sent), (first_give, second_keep, second_give) = attention(
         n_mp,
         blocks,
         [(0, half, n_mp - half, (0,), (0,)), (1, 0, n_mp, (1, 2), (1, 2))],
@@ -337,7 +320,6 @@
         [first_got, second, second_got],
         [bf16, f32, bf16],
         outputs,
-        sent,
     )
     first_got, second_got = swap(first_give, "mp", y_bits[-1]), swap(second_give, "seq", x_bit)
     first, second, sent = together(
@@ -353,10 +335,10 @@
     for bits in y_bits[:0:-1]:
         second = fold(second, "mp", bits)
     first, second = fold(first, "seq", x_bit), fold(second, "mp", y_bits[0])
-    returned = [swap(sent[block], "seq", core_bit) for block in range(blocks)]
+    returned = swap(sent, "seq", core_bit)
     first, second, returned = together(first, second, returned)
     total = jnp.concatenate([first, second], axis=1)
-    outputs = placing(n_mp, returned, *outputs)
+    outputs = placing(n_mp, blocks, returned, *outputs)
     count, give = 2 * rows, total.astype(bf16)
     got = [swap(give[n * count : (n + 1) * count], "seq", bits) for n, bits in enumerate(z_bits, 1)]
     got, outputs = together(got, outputs)

time: 59.3 us -> 60.8 us (1.025)
  local copies, waits for them, and re-layouts: 0.9 us -> 3.83 us
    unnamed x5 -> x9, local copies, waits for them, and re-layouts: 0.06 us -> 2.99 us
    ppermute x21 -> x20, waiting for transfers between devices: 21.1 us -> 20.5 us  [swap(): return lax.ppermute(array, axis, [(i, i ^ bits) for i in range(size)])]
    ppermute x21 -> x20, starting transfers between devices: 22.3 us -> 21.7 us  [swap(): return lax.ppermute(array, axis, [(i, i ^ bits) for i in range(size)])]
  transfers between devices with their start and end apart: 21 -> 20, of which waited for: 15 -> 14; matrix products, arithmetic and copies ran while one was open for 2% -> 2% of each run, Pallas kernels for 11% -> 10%
where the time goes in v8:
time: 60.8 us; the launch traced here: 60.5 us
  starting transfers between devices  21.7 us (36%)
  waiting for transfers between devices  20.5 us (34%)
  Pallas kernels  13.4 us (22%)
  local copies, waits for them, and re-layouts  3.83 us (6%)
  between operations  0.85 us (1%)
    ppermute x20, starting transfers between devices, swap(): return lax.ppermute(array, axis, [(i, i ^ bits) for i in range(size)])  21.7 us
    ppermute x20, waiting for transfers between devices, swap(): return lax.ppermute(array, axis, [(i, i ^ bits) for i in range(size)])  20.5 us
    pallas_call x2, Pallas kernels, attention(): pl.pallas_call(functools.partial(attention_kernel, n_mp, blocks, groups,...  9.71 us
    unnamed x9, local copies, waits for them, and re-layouts  2.99 us
    pallas_call x1, Pallas kernels, packing(): pl.pallas_call(functools.partial(packing_kernel, n_mp, blocks), in_specs=...  1.6 us
    pallas_call x1, Pallas kernels, placing(): pl.pallas_call(functools.partial(placing_kernel, n_mp, blocks), in_specs=...  1.37 us
  transfers between devices with their start and end apart: 20, of which 14 were waited for; matrix products, arithmetic and copies ran while one was open for 2% of the time, Pallas kernels for 10%

profile of v8, /device:TPU:0, one launch (start us, length us, event | category | flops | bytes accessed | tf_op | source)
XLA Modules:
  0.0 60.5 jit_solution(16971259891434016900)
XLA Ops:
  0.6 0.5 collective-permute-start
  1.1 0.1 collective-permute-start.1
  1.2 0.7 %constant_dynamic-slice_fusion.2 = (bf16[8,512]{1,0:T(8,128)(2,1)S(1)}, bf16[8,512]{1,0:T(8,128)(2,1)S(1)}, bf16[8,512]{1,0:T(8,128)(2,1)S(1)}, bf16[8,512]{1,0:T(8,128)(2,1)S(1)}) fusion(bf16[8,2048]{1,0:T(8,128)(2,1)} %param.6, s32[]{:T(128)S(6)} %select_n.2, s32[]{:T(128)S(6)} %add.35, bf16[8,2048]{1,0:T(8,128)(2,1)} %param.5), kind=kLoop, calls=%fused_computation.25 | loop fusion | bytes 65544 | tf_op jit(solution)/shard_map/slice | solution.py:291
  2.0 0.2 collective-permute-done
  2.2 0.3 collective-permute-done.1
  2.6 4.8 %collective-permute-start.6 = (bf16[16,2048]{1,0:T(8,128)(2,1)S(1)}, bf16[16,2048]{1,0:T(8,128)(2,1)S(1)}, u32[]{:S(2)}, u32[]{:S(2)}) collective-permute-start(bf16[16,2048]{1,0:T(8,128)(2,1)S(1)} %maximum_maximum_fusion), channel_id=1, source_target_pairs={{0,24},{2,26},{4,28},{6,30},{8,16},{10,18},{12,20},{14,22},{16,8},... | collective-permute-start | bytes 196616 | tf_op jit(solution)/shard_map/ppermute | solution.py:279
  7.4 0.0 collective-permute-start.5
  7.4 0.6 %collective-permute-start.4 = (bf16[16,2048]{1,0:T(8,128)(2,1)S(1)}, bf16[16,2048]{1,0:T(8,128)(2,1)S(1)}, u32[]{:S(2)}, u32[]{:S(2)}) collective-permute-start(bf16[16,2048]{1,0:T(8,128)(2,1)S(1)} %maximum_maximum_fusion), channel_id=1, source_target_pairs={{0,8},{2,10},{4,12},{6,14},{8,0},{10,2},{12,4},{14,6},{16,24},{18,... | collective-permute-start | bytes 196616 | tf_op jit(solution)/shard_map/ppermute | solution.py:279
  8.1 1.6 %shard_map.75 = (bf16[256,2048]{1,0:T(8,128)(2,1)S(1)}, bf16[256,2048]{1,0:T(8,128)(2,1)S(1)}) custom-call(bf16[256,4096]{1,0:T(8,128)(2,1)} %q_ref.4, bf16[256,4096]{1,0:T(8,128)(2,1)} %g_ref.4), custom_call_target="tpu_custom_call" | custom-call | bytes 4194304 | tf_op jit(solution)/shard_map/pallas_call | solution.py:208
  9.7 0.1 collective-permute-start.2
  9.7 0.5 collective-permute-start.3
  10.2 1.9 %collective-permute-done.4 = bf16[16,2048]{1,0:T(8,128)(2,1)S(1)} collective-permute-done((bf16[16,2048]{1,0:T(8,128)(2,1)S(1)}, bf16[16,2048]{1,0:T(8,128)(2,1)S(1)}, u32[]{:S(2)}, u32[]{:S(2)}) %collective-permute-start.4) | collective-permute-done | bytes 65568 | tf_op jit(solution)/shard_map/ppermute | solution.py:279
  12.1 1.2 %collective-permute-done.5 = bf16[16,2048]{1,0:T(8,128)(2,1)S(1)} collective-permute-done((bf16[16,2048]{1,0:T(8,128)(2,1)S(1)}, bf16[16,2048]{1,0:T(8,128)(2,1)S(1)}, u32[]{:S(2)}, u32[]{:S(2)}) %collective-permute-start.5) | collective-permute-done | bytes 65568 | tf_op jit(solution)/shard_map/ppermute | solution.py:279
  13.4 0.0 collective-permute-done.6
  13.4 1.6 %collective-permute-start.7 = (bf16[64,1024]{1,0:T(8,128)(2,1)S(1)}, bf16[64,1024]{1,0:T(8,128)(2,1)S(1)}, u32[]{:S(2)}, u32[]{:S(2)}) collective-permute-start(bf16[64,1024]{1,0:T(8,128)(2,1)S(1)} %pad_maximum_fusion), channel_id=1, source_target_pairs={{0,4},{2,6},{4,0},{6,2},{8,12},{10,14},{12,8},{14,10},{16,20},{18,... | collective-permute-start | bytes 393224 | tf_op jit(solution)/shard_map/ppermute | solution.py:279
  15.0 1.6 %collective-permute-start.8 = (bf16[64,1024]{1,0:T(8,128)(2,1)S(1)}, bf16[64,1024]{1,0:T(8,128)(2,1)S(1)}, u32[]{:S(2)}, u32[]{:S(2)}) collective-permute-start(bf16[64,1024]{1,0:T(8,128)(2,1)S(1)} %pad_maximum_fusion.1), channel_id=1, source_target_pairs={{0,1},{1,0},{2,3},{3,2},{4,5},{5,4},{6,7},{7,6},{8,9},{9,8},{10,11... | collective-permute-start | bytes 393224 | tf_op jit(solution)/shard_map/ppermute | solution.py:279
  16.6 2.0 %collective-permute-done.7 = bf16[64,1024]{1,0:T(8,128)(2,1)S(1)} collective-permute-done((bf16[64,1024]{1,0:T(8,128)(2,1)S(1)}, bf16[64,1024]{1,0:T(8,128)(2,1)S(1)}, u32[]{:S(2)}, u32[]{:S(2)}) %collective-permute-start.7) | collective-permute-done | bytes 131104 | tf_op jit(solution)/shard_map/ppermute | solution.py:279
  18.6 1.4 %collective-permute-done.8 = bf16[64,1024]{1,0:T(8,128)(2,1)S(1)} collective-permute-done((bf16[64,1024]{1,0:T(8,128)(2,1)S(1)}, bf16[64,1024]{1,0:T(8,128)(2,1)S(1)}, u32[]{:S(2)}, u32[]{:S(2)}) %collective-permute-start.8) | collective-permute-done | bytes 131104 | tf_op jit(solution)/shard_map/ppermute | solution.py:279
  20.1 0.6 collective-permute-start.10
  20.7 1.6 %collective-permute-start.9 = (bf16[128,1024]{1,0:T(8,128)(2,1)S(1)}, bf16[128,1024]{1,0:T(8,128)(2,1)S(1)}, u32[]{:S(2)}, u32[]{:S(2)}) collective-permute-start(bf16[128,1024]{1,0:T(8,128)(2,1)S(1)} %constant_dynamic-update-slice_fusion.refs_0_), channel_id=1, source_target_pairs={{0,1},{1,0},{2,3},{3,2},{4,5},{5,4},{6,7},{7,6},{8,9},{9,8},{10,11... | collective-permute-start | bytes 786440 | tf_op jit(solution)/shard_map/ppermute | solution.py:279
  22.3 0.0 collective-permute-done.2.sq_ref
  22.3 0.0 collective-permute-done.3.sg_ref
  22.3 3.2 %shard_map.76 = (bf16[256,4096]{1,0:T(8,128)(2,1)}, bf16[256,4096]{1,0:T(8,128)(2,1)}, bf16[256,4096]{1,0:T(8,128)(2,1)S(1)}, f32[128,1024]{1,0:T(8,128)S(1)}) custom-call(bf16[256,4096]{1,0:T(8,128)(2,1)} %q_ref.4, bf16[256,4096]{1,0:T(8,128)(2,1)} %g_ref.4, bf16[256,2048]{1,0:T(8,128)(2,1)S(1)} %collective-permute-done.2.sq_ref, ...), custom_call_target="tpu_custom_call" | custom-call | flops 402653184 | bytes 2097152 | tf_op jit(solution)/shard_map/pallas_call | solution.py:167
  25.5 1.4 %collective-permute-done.10.refs_2_ = bf16[128,1024]{1,0:T(8,128)(2,1)S(1)} collective-permute-done((bf16[128,1024]{1,0:T(8,128)(2,1)S(1)}, bf16[128,1024]{1,0:T(8,128)(2,1)S(1)}, u32[]{:S(2)}, u32[]{:S(2)}) %collective-permute-start.10) | collective-permute-done | bytes 262176 | tf_op jit(solution)/shard_map/ppermute | solution.py:279
  26.9 0.3 collective-permute-done.9.refs_0_
  27.2 6.5 %shard_map.77 = (bf16[256,4096]{1,0:T(8,128)(2,1)}, bf16[256,4096]{1,0:T(8,128)(2,1)}, bf16[256,4096]{1,0:T(8,128)(2,1)S(1)}, bf16[128,1024]{1,0:T(8,128)(2,1)S(...) custom-call(bf16[256,4096]{1,0:T(8,128)(2,1)} %q_ref.4, ...), custom_call_target="tpu_custom_call", output_to_operand_aliasing={{0}: (7, {}), {1}: (8, {}), {2}: (9, {})} | custom-call | flops 1207959552 | bytes 6291456 | tf_op jit(solution)/shard_map/pallas_call | solution.py:167
  33.8 1.6 %collective-permute-start.11 = (bf16[128,1024]{1,0:T(8,128)(2,1)S(1)}, bf16[128,1024]{1,0:T(8,128)(2,1)S(1)}, u32[]{:S(2)}, u32[]{:S(2)}) collective-permute-start(bf16[128,1024]{1,0:T(8,128)(2,1)S(1)} %get-tuple-element.47), channel_id=1, source_target_pairs={{0,1},{1,0},{2,3},{3,2},{4,5},{5,4},{6,7},{7,6},{8,9},{9,8},{10,11... | collective-permute-start | bytes 786440 | tf_op jit(solution)/shard_map/ppermute | solution.py:279
  35.4 1.5 %collective-permute-start.12 = (bf16[128,1024]{1,0:T(8,128)(2,1)S(1)}, bf16[128,1024]{1,0:T(8,128)(2,1)S(1)}, u32[]{:S(2)}, u32[]{:S(2)}) collective-permute-start(bf16[128,1024]{1,0:T(8,128)(2,1)S(1)} %get-tuple-element.49), channel_id=1, source_target_pairs={{0,4},{2,6},{4,0},{6,2},{8,12},{10,14},{12,8},{14,10},{16,20},{18,... | collective-permute-start | bytes 786440 | tf_op jit(solution)/shard_map/ppermute | solution.py:279
  36.8 3.4 %collective-permute-done.11 = bf16[128,1024]{1,0:T(8,128)(2,1)S(1)} collective-permute-done((bf16[128,1024]{1,0:T(8,128)(2,1)S(1)}, bf16[128,1024]{1,0:T(8,128)(2,1)S(1)}, u32[]{:S(2)}, u32[]{:S(2)}) %collective-permute-start.11) | collective-permute-done | bytes 262176 | tf_op jit(solution)/shard_map/ppermute | solution.py:279
  40.2 0.1 convert_add_fusion.1
  40.3 1.5 %collective-permute-done.12 = bf16[128,1024]{1,0:T(8,128)(2,1)S(1)} collective-permute-done((bf16[128,1024]{1,0:T(8,128)(2,1)S(1)}, bf16[128,1024]{1,0:T(8,128)(2,1)S(1)}, u32[]{:S(2)}, u32[]{:S(2)}) %collective-permute-start.12) | collective-permute-done | bytes 262176 | tf_op jit(solution)/shard_map/ppermute | solution.py:279
  41.7 0.1 convert_add_fusion
  41.8 0.1 collective-permute-start.15
  41.9 0.6 collective-permute-start.14
  42.5 1.6 %collective-permute-start.13 = (bf16[64,1024]{1,0:T(8,128)(2,1)S(1)}, bf16[64,1024]{1,0:T(8,128)(2,1)S(1)}, u32[]{:S(2)}, u32[]{:S(2)}) collective-permute-start(bf16[64,1024]{1,0:T(8,128)(2,1)S(1)} %slice.136), channel_id=1, source_target_pairs={{0,4},{2,6},{4,0},{6,2},{8,12},{10,14},{12,8},{14,10},{16,20},{18,... | collective-permute-start | bytes 393224 | tf_op jit(solution)/shard_map/ppermute | solution.py:279
  44.0 3.8 %collective-permute-done.14 = bf16[64,1024]{1,0:T(8,128)(2,1)S(1)} collective-permute-done((bf16[64,1024]{1,0:T(8,128)(2,1)S(1)}, bf16[64,1024]{1,0:T(8,128)(2,1)S(1)}, u32[]{:S(2)}, u32[]{:S(2)}) %collective-permute-start.14) | collective-permute-done | bytes 131104 | tf_op jit(solution)/shard_map/ppermute | solution.py:279
  47.9 0.3 collective-permute-done.13
  48.2 0.0 collective-permute-done.15.returned_ref
  48.2 1.3 %copy-done = bf16[256,4096]{1,0:T(8,128)(2,1)} copy-done((bf16[256,4096]{1,0:T(8,128)(2,1)}, bf16[256,4096]{1,0:T(8,128)(2,1)S(1)}, u32[]{:S(2)}) %copy-start) | copy-done | bytes 2097176
  49.7 2.5 %collective-permute-start.18 = (bf16[16,2048]{1,0:T(8,128)(2,1)S(1)}, bf16[16,2048]{1,0:T(8,128)(2,1)S(1)}, u32[]{:S(2)}, u32[]{:S(2)}) collective-permute-start(bf16[16,2048]{1,0:T(8,128)(2,1)S(1)} %get-tuple-element.68), channel_id=1, source_target_pairs={{0,24},{2,26},{4,28},{6,30},{8,16},{10,18},{12,20},{14,22},{16,8},... | collective-permute-start | bytes 196616 | tf_op jit(solution)/shard_map/ppermute | solution.py:279
  52.1 0.2 collective-permute-start.17
  52.3 1.8 %collective-permute-start.16 = (bf16[16,2048]{1,0:T(8,128)(2,1)S(1)}, bf16[16,2048]{1,0:T(8,128)(2,1)S(1)}, u32[]{:S(2)}, u32[]{:S(2)}) collective-permute-start(bf16[16,2048]{1,0:T(8,128)(2,1)S(1)} %get-tuple-element.70), channel_id=1, source_target_pairs={{0,8},{2,10},{4,12},{6,14},{8,0},{10,2},{12,4},{14,6},{16,24},{18,... | collective-permute-start | bytes 196616 | tf_op jit(solution)/shard_map/ppermute | solution.py:279
  54.1 1.6 %copy-done.1 = bf16[256,4096]{1,0:T(8,128)(2,1)S(1)} copy-done((bf16[256,4096]{1,0:T(8,128)(2,1)S(1)}, bf16[256,4096]{1,0:T(8,128)(2,1)}, u32[]{:S(2)}) %copy-start.1) | copy-done | bytes 2097176
  55.7 1.4 %shard_map.78 = (bf16[256,4096]{1,0:T(8,128)(2,1)}, bf16[256,4096]{1,0:T(8,128)(2,1)}) custom-call(bf16[256,4096]{1,0:T(8,128)(2,1)S(1)} %copy-done.1, bf16[256,4096]{1,0:T(8,128)(2,1)} %get-tuple-element.57._attended, bf16[256,4096]{1,0:T(8,128)(2,1)} %get-tuple-element.58._query_grad), custom_call_target="tpu_custom_call", output_to_operand_aliasing={{0}: (1, {}), {1}: (2, {})} | custom-call | tf_op jit(solution)/shard_map/pallas_call | solution.py:262
  57.1 1.4 %collective-permute-done.17 = bf16[16,2048]{1,0:T(8,128)(2,1)S(1)} collective-permute-done((bf16[16,2048]{1,0:T(8,128)(2,1)S(1)}, bf16[16,2048]{1,0:T(8,128)(2,1)S(1)}, u32[]{:S(2)}, u32[]{:S(2)}) %collective-permute-start.17) | collective-permute-done | bytes 65568 | tf_op jit(solution)/shard_map/ppermute | solution.py:279
  58.5 0.1 collective-permute-start.19
  58.6 1.2 %collective-permute-done.19.other_ref = bf16[8,2048]{1,0:T(8,128)(2,1)S(1)} collective-permute-done((bf16[8,2048]{1,0:T(8,128)(2,1)S(1)}, bf16[8,2048]{1,0:T(8,128)(2,1)S(1)}, u32[]{:S(2)}, u32[]{:S(2)}) %collective-permute-start.19) | collective-permute-done | bytes 32800 | tf_op jit(solution)/shard_map/ppermute | solution.py:279
  59.8 0.7 %shard_map.79 = (bf16[8,2048]{1,0:T(8,128)(2,1)}, bf16[8,2048]{1,0:T(8,128)(2,1)}) custom-call(bf16[8,2048]{1,0:T(8,128)(2,1)S(1)} %get-tuple-element.72.mine_ref, bf16[8,2048]{1,0:T(8,128)(2,1)S(1)} %collective-permute-done.19.other_ref), custom_call_target="tpu_custom_call" | custom-call | tf_op jit(solution)/shard_map/pallas_call | solution.py:235
  (25 shorter events, 0.3 us)
Async XLA Ops:
  0.6 1.6 %collective-permute-start = (bf16[8,2048]{1,0:T(8,128)(2,1)}, bf16[8,2048]{1,0:T(8,128)(2,1)S(1)}, u32[]{:S(2)}, u32[]{:S(2)}) collective-permute-start(bf16[8,2048]{1,0:T(8,128)(2,1)} %param.5), channel_id=1, source_target_pairs={{0,2},{2,0},{4,6},{6,4},{8,10},{10,8},{12,14},{14,12},{16,18},{18,... | collective-permute-start | bytes 98312 | tf_op jit(solution)/shard_map/ppermute | solution.py:279
  1.1 1.4 %collective-permute-start.1 = (bf16[8,2048]{1,0:T(8,128)(2,1)}, bf16[8,2048]{1,0:T(8,128)(2,1)S(1)}, u32[]{:S(2)}, u32[]{:S(2)}) collective-permute-start(bf16[8,2048]{1,0:T(8,128)(2,1)} %param.6), channel_id=1, source_target_pairs={{0,2},{2,0},{4,6},{6,4},{8,10},{10,8},{12,14},{14,12},{16,18},{18,... | collective-permute-start | bytes 98312 | tf_op jit(solution)/shard_map/ppermute | solution.py:279
  2.6 10.8 %collective-permute-start.6 = (bf16[16,2048]{1,0:T(8,128)(2,1)S(1)}, bf16[16,2048]{1,0:T(8,128)(2,1)S(1)}, u32[]{:S(2)}, u32[]{:S(2)}) collective-permute-start(bf16[16,2048]{1,0:T(8,128)(2,1)S(1)} %maximum_maximum_fusion), channel_id=1, source_target_pairs={{0,24},{2,26},{4,28},{6,30},{8,16},{10,18},{12,20},{14,22},{16,8},... | collective-permute-start | bytes 196616 | tf_op jit(solution)/shard_map/ppermute | solution.py:279
  7.4 6.0 %collective-permute-start.5 = (bf16[16,2048]{1,0:T(8,128)(2,1)S(1)}, bf16[16,2048]{1,0:T(8,128)(2,1)S(1)}, u32[]{:S(2)}, u32[]{:S(2)}) collective-permute-start(bf16[16,2048]{1,0:T(8,128)(2,1)S(1)} %maximum_maximum_fusion), channel_id=1, source_target_pairs={{0,16},{2,18},{4,20},{6,22},{8,24},{10,26},{12,28},{14,30},{16,0},... | collective-permute-start | bytes 196616 | tf_op jit(solution)/shard_map/ppermute | solution.py:279
  7.4 4.7 %collective-permute-start.4 = (bf16[16,2048]{1,0:T(8,128)(2,1)S(1)}, bf16[16,2048]{1,0:T(8,128)(2,1)S(1)}, u32[]{:S(2)}, u32[]{:S(2)}) collective-permute-start(bf16[16,2048]{1,0:T(8,128)(2,1)S(1)} %maximum_maximum_fusion), channel_id=1, source_target_pairs={{0,8},{2,10},{4,12},{6,14},{8,0},{10,2},{12,4},{14,6},{16,24},{18,... | collective-permute-start | bytes 196616 | tf_op jit(solution)/shard_map/ppermute | solution.py:279
  9.7 12.6 %collective-permute-start.2 = (bf16[256,2048]{1,0:T(8,128)(2,1)S(1)}, bf16[256,2048]{1,0:T(8,128)(2,1)S(1)}, u32[]{:S(2)}, u32[]{:S(2)}) collective-permute-start(bf16[256,2048]{1,0:T(8,128)(2,1)S(1)} %get-tuple-element.38), channel_id=1, source_target_pairs={{0,2},{2,0},{4,6},{6,4},{8,10},{10,8},{12,14},{14,12},{16,18},{18,... | collective-permute-start | bytes 3145736 | tf_op jit(solution)/shard_map/ppermute | solution.py:279
  9.7 12.5 %collective-permute-start.3 = (bf16[256,2048]{1,0:T(8,128)(2,1)S(1)}, bf16[256,2048]{1,0:T(8,128)(2,1)S(1)}, u32[]{:S(2)}, u32[]{:S(2)}) collective-permute-start(bf16[256,2048]{1,0:T(8,128)(2,1)S(1)} %get-tuple-element.39), channel_id=1, source_target_pairs={{0,2},{2,0},{4,6},{6,4},{8,10},{10,8},{12,14},{14,12},{16,18},{18,... | collective-permute-start | bytes 3145736 | tf_op jit(solution)/shard_map/ppermute | solution.py:279
  13.4 5.2 %collective-permute-start.7 = (bf16[64,1024]{1,0:T(8,128)(2,1)S(1)}, bf16[64,1024]{1,0:T(8,128)(2,1)S(1)}, u32[]{:S(2)}, u32[]{:S(2)}) collective-permute-start(bf16[64,1024]{1,0:T(8,128)(2,1)S(1)} %pad_maximum_fusion), channel_id=1, source_target_pairs={{0,4},{2,6},{4,0},{6,2},{8,12},{10,14},{12,8},{14,10},{16,20},{18,... | collective-permute-start | bytes 393224 | tf_op jit(solution)/shard_map/ppermute | solution.py:279
  15.0 5.0 %collective-permute-start.8 = (bf16[64,1024]{1,0:T(8,128)(2,1)S(1)}, bf16[64,1024]{1,0:T(8,128)(2,1)S(1)}, u32[]{:S(2)}, u32[]{:S(2)}) collective-permute-start(bf16[64,1024]{1,0:T(8,128)(2,1)S(1)} %pad_maximum_fusion.1), channel_id=1, source_target_pairs={{0,1},{1,0},{2,3},{3,2},{4,5},{5,4},{6,7},{7,6},{8,9},{9,8},{10,11... | collective-permute-start | bytes 393224 | tf_op jit(solution)/shard_map/ppermute | solution.py:279
  20.1 6.8 %collective-permute-start.10 = (bf16[128,1024]{1,0:T(8,128)(2,1)S(1)}, bf16[128,1024]{1,0:T(8,128)(2,1)S(1)}, u32[]{:S(2)}, u32[]{:S(2)}) collective-permute-start(bf16[128,1024]{1,0:T(8,128)(2,1)S(1)} %constant_dynamic-update-slice_fusion.5.refs_1_), channel_id=1, source_target_pairs={{0,4},{2,6},{4,0},{6,2},{8,12},{10,14},{12,8},{14,10},{16,20},{18,... | collective-permute-start | bytes 786440 | tf_op jit(solution)/shard_map/ppermute | solution.py:279
  20.7 6.6 %collective-permute-start.9 = (bf16[128,1024]{1,0:T(8,128)(2,1)S(1)}, bf16[128,1024]{1,0:T(8,128)(2,1)S(1)}, u32[]{:S(2)}, u32[]{:S(2)}) collective-permute-start(bf16[128,1024]{1,0:T(8,128)(2,1)S(1)} %constant_dynamic-update-slice_fusion.refs_0_), channel_id=1, source_target_pairs={{0,1},{1,0},{2,3},{3,2},{4,5},{5,4},{6,7},{7,6},{8,9},{9,8},{10,11... | collective-permute-start | bytes 786440 | tf_op jit(solution)/shard_map/ppermute | solution.py:279
  33.8 6.4 %collective-permute-start.11 = (bf16[128,1024]{1,0:T(8,128)(2,1)S(1)}, bf16[128,1024]{1,0:T(8,128)(2,1)S(1)}, u32[]{:S(2)}, u32[]{:S(2)}) collective-permute-start(bf16[128,1024]{1,0:T(8,128)(2,1)S(1)} %get-tuple-element.47), channel_id=1, source_target_pairs={{0,1},{1,0},{2,3},{3,2},{4,5},{5,4},{6,7},{7,6},{8,9},{9,8},{10,11... | collective-permute-start | bytes 786440 | tf_op jit(solution)/shard_map/ppermute | solution.py:279
  35.4 6.4 %collective-permute-start.12 = (bf16[128,1024]{1,0:T(8,128)(2,1)S(1)}, bf16[128,1024]{1,0:T(8,128)(2,1)S(1)}, u32[]{:S(2)}, u32[]{:S(2)}) collective-permute-start(bf16[128,1024]{1,0:T(8,128)(2,1)S(1)} %get-tuple-element.49), channel_id=1, source_target_pairs={{0,4},{2,6},{4,0},{6,2},{8,12},{10,14},{12,8},{14,10},{16,20},{18,... | collective-permute-start | bytes 786440 | tf_op jit(solution)/shard_map/ppermute | solution.py:279
  41.8 6.4 %collective-permute-start.15 = (bf16[256,4096]{1,0:T(8,128)(2,1)S(1)}, bf16[256,4096]{1,0:T(8,128)(2,1)S(1)}, u32[]{:S(2)}, u32[]{:S(2)}) collective-permute-start(bf16[256,4096]{1,0:T(8,128)(2,1)S(1)} %get-tuple-element.53), channel_id=1, source_target_pairs={{0,2},{2,0},{4,6},{6,4},{8,10},{10,8},{12,14},{14,12},{16,18},{18,... | collective-permute-start | bytes 6291464 | tf_op jit(solution)/shard_map/ppermute | solution.py:279
  41.9 6.0 %collective-permute-start.14 = (bf16[64,1024]{1,0:T(8,128)(2,1)S(1)}, bf16[64,1024]{1,0:T(8,128)(2,1)S(1)}, u32[]{:S(2)}, u32[]{:S(2)}) collective-permute-start(bf16[64,1024]{1,0:T(8,128)(2,1)S(1)} %slice.135), channel_id=1, source_target_pairs={{0,1},{1,0},{2,3},{3,2},{4,5},{5,4},{6,7},{7,6},{8,9},{9,8},{10,11... | collective-permute-start | bytes 393224 | tf_op jit(solution)/shard_map/ppermute | solution.py:279
  42.5 5.7 %collective-permute-start.13 = (bf16[64,1024]{1,0:T(8,128)(2,1)S(1)}, bf16[64,1024]{1,0:T(8,128)(2,1)S(1)}, u32[]{:S(2)}, u32[]{:S(2)}) collective-permute-start(bf16[64,1024]{1,0:T(8,128)(2,1)S(1)} %slice.136), channel_id=1, source_target_pairs={{0,4},{2,6},{4,0},{6,2},{8,12},{10,14},{12,8},{14,10},{16,20},{18,... | collective-permute-start | bytes 393224 | tf_op jit(solution)/shard_map/ppermute | solution.py:279
  48.2 1.3 %copy-start = (bf16[256,4096]{1,0:T(8,128)(2,1)}, bf16[256,4096]{1,0:T(8,128)(2,1)S(1)}, u32[]{:S(2)}) copy-start(bf16[256,4096]{1,0:T(8,128)(2,1)S(1)} %collective-permute-done.15.returned_ref) | copy-start | bytes 6291460
  49.7 7.4 %collective-permute-start.18 = (bf16[16,2048]{1,0:T(8,128)(2,1)S(1)}, bf16[16,2048]{1,0:T(8,128)(2,1)S(1)}, u32[]{:S(2)}, u32[]{:S(2)}) collective-permute-start(bf16[16,2048]{1,0:T(8,128)(2,1)S(1)} %get-tuple-element.68), channel_id=1, source_target_pairs={{0,24},{2,26},{4,28},{6,30},{8,16},{10,18},{12,20},{14,22},{16,8},... | collective-permute-start | bytes 196616 | tf_op jit(solution)/shard_map/ppermute | solution.py:279
  52.1 6.4 %collective-permute-start.17 = (bf16[16,2048]{1,0:T(8,128)(2,1)S(1)}, bf16[16,2048]{1,0:T(8,128)(2,1)S(1)}, u32[]{:S(2)}, u32[]{:S(2)}) collective-permute-start(bf16[16,2048]{1,0:T(8,128)(2,1)S(1)} %get-tuple-element.69), channel_id=1, source_target_pairs={{0,16},{2,18},{4,20},{6,22},{8,24},{10,26},{12,28},{14,30},{16,0},... | collective-permute-start | bytes 196616 | tf_op jit(solution)/shard_map/ppermute | solution.py:279
  52.3 6.2 %collective-permute-start.16 = (bf16[16,2048]{1,0:T(8,128)(2,1)S(1)}, bf16[16,2048]{1,0:T(8,128)(2,1)S(1)}, u32[]{:S(2)}, u32[]{:S(2)}) collective-permute-start(bf16[16,2048]{1,0:T(8,128)(2,1)S(1)} %get-tuple-element.70), channel_id=1, source_target_pairs={{0,8},{2,10},{4,12},{6,14},{8,0},{10,2},{12,4},{14,6},{16,24},{18,... | collective-permute-start | bytes 196616 | tf_op jit(solution)/shard_map/ppermute | solution.py:279
  54.1 1.6 %copy-start.1 = (bf16[256,4096]{1,0:T(8,128)(2,1)S(1)}, bf16[256,4096]{1,0:T(8,128)(2,1)}, u32[]{:S(2)}) copy-start(bf16[256,4096]{1,0:T(8,128)(2,1)} %copy-done) | copy-start | bytes 6291460
  58.5 1.3 %collective-permute-start.19 = (bf16[8,2048]{1,0:T(8,128)(2,1)S(1)}, bf16[8,2048]{1,0:T(8,128)(2,1)S(1)}, u32[]{:S(2)}, u32[]{:S(2)}) collective-permute-start(bf16[8,2048]{1,0:T(8,128)(2,1)S(1)} %get-tuple-element.71), channel_id=1, source_target_pairs={{0,2},{2,0},{4,6},{6,4},{8,10},{10,8},{12,14},{14,12},{16,18},{18,... | collective-permute-start | bytes 98312 | tf_op jit(solution)/shard_map/ppermute | solution.py:279

commit v9 on v7

--- a/solution.py
+++ b/solution.py
@@ -11,6 +11,7 @@
 DH = 128
 
 NT = (((1,), (1,)), ((), ()))
+TN = (((0,), (0,)), ((), ()))
 NN = (((1,), (0,)), ((), ()))
 
 bf16, f32 = jnp.bfloat16, jnp.float32
@@ -106,9 +107,6 @@
 
             def scores(n):
                 raw_ref[n] = dot(memory[0][n], tokens(0, n), NT)
-                if n == 0:
-                    for copy in inputs(k)[2:]:
-                        copy.wait()
                 prob_ref[n] = dot(memory[1][n], tokens(1, n), NT)
 
             def softmax(n):
@@ -120,8 +118,7 @@
 
             def results(n):
                 for m, pair_ref in enumerate((grad_ref, weight_ref)):
-                    result = dot(memory[m][n].T, pair_ref[n], NN).astype(bf16)
-                    result_buf[slot0 + k, m, :, cols[n]] = result.T
+                    result_buf[slot0 + k, m, :, cols[n]] = dot(pair_ref[n], memory[m][n], TN).astype(bf16)
 
             def gradients(n):
                 for m, pair_ref in enumerate((grad_ref, weight_ref)):
@@ -129,7 +126,7 @@
                     for i, t in enumerate(terms):
                         term_refs[t][rows, targets[m][n]] = term[i * size : (i + 1) * size].astype(term_refs[t].dtype)
 
-            for copy in inputs(k)[:2]:
+            for copy in inputs(k):
                 copy.wait()
             for n in range(heads + 2):
                 if n < heads:

time: 59.3 us -> 59.2 us (level)
  no operation moved by 1% of the time
where the time goes in v9:
time: 59.2 us; the launch traced here: 58.9 us
  starting transfers between devices  22.2 us (38%)
  waiting for transfers between devices  21.1 us (36%)
  Pallas kernels  13.6 us (23%)
  local copies, waits for them, and re-layouts  0.9 us (2%)
  between operations  0.84 us (1%)
    ppermute x21, starting transfers between devices, swap(): return lax.ppermute(array, axis, [(i, i ^ bits) for i in range(size)])  22.2 us
    ppermute x21, waiting for transfers between devices, swap(): return lax.ppermute(array, axis, [(i, i ^ bits) for i in range(size)])  21.1 us
    pallas_call x2, Pallas kernels, attention(): pl.pallas_call(functools.partial(attention_kernel, n_mp, blocks, groups,...  9.9 us
    pallas_call x1, Pallas kernels, packing(): pl.pallas_call(functools.partial(packing_kernel, n_mp, blocks), in_specs=...  1.6 us
    pallas_call x1, Pallas kernels, placing(): pl.pallas_call(functools.partial(placing_kernel, n_mp, blocks), in_specs=...  1.37 us
  transfers between devices with their start and end apart: 21, of which 15 were waited for; matrix products, arithmetic and copies ran while one was open for 2% of the time, Pallas kernels for 11%

profile of v9, /device:TPU:0, one launch (start us, length us, event | category | flops | bytes accessed | tf_op | source)
XLA Modules:
  0.0 58.9 jit_solution(787494491912704657)
XLA Ops:
  0.6 0.5 collective-permute-start
  1.1 0.1 collective-permute-start.1
  1.2 0.7 %constant_dynamic-slice_fusion.2 = (bf16[8,512]{1,0:T(8,128)(2,1)S(1)}, bf16[8,512]{1,0:T(8,128)(2,1)S(1)}, bf16[8,512]{1,0:T(8,128)(2,1)S(1)}, bf16[8,512]{1,0:T(8,128)(2,1)S(1)}) fusion(bf16[8,2048]{1,0:T(8,128)(2,1)} %param.6, s32[]{:T(128)S(6)} %select_n.2, s32[]{:T(128)S(6)} %add.35, bf16[8,2048]{1,0:T(8,128)(2,1)} %param.5), kind=kLoop, calls=%fused_computation.25 | loop fusion | bytes 65544 | tf_op jit(solution)/shard_map/slice | solution.py:303
  2.0 0.2 collective-permute-done
  2.2 0.3 collective-permute-done.1
  2.6 4.8 %collective-permute-start.6 = (bf16[16,2048]{1,0:T(8,128)(2,1)S(1)}, bf16[16,2048]{1,0:T(8,128)(2,1)S(1)}, u32[]{:S(2)}, u32[]{:S(2)}) collective-permute-start(bf16[16,2048]{1,0:T(8,128)(2,1)S(1)} %maximum_maximum_fusion), channel_id=1, source_target_pairs={{0,24},{2,26},{4,28},{6,30},{8,16},{10,18},{12,20},{14,22},{16,8},... | collective-permute-start | bytes 196616 | tf_op jit(solution)/shard_map/ppermute | solution.py:291
  7.4 0.0 collective-permute-start.5
  7.4 0.6 %collective-permute-start.4 = (bf16[16,2048]{1,0:T(8,128)(2,1)S(1)}, bf16[16,2048]{1,0:T(8,128)(2,1)S(1)}, u32[]{:S(2)}, u32[]{:S(2)}) collective-permute-start(bf16[16,2048]{1,0:T(8,128)(2,1)S(1)} %maximum_maximum_fusion), channel_id=1, source_target_pairs={{0,8},{2,10},{4,12},{6,14},{8,0},{10,2},{12,4},{14,6},{16,24},{18,... | collective-permute-start | bytes 196616 | tf_op jit(solution)/shard_map/ppermute | solution.py:291
  8.1 1.6 %shard_map.75 = (bf16[256,2048]{1,0:T(8,128)(2,1)S(1)}, bf16[256,2048]{1,0:T(8,128)(2,1)S(1)}) custom-call(bf16[256,4096]{1,0:T(8,128)(2,1)} %q_ref.4, bf16[256,4096]{1,0:T(8,128)(2,1)} %g_ref.4), custom_call_target="tpu_custom_call" | custom-call | bytes 4194304 | tf_op jit(solution)/shard_map/pallas_call | solution.py:214
  9.7 0.1 collective-permute-start.2
  9.7 0.5 collective-permute-start.3
  10.2 1.9 %collective-permute-done.4 = bf16[16,2048]{1,0:T(8,128)(2,1)S(1)} collective-permute-done((bf16[16,2048]{1,0:T(8,128)(2,1)S(1)}, bf16[16,2048]{1,0:T(8,128)(2,1)S(1)}, u32[]{:S(2)}, u32[]{:S(2)}) %collective-permute-start.4) | collective-permute-done | bytes 65568 | tf_op jit(solution)/shard_map/ppermute | solution.py:291
  12.1 1.2 %collective-permute-done.5 = bf16[16,2048]{1,0:T(8,128)(2,1)S(1)} collective-permute-done((bf16[16,2048]{1,0:T(8,128)(2,1)S(1)}, bf16[16,2048]{1,0:T(8,128)(2,1)S(1)}, u32[]{:S(2)}, u32[]{:S(2)}) %collective-permute-start.5) | collective-permute-done | bytes 65568 | tf_op jit(solution)/shard_map/ppermute | solution.py:291
  13.4 0.0 collective-permute-done.6
  13.4 1.6 %collective-permute-start.7 = (bf16[64,1024]{1,0:T(8,128)(2,1)S(1)}, bf16[64,1024]{1,0:T(8,128)(2,1)S(1)}, u32[]{:S(2)}, u32[]{:S(2)}) collective-permute-start(bf16[64,1024]{1,0:T(8,128)(2,1)S(1)} %pad_maximum_fusion), channel_id=1, source_target_pairs={{0,4},{2,6},{4,0},{6,2},{8,12},{10,14},{12,8},{14,10},{16,20},{18,... | collective-permute-start | bytes 393224 | tf_op jit(solution)/shard_map/ppermute | solution.py:291
  15.0 1.6 %collective-permute-start.8 = (bf16[64,1024]{1,0:T(8,128)(2,1)S(1)}, bf16[64,1024]{1,0:T(8,128)(2,1)S(1)}, u32[]{:S(2)}, u32[]{:S(2)}) collective-permute-start(bf16[64,1024]{1,0:T(8,128)(2,1)S(1)} %pad_maximum_fusion.1), channel_id=1, source_target_pairs={{0,1},{1,0},{2,3},{3,2},{4,5},{5,4},{6,7},{7,6},{8,9},{9,8},{10,11... | collective-permute-start | bytes 393224 | tf_op jit(solution)/shard_map/ppermute | solution.py:291
  16.6 2.0 %collective-permute-done.7 = bf16[64,1024]{1,0:T(8,128)(2,1)S(1)} collective-permute-done((bf16[64,1024]{1,0:T(8,128)(2,1)S(1)}, bf16[64,1024]{1,0:T(8,128)(2,1)S(1)}, u32[]{:S(2)}, u32[]{:S(2)}) %collective-permute-start.7) | collective-permute-done | bytes 131104 | tf_op jit(solution)/shard_map/ppermute | solution.py:291
  18.6 1.4 %collective-permute-done.8 = bf16[64,1024]{1,0:T(8,128)(2,1)S(1)} collective-permute-done((bf16[64,1024]{1,0:T(8,128)(2,1)S(1)}, bf16[64,1024]{1,0:T(8,128)(2,1)S(1)}, u32[]{:S(2)}, u32[]{:S(2)}) %collective-permute-start.8) | collective-permute-done | bytes 131104 | tf_op jit(solution)/shard_map/ppermute | solution.py:291
  20.1 0.6 %collective-permute-start.10 = (bf16[128,1024]{1,0:T(8,128)(2,1)S(1)}, bf16[128,1024]{1,0:T(8,128)(2,1)S(1)}, u32[]{:S(2)}, u32[]{:S(2)}) collective-permute-start(bf16[128,1024]{1,0:T(8,128)(2,1)S(1)} %constant_dynamic-update-slice_fusion.5.refs_1_), channel_id=1, source_target_pairs={{0,4},{2,6},{4,0},{6,2},{8,12},{10,14},{12,8},{14,10},{16,20},{18,... | collective-permute-start | bytes 786440 | tf_op jit(solution)/shard_map/ppermute | solution.py:291
  20.7 1.6 %collective-permute-start.9 = (bf16[128,1024]{1,0:T(8,128)(2,1)S(1)}, bf16[128,1024]{1,0:T(8,128)(2,1)S(1)}, u32[]{:S(2)}, u32[]{:S(2)}) collective-permute-start(bf16[128,1024]{1,0:T(8,128)(2,1)S(1)} %constant_dynamic-update-slice_fusion.refs_0_), channel_id=1, source_target_pairs={{0,1},{1,0},{2,3},{3,2},{4,5},{5,4},{6,7},{7,6},{8,9},{9,8},{10,11... | collective-permute-start | bytes 786440 | tf_op jit(solution)/shard_map/ppermute | solution.py:291
  22.3 0.0 collective-permute-done.2.sq_ref
  22.3 3.3 %shard_map.76 = (bf16[256,4096]{1,0:T(8,128)(2,1)}, bf16[256,4096]{1,0:T(8,128)(2,1)}, bf16[256,2048]{1,0:T(8,128)(2,1)S(1)}, f32[128,1024]{1,0:T(8,128)S(1)}) custom-call(bf16[256,4096]{1,0:T(8,128)(2,1)} %q_ref.4, bf16[256,4096]{1,0:T(8,128)(2,1)} %g_ref.4, bf16[256,2048]{1,0:T(8,128)(2,1)S(1)} %collective-permute-done.2.sq_ref, ...), custom_call_target="tpu_custom_call" | custom-call | flops 402653184 | bytes 2097152 | tf_op jit(solution)/shard_map/pallas_call | solution.py:171
  25.5 1.4 %collective-permute-done.10.refs_2_ = bf16[128,1024]{1,0:T(8,128)(2,1)S(1)} collective-permute-done((bf16[128,1024]{1,0:T(8,128)(2,1)S(1)}, bf16[128,1024]{1,0:T(8,128)(2,1)S(1)}, u32[]{:S(2)}, u32[]{:S(2)}) %collective-permute-start.10) | collective-permute-done | bytes 262176 | tf_op jit(solution)/shard_map/ppermute | solution.py:291
  26.9 0.3 collective-permute-done.9.refs_0_
  27.2 6.6 %shard_map.77 = (bf16[256,4096]{1,0:T(8,128)(2,1)}, bf16[256,4096]{1,0:T(8,128)(2,1)}, bf16[256,2048]{1,0:T(8,128)(2,1)S(1)}, bf16[256,2048]{1,0:T(8,128)(2,1)S(...) custom-call(bf16[256,4096]{1,0:T(8,128)(2,1)} %q_ref.4, ...), custom_call_target="tpu_custom_call", output_to_operand_aliasing={{0}: (7, {}), {1}: (8, {}), {2}: (9, {})} | custom-call | flops 1207959552 | bytes 6291456 | tf_op jit(solution)/shard_map/pallas_call | solution.py:171
  33.9 1.6 %collective-permute-start.11 = (bf16[128,1024]{1,0:T(8,128)(2,1)S(1)}, bf16[128,1024]{1,0:T(8,128)(2,1)S(1)}, u32[]{:S(2)}, u32[]{:S(2)}) collective-permute-start(bf16[128,1024]{1,0:T(8,128)(2,1)S(1)} %get-tuple-element.50), channel_id=1, source_target_pairs={{0,1},{1,0},{2,3},{3,2},{4,5},{5,4},{6,7},{7,6},{8,9},{9,8},{10,11... | collective-permute-start | bytes 786440 | tf_op jit(solution)/shard_map/ppermute | solution.py:291
  35.5 1.5 %collective-permute-start.12 = (bf16[128,1024]{1,0:T(8,128)(2,1)S(1)}, bf16[128,1024]{1,0:T(8,128)(2,1)S(1)}, u32[]{:S(2)}, u32[]{:S(2)}) collective-permute-start(bf16[128,1024]{1,0:T(8,128)(2,1)S(1)} %get-tuple-element.52), channel_id=1, source_target_pairs={{0,4},{2,6},{4,0},{6,2},{8,12},{10,14},{12,8},{14,10},{16,20},{18,... | collective-permute-start | bytes 786440 | tf_op jit(solution)/shard_map/ppermute | solution.py:291
  37.0 3.4 %collective-permute-done.11 = bf16[128,1024]{1,0:T(8,128)(2,1)S(1)} collective-permute-done((bf16[128,1024]{1,0:T(8,128)(2,1)S(1)}, bf16[128,1024]{1,0:T(8,128)(2,1)S(1)}, u32[]{:S(2)}, u32[]{:S(2)}) %collective-permute-start.11) | collective-permute-done | bytes 262176 | tf_op jit(solution)/shard_map/ppermute | solution.py:291
  40.3 0.1 convert_add_fusion.1
  40.4 1.5 %collective-permute-done.12 = bf16[128,1024]{1,0:T(8,128)(2,1)S(1)} collective-permute-done((bf16[128,1024]{1,0:T(8,128)(2,1)S(1)}, bf16[128,1024]{1,0:T(8,128)(2,1)S(1)}, u32[]{:S(2)}, u32[]{:S(2)}) %collective-permute-start.12) | collective-permute-done | bytes 262176 | tf_op jit(solution)/shard_map/ppermute | solution.py:291
  41.8 0.1 convert_add_fusion
  41.9 0.1 collective-permute-start.15
  42.0 0.5 collective-permute-start.16
  42.5 0.6 collective-permute-start.14
  43.1 1.6 %collective-permute-start.13 = (bf16[64,1024]{1,0:T(8,128)(2,1)S(1)}, bf16[64,1024]{1,0:T(8,128)(2,1)S(1)}, u32[]{:S(2)}, u32[]{:S(2)}) collective-permute-start(bf16[64,1024]{1,0:T(8,128)(2,1)S(1)} %slice.136), channel_id=1, source_target_pairs={{0,4},{2,6},{4,0},{6,2},{8,12},{10,14},{12,8},{14,10},{16,20},{18,... | collective-permute-start | bytes 393224 | tf_op jit(solution)/shard_map/ppermute | solution.py:291
  44.6 3.4 %collective-permute-done.14 = bf16[64,1024]{1,0:T(8,128)(2,1)S(1)} collective-permute-done((bf16[64,1024]{1,0:T(8,128)(2,1)S(1)}, bf16[64,1024]{1,0:T(8,128)(2,1)S(1)}, u32[]{:S(2)}, u32[]{:S(2)}) %collective-permute-start.14) | collective-permute-done | bytes 131104 | tf_op jit(solution)/shard_map/ppermute | solution.py:291
  48.1 0.3 collective-permute-done.13
  48.4 0.0 collective-permute-done.16.refs_1_
  48.5 2.5 %collective-permute-start.19 = (bf16[16,2048]{1,0:T(8,128)(2,1)S(1)}, bf16[16,2048]{1,0:T(8,128)(2,1)S(1)}, u32[]{:S(2)}, u32[]{:S(2)}) collective-permute-start(bf16[16,2048]{1,0:T(8,128)(2,1)S(1)} %get-tuple-element.74), channel_id=1, source_target_pairs={{0,24},{2,26},{4,28},{6,30},{8,16},{10,18},{12,20},{14,22},{16,8},... | collective-permute-start | bytes 196616 | tf_op jit(solution)/shard_map/ppermute | solution.py:291
  51.0 0.2 collective-permute-start.18
  51.2 1.8 %collective-permute-start.17 = (bf16[16,2048]{1,0:T(8,128)(2,1)S(1)}, bf16[16,2048]{1,0:T(8,128)(2,1)S(1)}, u32[]{:S(2)}, u32[]{:S(2)}) collective-permute-start(bf16[16,2048]{1,0:T(8,128)(2,1)S(1)} %get-tuple-element.76), channel_id=1, source_target_pairs={{0,8},{2,10},{4,12},{6,14},{8,0},{10,2},{12,4},{14,6},{16,24},{18,... | collective-permute-start | bytes 196616 | tf_op jit(solution)/shard_map/ppermute | solution.py:291
  53.0 1.4 %shard_map.78 = (bf16[256,4096]{1,0:T(8,128)(2,1)}, bf16[256,4096]{1,0:T(8,128)(2,1)}) custom-call(bf16[256,2048]{1,0:T(8,128)(2,1)S(1)} %collective-permute-done.15.refs_0_, bf16[256,2048]{1,0:T(8,128)(2,1)S(1)} %collective-permute-done.16.refs_1_, bf16[256,4096]{1,0:T(8,128)(2,1)} %get-tuple-element.63.refs_2_, ...), custom_call_target="tpu_custom_call", output_to_operand_aliasing={{0}: (2, {}), {1}: (3, {})} | custom-call | tf_op jit(solution)/shard_map/pallas_call | solution.py:274
  54.4 0.7 %collective-permute-done.19 = bf16[16,2048]{1,0:T(8,128)(2,1)S(1)} collective-permute-done((bf16[16,2048]{1,0:T(8,128)(2,1)S(1)}, bf16[16,2048]{1,0:T(8,128)(2,1)S(1)}, u32[]{:S(2)}, u32[]{:S(2)}) %collective-permute-start.19) | collective-permute-done | bytes 65568 | tf_op jit(solution)/shard_map/ppermute | solution.py:291
  55.0 1.8 %collective-permute-done.18 = bf16[16,2048]{1,0:T(8,128)(2,1)S(1)} collective-permute-done((bf16[16,2048]{1,0:T(8,128)(2,1)S(1)}, bf16[16,2048]{1,0:T(8,128)(2,1)S(1)}, u32[]{:S(2)}, u32[]{:S(2)}) %collective-permute-start.18) | collective-permute-done | bytes 65568 | tf_op jit(solution)/shard_map/ppermute | solution.py:291
  56.9 0.0 collective-permute-done.17
  56.9 0.1 collective-permute-start.20
  57.0 1.2 %collective-permute-done.20.other_ref = bf16[8,2048]{1,0:T(8,128)(2,1)S(1)} collective-permute-done((bf16[8,2048]{1,0:T(8,128)(2,1)S(1)}, bf16[8,2048]{1,0:T(8,128)(2,1)S(1)}, u32[]{:S(2)}, u32[]{:S(2)}) %collective-permute-start.20) | collective-permute-done | bytes 32800 | tf_op jit(solution)/shard_map/ppermute | solution.py:291
  58.2 0.7 %shard_map.79 = (bf16[8,2048]{1,0:T(8,128)(2,1)}, bf16[8,2048]{1,0:T(8,128)(2,1)}) custom-call(bf16[8,2048]{1,0:T(8,128)(2,1)S(1)} %get-tuple-element.78.mine_ref, bf16[8,2048]{1,0:T(8,128)(2,1)S(1)} %collective-permute-done.20.other_ref), custom_call_target="tpu_custom_call" | custom-call | tf_op jit(solution)/shard_map/pallas_call | solution.py:241
  (23 shorter events, 0.3 us)
Async XLA Ops:
  0.6 1.6 %collective-permute-start = (bf16[8,2048]{1,0:T(8,128)(2,1)}, bf16[8,2048]{1,0:T(8,128)(2,1)S(1)}, u32[]{:S(2)}, u32[]{:S(2)}) collective-permute-start(bf16[8,2048]{1,0:T(8,128)(2,1)} %param.5), channel_id=1, source_target_pairs={{0,2},{2,0},{4,6},{6,4},{8,10},{10,8},{12,14},{14,12},{16,18},{18,... | collective-permute-start | bytes 98312 | tf_op jit(solution)/shard_map/ppermute | solution.py:291
  1.1 1.4 %collective-permute-start.1 = (bf16[8,2048]{1,0:T(8,128)(2,1)}, bf16[8,2048]{1,0:T(8,128)(2,1)S(1)}, u32[]{:S(2)}, u32[]{:S(2)}) collective-permute-start(bf16[8,2048]{1,0:T(8,128)(2,1)} %param.6), channel_id=1, source_target_pairs={{0,2},{2,0},{4,6},{6,4},{8,10},{10,8},{12,14},{14,12},{16,18},{18,... | collective-permute-start | bytes 98312 | tf_op jit(solution)/shard_map/ppermute | solution.py:291
  2.6 10.8 %collective-permute-start.6 = (bf16[16,2048]{1,0:T(8,128)(2,1)S(1)}, bf16[16,2048]{1,0:T(8,128)(2,1)S(1)}, u32[]{:S(2)}, u32[]{:S(2)}) collective-permute-start(bf16[16,2048]{1,0:T(8,128)(2,1)S(1)} %maximum_maximum_fusion), channel_id=1, source_target_pairs={{0,24},{2,26},{4,28},{6,30},{8,16},{10,18},{12,20},{14,22},{16,8},... | collective-permute-start | bytes 196616 | tf_op jit(solution)/shard_map/ppermute | solution.py:291
  7.4 6.0 %collective-permute-start.5 = (bf16[16,2048]{1,0:T(8,128)(2,1)S(1)}, bf16[16,2048]{1,0:T(8,128)(2,1)S(1)}, u32[]{:S(2)}, u32[]{:S(2)}) collective-permute-start(bf16[16,2048]{1,0:T(8,128)(2,1)S(1)} %maximum_maximum_fusion), channel_id=1, source_target_pairs={{0,16},{2,18},{4,20},{6,22},{8,24},{10,26},{12,28},{14,30},{16,0},... | collective-permute-start | bytes 196616 | tf_op jit(solution)/shard_map/ppermute | solution.py:291
  7.4 4.7 %collective-permute-start.4 = (bf16[16,2048]{1,0:T(8,128)(2,1)S(1)}, bf16[16,2048]{1,0:T(8,128)(2,1)S(1)}, u32[]{:S(2)}, u32[]{:S(2)}) collective-permute-start(bf16[16,2048]{1,0:T(8,128)(2,1)S(1)} %maximum_maximum_fusion), channel_id=1, source_target_pairs={{0,8},{2,10},{4,12},{6,14},{8,0},{10,2},{12,4},{14,6},{16,24},{18,... | collective-permute-start | bytes 196616 | tf_op jit(solution)/shard_map/ppermute | solution.py:291
  9.7 12.6 %collective-permute-start.2 = (bf16[256,2048]{1,0:T(8,128)(2,1)S(1)}, bf16[256,2048]{1,0:T(8,128)(2,1)S(1)}, u32[]{:S(2)}, u32[]{:S(2)}) collective-permute-start(bf16[256,2048]{1,0:T(8,128)(2,1)S(1)} %get-tuple-element.41), channel_id=1, source_target_pairs={{0,2},{2,0},{4,6},{6,4},{8,10},{10,8},{12,14},{14,12},{16,18},{18,... | collective-permute-start | bytes 3145736 | tf_op jit(solution)/shard_map/ppermute | solution.py:291
  9.7 12.5 %collective-permute-start.3 = (bf16[256,2048]{1,0:T(8,128)(2,1)S(1)}, bf16[256,2048]{1,0:T(8,128)(2,1)S(1)}, u32[]{:S(2)}, u32[]{:S(2)}) collective-permute-start(bf16[256,2048]{1,0:T(8,128)(2,1)S(1)} %get-tuple-element.42), channel_id=1, source_target_pairs={{0,2},{2,0},{4,6},{6,4},{8,10},{10,8},{12,14},{14,12},{16,18},{18,... | collective-permute-start | bytes 3145736 | tf_op jit(solution)/shard_map/ppermute | solution.py:291
  13.4 5.2 %collective-permute-start.7 = (bf16[64,1024]{1,0:T(8,128)(2,1)S(1)}, bf16[64,1024]{1,0:T(8,128)(2,1)S(1)}, u32[]{:S(2)}, u32[]{:S(2)}) collective-permute-start(bf16[64,1024]{1,0:T(8,128)(2,1)S(1)} %pad_maximum_fusion), channel_id=1, source_target_pairs={{0,4},{2,6},{4,0},{6,2},{8,12},{10,14},{12,8},{14,10},{16,20},{18,... | collective-permute-start | bytes 393224 | tf_op jit(solution)/shard_map/ppermute | solution.py:291
  15.0 5.0 %collective-permute-start.8 = (bf16[64,1024]{1,0:T(8,128)(2,1)S(1)}, bf16[64,1024]{1,0:T(8,128)(2,1)S(1)}, u32[]{:S(2)}, u32[]{:S(2)}) collective-permute-start(bf16[64,1024]{1,0:T(8,128)(2,1)S(1)} %pad_maximum_fusion.1), channel_id=1, source_target_pairs={{0,1},{1,0},{2,3},{3,2},{4,5},{5,4},{6,7},{7,6},{8,9},{9,8},{10,11... | collective-permute-start | bytes 393224 | tf_op jit(solution)/shard_map/ppermute | solution.py:291
  20.1 6.8 %collective-permute-start.10 = (bf16[128,1024]{1,0:T(8,128)(2,1)S(1)}, bf16[128,1024]{1,0:T(8,128)(2,1)S(1)}, u32[]{:S(2)}, u32[]{:S(2)}) collective-permute-start(bf16[128,1024]{1,0:T(8,128)(2,1)S(1)} %constant_dynamic-update-slice_fusion.5.refs_1_), channel_id=1, source_target_pairs={{0,4},{2,6},{4,0},{6,2},{8,12},{10,14},{12,8},{14,10},{16,20},{18,... | collective-permute-start | bytes 786440 | tf_op jit(solution)/shard_map/ppermute | solution.py:291
  20.7 6.6 %collective-permute-start.9 = (bf16[128,1024]{1,0:T(8,128)(2,1)S(1)}, bf16[128,1024]{1,0:T(8,128)(2,1)S(1)}, u32[]{:S(2)}, u32[]{:S(2)}) collective-permute-start(bf16[128,1024]{1,0:T(8,128)(2,1)S(1)} %constant_dynamic-update-slice_fusion.refs_0_), channel_id=1, source_target_pairs={{0,1},{1,0},{2,3},{3,2},{4,5},{5,4},{6,7},{7,6},{8,9},{9,8},{10,11... | collective-permute-start | bytes 786440 | tf_op jit(solution)/shard_map/ppermute | solution.py:291
  33.9 6.4 %collective-permute-start.11 = (bf16[128,1024]{1,0:T(8,128)(2,1)S(1)}, bf16[128,1024]{1,0:T(8,128)(2,1)S(1)}, u32[]{:S(2)}, u32[]{:S(2)}) collective-permute-start(bf16[128,1024]{1,0:T(8,128)(2,1)S(1)} %get-tuple-element.50), channel_id=1, source_target_pairs={{0,1},{1,0},{2,3},{3,2},{4,5},{5,4},{6,7},{7,6},{8,9},{9,8},{10,11... | collective-permute-start | bytes 786440 | tf_op jit(solution)/shard_map/ppermute | solution.py:291
  35.5 6.4 %collective-permute-start.12 = (bf16[128,1024]{1,0:T(8,128)(2,1)S(1)}, bf16[128,1024]{1,0:T(8,128)(2,1)S(1)}, u32[]{:S(2)}, u32[]{:S(2)}) collective-permute-start(bf16[128,1024]{1,0:T(8,128)(2,1)S(1)} %get-tuple-element.52), channel_id=1, source_target_pairs={{0,4},{2,6},{4,0},{6,2},{8,12},{10,14},{12,8},{14,10},{16,20},{18,... | collective-permute-start | bytes 786440 | tf_op jit(solution)/shard_map/ppermute | solution.py:291
  41.9 6.5 %collective-permute-start.15 = (bf16[256,2048]{1,0:T(8,128)(2,1)S(1)}, bf16[256,2048]{1,0:T(8,128)(2,1)S(1)}, u32[]{:S(2)}, u32[]{:S(2)}) collective-permute-start(bf16[256,2048]{1,0:T(8,128)(2,1)S(1)} %get-tuple-element.57), channel_id=1, source_target_pairs={{0,2},{2,0},{4,6},{6,4},{8,10},{10,8},{12,14},{14,12},{16,18},{18,... | collective-permute-start | bytes 3145736 | tf_op jit(solution)/shard_map/ppermute | solution.py:291
  42.0 6.4 %collective-permute-start.16 = (bf16[256,2048]{1,0:T(8,128)(2,1)S(1)}, bf16[256,2048]{1,0:T(8,128)(2,1)S(1)}, u32[]{:S(2)}, u32[]{:S(2)}) collective-permute-start(bf16[256,2048]{1,0:T(8,128)(2,1)S(1)} %get-tuple-element.58), channel_id=1, source_target_pairs={{0,2},{2,0},{4,6},{6,4},{8,10},{10,8},{12,14},{14,12},{16,18},{18,... | collective-permute-start | bytes 3145736 | tf_op jit(solution)/shard_map/ppermute | solution.py:291
  42.5 5.5 %collective-permute-start.14 = (bf16[64,1024]{1,0:T(8,128)(2,1)S(1)}, bf16[64,1024]{1,0:T(8,128)(2,1)S(1)}, u32[]{:S(2)}, u32[]{:S(2)}) collective-permute-start(bf16[64,1024]{1,0:T(8,128)(2,1)S(1)} %slice.135), channel_id=1, source_target_pairs={{0,1},{1,0},{2,3},{3,2},{4,5},{5,4},{6,7},{7,6},{8,9},{9,8},{10,11... | collective-permute-start | bytes 393224 | tf_op jit(solution)/shard_map/ppermute | solution.py:291
  43.1 5.3 %collective-permute-start.13 = (bf16[64,1024]{1,0:T(8,128)(2,1)S(1)}, bf16[64,1024]{1,0:T(8,128)(2,1)S(1)}, u32[]{:S(2)}, u32[]{:S(2)}) collective-permute-start(bf16[64,1024]{1,0:T(8,128)(2,1)S(1)} %slice.136), channel_id=1, source_target_pairs={{0,4},{2,6},{4,0},{6,2},{8,12},{10,14},{12,8},{14,10},{16,20},{18,... | collective-permute-start | bytes 393224 | tf_op jit(solution)/shard_map/ppermute | solution.py:291
  48.5 6.5 %collective-permute-start.19 = (bf16[16,2048]{1,0:T(8,128)(2,1)S(1)}, bf16[16,2048]{1,0:T(8,128)(2,1)S(1)}, u32[]{:S(2)}, u32[]{:S(2)}) collective-permute-start(bf16[16,2048]{1,0:T(8,128)(2,1)S(1)} %get-tuple-element.74), channel_id=1, source_target_pairs={{0,24},{2,26},{4,28},{6,30},{8,16},{10,18},{12,20},{14,22},{16,8},... | collective-permute-start | bytes 196616 | tf_op jit(solution)/shard_map/ppermute | solution.py:291
  51.0 5.9 %collective-permute-start.18 = (bf16[16,2048]{1,0:T(8,128)(2,1)S(1)}, bf16[16,2048]{1,0:T(8,128)(2,1)S(1)}, u32[]{:S(2)}, u32[]{:S(2)}) collective-permute-start(bf16[16,2048]{1,0:T(8,128)(2,1)S(1)} %get-tuple-element.75), channel_id=1, source_target_pairs={{0,16},{2,18},{4,20},{6,22},{8,24},{10,26},{12,28},{14,30},{16,0},... | collective-permute-start | bytes 196616 | tf_op jit(solution)/shard_map/ppermute | solution.py:291
  51.2 5.7 %collective-permute-start.17 = (bf16[16,2048]{1,0:T(8,128)(2,1)S(1)}, bf16[16,2048]{1,0:T(8,128)(2,1)S(1)}, u32[]{:S(2)}, u32[]{:S(2)}) collective-permute-start(bf16[16,2048]{1,0:T(8,128)(2,1)S(1)} %get-tuple-element.76), channel_id=1, source_target_pairs={{0,8},{2,10},{4,12},{6,14},{8,0},{10,2},{12,4},{14,6},{16,24},{18,... | collective-permute-start | bytes 196616 | tf_op jit(solution)/shard_map/ppermute | solution.py:291
  56.9 1.3 %collective-permute-start.20 = (bf16[8,2048]{1,0:T(8,128)(2,1)S(1)}, bf16[8,2048]{1,0:T(8,128)(2,1)S(1)}, u32[]{:S(2)}, u32[]{:S(2)}) collective-permute-start(bf16[8,2048]{1,0:T(8,128)(2,1)S(1)} %get-tuple-element.77), channel_id=1, source_target_pairs={{0,2},{2,0},{4,6},{6,4},{8,10},{10,8},{12,14},{14,12},{16,18},{18,... | collective-permute-start | bytes 98312 | tf_op jit(solution)/shard_map/ppermute | solution.py:291

commit v10 on v9

--- a/solution.py
+++ b/solution.py
@@ -11,7 +11,6 @@
 DH = 128
 
 NT = (((1,), (1,)), ((), ()))
-TN = (((0,), (0,)), ((), ()))
 NN = (((1,), (0,)), ((), ()))
 
 bf16, f32 = jnp.bfloat16, jnp.float32
@@ -38,13 +37,14 @@
     return lambda r: pl.multiple_of((((my ^ r) * 2 + core) * blocks + block) * width, width)
 
 
-def attention_kernel(n_mp, blocks, groups, n_memory, q_ref, g_ref, sq_ref, sg_ref, *refs):
+def attention_kernel(n_mp, blocks, groups, n_memory, with_outputs, q_ref, g_ref, sq_ref, sg_ref, *refs):
     used = sorted({block for block, *_ in groups})
     memory_refs, refs = refs[:n_memory], refs[n_memory:]
     token_buf, result_buf, raw_ref, prob_ref, grad_ref, weight_ref, sems = refs[-7:]
-    n_terms = 1 + max(max(terms) for *_, terms in groups)
-    term_refs, refs = refs[-7 - n_terms : -7], refs[: -7 - n_terms]
-    attended_ref, query_grad_ref, *sent_refs = refs[-2 - len(used) :]
+    n_terms = max([1 + t for *_, terms in groups for t in terms], default=0)
+    term_refs, refs = refs[len(refs) - 7 - n_terms : -7], refs[: len(refs) - 7 - n_terms]
+    if with_outputs:
+        attended_ref, query_grad_ref, *sent_refs = refs[-2 - len(used) :]
     count, width = q_ref.shape[0], memory_refs[0].shape[1] // 2
     heads = width // DH
     step = min(DH, 2 * count)
@@ -54,7 +54,7 @@
     def of_group(block, r0, number, memories, terms, slot0):
         column = columns(n_mp, blocks, block, width, False)
         size = memory_refs[memories[0]].shape[0] // number
-        sent_ref = sent_refs[used.index(block)]
+        sent_ref = sent_refs[used.index(block)] if with_outputs else None
 
         def inputs(k):
             starts = (column(r0 + k), pl.multiple_of((block * n_mp + r0 + k) * width, width))
@@ -118,10 +118,11 @@
 
             def results(n):
                 for m, pair_ref in enumerate((grad_ref, weight_ref)):
-                    result_buf[slot0 + k, m, :, cols[n]] = dot(pair_ref[n], memory[m][n], TN).astype(bf16)
+                    result = dot(memory[m][n].T, pair_ref[n], NN).astype(bf16)
+                    result_buf[slot0 + k, m, :, cols[n]] = result.T
 
             def gradients(n):
-                for m, pair_ref in enumerate((grad_ref, weight_ref)):
+                for m, pair_ref in enumerate((grad_ref, weight_ref) if terms else ()):
                     term = dot(pair_ref[n], tokens(m, n), NN)
                     for i, t in enumerate(terms):
                         term_refs[t][rows, targets[m][n]] = term[i * size : (i + 1) * size].astype(term_refs[t].dtype)
@@ -133,15 +134,17 @@
                     scores(n)
                 if 1 <= n <= heads:
                     softmax(n - 1)
-                if n >= 2:
+                if n >= 2 and with_outputs:
                     results(n - 2)
-                    if n <= heads:
-                        gradients(n - 2)
-            for copy in outputs(k):
-                copy.start()
+                if 2 <= n <= heads:
+                    gradients(n - 2)
+            if with_outputs:
+                for copy in outputs(k):
+                    copy.start()
             gradients(heads - 1)
 
-        return [functools.partial(repeat, body) for body in (start_inputs, work, wait_outputs)]
+        bodies = (start_inputs, work) + ((wait_outputs,) if with_outputs else ())
+        return [functools.partial(repeat, body) for body in bodies]
 
     slot0, phases = 0, []
     for group in groups:
@@ -160,20 +163,23 @@
 
 
 def attention(n_mp, blocks, groups, tokens, memory, terms, outputs, sent):
+    with_outputs = outputs is not None
     rows, whole = tokens[0].shape
     width = memory[0].shape[1] // 2
     number = sum(n for _, _, n, *_ in groups)
     count = len(groups[0][3]) * memory[0].shape[0] // groups[0][2]
     used = sorted({block for block, *_ in groups})
     scratch = (width // DH, count, 2 * rows)
-    earlier = [*outputs] + [sent[block] for block in used if block in sent]
+    earlier = [*outputs] + [sent[block] for block in used if block in sent] if with_outputs else []
+    token_outs = [jax.ShapeDtypeStruct((rows, whole), bf16)] * 2
+    token_outs += [jax.ShapeDtypeStruct((rows, whole // blocks), bf16)] * len(used)
+    token_outs = token_outs if with_outputs else []
     first = 4 + len(memory)
     results = pl.pallas_call(
-        functools.partial(attention_kernel, n_mp, blocks, groups, len(memory)),
+        functools.partial(attention_kernel, n_mp, blocks, groups, len(memory), with_outputs),
         in_specs=[HBM] * 4 + [VMEM] * len(memory) + [HBM] * len(earlier),
-        out_specs=[HBM] * (2 + len(used)) + [VMEM] * len(terms),
-        out_shape=[jax.ShapeDtypeStruct((rows, whole), bf16)] * 2
-        + [jax.ShapeDtypeStruct((rows, whole // blocks), bf16)] * len(used)
+        out_specs=[HBM] * len(token_outs) + [VMEM] * len(terms),
+        out_shape=token_outs
         + [pltpu.VMEM(memory[0].shape, t) for t in terms],
         scratch_shapes=[pltpu.VMEM((number, 2, 2 * rows, width), bf16)] * 2
         + [pltpu.VMEM(scratch, t) for t in (f32, f32, bf16, bf16)]
@@ -186,6 +192,8 @@
             transcendentals=2 * rows * count * width * number // DH,
         ),
     )(*pinned(pltpu.HBM, *tokens[:2]), *tokens[2:], *pinned(pltpu.VMEM, *memory), *earlier)
+    if not with_outputs:
+        return outputs, sent, results
     sent = {**sent, **dict(zip(used, results[2:]))}
     return results[:2], sent, results[2 + len(used) :]
 
@@ -326,15 +334,14 @@
     outputs, sent, (first_keep,) = attention(
         n_mp, blocks, [(0, 0, half, (0,), (0,))], tokens, [first], [f32], [], {}
     )
-    outputs, sent, (first_give, second_keep, second_give) = attention(
-        n_mp,
-        blocks,
-        [(0, half, n_mp - half, (0,), (0,)), (1, 0, n_mp, (1, 2), (1, 2))],
-        tokens,
-        [first_got, second, second_got],
-        [bf16, f32, bf16],
-        outputs,
-        sent,
+    rest = [(0, half, n_mp - half, (0,), (0,)), (1, 0, n_mp, (1, 2), (1, 2))]
+    first_keep, second = together(first_keep, second)
+    memory = [first_got, second, second_got]
+    *_, (first_give, second_keep, second_give) = attention(
+        n_mp, blocks, rest, tokens, memory, [bf16, f32, bf16], None, {}
+    )
+    outputs, sent, _ = attention(
+        n_mp, blocks, [(*group[:4], ()) for group in rest], tokens, memory, [], outputs, sent
     )
     first_got, second_got = swap(first_give, "mp", y_bits[-1]), swap(second_give, "seq", x_bit)
     first, second, sent = together(

time: 59.2 us -> 58.3 us (0.985)
  waiting for transfers between devices: 21.1 us -> 17.3 us
  Pallas kernels: 13.6 us -> 17.4 us
  starting transfers between devices: 22.2 us -> 21.3 us
    pallas_call x2 -> x3, Pallas kernels: 9.9 us -> 13.8 us  [attention(): pl.pallas_call(functools.partial(attention_kernel, n_mp, blocks, groups,...]
    ppermute x21, waiting for transfers between devices: 21.1 us -> 17.3 us  [swap(): return lax.ppermute(array, axis, [(i, i ^ bits) for i in range(size)])]
    ppermute x21, starting transfers between devices: 22.2 us -> 21.3 us  [swap(): return lax.ppermute(array, axis, [(i, i ^ bits) for i in range(size)])]
  transfers between devices with their start and end apart: 21 -> 21, of which waited for: 15 -> 13; matrix products, arithmetic and copies ran while one was open for 2% -> 2% of each run, Pallas kernels for 11% -> 21%
where the time goes in v10:
time: 58.3 us; the launch traced here: 58 us
  starting transfers between devices  21.3 us (37%)
  Pallas kernels  17.4 us (30%)
  waiting for transfers between devices  17.3 us (30%)
  local copies, waits for them, and re-layouts  0.9 us (2%)
  between operations  0.86 us (1%)
    ppermute x21, starting transfers between devices, swap(): return lax.ppermute(array, axis, [(i, i ^ bits) for i in range(size)])  21.3 us
    ppermute x21, waiting for transfers between devices, swap(): return lax.ppermute(array, axis, [(i, i ^ bits) for i in range(size)])  17.3 us
    pallas_call x3, Pallas kernels, attention(): pl.pallas_call(functools.partial(attention_kernel, n_mp, blocks, groups,...  13.8 us
    pallas_call x1, Pallas kernels, packing(): pl.pallas_call(functools.partial(packing_kernel, n_mp, blocks), in_specs=...  1.6 us
    pallas_call x1, Pallas kernels, placing(): pl.pallas_call(functools.partial(placing_kernel, n_mp, blocks), in_specs=...  1.37 us
  transfers between devices with their start and end apart: 21, of which 13 were waited for; matrix products, arithmetic and copies ran while one was open for 2% of the time, Pallas kernels for 21%

profile of v10, /device:TPU:0, one launch (start us, length us, event | category | flops | bytes accessed | tf_op | source)
XLA Modules:
  0.0 58.0 jit_solution(561111328933434213)
XLA Ops:
  0.6 0.5 collective-permute-start
  1.1 0.1 collective-permute-start.1
  1.2 0.7 %constant_dynamic-slice_fusion.2 = (bf16[8,512]{1,0:T(8,128)(2,1)S(1)}, bf16[8,512]{1,0:T(8,128)(2,1)S(1)}, bf16[8,512]{1,0:T(8,128)(2,1)S(1)}, bf16[8,512]{1,0:T(8,128)(2,1)S(1)}) fusion(bf16[8,2048]{1,0:T(8,128)(2,1)} %param.6, s32[]{:T(128)S(6)} %select_n.2, s32[]{:T(128)S(6)} %add.35, bf16[8,2048]{1,0:T(8,128)(2,1)} %param.5), kind=kLoop, calls=%fused_computation.25 | loop fusion | bytes 65544 | tf_op jit(solution)/shard_map/slice | solution.py:311
  2.0 0.2 collective-permute-done
  2.2 0.3 collective-permute-done.1
  2.6 4.8 %collective-permute-start.6 = (bf16[16,2048]{1,0:T(8,128)(2,1)S(1)}, bf16[16,2048]{1,0:T(8,128)(2,1)S(1)}, u32[]{:S(2)}, u32[]{:S(2)}) collective-permute-start(bf16[16,2048]{1,0:T(8,128)(2,1)S(1)} %maximum_maximum_fusion), channel_id=1, source_target_pairs={{0,24},{2,26},{4,28},{6,30},{8,16},{10,18},{12,20},{14,22},{16,8},... | collective-permute-start | bytes 196616 | tf_op jit(solution)/shard_map/ppermute | solution.py:299
  7.4 0.0 collective-permute-start.5
  7.4 0.6 %collective-permute-start.4 = (bf16[16,2048]{1,0:T(8,128)(2,1)S(1)}, bf16[16,2048]{1,0:T(8,128)(2,1)S(1)}, u32[]{:S(2)}, u32[]{:S(2)}) collective-permute-start(bf16[16,2048]{1,0:T(8,128)(2,1)S(1)} %maximum_maximum_fusion), channel_id=1, source_target_pairs={{0,8},{2,10},{4,12},{6,14},{8,0},{10,2},{12,4},{14,6},{16,24},{18,... | collective-permute-start | bytes 196616 | tf_op jit(solution)/shard_map/ppermute | solution.py:299
  8.1 1.6 %shard_map.75 = (bf16[256,2048]{1,0:T(8,128)(2,1)S(1)}, bf16[256,2048]{1,0:T(8,128)(2,1)S(1)}) custom-call(bf16[256,4096]{1,0:T(8,128)(2,1)} %q_ref.6, bf16[256,4096]{1,0:T(8,128)(2,1)} %g_ref.6), custom_call_target="tpu_custom_call" | custom-call | bytes 4194304 | tf_op jit(solution)/shard_map/pallas_call | solution.py:222
  9.7 0.1 collective-permute-start.2
  9.7 0.5 collective-permute-start.3
  10.2 1.9 %collective-permute-done.4 = bf16[16,2048]{1,0:T(8,128)(2,1)S(1)} collective-permute-done((bf16[16,2048]{1,0:T(8,128)(2,1)S(1)}, bf16[16,2048]{1,0:T(8,128)(2,1)S(1)}, u32[]{:S(2)}, u32[]{:S(2)}) %collective-permute-start.4) | collective-permute-done | bytes 65568 | tf_op jit(solution)/shard_map/ppermute | solution.py:299
  12.1 1.2 %collective-permute-done.5 = bf16[16,2048]{1,0:T(8,128)(2,1)S(1)} collective-permute-done((bf16[16,2048]{1,0:T(8,128)(2,1)S(1)}, bf16[16,2048]{1,0:T(8,128)(2,1)S(1)}, u32[]{:S(2)}, u32[]{:S(2)}) %collective-permute-start.5) | collective-permute-done | bytes 65568 | tf_op jit(solution)/shard_map/ppermute | solution.py:299
  13.4 0.0 collective-permute-done.6
  13.4 1.6 %collective-permute-start.7 = (bf16[64,1024]{1,0:T(8,128)(2,1)S(1)}, bf16[64,1024]{1,0:T(8,128)(2,1)S(1)}, u32[]{:S(2)}, u32[]{:S(2)}) collective-permute-start(bf16[64,1024]{1,0:T(8,128)(2,1)S(1)} %pad_maximum_fusion), channel_id=1, source_target_pairs={{0,4},{2,6},{4,0},{6,2},{8,12},{10,14},{12,8},{14,10},{16,20},{18,... | collective-permute-start | bytes 393224 | tf_op jit(solution)/shard_map/ppermute | solution.py:299
  15.0 1.6 %collective-permute-start.8 = (bf16[64,1024]{1,0:T(8,128)(2,1)S(1)}, bf16[64,1024]{1,0:T(8,128)(2,1)S(1)}, u32[]{:S(2)}, u32[]{:S(2)}) collective-permute-start(bf16[64,1024]{1,0:T(8,128)(2,1)S(1)} %pad_maximum_fusion.1), channel_id=1, source_target_pairs={{0,1},{1,0},{2,3},{3,2},{4,5},{5,4},{6,7},{7,6},{8,9},{9,8},{10,11... | collective-permute-start | bytes 393224 | tf_op jit(solution)/shard_map/ppermute | solution.py:299
  16.6 2.0 %collective-permute-done.7 = bf16[64,1024]{1,0:T(8,128)(2,1)S(1)} collective-permute-done((bf16[64,1024]{1,0:T(8,128)(2,1)S(1)}, bf16[64,1024]{1,0:T(8,128)(2,1)S(1)}, u32[]{:S(2)}, u32[]{:S(2)}) %collective-permute-start.7) | collective-permute-done | bytes 131104 | tf_op jit(solution)/shard_map/ppermute | solution.py:299
  18.6 1.4 %collective-permute-done.8 = bf16[64,1024]{1,0:T(8,128)(2,1)S(1)} collective-permute-done((bf16[64,1024]{1,0:T(8,128)(2,1)S(1)}, bf16[64,1024]{1,0:T(8,128)(2,1)S(1)}, u32[]{:S(2)}, u32[]{:S(2)}) %collective-permute-start.8) | collective-permute-done | bytes 131104 | tf_op jit(solution)/shard_map/ppermute | solution.py:299
  20.1 0.6 %collective-permute-start.10 = (bf16[128,1024]{1,0:T(8,128)(2,1)S(1)}, bf16[128,1024]{1,0:T(8,128)(2,1)S(1)}, u32[]{:S(2)}, u32[]{:S(2)}) collective-permute-start(bf16[128,1024]{1,0:T(8,128)(2,1)S(1)} %constant_dynamic-update-slice_fusion.5.refs_1_), channel_id=1, source_target_pairs={{0,4},{2,6},{4,0},{6,2},{8,12},{10,14},{12,8},{14,10},{16,20},{18,... | collective-permute-start | bytes 786440 | tf_op jit(solution)/shard_map/ppermute | solution.py:299
  20.7 1.6 %collective-permute-start.9 = (bf16[128,1024]{1,0:T(8,128)(2,1)S(1)}, bf16[128,1024]{1,0:T(8,128)(2,1)S(1)}, u32[]{:S(2)}, u32[]{:S(2)}) collective-permute-start(bf16[128,1024]{1,0:T(8,128)(2,1)S(1)} %constant_dynamic-update-slice_fusion.refs_0_), channel_id=1, source_target_pairs={{0,1},{1,0},{2,3},{3,2},{4,5},{5,4},{6,7},{7,6},{8,9},{9,8},{10,11... | collective-permute-start | bytes 786440 | tf_op jit(solution)/shard_map/ppermute | solution.py:299
  22.3 0.0 collective-permute-done.2.sq_ref
  22.3 0.0 collective-permute-done.3.sg_ref
  22.3 3.2 %shard_map.76 = (bf16[256,4096]{1,0:T(8,128)(2,1)}, bf16[256,4096]{1,0:T(8,128)(2,1)}, bf16[256,2048]{1,0:T(8,128)(2,1)S(1)}, f32[128,1024]{1,0:T(8,128)S(1)}) custom-call(bf16[256,4096]{1,0:T(8,128)(2,1)} %q_ref.6, bf16[256,4096]{1,0:T(8,128)(2,1)} %g_ref.6, bf16[256,2048]{1,0:T(8,128)(2,1)S(1)} %collective-permute-done.2.sq_ref, ...), custom_call_target="tpu_custom_call" | custom-call | flops 402653184 | bytes 2097152 | tf_op jit(solution)/shard_map/pallas_call | solution.py:178
  25.5 1.4 %collective-permute-done.10.refs_2_ = bf16[128,1024]{1,0:T(8,128)(2,1)S(1)} collective-permute-done((bf16[128,1024]{1,0:T(8,128)(2,1)S(1)}, bf16[128,1024]{1,0:T(8,128)(2,1)S(1)}, u32[]{:S(2)}, u32[]{:S(2)}) %collective-permute-start.10) | collective-permute-done | bytes 262176 | tf_op jit(solution)/shard_map/ppermute | solution.py:299
  26.9 0.3 collective-permute-done.9.refs_0_
  27.2 4.6 %shard_map.77 = (bf16[128,1024]{1,0:T(8,128)(2,1)S(1)}, f32[128,1024]{1,0:T(8,128)S(1)}, bf16[128,1024]{1,0:T(8,128)(2,1)S(1)}) custom-call(bf16[256,4096]{1,0:T(8,128)(2,1)} %q_ref.6, bf16[256,4096]{1,0:T(8,128)(2,1)} %g_ref.6, bf16[256,2048]{1,0:T(8,128)(2,1)S(1)} %collective-permute-done.2.sq_ref, bf16[256,2048]{1,0:T(8,128)(2,1)S(1)} %collective-permute-done.3.sg_ref, ...), custom_call_target="tpu_custom_call" | custom-call | flops 1207959552 | bytes 6291456 | tf_op jit(solution)/shard_map/pallas_call | solution.py:178
  31.9 1.6 %collective-permute-start.11 = (bf16[128,1024]{1,0:T(8,128)(2,1)S(1)}, bf16[128,1024]{1,0:T(8,128)(2,1)S(1)}, u32[]{:S(2)}, u32[]{:S(2)}) collective-permute-start(bf16[128,1024]{1,0:T(8,128)(2,1)S(1)} %get-tuple-element.51), channel_id=1, source_target_pairs={{0,1},{1,0},{2,3},{3,2},{4,5},{5,4},{6,7},{7,6},{8,9},{9,8},{10,11... | collective-permute-start | bytes 786440 | tf_op jit(solution)/shard_map/ppermute | solution.py:299
  33.4 1.5 %collective-permute-start.12 = (bf16[128,1024]{1,0:T(8,128)(2,1)S(1)}, bf16[128,1024]{1,0:T(8,128)(2,1)S(1)}, u32[]{:S(2)}, u32[]{:S(2)}) collective-permute-start(bf16[128,1024]{1,0:T(8,128)(2,1)S(1)} %get-tuple-element.53), channel_id=1, source_target_pairs={{0,4},{2,6},{4,0},{6,2},{8,12},{10,14},{12,8},{14,10},{16,20},{18,... | collective-permute-start | bytes 786440 | tf_op jit(solution)/shard_map/ppermute | solution.py:299
  34.9 6.0 %shard_map.78 = (bf16[256,4096]{1,0:T(8,128)(2,1)}, bf16[256,4096]{1,0:T(8,128)(2,1)}, bf16[256,2048]{1,0:T(8,128)(2,1)S(1)}, bf16[256,2048]{1,0:T(8,128)(2,1)S(1)}) custom-call(bf16[256,4096]{1,0:T(8,128)(2,1)} %q_ref.6, bf16[256,4096]{1,0:T(8,128)(2,1)} %g_ref.6, ...), custom_call_target="tpu_custom_call", output_to_operand_aliasing={{0}: (7, {}), {1}: (8, {}), {2}: (9, {})} | custom-call | flops 1207959552 | bytes 6291456 | tf_op jit(solution)/shard_map/pallas_call | solution.py:178
  40.9 0.0 collective-permute-done.11
  40.9 0.1 convert_add_fusion.1
  41.0 0.0 collective-permute-done.12
  41.0 0.1 convert_add_fusion
  41.1 0.1 collective-permute-start.15
  41.1 0.5 collective-permute-start.16
  41.7 0.6 collective-permute-start.14
  42.2 0.6 %collective-permute-start.13 = (bf16[64,1024]{1,0:T(8,128)(2,1)S(1)}, bf16[64,1024]{1,0:T(8,128)(2,1)S(1)}, u32[]{:S(2)}, u32[]{:S(2)}) collective-permute-start(bf16[64,1024]{1,0:T(8,128)(2,1)S(1)} %slice.136), channel_id=1, source_target_pairs={{0,4},{2,6},{4,0},{6,2},{8,12},{10,14},{12,8},{14,10},{16,20},{18,... | collective-permute-start | bytes 393224 | tf_op jit(solution)/shard_map/ppermute | solution.py:299
  42.8 4.4 %collective-permute-done.14 = bf16[64,1024]{1,0:T(8,128)(2,1)S(1)} collective-permute-done((bf16[64,1024]{1,0:T(8,128)(2,1)S(1)}, bf16[64,1024]{1,0:T(8,128)(2,1)S(1)}, u32[]{:S(2)}, u32[]{:S(2)}) %collective-permute-start.14) | collective-permute-done | bytes 131104 | tf_op jit(solution)/shard_map/ppermute | solution.py:299
  47.2 0.3 collective-permute-done.13
  47.7 2.4 %collective-permute-start.19 = (bf16[16,2048]{1,0:T(8,128)(2,1)S(1)}, bf16[16,2048]{1,0:T(8,128)(2,1)S(1)}, u32[]{:S(2)}, u32[]{:S(2)}) collective-permute-start(bf16[16,2048]{1,0:T(8,128)(2,1)S(1)} %get-tuple-element.78), channel_id=1, source_target_pairs={{0,24},{2,26},{4,28},{6,30},{8,16},{10,18},{12,20},{14,22},{16,8},... | collective-permute-start | bytes 196616 | tf_op jit(solution)/shard_map/ppermute | solution.py:299
  50.1 0.2 collective-permute-start.18
  50.3 1.8 %collective-permute-start.17 = (bf16[16,2048]{1,0:T(8,128)(2,1)S(1)}, bf16[16,2048]{1,0:T(8,128)(2,1)S(1)}, u32[]{:S(2)}, u32[]{:S(2)}) collective-permute-start(bf16[16,2048]{1,0:T(8,128)(2,1)S(1)} %get-tuple-element.80), channel_id=1, source_target_pairs={{0,8},{2,10},{4,12},{6,14},{8,0},{10,2},{12,4},{14,6},{16,24},{18,... | collective-permute-start | bytes 196616 | tf_op jit(solution)/shard_map/ppermute | solution.py:299
  52.1 1.4 %shard_map.79 = (bf16[256,4096]{1,0:T(8,128)(2,1)}, bf16[256,4096]{1,0:T(8,128)(2,1)}) custom-call(bf16[256,2048]{1,0:T(8,128)(2,1)S(1)} %collective-permute-done.15.refs_0_, bf16[256,2048]{1,0:T(8,128)(2,1)S(1)} %collective-permute-done.16.refs_1_, bf16[256,4096]{1,0:T(8,128)(2,1)} %get-tuple-element.67.refs_2_, ...), custom_call_target="tpu_custom_call", output_to_operand_aliasing={{0}: (2, {}), {1}: (3, {})} | custom-call | tf_op jit(solution)/shard_map/pallas_call | solution.py:282
  53.5 0.7 %collective-permute-done.19 = bf16[16,2048]{1,0:T(8,128)(2,1)S(1)} collective-permute-done((bf16[16,2048]{1,0:T(8,128)(2,1)S(1)}, bf16[16,2048]{1,0:T(8,128)(2,1)S(1)}, u32[]{:S(2)}, u32[]{:S(2)}) %collective-permute-start.19) | collective-permute-done | bytes 65568 | tf_op jit(solution)/shard_map/ppermute | solution.py:299
  54.2 1.8 %collective-permute-done.18 = bf16[16,2048]{1,0:T(8,128)(2,1)S(1)} collective-permute-done((bf16[16,2048]{1,0:T(8,128)(2,1)S(1)}, bf16[16,2048]{1,0:T(8,128)(2,1)S(1)}, u32[]{:S(2)}, u32[]{:S(2)}) %collective-permute-start.18) | collective-permute-done | bytes 65568 | tf_op jit(solution)/shard_map/ppermute | solution.py:299
  56.1 0.1 collective-permute-start.20
  56.2 1.2 %collective-permute-done.20.other_ref = bf16[8,2048]{1,0:T(8,128)(2,1)S(1)} collective-permute-done((bf16[8,2048]{1,0:T(8,128)(2,1)S(1)}, bf16[8,2048]{1,0:T(8,128)(2,1)S(1)}, u32[]{:S(2)}, u32[]{:S(2)}) %collective-permute-start.20) | collective-permute-done | bytes 32800 | tf_op jit(solution)/shard_map/ppermute | solution.py:299
  57.3 0.7 %shard_map.80 = (bf16[8,2048]{1,0:T(8,128)(2,1)}, bf16[8,2048]{1,0:T(8,128)(2,1)}) custom-call(bf16[8,2048]{1,0:T(8,128)(2,1)S(1)} %get-tuple-element.82.mine_ref, bf16[8,2048]{1,0:T(8,128)(2,1)S(1)} %collective-permute-done.20.other_ref), custom_call_target="tpu_custom_call" | custom-call | tf_op jit(solution)/shard_map/pallas_call | solution.py:249
  (24 shorter events, 0.3 us)
Async XLA Ops:
  0.6 1.6 %collective-permute-start = (bf16[8,2048]{1,0:T(8,128)(2,1)}, bf16[8,2048]{1,0:T(8,128)(2,1)S(1)}, u32[]{:S(2)}, u32[]{:S(2)}) collective-permute-start(bf16[8,2048]{1,0:T(8,128)(2,1)} %param.5), channel_id=1, source_target_pairs={{0,2},{2,0},{4,6},{6,4},{8,10},{10,8},{12,14},{14,12},{16,18},{18,... | collective-permute-start | bytes 98312 | tf_op jit(solution)/shard_map/ppermute | solution.py:299
  1.1 1.4 %collective-permute-start.1 = (bf16[8,2048]{1,0:T(8,128)(2,1)}, bf16[8,2048]{1,0:T(8,128)(2,1)S(1)}, u32[]{:S(2)}, u32[]{:S(2)}) collective-permute-start(bf16[8,2048]{1,0:T(8,128)(2,1)} %param.6), channel_id=1, source_target_pairs={{0,2},{2,0},{4,6},{6,4},{8,10},{10,8},{12,14},{14,12},{16,18},{18,... | collective-permute-start | bytes 98312 | tf_op jit(solution)/shard_map/ppermute | solution.py:299
  2.6 10.8 %collective-permute-start.6 = (bf16[16,2048]{1,0:T(8,128)(2,1)S(1)}, bf16[16,2048]{1,0:T(8,128)(2,1)S(1)}, u32[]{:S(2)}, u32[]{:S(2)}) collective-permute-start(bf16[16,2048]{1,0:T(8,128)(2,1)S(1)} %maximum_maximum_fusion), channel_id=1, source_target_pairs={{0,24},{2,26},{4,28},{6,30},{8,16},{10,18},{12,20},{14,22},{16,8},... | collective-permute-start | bytes 196616 | tf_op jit(solution)/shard_map/ppermute | solution.py:299
  7.4 6.0 %collective-permute-start.5 = (bf16[16,2048]{1,0:T(8,128)(2,1)S(1)}, bf16[16,2048]{1,0:T(8,128)(2,1)S(1)}, u32[]{:S(2)}, u32[]{:S(2)}) collective-permute-start(bf16[16,2048]{1,0:T(8,128)(2,1)S(1)} %maximum_maximum_fusion), channel_id=1, source_target_pairs={{0,16},{2,18},{4,20},{6,22},{8,24},{10,26},{12,28},{14,30},{16,0},... | collective-permute-start | bytes 196616 | tf_op jit(solution)/shard_map/ppermute | solution.py:299
  7.4 4.7 %collective-permute-start.4 = (bf16[16,2048]{1,0:T(8,128)(2,1)S(1)}, bf16[16,2048]{1,0:T(8,128)(2,1)S(1)}, u32[]{:S(2)}, u32[]{:S(2)}) collective-permute-start(bf16[16,2048]{1,0:T(8,128)(2,1)S(1)} %maximum_maximum_fusion), channel_id=1, source_target_pairs={{0,8},{2,10},{4,12},{6,14},{8,0},{10,2},{12,4},{14,6},{16,24},{18,... | collective-permute-start | bytes 196616 | tf_op jit(solution)/shard_map/ppermute | solution.py:299
  9.7 12.6 %collective-permute-start.2 = (bf16[256,2048]{1,0:T(8,128)(2,1)S(1)}, bf16[256,2048]{1,0:T(8,128)(2,1)S(1)}, u32[]{:S(2)}, u32[]{:S(2)}) collective-permute-start(bf16[256,2048]{1,0:T(8,128)(2,1)S(1)} %get-tuple-element.43), channel_id=1, source_target_pairs={{0,2},{2,0},{4,6},{6,4},{8,10},{10,8},{12,14},{14,12},{16,18},{18,... | collective-permute-start | bytes 3145736 | tf_op jit(solution)/shard_map/ppermute | solution.py:299
  9.7 12.5 %collective-permute-start.3 = (bf16[256,2048]{1,0:T(8,128)(2,1)S(1)}, bf16[256,2048]{1,0:T(8,128)(2,1)S(1)}, u32[]{:S(2)}, u32[]{:S(2)}) collective-permute-start(bf16[256,2048]{1,0:T(8,128)(2,1)S(1)} %get-tuple-element.44), channel_id=1, source_target_pairs={{0,2},{2,0},{4,6},{6,4},{8,10},{10,8},{12,14},{14,12},{16,18},{18,... | collective-permute-start | bytes 3145736 | tf_op jit(solution)/shard_map/ppermute | solution.py:299
  13.4 5.2 %collective-permute-start.7 = (bf16[64,1024]{1,0:T(8,128)(2,1)S(1)}, bf16[64,1024]{1,0:T(8,128)(2,1)S(1)}, u32[]{:S(2)}, u32[]{:S(2)}) collective-permute-start(bf16[64,1024]{1,0:T(8,128)(2,1)S(1)} %pad_maximum_fusion), channel_id=1, source_target_pairs={{0,4},{2,6},{4,0},{6,2},{8,12},{10,14},{12,8},{14,10},{16,20},{18,... | collective-permute-start | bytes 393224 | tf_op jit(solution)/shard_map/ppermute | solution.py:299
  15.0 5.0 %collective-permute-start.8 = (bf16[64,1024]{1,0:T(8,128)(2,1)S(1)}, bf16[64,1024]{1,0:T(8,128)(2,1)S(1)}, u32[]{:S(2)}, u32[]{:S(2)}) collective-permute-start(bf16[64,1024]{1,0:T(8,128)(2,1)S(1)} %pad_maximum_fusion.1), channel_id=1, source_target_pairs={{0,1},{1,0},{2,3},{3,2},{4,5},{5,4},{6,7},{7,6},{8,9},{9,8},{10,11... | collective-permute-start | bytes 393224 | tf_op jit(solution)/shard_map/ppermute | solution.py:299
  20.1 6.8 %collective-permute-start.10 = (bf16[128,1024]{1,0:T(8,128)(2,1)S(1)}, bf16[128,1024]{1,0:T(8,128)(2,1)S(1)}, u32[]{:S(2)}, u32[]{:S(2)}) collective-permute-start(bf16[128,1024]{1,0:T(8,128)(2,1)S(1)} %constant_dynamic-update-slice_fusion.5.refs_1_), channel_id=1, source_target_pairs={{0,4},{2,6},{4,0},{6,2},{8,12},{10,14},{12,8},{14,10},{16,20},{18,... | collective-permute-start | bytes 786440 | tf_op jit(solution)/shard_map/ppermute | solution.py:299
  20.7 6.6 %collective-permute-start.9 = (bf16[128,1024]{1,0:T(8,128)(2,1)S(1)}, bf16[128,1024]{1,0:T(8,128)(2,1)S(1)}, u32[]{:S(2)}, u32[]{:S(2)}) collective-permute-start(bf16[128,1024]{1,0:T(8,128)(2,1)S(1)} %constant_dynamic-update-slice_fusion.refs_0_), channel_id=1, source_target_pairs={{0,1},{1,0},{2,3},{3,2},{4,5},{5,4},{6,7},{7,6},{8,9},{9,8},{10,11... | collective-permute-start | bytes 786440 | tf_op jit(solution)/shard_map/ppermute | solution.py:299
  31.9 9.1 %collective-permute-start.11 = (bf16[128,1024]{1,0:T(8,128)(2,1)S(1)}, bf16[128,1024]{1,0:T(8,128)(2,1)S(1)}, u32[]{:S(2)}, u32[]{:S(2)}) collective-permute-start(bf16[128,1024]{1,0:T(8,128)(2,1)S(1)} %get-tuple-element.51), channel_id=1, source_target_pairs={{0,1},{1,0},{2,3},{3,2},{4,5},{5,4},{6,7},{7,6},{8,9},{9,8},{10,11... | collective-permute-start | bytes 786440 | tf_op jit(solution)/shard_map/ppermute | solution.py:299
  33.4 7.5 %collective-permute-start.12 = (bf16[128,1024]{1,0:T(8,128)(2,1)S(1)}, bf16[128,1024]{1,0:T(8,128)(2,1)S(1)}, u32[]{:S(2)}, u32[]{:S(2)}) collective-permute-start(bf16[128,1024]{1,0:T(8,128)(2,1)S(1)} %get-tuple-element.53), channel_id=1, source_target_pairs={{0,4},{2,6},{4,0},{6,2},{8,12},{10,14},{12,8},{14,10},{16,20},{18,... | collective-permute-start | bytes 786440 | tf_op jit(solution)/shard_map/ppermute | solution.py:299
  41.1 6.5 %collective-permute-start.15 = (bf16[256,2048]{1,0:T(8,128)(2,1)S(1)}, bf16[256,2048]{1,0:T(8,128)(2,1)S(1)}, u32[]{:S(2)}, u32[]{:S(2)}) collective-permute-start(bf16[256,2048]{1,0:T(8,128)(2,1)S(1)} %get-tuple-element.61), channel_id=1, source_target_pairs={{0,2},{2,0},{4,6},{6,4},{8,10},{10,8},{12,14},{14,12},{16,18},{18,... | collective-permute-start | bytes 3145736 | tf_op jit(solution)/shard_map/ppermute | solution.py:299
  41.1 6.4 %collective-permute-start.16 = (bf16[256,2048]{1,0:T(8,128)(2,1)S(1)}, bf16[256,2048]{1,0:T(8,128)(2,1)S(1)}, u32[]{:S(2)}, u32[]{:S(2)}) collective-permute-start(bf16[256,2048]{1,0:T(8,128)(2,1)S(1)} %get-tuple-element.62), channel_id=1, source_target_pairs={{0,2},{2,0},{4,6},{6,4},{8,10},{10,8},{12,14},{14,12},{16,18},{18,... | collective-permute-start | bytes 3145736 | tf_op jit(solution)/shard_map/ppermute | solution.py:299
  41.7 5.5 %collective-permute-start.14 = (bf16[64,1024]{1,0:T(8,128)(2,1)S(1)}, bf16[64,1024]{1,0:T(8,128)(2,1)S(1)}, u32[]{:S(2)}, u32[]{:S(2)}) collective-permute-start(bf16[64,1024]{1,0:T(8,128)(2,1)S(1)} %slice.135), channel_id=1, source_target_pairs={{0,1},{1,0},{2,3},{3,2},{4,5},{5,4},{6,7},{7,6},{8,9},{9,8},{10,11... | collective-permute-start | bytes 393224 | tf_op jit(solution)/shard_map/ppermute | solution.py:299
  42.2 5.3 %collective-permute-start.13 = (bf16[64,1024]{1,0:T(8,128)(2,1)S(1)}, bf16[64,1024]{1,0:T(8,128)(2,1)S(1)}, u32[]{:S(2)}, u32[]{:S(2)}) collective-permute-start(bf16[64,1024]{1,0:T(8,128)(2,1)S(1)} %slice.136), channel_id=1, source_target_pairs={{0,4},{2,6},{4,0},{6,2},{8,12},{10,14},{12,8},{14,10},{16,20},{18,... | collective-permute-start | bytes 393224 | tf_op jit(solution)/shard_map/ppermute | solution.py:299
  47.7 6.6 %collective-permute-start.19 = (bf16[16,2048]{1,0:T(8,128)(2,1)S(1)}, bf16[16,2048]{1,0:T(8,128)(2,1)S(1)}, u32[]{:S(2)}, u32[]{:S(2)}) collective-permute-start(bf16[16,2048]{1,0:T(8,128)(2,1)S(1)} %get-tuple-element.78), channel_id=1, source_target_pairs={{0,24},{2,26},{4,28},{6,30},{8,16},{10,18},{12,20},{14,22},{16,8},... | collective-permute-start | bytes 196616 | tf_op jit(solution)/shard_map/ppermute | solution.py:299
  50.1 5.9 %collective-permute-start.18 = (bf16[16,2048]{1,0:T(8,128)(2,1)S(1)}, bf16[16,2048]{1,0:T(8,128)(2,1)S(1)}, u32[]{:S(2)}, u32[]{:S(2)}) collective-permute-start(bf16[16,2048]{1,0:T(8,128)(2,1)S(1)} %get-tuple-element.79), channel_id=1, source_target_pairs={{0,16},{2,18},{4,20},{6,22},{8,24},{10,26},{12,28},{14,30},{16,0},... | collective-permute-start | bytes 196616 | tf_op jit(solution)/shard_map/ppermute | solution.py:299
  50.3 5.7 %collective-permute-start.17 = (bf16[16,2048]{1,0:T(8,128)(2,1)S(1)}, bf16[16,2048]{1,0:T(8,128)(2,1)S(1)}, u32[]{:S(2)}, u32[]{:S(2)}) collective-permute-start(bf16[16,2048]{1,0:T(8,128)(2,1)S(1)} %get-tuple-element.80), channel_id=1, source_target_pairs={{0,8},{2,10},{4,12},{6,14},{8,0},{10,2},{12,4},{14,6},{16,24},{18,... | collective-permute-start | bytes 196616 | tf_op jit(solution)/shard_map/ppermute | solution.py:299
  56.1 1.3 %collective-permute-start.20 = (bf16[8,2048]{1,0:T(8,128)(2,1)S(1)}, bf16[8,2048]{1,0:T(8,128)(2,1)S(1)}, u32[]{:S(2)}, u32[]{:S(2)}) collective-permute-start(bf16[8,2048]{1,0:T(8,128)(2,1)S(1)} %get-tuple-element.81), channel_id=1, source_target_pairs={{0,2},{2,0},{4,6},{6,4},{8,10},{10,8},{12,14},{14,12},{16,18},{18,... | collective-permute-start | bytes 98312 | tf_op jit(solution)/shard_map/ppermute | solution.py:299

commit v11 on v10

--- a/solution.py
+++ b/solution.py
@@ -41,7 +41,7 @@
     used = sorted({block for block, *_ in groups})
     memory_refs, refs = refs[:n_memory], refs[n_memory:]
     token_buf, result_buf, raw_ref, prob_ref, grad_ref, weight_ref, sems = refs[-7:]
-    n_terms = max([1 + t for *_, terms in groups for t in terms], default=0)
+    n_terms = max([1 + t for *_, terms in groups for t in terms if t is not None], default=0)
     term_refs, refs = refs[len(refs) - 7 - n_terms : -7], refs[: len(refs) - 7 - n_terms]
     if with_outputs:
         attended_ref, query_grad_ref, *sent_refs = refs[-2 - len(used) :]
@@ -123,9 +123,14 @@
 
             def gradients(n):
                 for m, pair_ref in enumerate((grad_ref, weight_ref) if terms else ()):
-                    term = dot(pair_ref[n], tokens(m, n), NN)
+                    if None not in terms:
+                        whole = dot(pair_ref[n], tokens(m, n), NN)
                     for i, t in enumerate(terms):
-                        term_refs[t][rows, targets[m][n]] = term[i * size : (i + 1) * size].astype(term_refs[t].dtype)
+                        if t is None:
+                            continue
+                        part = slice(i * size, (i + 1) * size)
+                        term = dot(pair_ref[n, part], tokens(m, n), NN) if None in terms else whole[part]
+                        term_refs[t][rows, targets[m][n]] = term.astype(term_refs[t].dtype)
 
             for copy in inputs(k):
                 copy.wait()
@@ -334,19 +339,26 @@
     outputs, sent, (first_keep,) = attention(
         n_mp, blocks, [(0, 0, half, (0,), (0,))], tokens, [first], [f32], [], {}
     )
-    rest = [(0, half, n_mp - half, (0,), (0,)), (1, 0, n_mp, (1, 2), (1, 2))]
     first_keep, second = together(first_keep, second)
-    memory = [first_got, second, second_got]
-    *_, (first_give, second_keep, second_give) = attention(
-        n_mp, blocks, rest, tokens, memory, [bf16, f32, bf16], None, {}
-    )
-    outputs, sent, _ = attention(
-        n_mp, blocks, [(*group[:4], ()) for group in rest], tokens, memory, [], outputs, sent
-    )
-    first_got, second_got = swap(first_give, "mp", y_bits[-1]), swap(second_give, "seq", x_bit)
-    first, second, sent = together(
-        first_keep + first_got.astype(f32), second_keep + second_got.astype(f32), sent
-    )
+    of_first = (0, half, n_mp - half, (0,))
+    *_, (first_give, second_give) = attention(
+        n_mp,
+        blocks,
+        [(*of_first, (0,)), (1, 0, n_mp, (1, 2), (None, 1))],
+        tokens,
+        [first_got, second, second_got],
+        [bf16, bf16],
+        None,
+        {},
+    )
+    outputs, sent, (second_keep,) = attention(
+        n_mp, blocks, [(1, 0, n_mp, (0, 1), (0, None))], tokens, [second, second_got], [f32], outputs, sent
+    )
+    first_terms, second_terms = swap(first_give, "mp", y_bits[-1]), swap(second_give, "seq", x_bit)
+    first, second, sent[1], first_got = together(
+        first_keep + first_terms.astype(f32), second_keep + second_terms.astype(f32), sent[1], first_got
+    )
+    outputs, sent, _ = attention(n_mp, blocks, [(*of_first, ())], tokens, [first_got], [], outputs, sent)
 
     def fold(total, axis, bits):
         middle = total.shape[0] // 2
@@ -357,8 +369,8 @@
     for bits in y_bits[:0:-1]:
         second = fold(second, "mp", bits)
     first, second = fold(first, "seq", x_bit), fold(second, "mp", y_bits[0])
-    returned = [swap(sent[block], "seq", core_bit) for block in range(blocks)]
-    first, second, returned = together(first, second, returned)
+    first, second, sent[0], returned = together(first, second, sent[0], swap(sent[1], "seq", core_bit))
+    returned = [swap(sent[0], "seq", core_bit), returned]
     total = jnp.concatenate([first, second], axis=1)
     outputs = placing(n_mp, returned, *outputs)
     count, give = 2 * rows, total.astype(bf16)

time: 58.3 us -> 59.3 us (1.017)
  Pallas kernels: 17.4 us -> 19.3 us
  starting transfers between devices: 21.3 us -> 20 us
    pallas_call x3 -> x4, Pallas kernels: 13.8 us -> 15.6 us  [attention(): pl.pallas_call(functools.partial(attention_kernel, n_mp, blocks, groups,...]
    ppermute x21, starting transfers between devices: 21.3 us -> 20 us  [swap(): return lax.ppermute(array, axis, [(i, i ^ bits) for i in range(size)])]
  transfers between devices with their start and end apart: 21 -> 21, of which waited for: 13 -> 15; matrix products, arithmetic and copies ran while one was open for 2% -> 2% of each run, Pallas kernels for 21% -> 24%
where the time goes in v11:
time: 59.3 us; the launch traced here: 59 us
  starting transfers between devices  20 us (34%)
  Pallas kernels  19.3 us (33%)
  waiting for transfers between devices  17.7 us (30%)
  local copies, waits for them, and re-layouts  0.9 us (2%)
  between operations  0.86 us (1%)
    ppermute x21, starting transfers between devices, swap(): return lax.ppermute(array, axis, [(i, i ^ bits) for i in range(size)])  20 us
    ppermute x21, waiting for transfers between devices, swap(): return lax.ppermute(array, axis, [(i, i ^ bits) for i in range(size)])  17.7 us
    pallas_call x4, Pallas kernels, attention(): pl.pallas_call(functools.partial(attention_kernel, n_mp, blocks, groups,...  15.6 us
    pallas_call x1, Pallas kernels, packing(): pl.pallas_call(functools.partial(packing_kernel, n_mp, blocks), in_specs=...  1.58 us
    pallas_call x1, Pallas kernels, placing(): pl.pallas_call(functools.partial(placing_kernel, n_mp, blocks), in_specs=...  1.37 us
  transfers between devices with their start and end apart: 21, of which 15 were waited for; matrix products, arithmetic and copies ran while one was open for 2% of the time, Pallas kernels for 24%

profile of v11, /device:TPU:0, one launch (start us, length us, event | category | flops | bytes accessed | tf_op | source)
XLA Modules:
  0.0 59.0 jit_solution(6565006022287149117)
XLA Ops:
  0.6 0.5 collective-permute-start.1
  1.1 0.1 collective-permute-start
  1.2 0.7 %constant_dynamic-slice_fusion.2 = (bf16[8,512]{1,0:T(8,128)(2,1)S(1)}, bf16[8,512]{1,0:T(8,128)(2,1)S(1)}, bf16[8,512]{1,0:T(8,128)(2,1)S(1)}, bf16[8,512]{1,0:T(8,128)(2,1)S(1)}) fusion(bf16[8,2048]{1,0:T(8,128)(2,1)} %param.6, s32[]{:T(128)S(6)} %select_n.2, s32[]{:T(128)S(6)} %add.35, bf16[8,2048]{1,0:T(8,128)(2,1)} %param.5), kind=kLoop, calls=%fused_computation.25 | loop fusion | bytes 65544 | tf_op jit(solution)/shard_map/slice | solution.py:316
  2.0 0.2 collective-permute-done.1
  2.2 0.3 collective-permute-done
  2.6 2.8 %collective-permute-start.4 = (bf16[16,2048]{1,0:T(8,128)(2,1)S(1)}, bf16[16,2048]{1,0:T(8,128)(2,1)S(1)}, u32[]{:S(2)}, u32[]{:S(2)}) collective-permute-start(bf16[16,2048]{1,0:T(8,128)(2,1)S(1)} %maximum_maximum_fusion), channel_id=1, source_target_pairs={{0,8},{2,10},{4,12},{6,14},{8,0},{10,2},{12,4},{14,6},{16,24},{18,... | collective-permute-start | bytes 196616 | tf_op jit(solution)/shard_map/ppermute | solution.py:304
  5.4 2.7 %collective-permute-start.5 = (bf16[16,2048]{1,0:T(8,128)(2,1)S(1)}, bf16[16,2048]{1,0:T(8,128)(2,1)S(1)}, u32[]{:S(2)}, u32[]{:S(2)}) collective-permute-start(bf16[16,2048]{1,0:T(8,128)(2,1)S(1)} %maximum_maximum_fusion), channel_id=1, source_target_pairs={{0,16},{2,18},{4,20},{6,22},{8,24},{10,26},{12,28},{14,30},{16,0},... | collective-permute-start | bytes 196616 | tf_op jit(solution)/shard_map/ppermute | solution.py:304
  8.0 1.6 %shard_map.75 = (bf16[256,2048]{1,0:T(8,128)(2,1)S(1)}, bf16[256,2048]{1,0:T(8,128)(2,1)S(1)}) custom-call(bf16[256,4096]{1,0:T(8,128)(2,1)} %q_ref.8, bf16[256,4096]{1,0:T(8,128)(2,1)} %g_ref.8), custom_call_target="tpu_custom_call" | custom-call | bytes 4194304 | tf_op jit(solution)/shard_map/pallas_call | solution.py:227
  9.6 0.1 collective-permute-start.2
  9.7 0.5 collective-permute-start.3
  10.2 0.0 collective-permute-done.4
  10.2 2.8 %collective-permute-done.5 = bf16[16,2048]{1,0:T(8,128)(2,1)S(1)} collective-permute-done((bf16[16,2048]{1,0:T(8,128)(2,1)S(1)}, bf16[16,2048]{1,0:T(8,128)(2,1)S(1)}, u32[]{:S(2)}, u32[]{:S(2)}) %collective-permute-start.5) | collective-permute-done | bytes 65568 | tf_op jit(solution)/shard_map/ppermute | solution.py:304
  13.1 1.1 %collective-permute-done.6 = bf16[16,2048]{1,0:T(8,128)(2,1)S(1)} collective-permute-done((bf16[16,2048]{1,0:T(8,128)(2,1)S(1)}, bf16[16,2048]{1,0:T(8,128)(2,1)S(1)}, u32[]{:S(2)}, u32[]{:S(2)}) %collective-permute-start.6) | collective-permute-done | bytes 65568 | tf_op jit(solution)/shard_map/ppermute | solution.py:304
  14.2 1.6 %collective-permute-start.7 = (bf16[64,1024]{1,0:T(8,128)(2,1)S(1)}, bf16[64,1024]{1,0:T(8,128)(2,1)S(1)}, u32[]{:S(2)}, u32[]{:S(2)}) collective-permute-start(bf16[64,1024]{1,0:T(8,128)(2,1)S(1)} %pad_maximum_fusion), channel_id=1, source_target_pairs={{0,4},{2,6},{4,0},{6,2},{8,12},{10,14},{12,8},{14,10},{16,20},{18,... | collective-permute-start | bytes 393224 | tf_op jit(solution)/shard_map/ppermute | solution.py:304
  15.8 1.6 %collective-permute-start.8 = (bf16[64,1024]{1,0:T(8,128)(2,1)S(1)}, bf16[64,1024]{1,0:T(8,128)(2,1)S(1)}, u32[]{:S(2)}, u32[]{:S(2)}) collective-permute-start(bf16[64,1024]{1,0:T(8,128)(2,1)S(1)} %pad_maximum_fusion.1), channel_id=1, source_target_pairs={{0,1},{1,0},{2,3},{3,2},{4,5},{5,4},{6,7},{7,6},{8,9},{9,8},{10,11... | collective-permute-start | bytes 393224 | tf_op jit(solution)/shard_map/ppermute | solution.py:304
  17.3 1.9 %collective-permute-done.7 = bf16[64,1024]{1,0:T(8,128)(2,1)S(1)} collective-permute-done((bf16[64,1024]{1,0:T(8,128)(2,1)S(1)}, bf16[64,1024]{1,0:T(8,128)(2,1)S(1)}, u32[]{:S(2)}, u32[]{:S(2)}) %collective-permute-start.7) | collective-permute-done | bytes 131104 | tf_op jit(solution)/shard_map/ppermute | solution.py:304
  19.2 1.6 %collective-permute-done.8 = bf16[64,1024]{1,0:T(8,128)(2,1)S(1)} collective-permute-done((bf16[64,1024]{1,0:T(8,128)(2,1)S(1)}, bf16[64,1024]{1,0:T(8,128)(2,1)S(1)}, u32[]{:S(2)}, u32[]{:S(2)}) %collective-permute-start.8) | collective-permute-done | bytes 131104 | tf_op jit(solution)/shard_map/ppermute | solution.py:304
  20.8 1.6 %collective-permute-start.9 = (bf16[128,1024]{1,0:T(8,128)(2,1)S(1)}, bf16[128,1024]{1,0:T(8,128)(2,1)S(1)}, u32[]{:S(2)}, u32[]{:S(2)}) collective-permute-start(bf16[128,1024]{1,0:T(8,128)(2,1)S(1)} %constant_dynamic-update-slice_fusion.refs_0_), channel_id=1, source_target_pairs={{0,1},{1,0},{2,3},{3,2},{4,5},{5,4},{6,7},{7,6},{8,9},{9,8},{10,11... | collective-permute-start | bytes 786440 | tf_op jit(solution)/shard_map/ppermute | solution.py:304
  22.4 0.6 %collective-permute-start.10 = (bf16[128,1024]{1,0:T(8,128)(2,1)S(1)}, bf16[128,1024]{1,0:T(8,128)(2,1)S(1)}, u32[]{:S(2)}, u32[]{:S(2)}) collective-permute-start(bf16[128,1024]{1,0:T(8,128)(2,1)S(1)} %constant_dynamic-update-slice_fusion.5.refs_1_.refs_0_), channel_id=1, source_target_pairs={{0,4},{2,6},{4,0},{6,2},{8,12},{10,14},{12,8},{14,10},{16,20},{18,... | collective-permute-start | bytes 786440 | tf_op jit(solution)/shard_map/ppermute | solution.py:304
  23.0 3.2 %shard_map.76 = (bf16[256,4096]{1,0:T(8,128)(2,1)}, bf16[256,4096]{1,0:T(8,128)(2,1)}, bf16[256,2048]{1,0:T(8,128)(2,1)S(1)}, f32[128,1024]{1,0:T(8,128)S(1)}) custom-call(bf16[256,4096]{1,0:T(8,128)(2,1)} %q_ref.8, bf16[256,4096]{1,0:T(8,128)(2,1)} %g_ref.8, bf16[256,2048]{1,0:T(8,128)(2,1)S(1)} %collective-permute-done.2.sq_ref, ...), custom_call_target="tpu_custom_call" | custom-call | flops 402653184 | bytes 2097152 | tf_op jit(solution)/shard_map/pallas_call | solution.py:183
  26.2 1.0 %collective-permute-done.9.refs_0_ = bf16[128,1024]{1,0:T(8,128)(2,1)S(1)} collective-permute-done((bf16[128,1024]{1,0:T(8,128)(2,1)S(1)}, bf16[128,1024]{1,0:T(8,128)(2,1)S(1)}, u32[]{:S(2)}, u32[]{:S(2)}) %collective-permute-start.9) | collective-permute-done | bytes 262176 | tf_op jit(solution)/shard_map/ppermute | solution.py:304
  27.2 1.6 %collective-permute-done.10.refs_2_.refs_1_ = bf16[128,1024]{1,0:T(8,128)(2,1)S(1)} collective-permute-done((bf16[128,1024]{1,0:T(8,128)(2,1)S(1)}, bf16[128,1024]{1,0:T(8,128)(2,1)S(1)}, u32[]{:S(2)}, u32[]{:S(2)}) %collective-permute-start.10) | collective-permute-done | bytes 262176 | tf_op jit(solution)/shard_map/ppermute | solution.py:304
  28.8 4.5 %shard_map.77 = (bf16[128,1024]{1,0:T(8,128)(2,1)S(1)}, bf16[128,1024]{1,0:T(8,128)(2,1)S(1)}) custom-call(bf16[256,4096]{1,0:T(8,128)(2,1)} %q_ref.8, bf16[256,4096]{1,0:T(8,128)(2,1)} %g_ref.8, bf16[256,2048]{1,0:T(8,128)(2,1)S(1)} %collective-permute-done.2.sq_ref, bf16[256,2048]{1,0:T(8,128)(2,1)S(1)} %collective-permute-done.3.sg_ref, ...), custom_call_target="tpu_custom_call" | custom-call | flops 1207959552 | bytes 6291456 | tf_op jit(solution)/shard_map/pallas_call | solution.py:183
  33.4 0.6 collective-permute-start.11
  34.0 0.6 collective-permute-start.12
  34.5 4.8 %shard_map.78 = (bf16[256,4096]{1,0:T(8,128)(2,1)}, bf16[256,4096]{1,0:T(8,128)(2,1)}, bf16[256,2048]{1,0:T(8,128)(2,1)S(1)}, f32[128,1024]{1,0:T(8,128)S(1)}) custom-call(bf16[256,4096]{1,0:T(8,128)(2,1)} %q_ref.8, bf16[256,4096]{1,0:T(8,128)(2,1)} %g_ref.8, ...), custom_call_target="tpu_custom_call", output_to_operand_aliasing={{0}: (6, {}), {1}: (7, {})} | custom-call | flops 805306368 | bytes 4194304 | tf_op jit(solution)/shard_map/pallas_call | solution.py:183
  39.3 0.5 collective-permute-done.11
  39.8 0.1 convert_add_fusion.1
  39.9 0.4 collective-permute-done.12
  40.3 0.1 convert_add_fusion
  40.4 0.1 collective-permute-start.15
  40.5 0.6 %collective-permute-start.13 = (bf16[64,1024]{1,0:T(8,128)(2,1)S(1)}, bf16[64,1024]{1,0:T(8,128)(2,1)S(1)}, u32[]{:S(2)}, u32[]{:S(2)}) collective-permute-start(bf16[64,1024]{1,0:T(8,128)(2,1)S(1)} %slice.136), channel_id=1, source_target_pairs={{0,4},{2,6},{4,0},{6,2},{8,12},{10,14},{12,8},{14,10},{16,20},{18,... | collective-permute-start | bytes 393224 | tf_op jit(solution)/shard_map/ppermute | solution.py:304
  41.1 1.6 %collective-permute-start.14 = (bf16[64,1024]{1,0:T(8,128)(2,1)S(1)}, bf16[64,1024]{1,0:T(8,128)(2,1)S(1)}, u32[]{:S(2)}, u32[]{:S(2)}) collective-permute-start(bf16[64,1024]{1,0:T(8,128)(2,1)S(1)} %slice.135), channel_id=1, source_target_pairs={{0,1},{1,0},{2,3},{3,2},{4,5},{5,4},{6,7},{7,6},{8,9},{9,8},{10,11... | collective-permute-start | bytes 393224 | tf_op jit(solution)/shard_map/ppermute | solution.py:304
  42.7 3.1 %shard_map.79 = (bf16[256,4096]{1,0:T(8,128)(2,1)}, bf16[256,4096]{1,0:T(8,128)(2,1)}, bf16[256,2048]{1,0:T(8,128)(2,1)S(1)}) custom-call(bf16[256,4096]{1,0:T(8,128)(2,1)} %q_ref.8, bf16[256,4096]{1,0:T(8,128)(2,1)} %g_ref.8, bf16[256,2048]{1,0:T(8,128)(2,1)S(1)} %collective-permute-done.2.sq_ref, ...), custom_call_target="tpu_custom_call", output_to_operand_aliasing={{0}: (5, {}), {1}: (6, {}), {2}: (7, {})} | custom-call | flops 402653184 | bytes 2097152 | tf_op jit(solution)/shard_map/pallas_call | solution.py:183
  45.9 0.6 collective-permute-done.13
  46.5 0.3 collective-permute-done.14
  46.9 0.1 collective-permute-start.19
  47.1 1.2 %collective-permute-start.16 = (bf16[16,2048]{1,0:T(8,128)(2,1)S(1)}, bf16[16,2048]{1,0:T(8,128)(2,1)S(1)}, u32[]{:S(2)}, u32[]{:S(2)}) collective-permute-start(bf16[16,2048]{1,0:T(8,128)(2,1)S(1)} %get-tuple-element.84), channel_id=1, source_target_pairs={{0,8},{2,10},{4,12},{6,14},{8,0},{10,2},{12,4},{14,6},{16,24},{18,... | collective-permute-start | bytes 196616 | tf_op jit(solution)/shard_map/ppermute | solution.py:304
  48.2 2.6 %collective-permute-start.17 = (bf16[16,2048]{1,0:T(8,128)(2,1)S(1)}, bf16[16,2048]{1,0:T(8,128)(2,1)S(1)}, u32[]{:S(2)}, u32[]{:S(2)}) collective-permute-start(bf16[16,2048]{1,0:T(8,128)(2,1)S(1)} %get-tuple-element.83), channel_id=1, source_target_pairs={{0,16},{2,18},{4,20},{6,22},{8,24},{10,26},{12,28},{14,30},{16,0},... | collective-permute-start | bytes 196616 | tf_op jit(solution)/shard_map/ppermute | solution.py:304
  50.9 0.7 %collective-permute-start.18 = (bf16[16,2048]{1,0:T(8,128)(2,1)S(1)}, bf16[16,2048]{1,0:T(8,128)(2,1)S(1)}, u32[]{:S(2)}, u32[]{:S(2)}) collective-permute-start(bf16[16,2048]{1,0:T(8,128)(2,1)S(1)} %get-tuple-element.82), channel_id=1, source_target_pairs={{0,24},{2,26},{4,28},{6,30},{8,16},{10,18},{12,20},{14,22},{16,8},... | collective-permute-start | bytes 196616 | tf_op jit(solution)/shard_map/ppermute | solution.py:304
  51.5 0.0 collective-permute-done.19.refs_0_
  51.5 1.4 %shard_map.80 = (bf16[256,4096]{1,0:T(8,128)(2,1)}, bf16[256,4096]{1,0:T(8,128)(2,1)}) custom-call(bf16[256,2048]{1,0:T(8,128)(2,1)S(1)} %collective-permute-done.19.refs_0_, bf16[256,2048]{1,0:T(8,128)(2,1)S(1)} %collective-permute-done.15.refs_1_, bf16[256,4096]{1,0:T(8,128)(2,1)} %get-tuple-element.71.refs_2_, ...), custom_call_target="tpu_custom_call", output_to_operand_aliasing={{0}: (2, {}), {1}: (3, {})} | custom-call | tf_op jit(solution)/shard_map/pallas_call | solution.py:287
  52.9 0.0 collective-permute-done.16
  52.9 2.4 %collective-permute-done.17 = bf16[16,2048]{1,0:T(8,128)(2,1)S(1)} collective-permute-done((bf16[16,2048]{1,0:T(8,128)(2,1)S(1)}, bf16[16,2048]{1,0:T(8,128)(2,1)S(1)}, u32[]{:S(2)}, u32[]{:S(2)}) %collective-permute-start.17) | collective-permute-done | bytes 65568 | tf_op jit(solution)/shard_map/ppermute | solution.py:304
  55.3 1.7 %collective-permute-done.18 = bf16[16,2048]{1,0:T(8,128)(2,1)S(1)} collective-permute-done((bf16[16,2048]{1,0:T(8,128)(2,1)S(1)}, bf16[16,2048]{1,0:T(8,128)(2,1)S(1)}, u32[]{:S(2)}, u32[]{:S(2)}) %collective-permute-start.18) | collective-permute-done | bytes 65568 | tf_op jit(solution)/shard_map/ppermute | solution.py:304
  57.0 0.1 collective-permute-start.20
  57.1 1.2 %collective-permute-done.20.other_ref = bf16[8,2048]{1,0:T(8,128)(2,1)S(1)} collective-permute-done((bf16[8,2048]{1,0:T(8,128)(2,1)S(1)}, bf16[8,2048]{1,0:T(8,128)(2,1)S(1)}, u32[]{:S(2)}, u32[]{:S(2)}) %collective-permute-start.20) | collective-permute-done | bytes 32800 | tf_op jit(solution)/shard_map/ppermute | solution.py:304
  58.3 0.7 %shard_map.81 = (bf16[8,2048]{1,0:T(8,128)(2,1)}, bf16[8,2048]{1,0:T(8,128)(2,1)}) custom-call(bf16[8,2048]{1,0:T(8,128)(2,1)S(1)} %get-tuple-element.86.mine_ref, bf16[8,2048]{1,0:T(8,128)(2,1)S(1)} %collective-permute-done.20.other_ref), custom_call_target="tpu_custom_call" | custom-call | tf_op jit(solution)/shard_map/pallas_call | solution.py:254
  (25 shorter events, 0.3 us)
Async XLA Ops:
  0.6 1.6 %collective-permute-start.1 = (bf16[8,2048]{1,0:T(8,128)(2,1)}, bf16[8,2048]{1,0:T(8,128)(2,1)S(1)}, u32[]{:S(2)}, u32[]{:S(2)}) collective-permute-start(bf16[8,2048]{1,0:T(8,128)(2,1)} %param.6), channel_id=1, source_target_pairs={{0,2},{2,0},{4,6},{6,4},{8,10},{10,8},{12,14},{14,12},{16,18},{18,... | collective-permute-start | bytes 98312 | tf_op jit(solution)/shard_map/ppermute | solution.py:304
  1.1 1.4 %collective-permute-start = (bf16[8,2048]{1,0:T(8,128)(2,1)}, bf16[8,2048]{1,0:T(8,128)(2,1)S(1)}, u32[]{:S(2)}, u32[]{:S(2)}) collective-permute-start(bf16[8,2048]{1,0:T(8,128)(2,1)} %param.5), channel_id=1, source_target_pairs={{0,2},{2,0},{4,6},{6,4},{8,10},{10,8},{12,14},{14,12},{16,18},{18,... | collective-permute-start | bytes 98312 | tf_op jit(solution)/shard_map/ppermute | solution.py:304
  2.6 7.6 %collective-permute-start.4 = (bf16[16,2048]{1,0:T(8,128)(2,1)S(1)}, bf16[16,2048]{1,0:T(8,128)(2,1)S(1)}, u32[]{:S(2)}, u32[]{:S(2)}) collective-permute-start(bf16[16,2048]{1,0:T(8,128)(2,1)S(1)} %maximum_maximum_fusion), channel_id=1, source_target_pairs={{0,8},{2,10},{4,12},{6,14},{8,0},{10,2},{12,4},{14,6},{16,24},{18,... | collective-permute-start | bytes 196616 | tf_op jit(solution)/shard_map/ppermute | solution.py:304
  5.4 7.7 %collective-permute-start.5 = (bf16[16,2048]{1,0:T(8,128)(2,1)S(1)}, bf16[16,2048]{1,0:T(8,128)(2,1)S(1)}, u32[]{:S(2)}, u32[]{:S(2)}) collective-permute-start(bf16[16,2048]{1,0:T(8,128)(2,1)S(1)} %maximum_maximum_fusion), channel_id=1, source_target_pairs={{0,16},{2,18},{4,20},{6,22},{8,24},{10,26},{12,28},{14,30},{16,0},... | collective-permute-start | bytes 196616 | tf_op jit(solution)/shard_map/ppermute | solution.py:304
  8.0 6.1 %collective-permute-start.6 = (bf16[16,2048]{1,0:T(8,128)(2,1)S(1)}, bf16[16,2048]{1,0:T(8,128)(2,1)S(1)}, u32[]{:S(2)}, u32[]{:S(2)}) collective-permute-start(bf16[16,2048]{1,0:T(8,128)(2,1)S(1)} %maximum_maximum_fusion), channel_id=1, source_target_pairs={{0,24},{2,26},{4,28},{6,30},{8,16},{10,18},{12,20},{14,22},{16,8},... | collective-permute-start | bytes 196616 | tf_op jit(solution)/shard_map/ppermute | solution.py:304
  9.6 13.4 %collective-permute-start.2 = (bf16[256,2048]{1,0:T(8,128)(2,1)S(1)}, bf16[256,2048]{1,0:T(8,128)(2,1)S(1)}, u32[]{:S(2)}, u32[]{:S(2)}) collective-permute-start(bf16[256,2048]{1,0:T(8,128)(2,1)S(1)} %get-tuple-element.45), channel_id=1, source_target_pairs={{0,2},{2,0},{4,6},{6,4},{8,10},{10,8},{12,14},{14,12},{16,18},{18,... | collective-permute-start | bytes 3145736 | tf_op jit(solution)/shard_map/ppermute | solution.py:304
  9.7 13.3 %collective-permute-start.3 = (bf16[256,2048]{1,0:T(8,128)(2,1)S(1)}, bf16[256,2048]{1,0:T(8,128)(2,1)S(1)}, u32[]{:S(2)}, u32[]{:S(2)}) collective-permute-start(bf16[256,2048]{1,0:T(8,128)(2,1)S(1)} %get-tuple-element.46), channel_id=1, source_target_pairs={{0,2},{2,0},{4,6},{6,4},{8,10},{10,8},{12,14},{14,12},{16,18},{18,... | collective-permute-start | bytes 3145736 | tf_op jit(solution)/shard_map/ppermute | solution.py:304
  14.2 5.0 %collective-permute-start.7 = (bf16[64,1024]{1,0:T(8,128)(2,1)S(1)}, bf16[64,1024]{1,0:T(8,128)(2,1)S(1)}, u32[]{:S(2)}, u32[]{:S(2)}) collective-permute-start(bf16[64,1024]{1,0:T(8,128)(2,1)S(1)} %pad_maximum_fusion), channel_id=1, source_target_pairs={{0,4},{2,6},{4,0},{6,2},{8,12},{10,14},{12,8},{14,10},{16,20},{18,... | collective-permute-start | bytes 393224 | tf_op jit(solution)/shard_map/ppermute | solution.py:304
  15.8 5.0 %collective-permute-start.8 = (bf16[64,1024]{1,0:T(8,128)(2,1)S(1)}, bf16[64,1024]{1,0:T(8,128)(2,1)S(1)}, u32[]{:S(2)}, u32[]{:S(2)}) collective-permute-start(bf16[64,1024]{1,0:T(8,128)(2,1)S(1)} %pad_maximum_fusion.1), channel_id=1, source_target_pairs={{0,1},{1,0},{2,3},{3,2},{4,5},{5,4},{6,7},{7,6},{8,9},{9,8},{10,11... | collective-permute-start | bytes 393224 | tf_op jit(solution)/shard_map/ppermute | solution.py:304
  20.8 6.4 %collective-permute-start.9 = (bf16[128,1024]{1,0:T(8,128)(2,1)S(1)}, bf16[128,1024]{1,0:T(8,128)(2,1)S(1)}, u32[]{:S(2)}, u32[]{:S(2)}) collective-permute-start(bf16[128,1024]{1,0:T(8,128)(2,1)S(1)} %constant_dynamic-update-slice_fusion.refs_0_), channel_id=1, source_target_pairs={{0,1},{1,0},{2,3},{3,2},{4,5},{5,4},{6,7},{7,6},{8,9},{9,8},{10,11... | collective-permute-start | bytes 786440 | tf_op jit(solution)/shard_map/ppermute | solution.py:304
  22.4 6.4 %collective-permute-start.10 = (bf16[128,1024]{1,0:T(8,128)(2,1)S(1)}, bf16[128,1024]{1,0:T(8,128)(2,1)S(1)}, u32[]{:S(2)}, u32[]{:S(2)}) collective-permute-start(bf16[128,1024]{1,0:T(8,128)(2,1)S(1)} %constant_dynamic-update-slice_fusion.5.refs_1_.refs_0_), channel_id=1, source_target_pairs={{0,4},{2,6},{4,0},{6,2},{8,12},{10,14},{12,8},{14,10},{16,20},{18,... | collective-permute-start | bytes 786440 | tf_op jit(solution)/shard_map/ppermute | solution.py:304
  33.4 6.4 %collective-permute-start.11 = (bf16[128,1024]{1,0:T(8,128)(2,1)S(1)}, bf16[128,1024]{1,0:T(8,128)(2,1)S(1)}, u32[]{:S(2)}, u32[]{:S(2)}) collective-permute-start(bf16[128,1024]{1,0:T(8,128)(2,1)S(1)} %get-tuple-element.53), channel_id=1, source_target_pairs={{0,1},{1,0},{2,3},{3,2},{4,5},{5,4},{6,7},{7,6},{8,9},{9,8},{10,11... | collective-permute-start | bytes 786440 | tf_op jit(solution)/shard_map/ppermute | solution.py:304
  34.0 6.4 %collective-permute-start.12 = (bf16[128,1024]{1,0:T(8,128)(2,1)S(1)}, bf16[128,1024]{1,0:T(8,128)(2,1)S(1)}, u32[]{:S(2)}, u32[]{:S(2)}) collective-permute-start(bf16[128,1024]{1,0:T(8,128)(2,1)S(1)} %get-tuple-element.57), channel_id=1, source_target_pairs={{0,4},{2,6},{4,0},{6,2},{8,12},{10,14},{12,8},{14,10},{16,20},{18,... | collective-permute-start | bytes 786440 | tf_op jit(solution)/shard_map/ppermute | solution.py:304
  40.4 6.5 %collective-permute-start.15 = (bf16[256,2048]{1,0:T(8,128)(2,1)S(1)}, bf16[256,2048]{1,0:T(8,128)(2,1)S(1)}, u32[]{:S(2)}, u32[]{:S(2)}) collective-permute-start(bf16[256,2048]{1,0:T(8,128)(2,1)S(1)} %get-tuple-element.66), channel_id=1, source_target_pairs={{0,2},{2,0},{4,6},{6,4},{8,10},{10,8},{12,14},{14,12},{16,18},{18,... | collective-permute-start | bytes 3145736 | tf_op jit(solution)/shard_map/ppermute | solution.py:304
  40.5 6.0 %collective-permute-start.13 = (bf16[64,1024]{1,0:T(8,128)(2,1)S(1)}, bf16[64,1024]{1,0:T(8,128)(2,1)S(1)}, u32[]{:S(2)}, u32[]{:S(2)}) collective-permute-start(bf16[64,1024]{1,0:T(8,128)(2,1)S(1)} %slice.136), channel_id=1, source_target_pairs={{0,4},{2,6},{4,0},{6,2},{8,12},{10,14},{12,8},{14,10},{16,20},{18,... | collective-permute-start | bytes 393224 | tf_op jit(solution)/shard_map/ppermute | solution.py:304
  41.1 5.7 %collective-permute-start.14 = (bf16[64,1024]{1,0:T(8,128)(2,1)S(1)}, bf16[64,1024]{1,0:T(8,128)(2,1)S(1)}, u32[]{:S(2)}, u32[]{:S(2)}) collective-permute-start(bf16[64,1024]{1,0:T(8,128)(2,1)S(1)} %slice.135), channel_id=1, source_target_pairs={{0,1},{1,0},{2,3},{3,2},{4,5},{5,4},{6,7},{7,6},{8,9},{9,8},{10,11... | collective-permute-start | bytes 393224 | tf_op jit(solution)/shard_map/ppermute | solution.py:304
  46.9 4.7 %collective-permute-start.19 = (bf16[256,2048]{1,0:T(8,128)(2,1)S(1)}, bf16[256,2048]{1,0:T(8,128)(2,1)S(1)}, u32[]{:S(2)}, u32[]{:S(2)}) collective-permute-start(bf16[256,2048]{1,0:T(8,128)(2,1)S(1)} %get-tuple-element.69), channel_id=1, source_target_pairs={{0,2},{2,0},{4,6},{6,4},{8,10},{10,8},{12,14},{14,12},{16,18},{18,... | collective-permute-start | bytes 3145736 | tf_op jit(solution)/shard_map/ppermute | solution.py:304
  47.1 5.8 %collective-permute-start.16 = (bf16[16,2048]{1,0:T(8,128)(2,1)S(1)}, bf16[16,2048]{1,0:T(8,128)(2,1)S(1)}, u32[]{:S(2)}, u32[]{:S(2)}) collective-permute-start(bf16[16,2048]{1,0:T(8,128)(2,1)S(1)} %get-tuple-element.84), channel_id=1, source_target_pairs={{0,8},{2,10},{4,12},{6,14},{8,0},{10,2},{12,4},{14,6},{16,24},{18,... | collective-permute-start | bytes 196616 | tf_op jit(solution)/shard_map/ppermute | solution.py:304
  48.2 7.0 %collective-permute-start.17 = (bf16[16,2048]{1,0:T(8,128)(2,1)S(1)}, bf16[16,2048]{1,0:T(8,128)(2,1)S(1)}, u32[]{:S(2)}, u32[]{:S(2)}) collective-permute-start(bf16[16,2048]{1,0:T(8,128)(2,1)S(1)} %get-tuple-element.83), channel_id=1, source_target_pairs={{0,16},{2,18},{4,20},{6,22},{8,24},{10,26},{12,28},{14,30},{16,0},... | collective-permute-start | bytes 196616 | tf_op jit(solution)/shard_map/ppermute | solution.py:304
  50.9 6.1 %collective-permute-start.18 = (bf16[16,2048]{1,0:T(8,128)(2,1)S(1)}, bf16[16,2048]{1,0:T(8,128)(2,1)S(1)}, u32[]{:S(2)}, u32[]{:S(2)}) collective-permute-start(bf16[16,2048]{1,0:T(8,128)(2,1)S(1)} %get-tuple-element.82), channel_id=1, source_target_pairs={{0,24},{2,26},{4,28},{6,30},{8,16},{10,18},{12,20},{14,22},{16,8},... | collective-permute-start | bytes 196616 | tf_op jit(solution)/shard_map/ppermute | solution.py:304
  57.0 1.3 %collective-permute-start.20 = (bf16[8,2048]{1,0:T(8,128)(2,1)S(1)}, bf16[8,2048]{1,0:T(8,128)(2,1)S(1)}, u32[]{:S(2)}, u32[]{:S(2)}) collective-permute-start(bf16[8,2048]{1,0:T(8,128)(2,1)S(1)} %get-tuple-element.85), channel_id=1, source_target_pairs={{0,2},{2,0},{4,6},{6,4},{8,10},{10,8},{12,14},{14,12},{16,18},{18,... | collective-permute-start | bytes 98312 | tf_op jit(solution)/shard_map/ppermute | solution.py:304

commit v12 on v11

--- a/solution.py
+++ b/solution.py
@@ -304,7 +304,7 @@
         return lax.ppermute(array, axis, [(i, i ^ bits) for i in range(size)])
 
     core_bit, x_bit = 1, 2
-    z_bits = range(4, n_seq, 4)
+    z_bits = range(n_seq - 4, 0, -4)
     y_bits = [1 << b for b in range(n_mp.bit_length() - 1)]
     rows, part = memory_keys.shape
     share, blocks = part // 2, 2

time: 59.3 us -> 58 us (0.978)
  waiting for transfers between devices: 17.7 us -> 16.5 us
    ppermute x21, waiting for transfers between devices: 17.7 us -> 16.5 us  [swap(): return lax.ppermute(array, axis, [(i, i ^ bits) for i in range(size)])]
  transfers between devices with their start and end apart: 21 -> 21, of which waited for: 15 -> 14; matrix products, arithmetic and copies ran while one was open for 2% -> 2% of each run, Pallas kernels for 24% -> 24%
where the time goes in v12:
time: 58 us; the launch traced here: 57.7 us
  starting transfers between devices  19.9 us (34%)
  Pallas kernels  19.3 us (33%)
  waiting for transfers between devices  16.5 us (28%)
  local copies, waits for them, and re-layouts  0.9 us (2%)
  between operations  0.86 us (1%)
    ppermute x21, starting transfers between devices, swap(): return lax.ppermute(array, axis, [(i, i ^ bits) for i in range(size)])  19.9 us
    ppermute x21, waiting for transfers between devices, swap(): return lax.ppermute(array, axis, [(i, i ^ bits) for i in range(size)])  16.5 us
    pallas_call x4, Pallas kernels, attention(): pl.pallas_call(functools.partial(attention_kernel, n_mp, blocks, groups,...  15.7 us
    pallas_call x1, Pallas kernels, packing(): pl.pallas_call(functools.partial(packing_kernel, n_mp, blocks), in_specs=...  1.58 us
    pallas_call x1, Pallas kernels, placing(): pl.pallas_call(functools.partial(placing_kernel, n_mp, blocks), in_specs=...  1.37 us
  transfers between devices with their start and end apart: 21, of which 14 were waited for; matrix products, arithmetic and copies ran while one was open for 2% of the time, Pallas kernels for 24%

profile of v12, /device:TPU:0, one launch (start us, length us, event | category | flops | bytes accessed | tf_op | source)
XLA Modules:
  0.0 57.7 jit_solution(14930081597350220430)
XLA Ops:
  0.6 0.5 collective-permute-start.1
  1.1 0.1 collective-permute-start
  1.2 0.7 %constant_dynamic-slice_fusion.2 = (bf16[8,512]{1,0:T(8,128)(2,1)S(1)}, bf16[8,512]{1,0:T(8,128)(2,1)S(1)}, bf16[8,512]{1,0:T(8,128)(2,1)S(1)}, bf16[8,512]{1,0:T(8,128)(2,1)S(1)}) fusion(bf16[8,2048]{1,0:T(8,128)(2,1)} %param.6, s32[]{:T(128)S(6)} %select_n.2, s32[]{:T(128)S(6)} %add.35, bf16[8,2048]{1,0:T(8,128)(2,1)} %param.5), kind=kLoop, calls=%fused_computation.25 | loop fusion | bytes 65544 | tf_op jit(solution)/shard_map/slice | solution.py:316
  2.0 0.2 collective-permute-done.1
  2.2 0.3 collective-permute-done
  2.6 4.8 %collective-permute-start.4 = (bf16[16,2048]{1,0:T(8,128)(2,1)S(1)}, bf16[16,2048]{1,0:T(8,128)(2,1)S(1)}, u32[]{:S(2)}, u32[]{:S(2)}) collective-permute-start(bf16[16,2048]{1,0:T(8,128)(2,1)S(1)} %maximum_maximum_fusion), channel_id=1, source_target_pairs={{0,24},{2,26},{4,28},{6,30},{8,16},{10,18},{12,20},{14,22},{16,8},... | collective-permute-start | bytes 196616 | tf_op jit(solution)/shard_map/ppermute | solution.py:304
  7.4 0.1 collective-permute-start.5
  7.5 0.6 collective-permute-start.6
  8.1 1.6 %shard_map.75 = (bf16[256,2048]{1,0:T(8,128)(2,1)S(1)}, bf16[256,2048]{1,0:T(8,128)(2,1)S(1)}) custom-call(bf16[256,4096]{1,0:T(8,128)(2,1)} %q_ref.8, bf16[256,4096]{1,0:T(8,128)(2,1)} %g_ref.8), custom_call_target="tpu_custom_call" | custom-call | bytes 4194304 | tf_op jit(solution)/shard_map/pallas_call | solution.py:227
  9.7 0.1 collective-permute-start.2
  9.7 0.5 collective-permute-start.3
  10.2 3.1 %collective-permute-done.5 = bf16[16,2048]{1,0:T(8,128)(2,1)S(1)} collective-permute-done((bf16[16,2048]{1,0:T(8,128)(2,1)S(1)}, bf16[16,2048]{1,0:T(8,128)(2,1)S(1)}, u32[]{:S(2)}, u32[]{:S(2)}) %collective-permute-start.5) | collective-permute-done | bytes 65568 | tf_op jit(solution)/shard_map/ppermute | solution.py:304
  13.4 0.0 collective-permute-done.6
  13.4 1.6 %collective-permute-start.7 = (bf16[64,1024]{1,0:T(8,128)(2,1)S(1)}, bf16[64,1024]{1,0:T(8,128)(2,1)S(1)}, u32[]{:S(2)}, u32[]{:S(2)}) collective-permute-start(bf16[64,1024]{1,0:T(8,128)(2,1)S(1)} %pad_maximum_fusion), channel_id=1, source_target_pairs={{0,4},{2,6},{4,0},{6,2},{8,12},{10,14},{12,8},{14,10},{16,20},{18,... | collective-permute-start | bytes 393224 | tf_op jit(solution)/shard_map/ppermute | solution.py:304
  15.0 1.6 %collective-permute-start.8 = (bf16[64,1024]{1,0:T(8,128)(2,1)S(1)}, bf16[64,1024]{1,0:T(8,128)(2,1)S(1)}, u32[]{:S(2)}, u32[]{:S(2)}) collective-permute-start(bf16[64,1024]{1,0:T(8,128)(2,1)S(1)} %pad_maximum_fusion.1), channel_id=1, source_target_pairs={{0,1},{1,0},{2,3},{3,2},{4,5},{5,4},{6,7},{7,6},{8,9},{9,8},{10,11... | collective-permute-start | bytes 393224 | tf_op jit(solution)/shard_map/ppermute | solution.py:304
  16.6 2.2 %collective-permute-done.7 = bf16[64,1024]{1,0:T(8,128)(2,1)S(1)} collective-permute-done((bf16[64,1024]{1,0:T(8,128)(2,1)S(1)}, bf16[64,1024]{1,0:T(8,128)(2,1)S(1)}, u32[]{:S(2)}, u32[]{:S(2)}) %collective-permute-start.7) | collective-permute-done | bytes 131104 | tf_op jit(solution)/shard_map/ppermute | solution.py:304
  18.8 1.3 %collective-permute-done.8 = bf16[64,1024]{1,0:T(8,128)(2,1)S(1)} collective-permute-done((bf16[64,1024]{1,0:T(8,128)(2,1)S(1)}, bf16[64,1024]{1,0:T(8,128)(2,1)S(1)}, u32[]{:S(2)}, u32[]{:S(2)}) %collective-permute-start.8) | collective-permute-done | bytes 131104 | tf_op jit(solution)/shard_map/ppermute | solution.py:304
  20.1 1.6 %collective-permute-start.9 = (bf16[128,1024]{1,0:T(8,128)(2,1)S(1)}, bf16[128,1024]{1,0:T(8,128)(2,1)S(1)}, u32[]{:S(2)}, u32[]{:S(2)}) collective-permute-start(bf16[128,1024]{1,0:T(8,128)(2,1)S(1)} %constant_dynamic-update-slice_fusion.refs_0_), channel_id=1, source_target_pairs={{0,1},{1,0},{2,3},{3,2},{4,5},{5,4},{6,7},{7,6},{8,9},{9,8},{10,11... | collective-permute-start | bytes 786440 | tf_op jit(solution)/shard_map/ppermute | solution.py:304
  21.7 0.6 %collective-permute-start.10 = (bf16[128,1024]{1,0:T(8,128)(2,1)S(1)}, bf16[128,1024]{1,0:T(8,128)(2,1)S(1)}, u32[]{:S(2)}, u32[]{:S(2)}) collective-permute-start(bf16[128,1024]{1,0:T(8,128)(2,1)S(1)} %constant_dynamic-update-slice_fusion.5.refs_1_.refs_0_), channel_id=1, source_target_pairs={{0,4},{2,6},{4,0},{6,2},{8,12},{10,14},{12,8},{14,10},{16,20},{18,... | collective-permute-start | bytes 786440 | tf_op jit(solution)/shard_map/ppermute | solution.py:304
  22.3 0.0 collective-permute-done.2.sq_ref
  22.3 0.0 collective-permute-done.3.sg_ref
  22.3 3.2 %shard_map.76 = (bf16[256,4096]{1,0:T(8,128)(2,1)}, bf16[256,4096]{1,0:T(8,128)(2,1)}, bf16[256,2048]{1,0:T(8,128)(2,1)S(1)}, f32[128,1024]{1,0:T(8,128)S(1)}) custom-call(bf16[256,4096]{1,0:T(8,128)(2,1)} %q_ref.8, bf16[256,4096]{1,0:T(8,128)(2,1)} %g_ref.8, bf16[256,2048]{1,0:T(8,128)(2,1)S(1)} %collective-permute-done.2.sq_ref, ...), custom_call_target="tpu_custom_call" | custom-call | flops 402653184 | bytes 2097152 | tf_op jit(solution)/shard_map/pallas_call | solution.py:183
  25.5 1.6 %collective-permute-done.9.refs_0_ = bf16[128,1024]{1,0:T(8,128)(2,1)S(1)} collective-permute-done((bf16[128,1024]{1,0:T(8,128)(2,1)S(1)}, bf16[128,1024]{1,0:T(8,128)(2,1)S(1)}, u32[]{:S(2)}, u32[]{:S(2)}) %collective-permute-start.9) | collective-permute-done | bytes 262176 | tf_op jit(solution)/shard_map/ppermute | solution.py:304
  27.0 1.3 %collective-permute-done.10.refs_2_.refs_1_ = bf16[128,1024]{1,0:T(8,128)(2,1)S(1)} collective-permute-done((bf16[128,1024]{1,0:T(8,128)(2,1)S(1)}, bf16[128,1024]{1,0:T(8,128)(2,1)S(1)}, u32[]{:S(2)}, u32[]{:S(2)}) %collective-permute-start.10) | collective-permute-done | bytes 262176 | tf_op jit(solution)/shard_map/ppermute | solution.py:304
  28.4 4.5 %shard_map.77 = (bf16[128,1024]{1,0:T(8,128)(2,1)S(1)}, bf16[128,1024]{1,0:T(8,128)(2,1)S(1)}) custom-call(bf16[256,4096]{1,0:T(8,128)(2,1)} %q_ref.8, bf16[256,4096]{1,0:T(8,128)(2,1)} %g_ref.8, bf16[256,2048]{1,0:T(8,128)(2,1)S(1)} %collective-permute-done.2.sq_ref, bf16[256,2048]{1,0:T(8,128)(2,1)S(1)} %collective-permute-done.3.sg_ref, ...), custom_call_target="tpu_custom_call" | custom-call | flops 1207959552 | bytes 6291456 | tf_op jit(solution)/shard_map/pallas_call | solution.py:183
  32.9 0.6 %collective-permute-start.11 = (bf16[128,1024]{1,0:T(8,128)(2,1)S(1)}, bf16[128,1024]{1,0:T(8,128)(2,1)S(1)}, u32[]{:S(2)}, u32[]{:S(2)}) collective-permute-start(bf16[128,1024]{1,0:T(8,128)(2,1)S(1)} %get-tuple-element.53), channel_id=1, source_target_pairs={{0,1},{1,0},{2,3},{3,2},{4,5},{5,4},{6,7},{7,6},{8,9},{9,8},{10,11... | collective-permute-start | bytes 786440 | tf_op jit(solution)/shard_map/ppermute | solution.py:304
  33.5 0.5 collective-permute-start.12
  34.0 4.8 %shard_map.78 = (bf16[256,4096]{1,0:T(8,128)(2,1)}, bf16[256,4096]{1,0:T(8,128)(2,1)}, bf16[256,2048]{1,0:T(8,128)(2,1)S(1)}, f32[128,1024]{1,0:T(8,128)S(1)}) custom-call(bf16[256,4096]{1,0:T(8,128)(2,1)} %q_ref.8, bf16[256,4096]{1,0:T(8,128)(2,1)} %g_ref.8, ...), custom_call_target="tpu_custom_call", output_to_operand_aliasing={{0}: (6, {}), {1}: (7, {})} | custom-call | flops 805306368 | bytes 4194304 | tf_op jit(solution)/shard_map/pallas_call | solution.py:183
  38.8 0.5 collective-permute-done.11
  39.3 0.1 convert_add_fusion.1
  39.4 0.5 collective-permute-done.12
  39.9 0.1 convert_add_fusion
  39.9 0.1 collective-permute-start.15
  40.0 0.6 %collective-permute-start.13 = (bf16[64,1024]{1,0:T(8,128)(2,1)S(1)}, bf16[64,1024]{1,0:T(8,128)(2,1)S(1)}, u32[]{:S(2)}, u32[]{:S(2)}) collective-permute-start(bf16[64,1024]{1,0:T(8,128)(2,1)S(1)} %slice.136), channel_id=1, source_target_pairs={{0,4},{2,6},{4,0},{6,2},{8,12},{10,14},{12,8},{14,10},{16,20},{18,... | collective-permute-start | bytes 393224 | tf_op jit(solution)/shard_map/ppermute | solution.py:304
  40.6 1.6 %collective-permute-start.14 = (bf16[64,1024]{1,0:T(8,128)(2,1)S(1)}, bf16[64,1024]{1,0:T(8,128)(2,1)S(1)}, u32[]{:S(2)}, u32[]{:S(2)}) collective-permute-start(bf16[64,1024]{1,0:T(8,128)(2,1)S(1)} %slice.135), channel_id=1, source_target_pairs={{0,1},{1,0},{2,3},{3,2},{4,5},{5,4},{6,7},{7,6},{8,9},{9,8},{10,11... | collective-permute-start | bytes 393224 | tf_op jit(solution)/shard_map/ppermute | solution.py:304
  42.2 3.1 %shard_map.79 = (bf16[256,4096]{1,0:T(8,128)(2,1)}, bf16[256,4096]{1,0:T(8,128)(2,1)}, bf16[256,2048]{1,0:T(8,128)(2,1)S(1)}) custom-call(bf16[256,4096]{1,0:T(8,128)(2,1)} %q_ref.8, bf16[256,4096]{1,0:T(8,128)(2,1)} %g_ref.8, bf16[256,2048]{1,0:T(8,128)(2,1)S(1)} %collective-permute-done.2.sq_ref, ...), custom_call_target="tpu_custom_call", output_to_operand_aliasing={{0}: (5, {}), {1}: (6, {}), {2}: (7, {})} | custom-call | flops 402653184 | bytes 2097152 | tf_op jit(solution)/shard_map/pallas_call | solution.py:183
  45.4 0.6 %collective-permute-done.13 = bf16[64,1024]{1,0:T(8,128)(2,1)S(1)} collective-permute-done((bf16[64,1024]{1,0:T(8,128)(2,1)S(1)}, bf16[64,1024]{1,0:T(8,128)(2,1)S(1)}, u32[]{:S(2)}, u32[]{:S(2)}) %collective-permute-start.13) | collective-permute-done | bytes 131104 | tf_op jit(solution)/shard_map/ppermute | solution.py:304
  46.0 0.3 collective-permute-done.14
  46.4 0.1 collective-permute-start.19
  46.6 2.4 %collective-permute-start.16 = (bf16[16,2048]{1,0:T(8,128)(2,1)S(1)}, bf16[16,2048]{1,0:T(8,128)(2,1)S(1)}, u32[]{:S(2)}, u32[]{:S(2)}) collective-permute-start(bf16[16,2048]{1,0:T(8,128)(2,1)S(1)} %get-tuple-element.84), channel_id=1, source_target_pairs={{0,24},{2,26},{4,28},{6,30},{8,16},{10,18},{12,20},{14,22},{16,8},... | collective-permute-start | bytes 196616 | tf_op jit(solution)/shard_map/ppermute | solution.py:304
  48.9 0.1 collective-permute-start.17
  49.0 2.0 %collective-permute-start.18 = (bf16[16,2048]{1,0:T(8,128)(2,1)S(1)}, bf16[16,2048]{1,0:T(8,128)(2,1)S(1)}, u32[]{:S(2)}, u32[]{:S(2)}) collective-permute-start(bf16[16,2048]{1,0:T(8,128)(2,1)S(1)} %get-tuple-element.82), channel_id=1, source_target_pairs={{0,8},{2,10},{4,12},{6,14},{8,0},{10,2},{12,4},{14,6},{16,24},{18,... | collective-permute-start | bytes 196616 | tf_op jit(solution)/shard_map/ppermute | solution.py:304
  51.0 1.4 %shard_map.80 = (bf16[256,4096]{1,0:T(8,128)(2,1)}, bf16[256,4096]{1,0:T(8,128)(2,1)}) custom-call(bf16[256,2048]{1,0:T(8,128)(2,1)S(1)} %collective-permute-done.19.refs_0_, bf16[256,2048]{1,0:T(8,128)(2,1)S(1)} %collective-permute-done.15.refs_1_, bf16[256,4096]{1,0:T(8,128)(2,1)} %get-tuple-element.71.refs_2_, ...), custom_call_target="tpu_custom_call", output_to_operand_aliasing={{0}: (2, {}), {1}: (3, {})} | custom-call | tf_op jit(solution)/shard_map/pallas_call | solution.py:287
  52.4 1.0 %collective-permute-done.16 = bf16[16,2048]{1,0:T(8,128)(2,1)S(1)} collective-permute-done((bf16[16,2048]{1,0:T(8,128)(2,1)S(1)}, bf16[16,2048]{1,0:T(8,128)(2,1)S(1)}, u32[]{:S(2)}, u32[]{:S(2)}) %collective-permute-start.16) | collective-permute-done | bytes 65568 | tf_op jit(solution)/shard_map/ppermute | solution.py:304
  53.4 2.3 %collective-permute-done.17 = bf16[16,2048]{1,0:T(8,128)(2,1)S(1)} collective-permute-done((bf16[16,2048]{1,0:T(8,128)(2,1)S(1)}, bf16[16,2048]{1,0:T(8,128)(2,1)S(1)}, u32[]{:S(2)}, u32[]{:S(2)}) %collective-permute-start.17) | collective-permute-done | bytes 65568 | tf_op jit(solution)/shard_map/ppermute | solution.py:304
  55.8 0.1 collective-permute-start.20
  55.9 1.2 %collective-permute-done.20.other_ref = bf16[8,2048]{1,0:T(8,128)(2,1)S(1)} collective-permute-done((bf16[8,2048]{1,0:T(8,128)(2,1)S(1)}, bf16[8,2048]{1,0:T(8,128)(2,1)S(1)}, u32[]{:S(2)}, u32[]{:S(2)}) %collective-permute-start.20) | collective-permute-done | bytes 32800 | tf_op jit(solution)/shard_map/ppermute | solution.py:304
  57.0 0.7 %shard_map.81 = (bf16[8,2048]{1,0:T(8,128)(2,1)}, bf16[8,2048]{1,0:T(8,128)(2,1)}) custom-call(bf16[8,2048]{1,0:T(8,128)(2,1)S(1)} %get-tuple-element.86.mine_ref, bf16[8,2048]{1,0:T(8,128)(2,1)S(1)} %collective-permute-done.20.other_ref), custom_call_target="tpu_custom_call" | custom-call | tf_op jit(solution)/shard_map/pallas_call | solution.py:254
  (25 shorter events, 0.3 us)
Async XLA Ops:
  0.6 1.6 %collective-permute-start.1 = (bf16[8,2048]{1,0:T(8,128)(2,1)}, bf16[8,2048]{1,0:T(8,128)(2,1)S(1)}, u32[]{:S(2)}, u32[]{:S(2)}) collective-permute-start(bf16[8,2048]{1,0:T(8,128)(2,1)} %param.6), channel_id=1, source_target_pairs={{0,2},{2,0},{4,6},{6,4},{8,10},{10,8},{12,14},{14,12},{16,18},{18,... | collective-permute-start | bytes 98312 | tf_op jit(solution)/shard_map/ppermute | solution.py:304
  1.1 1.4 %collective-permute-start = (bf16[8,2048]{1,0:T(8,128)(2,1)}, bf16[8,2048]{1,0:T(8,128)(2,1)S(1)}, u32[]{:S(2)}, u32[]{:S(2)}) collective-permute-start(bf16[8,2048]{1,0:T(8,128)(2,1)} %param.5), channel_id=1, source_target_pairs={{0,2},{2,0},{4,6},{6,4},{8,10},{10,8},{12,14},{14,12},{16,18},{18,... | collective-permute-start | bytes 98312 | tf_op jit(solution)/shard_map/ppermute | solution.py:304
  2.6 7.7 %collective-permute-start.4 = (bf16[16,2048]{1,0:T(8,128)(2,1)S(1)}, bf16[16,2048]{1,0:T(8,128)(2,1)S(1)}, u32[]{:S(2)}, u32[]{:S(2)}) collective-permute-start(bf16[16,2048]{1,0:T(8,128)(2,1)S(1)} %maximum_maximum_fusion), channel_id=1, source_target_pairs={{0,24},{2,26},{4,28},{6,30},{8,16},{10,18},{12,20},{14,22},{16,8},... | collective-permute-start | bytes 196616 | tf_op jit(solution)/shard_map/ppermute | solution.py:304
  7.4 6.0 %collective-permute-start.5 = (bf16[16,2048]{1,0:T(8,128)(2,1)S(1)}, bf16[16,2048]{1,0:T(8,128)(2,1)S(1)}, u32[]{:S(2)}, u32[]{:S(2)}) collective-permute-start(bf16[16,2048]{1,0:T(8,128)(2,1)S(1)} %maximum_maximum_fusion), channel_id=1, source_target_pairs={{0,16},{2,18},{4,20},{6,22},{8,24},{10,26},{12,28},{14,30},{16,0},... | collective-permute-start | bytes 196616 | tf_op jit(solution)/shard_map/ppermute | solution.py:304
  7.5 5.9 %collective-permute-start.6 = (bf16[16,2048]{1,0:T(8,128)(2,1)S(1)}, bf16[16,2048]{1,0:T(8,128)(2,1)S(1)}, u32[]{:S(2)}, u32[]{:S(2)}) collective-permute-start(bf16[16,2048]{1,0:T(8,128)(2,1)S(1)} %maximum_maximum_fusion), channel_id=1, source_target_pairs={{0,8},{2,10},{4,12},{6,14},{8,0},{10,2},{12,4},{14,6},{16,24},{18,... | collective-permute-start | bytes 196616 | tf_op jit(solution)/shard_map/ppermute | solution.py:304
  9.7 12.6 %collective-permute-start.2 = (bf16[256,2048]{1,0:T(8,128)(2,1)S(1)}, bf16[256,2048]{1,0:T(8,128)(2,1)S(1)}, u32[]{:S(2)}, u32[]{:S(2)}) collective-permute-start(bf16[256,2048]{1,0:T(8,128)(2,1)S(1)} %get-tuple-element.45), channel_id=1, source_target_pairs={{0,2},{2,0},{4,6},{6,4},{8,10},{10,8},{12,14},{14,12},{16,18},{18,... | collective-permute-start | bytes 3145736 | tf_op jit(solution)/shard_map/ppermute | solution.py:304
  9.7 12.5 %collective-permute-start.3 = (bf16[256,2048]{1,0:T(8,128)(2,1)S(1)}, bf16[256,2048]{1,0:T(8,128)(2,1)S(1)}, u32[]{:S(2)}, u32[]{:S(2)}) collective-permute-start(bf16[256,2048]{1,0:T(8,128)(2,1)S(1)} %get-tuple-element.46), channel_id=1, source_target_pairs={{0,2},{2,0},{4,6},{6,4},{8,10},{10,8},{12,14},{14,12},{16,18},{18,... | collective-permute-start | bytes 3145736 | tf_op jit(solution)/shard_map/ppermute | solution.py:304
  13.4 5.3 %collective-permute-start.7 = (bf16[64,1024]{1,0:T(8,128)(2,1)S(1)}, bf16[64,1024]{1,0:T(8,128)(2,1)S(1)}, u32[]{:S(2)}, u32[]{:S(2)}) collective-permute-start(bf16[64,1024]{1,0:T(8,128)(2,1)S(1)} %pad_maximum_fusion), channel_id=1, source_target_pairs={{0,4},{2,6},{4,0},{6,2},{8,12},{10,14},{12,8},{14,10},{16,20},{18,... | collective-permute-start | bytes 393224 | tf_op jit(solution)/shard_map/ppermute | solution.py:304
  15.0 5.0 %collective-permute-start.8 = (bf16[64,1024]{1,0:T(8,128)(2,1)S(1)}, bf16[64,1024]{1,0:T(8,128)(2,1)S(1)}, u32[]{:S(2)}, u32[]{:S(2)}) collective-permute-start(bf16[64,1024]{1,0:T(8,128)(2,1)S(1)} %pad_maximum_fusion.1), channel_id=1, source_target_pairs={{0,1},{1,0},{2,3},{3,2},{4,5},{5,4},{6,7},{7,6},{8,9},{9,8},{10,11... | collective-permute-start | bytes 393224 | tf_op jit(solution)/shard_map/ppermute | solution.py:304
  20.1 7.0 %collective-permute-start.9 = (bf16[128,1024]{1,0:T(8,128)(2,1)S(1)}, bf16[128,1024]{1,0:T(8,128)(2,1)S(1)}, u32[]{:S(2)}, u32[]{:S(2)}) collective-permute-start(bf16[128,1024]{1,0:T(8,128)(2,1)S(1)} %constant_dynamic-update-slice_fusion.refs_0_), channel_id=1, source_target_pairs={{0,1},{1,0},{2,3},{3,2},{4,5},{5,4},{6,7},{7,6},{8,9},{9,8},{10,11... | collective-permute-start | bytes 786440 | tf_op jit(solution)/shard_map/ppermute | solution.py:304
  21.7 6.7 %collective-permute-start.10 = (bf16[128,1024]{1,0:T(8,128)(2,1)S(1)}, bf16[128,1024]{1,0:T(8,128)(2,1)S(1)}, u32[]{:S(2)}, u32[]{:S(2)}) collective-permute-start(bf16[128,1024]{1,0:T(8,128)(2,1)S(1)} %constant_dynamic-update-slice_fusion.5.refs_1_.refs_0_), channel_id=1, source_target_pairs={{0,4},{2,6},{4,0},{6,2},{8,12},{10,14},{12,8},{14,10},{16,20},{18,... | collective-permute-start | bytes 786440 | tf_op jit(solution)/shard_map/ppermute | solution.py:304
  32.9 6.4 %collective-permute-start.11 = (bf16[128,1024]{1,0:T(8,128)(2,1)S(1)}, bf16[128,1024]{1,0:T(8,128)(2,1)S(1)}, u32[]{:S(2)}, u32[]{:S(2)}) collective-permute-start(bf16[128,1024]{1,0:T(8,128)(2,1)S(1)} %get-tuple-element.53), channel_id=1, source_target_pairs={{0,1},{1,0},{2,3},{3,2},{4,5},{5,4},{6,7},{7,6},{8,9},{9,8},{10,11... | collective-permute-start | bytes 786440 | tf_op jit(solution)/shard_map/ppermute | solution.py:304
  33.5 6.4 %collective-permute-start.12 = (bf16[128,1024]{1,0:T(8,128)(2,1)S(1)}, bf16[128,1024]{1,0:T(8,128)(2,1)S(1)}, u32[]{:S(2)}, u32[]{:S(2)}) collective-permute-start(bf16[128,1024]{1,0:T(8,128)(2,1)S(1)} %get-tuple-element.57), channel_id=1, source_target_pairs={{0,4},{2,6},{4,0},{6,2},{8,12},{10,14},{12,8},{14,10},{16,20},{18,... | collective-permute-start | bytes 786440 | tf_op jit(solution)/shard_map/ppermute | solution.py:304
  39.9 6.4 %collective-permute-start.15 = (bf16[256,2048]{1,0:T(8,128)(2,1)S(1)}, bf16[256,2048]{1,0:T(8,128)(2,1)S(1)}, u32[]{:S(2)}, u32[]{:S(2)}) collective-permute-start(bf16[256,2048]{1,0:T(8,128)(2,1)S(1)} %get-tuple-element.66), channel_id=1, source_target_pairs={{0,2},{2,0},{4,6},{6,4},{8,10},{10,8},{12,14},{14,12},{16,18},{18,... | collective-permute-start | bytes 3145736 | tf_op jit(solution)/shard_map/ppermute | solution.py:304
  40.0 6.0 %collective-permute-start.13 = (bf16[64,1024]{1,0:T(8,128)(2,1)S(1)}, bf16[64,1024]{1,0:T(8,128)(2,1)S(1)}, u32[]{:S(2)}, u32[]{:S(2)}) collective-permute-start(bf16[64,1024]{1,0:T(8,128)(2,1)S(1)} %slice.136), channel_id=1, source_target_pairs={{0,4},{2,6},{4,0},{6,2},{8,12},{10,14},{12,8},{14,10},{16,20},{18,... | collective-permute-start | bytes 393224 | tf_op jit(solution)/shard_map/ppermute | solution.py:304
  40.6 5.7 %collective-permute-start.14 = (bf16[64,1024]{1,0:T(8,128)(2,1)S(1)}, bf16[64,1024]{1,0:T(8,128)(2,1)S(1)}, u32[]{:S(2)}, u32[]{:S(2)}) collective-permute-start(bf16[64,1024]{1,0:T(8,128)(2,1)S(1)} %slice.135), channel_id=1, source_target_pairs={{0,1},{1,0},{2,3},{3,2},{4,5},{5,4},{6,7},{7,6},{8,9},{9,8},{10,11... | collective-permute-start | bytes 393224 | tf_op jit(solution)/shard_map/ppermute | solution.py:304
  46.4 4.7 %collective-permute-start.19 = (bf16[256,2048]{1,0:T(8,128)(2,1)S(1)}, bf16[256,2048]{1,0:T(8,128)(2,1)S(1)}, u32[]{:S(2)}, u32[]{:S(2)}) collective-permute-start(bf16[256,2048]{1,0:T(8,128)(2,1)S(1)} %get-tuple-element.69), channel_id=1, source_target_pairs={{0,2},{2,0},{4,6},{6,4},{8,10},{10,8},{12,14},{14,12},{16,18},{18,... | collective-permute-start | bytes 3145736 | tf_op jit(solution)/shard_map/ppermute | solution.py:304
  46.6 6.8 %collective-permute-start.16 = (bf16[16,2048]{1,0:T(8,128)(2,1)S(1)}, bf16[16,2048]{1,0:T(8,128)(2,1)S(1)}, u32[]{:S(2)}, u32[]{:S(2)}) collective-permute-start(bf16[16,2048]{1,0:T(8,128)(2,1)S(1)} %get-tuple-element.84), channel_id=1, source_target_pairs={{0,24},{2,26},{4,28},{6,30},{8,16},{10,18},{12,20},{14,22},{16,8},... | collective-permute-start | bytes 196616 | tf_op jit(solution)/shard_map/ppermute | solution.py:304
  48.9 6.8 %collective-permute-start.17 = (bf16[16,2048]{1,0:T(8,128)(2,1)S(1)}, bf16[16,2048]{1,0:T(8,128)(2,1)S(1)}, u32[]{:S(2)}, u32[]{:S(2)}) collective-permute-start(bf16[16,2048]{1,0:T(8,128)(2,1)S(1)} %get-tuple-element.83), channel_id=1, source_target_pairs={{0,16},{2,18},{4,20},{6,22},{8,24},{10,26},{12,28},{14,30},{16,0},... | collective-permute-start | bytes 196616 | tf_op jit(solution)/shard_map/ppermute | solution.py:304
  49.0 6.7 %collective-permute-start.18 = (bf16[16,2048]{1,0:T(8,128)(2,1)S(1)}, bf16[16,2048]{1,0:T(8,128)(2,1)S(1)}, u32[]{:S(2)}, u32[]{:S(2)}) collective-permute-start(bf16[16,2048]{1,0:T(8,128)(2,1)S(1)} %get-tuple-element.82), channel_id=1, source_target_pairs={{0,8},{2,10},{4,12},{6,14},{8,0},{10,2},{12,4},{14,6},{16,24},{18,... | collective-permute-start | bytes 196616 | tf_op jit(solution)/shard_map/ppermute | solution.py:304
  55.8 1.3 %collective-permute-start.20 = (bf16[8,2048]{1,0:T(8,128)(2,1)S(1)}, bf16[8,2048]{1,0:T(8,128)(2,1)S(1)}, u32[]{:S(2)}, u32[]{:S(2)}) collective-permute-start(bf16[8,2048]{1,0:T(8,128)(2,1)S(1)} %get-tuple-element.85), channel_id=1, source_target_pairs={{0,2},{2,0},{4,6},{6,4},{8,10},{10,8},{12,14},{14,12},{16,18},{18,... | collective-permute-start | bytes 98312 | tf_op jit(solution)/shard_map/ppermute | solution.py:304

commit v13 on v12

--- a/solution.py
+++ b/solution.py
@@ -369,8 +369,8 @@
     for bits in y_bits[:0:-1]:
         second = fold(second, "mp", bits)
     first, second = fold(first, "seq", x_bit), fold(second, "mp", y_bits[0])
-    first, second, sent[0], returned = together(first, second, sent[0], swap(sent[1], "seq", core_bit))
-    returned = [swap(sent[0], "seq", core_bit), returned]
+    returned = [swap(sent[block], "seq", core_bit) for block in range(blocks)]
+    first, second, returned[1] = together(first, second, returned[1])
     total = jnp.concatenate([first, second], axis=1)
     outputs = placing(n_mp, returned, *outputs)
     count, give = 2 * rows, total.astype(bf16)

time: 58 us -> 57.7 us (level)
  transfers between devices with their start and end apart: 21 -> 21, of which waited for: 14 -> 14; matrix products, arithmetic and copies ran while one was open for 2% -> 2% of each run, Pallas kernels for 24% -> 25%
where the time goes in v13:
time: 57.7 us; the launch traced here: 57.4 us
  starting transfers between devices  19.9 us (34%)
  Pallas kernels  19.3 us (33%)
  waiting for transfers between devices  16.2 us (28%)
  local copies, waits for them, and re-layouts  0.9 us (2%)
  between operations  0.87 us (2%)
    ppermute x21, starting transfers between devices, swap(): return lax.ppermute(array, axis, [(i, i ^ bits) for i in range(size)])  19.9 us
    ppermute x21, waiting for transfers between devices, swap(): return lax.ppermute(array, axis, [(i, i ^ bits) for i in range(size)])  16.2 us
    pallas_call x4, Pallas kernels, attention(): pl.pallas_call(functools.partial(attention_kernel, n_mp, blocks, groups,...  15.7 us
    pallas_call x1, Pallas kernels, packing(): pl.pallas_call(functools.partial(packing_kernel, n_mp, blocks), in_specs=...  1.58 us
    pallas_call x1, Pallas kernels, placing(): pl.pallas_call(functools.partial(placing_kernel, n_mp, blocks), in_specs=...  1.37 us
  transfers between devices with their start and end apart: 21, of which 14 were waited for; matrix products, arithmetic and copies ran while one was open for 2% of the time, Pallas kernels for 25%

profile of v13, /device:TPU:0, one launch (start us, length us, event | category | flops | bytes accessed | tf_op | source)
XLA Modules:
  0.0 57.4 jit_solution(2799529089885620135)
XLA Ops:
  0.6 0.5 collective-permute-start.1
  1.1 0.1 collective-permute-start
  1.2 0.7 %constant_dynamic-slice_fusion.2 = (bf16[8,512]{1,0:T(8,128)(2,1)S(1)}, bf16[8,512]{1,0:T(8,128)(2,1)S(1)}, bf16[8,512]{1,0:T(8,128)(2,1)S(1)}, bf16[8,512]{1,0:T(8,128)(2,1)S(1)}) fusion(bf16[8,2048]{1,0:T(8,128)(2,1)} %param.6, s32[]{:T(128)S(6)} %select_n.2, s32[]{:T(128)S(6)} %add.35, bf16[8,2048]{1,0:T(8,128)(2,1)} %param.5), kind=kLoop, calls=%fused_computation.25 | loop fusion | bytes 65544 | tf_op jit(solution)/shard_map/slice | solution.py:316
  2.0 0.2 collective-permute-done.1
  2.2 0.3 collective-permute-done
  2.6 4.8 %collective-permute-start.4 = (bf16[16,2048]{1,0:T(8,128)(2,1)S(1)}, bf16[16,2048]{1,0:T(8,128)(2,1)S(1)}, u32[]{:S(2)}, u32[]{:S(2)}) collective-permute-start(bf16[16,2048]{1,0:T(8,128)(2,1)S(1)} %maximum_maximum_fusion), channel_id=1, source_target_pairs={{0,24},{2,26},{4,28},{6,30},{8,16},{10,18},{12,20},{14,22},{16,8},... | collective-permute-start | bytes 196616 | tf_op jit(solution)/shard_map/ppermute | solution.py:304
  7.4 0.1 collective-permute-start.5
  7.5 0.6 collective-permute-start.6
  8.1 1.6 %shard_map.75 = (bf16[256,2048]{1,0:T(8,128)(2,1)S(1)}, bf16[256,2048]{1,0:T(8,128)(2,1)S(1)}) custom-call(bf16[256,4096]{1,0:T(8,128)(2,1)} %q_ref.8, bf16[256,4096]{1,0:T(8,128)(2,1)} %g_ref.8), custom_call_target="tpu_custom_call" | custom-call | bytes 4194304 | tf_op jit(solution)/shard_map/pallas_call | solution.py:227
  9.7 0.1 collective-permute-start.2
  9.7 0.5 collective-permute-start.3
  10.2 3.1 %collective-permute-done.5 = bf16[16,2048]{1,0:T(8,128)(2,1)S(1)} collective-permute-done((bf16[16,2048]{1,0:T(8,128)(2,1)S(1)}, bf16[16,2048]{1,0:T(8,128)(2,1)S(1)}, u32[]{:S(2)}, u32[]{:S(2)}) %collective-permute-start.5) | collective-permute-done | bytes 65568 | tf_op jit(solution)/shard_map/ppermute | solution.py:304
  13.4 0.0 collective-permute-done.6
  13.4 1.6 %collective-permute-start.7 = (bf16[64,1024]{1,0:T(8,128)(2,1)S(1)}, bf16[64,1024]{1,0:T(8,128)(2,1)S(1)}, u32[]{:S(2)}, u32[]{:S(2)}) collective-permute-start(bf16[64,1024]{1,0:T(8,128)(2,1)S(1)} %pad_maximum_fusion), channel_id=1, source_target_pairs={{0,4},{2,6},{4,0},{6,2},{8,12},{10,14},{12,8},{14,10},{16,20},{18,... | collective-permute-start | bytes 393224 | tf_op jit(solution)/shard_map/ppermute | solution.py:304
  15.0 1.6 %collective-permute-start.8 = (bf16[64,1024]{1,0:T(8,128)(2,1)S(1)}, bf16[64,1024]{1,0:T(8,128)(2,1)S(1)}, u32[]{:S(2)}, u32[]{:S(2)}) collective-permute-start(bf16[64,1024]{1,0:T(8,128)(2,1)S(1)} %pad_maximum_fusion.1), channel_id=1, source_target_pairs={{0,1},{1,0},{2,3},{3,2},{4,5},{5,4},{6,7},{7,6},{8,9},{9,8},{10,11... | collective-permute-start | bytes 393224 | tf_op jit(solution)/shard_map/ppermute | solution.py:304
  16.6 2.2 %collective-permute-done.7 = bf16[64,1024]{1,0:T(8,128)(2,1)S(1)} collective-permute-done((bf16[64,1024]{1,0:T(8,128)(2,1)S(1)}, bf16[64,1024]{1,0:T(8,128)(2,1)S(1)}, u32[]{:S(2)}, u32[]{:S(2)}) %collective-permute-start.7) | collective-permute-done | bytes 131104 | tf_op jit(solution)/shard_map/ppermute | solution.py:304
  18.8 1.3 %collective-permute-done.8 = bf16[64,1024]{1,0:T(8,128)(2,1)S(1)} collective-permute-done((bf16[64,1024]{1,0:T(8,128)(2,1)S(1)}, bf16[64,1024]{1,0:T(8,128)(2,1)S(1)}, u32[]{:S(2)}, u32[]{:S(2)}) %collective-permute-start.8) | collective-permute-done | bytes 131104 | tf_op jit(solution)/shard_map/ppermute | solution.py:304
  20.1 1.6 %collective-permute-start.9 = (bf16[128,1024]{1,0:T(8,128)(2,1)S(1)}, bf16[128,1024]{1,0:T(8,128)(2,1)S(1)}, u32[]{:S(2)}, u32[]{:S(2)}) collective-permute-start(bf16[128,1024]{1,0:T(8,128)(2,1)S(1)} %constant_dynamic-update-slice_fusion.refs_0_), channel_id=1, source_target_pairs={{0,1},{1,0},{2,3},{3,2},{4,5},{5,4},{6,7},{7,6},{8,9},{9,8},{10,11... | collective-permute-start | bytes 786440 | tf_op jit(solution)/shard_map/ppermute | solution.py:304
  21.7 0.6 %collective-permute-start.10 = (bf16[128,1024]{1,0:T(8,128)(2,1)S(1)}, bf16[128,1024]{1,0:T(8,128)(2,1)S(1)}, u32[]{:S(2)}, u32[]{:S(2)}) collective-permute-start(bf16[128,1024]{1,0:T(8,128)(2,1)S(1)} %constant_dynamic-update-slice_fusion.5.refs_1_.refs_0_), channel_id=1, source_target_pairs={{0,4},{2,6},{4,0},{6,2},{8,12},{10,14},{12,8},{14,10},{16,20},{18,... | collective-permute-start | bytes 786440 | tf_op jit(solution)/shard_map/ppermute | solution.py:304
  22.3 3.2 %shard_map.76 = (bf16[256,4096]{1,0:T(8,128)(2,1)}, bf16[256,4096]{1,0:T(8,128)(2,1)}, bf16[256,2048]{1,0:T(8,128)(2,1)S(1)}, f32[128,1024]{1,0:T(8,128)S(1)}) custom-call(bf16[256,4096]{1,0:T(8,128)(2,1)} %q_ref.8, bf16[256,4096]{1,0:T(8,128)(2,1)} %g_ref.8, bf16[256,2048]{1,0:T(8,128)(2,1)S(1)} %collective-permute-done.2.sq_ref, ...), custom_call_target="tpu_custom_call" | custom-call | flops 402653184 | bytes 2097152 | tf_op jit(solution)/shard_map/pallas_call | solution.py:183
  25.5 1.6 %collective-permute-done.9.refs_0_ = bf16[128,1024]{1,0:T(8,128)(2,1)S(1)} collective-permute-done((bf16[128,1024]{1,0:T(8,128)(2,1)S(1)}, bf16[128,1024]{1,0:T(8,128)(2,1)S(1)}, u32[]{:S(2)}, u32[]{:S(2)}) %collective-permute-start.9) | collective-permute-done | bytes 262176 | tf_op jit(solution)/shard_map/ppermute | solution.py:304
  27.0 1.3 %collective-permute-done.10.refs_2_.refs_1_ = bf16[128,1024]{1,0:T(8,128)(2,1)S(1)} collective-permute-done((bf16[128,1024]{1,0:T(8,128)(2,1)S(1)}, bf16[128,1024]{1,0:T(8,128)(2,1)S(1)}, u32[]{:S(2)}, u32[]{:S(2)}) %collective-permute-start.10) | collective-permute-done | bytes 262176 | tf_op jit(solution)/shard_map/ppermute | solution.py:304
  28.4 4.5 %shard_map.77 = (bf16[128,1024]{1,0:T(8,128)(2,1)S(1)}, bf16[128,1024]{1,0:T(8,128)(2,1)S(1)}) custom-call(bf16[256,4096]{1,0:T(8,128)(2,1)} %q_ref.8, bf16[256,4096]{1,0:T(8,128)(2,1)} %g_ref.8, bf16[256,2048]{1,0:T(8,128)(2,1)S(1)} %collective-permute-done.2.sq_ref, bf16[256,2048]{1,0:T(8,128)(2,1)S(1)} %collective-permute-done.3.sg_ref, ...), custom_call_target="tpu_custom_call" | custom-call | flops 1207959552 | bytes 6291456 | tf_op jit(solution)/shard_map/pallas_call | solution.py:183
  32.9 0.6 %collective-permute-start.11 = (bf16[128,1024]{1,0:T(8,128)(2,1)S(1)}, bf16[128,1024]{1,0:T(8,128)(2,1)S(1)}, u32[]{:S(2)}, u32[]{:S(2)}) collective-permute-start(bf16[128,1024]{1,0:T(8,128)(2,1)S(1)} %get-tuple-element.52), channel_id=1, source_target_pairs={{0,1},{1,0},{2,3},{3,2},{4,5},{5,4},{6,7},{7,6},{8,9},{9,8},{10,11... | collective-permute-start | bytes 786440 | tf_op jit(solution)/shard_map/ppermute | solution.py:304
  33.5 0.5 collective-permute-start.12
  34.0 4.8 %shard_map.78 = (bf16[256,4096]{1,0:T(8,128)(2,1)}, bf16[256,4096]{1,0:T(8,128)(2,1)}, bf16[256,2048]{1,0:T(8,128)(2,1)S(1)}, f32[128,1024]{1,0:T(8,128)S(1)}) custom-call(bf16[256,4096]{1,0:T(8,128)(2,1)} %q_ref.8, bf16[256,4096]{1,0:T(8,128)(2,1)} %g_ref.8, ...), custom_call_target="tpu_custom_call", output_to_operand_aliasing={{0}: (6, {}), {1}: (7, {})} | custom-call | flops 805306368 | bytes 4194304 | tf_op jit(solution)/shard_map/pallas_call | solution.py:183
  38.8 0.5 collective-permute-done.11
  39.3 0.1 convert_add_fusion.1
  39.4 0.5 collective-permute-done.12
  39.9 0.1 convert_add_fusion
  39.9 0.1 collective-permute-start.15
  40.0 0.6 %collective-permute-start.13 = (bf16[64,1024]{1,0:T(8,128)(2,1)S(1)}, bf16[64,1024]{1,0:T(8,128)(2,1)S(1)}, u32[]{:S(2)}, u32[]{:S(2)}) collective-permute-start(bf16[64,1024]{1,0:T(8,128)(2,1)S(1)} %slice.136), channel_id=1, source_target_pairs={{0,4},{2,6},{4,0},{6,2},{8,12},{10,14},{12,8},{14,10},{16,20},{18,... | collective-permute-start | bytes 393224 | tf_op jit(solution)/shard_map/ppermute | solution.py:304
  40.6 1.6 %collective-permute-start.14 = (bf16[64,1024]{1,0:T(8,128)(2,1)S(1)}, bf16[64,1024]{1,0:T(8,128)(2,1)S(1)}, u32[]{:S(2)}, u32[]{:S(2)}) collective-permute-start(bf16[64,1024]{1,0:T(8,128)(2,1)S(1)} %slice.135), channel_id=1, source_target_pairs={{0,1},{1,0},{2,3},{3,2},{4,5},{5,4},{6,7},{7,6},{8,9},{9,8},{10,11... | collective-permute-start | bytes 393224 | tf_op jit(solution)/shard_map/ppermute | solution.py:304
  42.2 3.1 %shard_map.79 = (bf16[256,4096]{1,0:T(8,128)(2,1)}, bf16[256,4096]{1,0:T(8,128)(2,1)}, bf16[256,2048]{1,0:T(8,128)(2,1)S(1)}) custom-call(bf16[256,4096]{1,0:T(8,128)(2,1)} %q_ref.8, bf16[256,4096]{1,0:T(8,128)(2,1)} %g_ref.8, bf16[256,2048]{1,0:T(8,128)(2,1)S(1)} %collective-permute-done.2.sq_ref, ...), custom_call_target="tpu_custom_call", output_to_operand_aliasing={{0}: (5, {}), {1}: (6, {}), {2}: (7, {})} | custom-call | flops 402653184 | bytes 2097152 | tf_op jit(solution)/shard_map/pallas_call | solution.py:183
  45.4 0.1 collective-permute-start.19
  45.4 0.5 collective-permute-done.13
  46.0 0.3 collective-permute-done.14
  46.5 2.4 %collective-permute-start.16 = (bf16[16,2048]{1,0:T(8,128)(2,1)S(1)}, bf16[16,2048]{1,0:T(8,128)(2,1)S(1)}, u32[]{:S(2)}, u32[]{:S(2)}) collective-permute-start(bf16[16,2048]{1,0:T(8,128)(2,1)S(1)} %get-tuple-element.82), channel_id=1, source_target_pairs={{0,24},{2,26},{4,28},{6,30},{8,16},{10,18},{12,20},{14,22},{16,8},... | collective-permute-start | bytes 196616 | tf_op jit(solution)/shard_map/ppermute | solution.py:304
  48.8 0.1 collective-permute-start.17
  48.9 2.0 %collective-permute-start.18 = (bf16[16,2048]{1,0:T(8,128)(2,1)S(1)}, bf16[16,2048]{1,0:T(8,128)(2,1)S(1)}, u32[]{:S(2)}, u32[]{:S(2)}) collective-permute-start(bf16[16,2048]{1,0:T(8,128)(2,1)S(1)} %get-tuple-element.80), channel_id=1, source_target_pairs={{0,8},{2,10},{4,12},{6,14},{8,0},{10,2},{12,4},{14,6},{16,24},{18,... | collective-permute-start | bytes 196616 | tf_op jit(solution)/shard_map/ppermute | solution.py:304
  50.9 0.0 collective-permute-done.19.refs_0_
  50.9 1.4 %shard_map.80 = (bf16[256,4096]{1,0:T(8,128)(2,1)}, bf16[256,4096]{1,0:T(8,128)(2,1)}) custom-call(bf16[256,2048]{1,0:T(8,128)(2,1)S(1)} %collective-permute-done.19.refs_0_, bf16[256,2048]{1,0:T(8,128)(2,1)S(1)} %collective-permute-done.15.refs_1_, bf16[256,4096]{1,0:T(8,128)(2,1)} %get-tuple-element.69.refs_2_, ...), custom_call_target="tpu_custom_call", output_to_operand_aliasing={{0}: (2, {}), {1}: (3, {})} | custom-call | tf_op jit(solution)/shard_map/pallas_call | solution.py:287
  52.3 0.5 collective-permute-done.16
  52.8 2.5 %collective-permute-done.17 = bf16[16,2048]{1,0:T(8,128)(2,1)S(1)} collective-permute-done((bf16[16,2048]{1,0:T(8,128)(2,1)S(1)}, bf16[16,2048]{1,0:T(8,128)(2,1)S(1)}, u32[]{:S(2)}, u32[]{:S(2)}) %collective-permute-start.17) | collective-permute-done | bytes 65568 | tf_op jit(solution)/shard_map/ppermute | solution.py:304
  55.4 0.0 collective-permute-done.18
  55.4 0.1 collective-permute-start.20
  55.5 1.2 %collective-permute-done.20.other_ref = bf16[8,2048]{1,0:T(8,128)(2,1)S(1)} collective-permute-done((bf16[8,2048]{1,0:T(8,128)(2,1)S(1)}, bf16[8,2048]{1,0:T(8,128)(2,1)S(1)}, u32[]{:S(2)}, u32[]{:S(2)}) %collective-permute-start.20) | collective-permute-done | bytes 32800 | tf_op jit(solution)/shard_map/ppermute | solution.py:304
  56.7 0.7 %shard_map.81 = (bf16[8,2048]{1,0:T(8,128)(2,1)}, bf16[8,2048]{1,0:T(8,128)(2,1)}) custom-call(bf16[8,2048]{1,0:T(8,128)(2,1)S(1)} %get-tuple-element.84.mine_ref, bf16[8,2048]{1,0:T(8,128)(2,1)S(1)} %collective-permute-done.20.other_ref), custom_call_target="tpu_custom_call" | custom-call | tf_op jit(solution)/shard_map/pallas_call | solution.py:254
  (25 shorter events, 0.3 us)
Async XLA Ops:
  0.6 1.6 %collective-permute-start.1 = (bf16[8,2048]{1,0:T(8,128)(2,1)}, bf16[8,2048]{1,0:T(8,128)(2,1)S(1)}, u32[]{:S(2)}, u32[]{:S(2)}) collective-permute-start(bf16[8,2048]{1,0:T(8,128)(2,1)} %param.6), channel_id=1, source_target_pairs={{0,2},{2,0},{4,6},{6,4},{8,10},{10,8},{12,14},{14,12},{16,18},{18,... | collective-permute-start | bytes 98312 | tf_op jit(solution)/shard_map/ppermute | solution.py:304
  1.1 1.4 %collective-permute-start = (bf16[8,2048]{1,0:T(8,128)(2,1)}, bf16[8,2048]{1,0:T(8,128)(2,1)S(1)}, u32[]{:S(2)}, u32[]{:S(2)}) collective-permute-start(bf16[8,2048]{1,0:T(8,128)(2,1)} %param.5), channel_id=1, source_target_pairs={{0,2},{2,0},{4,6},{6,4},{8,10},{10,8},{12,14},{14,12},{16,18},{18,... | collective-permute-start | bytes 98312 | tf_op jit(solution)/shard_map/ppermute | solution.py:304
  2.6 7.7 %collective-permute-start.4 = (bf16[16,2048]{1,0:T(8,128)(2,1)S(1)}, bf16[16,2048]{1,0:T(8,128)(2,1)S(1)}, u32[]{:S(2)}, u32[]{:S(2)}) collective-permute-start(bf16[16,2048]{1,0:T(8,128)(2,1)S(1)} %maximum_maximum_fusion), channel_id=1, source_target_pairs={{0,24},{2,26},{4,28},{6,30},{8,16},{10,18},{12,20},{14,22},{16,8},... | collective-permute-start | bytes 196616 | tf_op jit(solution)/shard_map/ppermute | solution.py:304
  7.4 6.0 %collective-permute-start.5 = (bf16[16,2048]{1,0:T(8,128)(2,1)S(1)}, bf16[16,2048]{1,0:T(8,128)(2,1)S(1)}, u32[]{:S(2)}, u32[]{:S(2)}) collective-permute-start(bf16[16,2048]{1,0:T(8,128)(2,1)S(1)} %maximum_maximum_fusion), channel_id=1, source_target_pairs={{0,16},{2,18},{4,20},{6,22},{8,24},{10,26},{12,28},{14,30},{16,0},... | collective-permute-start | bytes 196616 | tf_op jit(solution)/shard_map/ppermute | solution.py:304
  7.5 5.9 %collective-permute-start.6 = (bf16[16,2048]{1,0:T(8,128)(2,1)S(1)}, bf16[16,2048]{1,0:T(8,128)(2,1)S(1)}, u32[]{:S(2)}, u32[]{:S(2)}) collective-permute-start(bf16[16,2048]{1,0:T(8,128)(2,1)S(1)} %maximum_maximum_fusion), channel_id=1, source_target_pairs={{0,8},{2,10},{4,12},{6,14},{8,0},{10,2},{12,4},{14,6},{16,24},{18,... | collective-permute-start | bytes 196616 | tf_op jit(solution)/shard_map/ppermute | solution.py:304
  9.7 12.6 %collective-permute-start.2 = (bf16[256,2048]{1,0:T(8,128)(2,1)S(1)}, bf16[256,2048]{1,0:T(8,128)(2,1)S(1)}, u32[]{:S(2)}, u32[]{:S(2)}) collective-permute-start(bf16[256,2048]{1,0:T(8,128)(2,1)S(1)} %get-tuple-element.44), channel_id=1, source_target_pairs={{0,2},{2,0},{4,6},{6,4},{8,10},{10,8},{12,14},{14,12},{16,18},{18,... | collective-permute-start | bytes 3145736 | tf_op jit(solution)/shard_map/ppermute | solution.py:304
  9.7 12.5 %collective-permute-start.3 = (bf16[256,2048]{1,0:T(8,128)(2,1)S(1)}, bf16[256,2048]{1,0:T(8,128)(2,1)S(1)}, u32[]{:S(2)}, u32[]{:S(2)}) collective-permute-start(bf16[256,2048]{1,0:T(8,128)(2,1)S(1)} %get-tuple-element.45), channel_id=1, source_target_pairs={{0,2},{2,0},{4,6},{6,4},{8,10},{10,8},{12,14},{14,12},{16,18},{18,... | collective-permute-start | bytes 3145736 | tf_op jit(solution)/shard_map/ppermute | solution.py:304
  13.4 5.3 %collective-permute-start.7 = (bf16[64,1024]{1,0:T(8,128)(2,1)S(1)}, bf16[64,1024]{1,0:T(8,128)(2,1)S(1)}, u32[]{:S(2)}, u32[]{:S(2)}) collective-permute-start(bf16[64,1024]{1,0:T(8,128)(2,1)S(1)} %pad_maximum_fusion), channel_id=1, source_target_pairs={{0,4},{2,6},{4,0},{6,2},{8,12},{10,14},{12,8},{14,10},{16,20},{18,... | collective-permute-start | bytes 393224 | tf_op jit(solution)/shard_map/ppermute | solution.py:304
  15.0 5.0 %collective-permute-start.8 = (bf16[64,1024]{1,0:T(8,128)(2,1)S(1)}, bf16[64,1024]{1,0:T(8,128)(2,1)S(1)}, u32[]{:S(2)}, u32[]{:S(2)}) collective-permute-start(bf16[64,1024]{1,0:T(8,128)(2,1)S(1)} %pad_maximum_fusion.1), channel_id=1, source_target_pairs={{0,1},{1,0},{2,3},{3,2},{4,5},{5,4},{6,7},{7,6},{8,9},{9,8},{10,11... | collective-permute-start | bytes 393224 | tf_op jit(solution)/shard_map/ppermute | solution.py:304
  20.1 7.0 %collective-permute-start.9 = (bf16[128,1024]{1,0:T(8,128)(2,1)S(1)}, bf16[128,1024]{1,0:T(8,128)(2,1)S(1)}, u32[]{:S(2)}, u32[]{:S(2)}) collective-permute-start(bf16[128,1024]{1,0:T(8,128)(2,1)S(1)} %constant_dynamic-update-slice_fusion.refs_0_), channel_id=1, source_target_pairs={{0,1},{1,0},{2,3},{3,2},{4,5},{5,4},{6,7},{7,6},{8,9},{9,8},{10,11... | collective-permute-start | bytes 786440 | tf_op jit(solution)/shard_map/ppermute | solution.py:304
  21.7 6.7 %collective-permute-start.10 = (bf16[128,1024]{1,0:T(8,128)(2,1)S(1)}, bf16[128,1024]{1,0:T(8,128)(2,1)S(1)}, u32[]{:S(2)}, u32[]{:S(2)}) collective-permute-start(bf16[128,1024]{1,0:T(8,128)(2,1)S(1)} %constant_dynamic-update-slice_fusion.5.refs_1_.refs_0_), channel_id=1, source_target_pairs={{0,4},{2,6},{4,0},{6,2},{8,12},{10,14},{12,8},{14,10},{16,20},{18,... | collective-permute-start | bytes 786440 | tf_op jit(solution)/shard_map/ppermute | solution.py:304
  32.9 6.4 %collective-permute-start.11 = (bf16[128,1024]{1,0:T(8,128)(2,1)S(1)}, bf16[128,1024]{1,0:T(8,128)(2,1)S(1)}, u32[]{:S(2)}, u32[]{:S(2)}) collective-permute-start(bf16[128,1024]{1,0:T(8,128)(2,1)S(1)} %get-tuple-element.52), channel_id=1, source_target_pairs={{0,1},{1,0},{2,3},{3,2},{4,5},{5,4},{6,7},{7,6},{8,9},{9,8},{10,11... | collective-permute-start | bytes 786440 | tf_op jit(solution)/shard_map/ppermute | solution.py:304
  33.5 6.4 %collective-permute-start.12 = (bf16[128,1024]{1,0:T(8,128)(2,1)S(1)}, bf16[128,1024]{1,0:T(8,128)(2,1)S(1)}, u32[]{:S(2)}, u32[]{:S(2)}) collective-permute-start(bf16[128,1024]{1,0:T(8,128)(2,1)S(1)} %get-tuple-element.56), channel_id=1, source_target_pairs={{0,4},{2,6},{4,0},{6,2},{8,12},{10,14},{12,8},{14,10},{16,20},{18,... | collective-permute-start | bytes 786440 | tf_op jit(solution)/shard_map/ppermute | solution.py:304
  39.9 6.4 %collective-permute-start.15 = (bf16[256,2048]{1,0:T(8,128)(2,1)S(1)}, bf16[256,2048]{1,0:T(8,128)(2,1)S(1)}, u32[]{:S(2)}, u32[]{:S(2)}) collective-permute-start(bf16[256,2048]{1,0:T(8,128)(2,1)S(1)} %get-tuple-element.60), channel_id=1, source_target_pairs={{0,2},{2,0},{4,6},{6,4},{8,10},{10,8},{12,14},{14,12},{16,18},{18,... | collective-permute-start | bytes 3145736 | tf_op jit(solution)/shard_map/ppermute | solution.py:304
  40.0 6.0 %collective-permute-start.13 = (bf16[64,1024]{1,0:T(8,128)(2,1)S(1)}, bf16[64,1024]{1,0:T(8,128)(2,1)S(1)}, u32[]{:S(2)}, u32[]{:S(2)}) collective-permute-start(bf16[64,1024]{1,0:T(8,128)(2,1)S(1)} %slice.136), channel_id=1, source_target_pairs={{0,4},{2,6},{4,0},{6,2},{8,12},{10,14},{12,8},{14,10},{16,20},{18,... | collective-permute-start | bytes 393224 | tf_op jit(solution)/shard_map/ppermute | solution.py:304
  40.6 5.7 %collective-permute-start.14 = (bf16[64,1024]{1,0:T(8,128)(2,1)S(1)}, bf16[64,1024]{1,0:T(8,128)(2,1)S(1)}, u32[]{:S(2)}, u32[]{:S(2)}) collective-permute-start(bf16[64,1024]{1,0:T(8,128)(2,1)S(1)} %slice.135), channel_id=1, source_target_pairs={{0,1},{1,0},{2,3},{3,2},{4,5},{5,4},{6,7},{7,6},{8,9},{9,8},{10,11... | collective-permute-start | bytes 393224 | tf_op jit(solution)/shard_map/ppermute | solution.py:304
  45.4 5.6 %collective-permute-start.19 = (bf16[256,2048]{1,0:T(8,128)(2,1)S(1)}, bf16[256,2048]{1,0:T(8,128)(2,1)S(1)}, u32[]{:S(2)}, u32[]{:S(2)}) collective-permute-start(bf16[256,2048]{1,0:T(8,128)(2,1)S(1)} %get-tuple-element.67), channel_id=1, source_target_pairs={{0,2},{2,0},{4,6},{6,4},{8,10},{10,8},{12,14},{14,12},{16,18},{18,... | collective-permute-start | bytes 3145736 | tf_op jit(solution)/shard_map/ppermute | solution.py:304
  46.5 6.4 %collective-permute-start.16 = (bf16[16,2048]{1,0:T(8,128)(2,1)S(1)}, bf16[16,2048]{1,0:T(8,128)(2,1)S(1)}, u32[]{:S(2)}, u32[]{:S(2)}) collective-permute-start(bf16[16,2048]{1,0:T(8,128)(2,1)S(1)} %get-tuple-element.82), channel_id=1, source_target_pairs={{0,24},{2,26},{4,28},{6,30},{8,16},{10,18},{12,20},{14,22},{16,8},... | collective-permute-start | bytes 196616 | tf_op jit(solution)/shard_map/ppermute | solution.py:304
  48.8 6.6 %collective-permute-start.17 = (bf16[16,2048]{1,0:T(8,128)(2,1)S(1)}, bf16[16,2048]{1,0:T(8,128)(2,1)S(1)}, u32[]{:S(2)}, u32[]{:S(2)}) collective-permute-start(bf16[16,2048]{1,0:T(8,128)(2,1)S(1)} %get-tuple-element.81), channel_id=1, source_target_pairs={{0,16},{2,18},{4,20},{6,22},{8,24},{10,26},{12,28},{14,30},{16,0},... | collective-permute-start | bytes 196616 | tf_op jit(solution)/shard_map/ppermute | solution.py:304
  48.9 6.5 %collective-permute-start.18 = (bf16[16,2048]{1,0:T(8,128)(2,1)S(1)}, bf16[16,2048]{1,0:T(8,128)(2,1)S(1)}, u32[]{:S(2)}, u32[]{:S(2)}) collective-permute-start(bf16[16,2048]{1,0:T(8,128)(2,1)S(1)} %get-tuple-element.80), channel_id=1, source_target_pairs={{0,8},{2,10},{4,12},{6,14},{8,0},{10,2},{12,4},{14,6},{16,24},{18,... | collective-permute-start | bytes 196616 | tf_op jit(solution)/shard_map/ppermute | solution.py:304
  55.4 1.3 %collective-permute-start.20 = (bf16[8,2048]{1,0:T(8,128)(2,1)S(1)}, bf16[8,2048]{1,0:T(8,128)(2,1)S(1)}, u32[]{:S(2)}, u32[]{:S(2)}) collective-permute-start(bf16[8,2048]{1,0:T(8,128)(2,1)S(1)} %get-tuple-element.83), channel_id=1, source_target_pairs={{0,2},{2,0},{4,6},{6,4},{8,10},{10,8},{12,14},{14,12},{16,18},{18,... | collective-permute-start | bytes 98312 | tf_op jit(solution)/shard_map/ppermute | solution.py:304

commit v14 on v13

--- a/solution.py
+++ b/solution.py
@@ -333,7 +333,7 @@
         first = wider(first, swap(first, "mp", bits))
     for bits in y_bits[1:]:
         second = wider(second, swap(second, "mp", bits))
-    first_got, second_got = swap(first, "mp", y_bits[-1]), swap(second, "seq", x_bit)
+    second_got, first_got = swap(second, "seq", x_bit), swap(first, "mp", y_bits[-1])
 
     half = n_mp // 2
     outputs, sent, (first_keep,) = attention(

time: 57.7 us -> 57.7 us (level)
  no operation moved by 1% of the time
where the time goes in v14:
time: 57.7 us; the launch traced here: 57.4 us
  starting transfers between devices  19.9 us (34%)
  Pallas kernels  19.3 us (33%)
  waiting for transfers between devices  16.2 us (28%)
  local copies, waits for them, and re-layouts  0.9 us (2%)
  between operations  0.87 us (2%)
    ppermute x21, starting transfers between devices, swap(): return lax.ppermute(array, axis, [(i, i ^ bits) for i in range(size)])  19.9 us
    ppermute x21, waiting for transfers between devices, swap(): return lax.ppermute(array, axis, [(i, i ^ bits) for i in range(size)])  16.2 us
    pallas_call x4, Pallas kernels, attention(): pl.pallas_call(functools.partial(attention_kernel, n_mp, blocks, groups,...  15.7 us
    pallas_call x1, Pallas kernels, packing(): pl.pallas_call(functools.partial(packing_kernel, n_mp, blocks), in_specs=...  1.58 us
    pallas_call x1, Pallas kernels, placing(): pl.pallas_call(functools.partial(placing_kernel, n_mp, blocks), in_specs=...  1.37 us
  transfers between devices with their start and end apart: 21, of which 14 were waited for; matrix products, arithmetic and copies ran while one was open for 2% of the time, Pallas kernels for 25%

profile of v14, /device:TPU:0, one launch (start us, length us, event | category | flops | bytes accessed | tf_op | source)
XLA Modules:
  0.0 57.4 jit_solution(2799529089885620135)
XLA Ops:
  0.6 0.5 collective-permute-start.1
  1.1 0.1 collective-permute-start
  1.2 0.7 %constant_dynamic-slice_fusion.2 = (bf16[8,512]{1,0:T(8,128)(2,1)S(1)}, bf16[8,512]{1,0:T(8,128)(2,1)S(1)}, bf16[8,512]{1,0:T(8,128)(2,1)S(1)}, bf16[8,512]{1,0:T(8,128)(2,1)S(1)}) fusion(bf16[8,2048]{1,0:T(8,128)(2,1)} %param.6, s32[]{:T(128)S(6)} %select_n.2, s32[]{:T(128)S(6)} %add.35, bf16[8,2048]{1,0:T(8,128)(2,1)} %param.5), kind=kLoop, calls=%fused_computation.25 | loop fusion | bytes 65544 | tf_op jit(solution)/shard_map/slice | solution.py:316
  2.0 0.2 collective-permute-done.1
  2.2 0.3 collective-permute-done
  2.6 4.8 %collective-permute-start.4 = (bf16[16,2048]{1,0:T(8,128)(2,1)S(1)}, bf16[16,2048]{1,0:T(8,128)(2,1)S(1)}, u32[]{:S(2)}, u32[]{:S(2)}) collective-permute-start(bf16[16,2048]{1,0:T(8,128)(2,1)S(1)} %maximum_maximum_fusion), channel_id=1, source_target_pairs={{0,24},{2,26},{4,28},{6,30},{8,16},{10,18},{12,20},{14,22},{16,8},... | collective-permute-start | bytes 196616 | tf_op jit(solution)/shard_map/ppermute | solution.py:304
  7.4 0.1 collective-permute-start.5
  7.5 0.6 collective-permute-start.6
  8.1 1.6 %shard_map.75 = (bf16[256,2048]{1,0:T(8,128)(2,1)S(1)}, bf16[256,2048]{1,0:T(8,128)(2,1)S(1)}) custom-call(bf16[256,4096]{1,0:T(8,128)(2,1)} %q_ref.8, bf16[256,4096]{1,0:T(8,128)(2,1)} %g_ref.8), custom_call_target="tpu_custom_call" | custom-call | bytes 4194304 | tf_op jit(solution)/shard_map/pallas_call | solution.py:227
  9.7 0.1 collective-permute-start.2
  9.7 0.5 collective-permute-start.3
  10.2 3.1 %collective-permute-done.5 = bf16[16,2048]{1,0:T(8,128)(2,1)S(1)} collective-permute-done((bf16[16,2048]{1,0:T(8,128)(2,1)S(1)}, bf16[16,2048]{1,0:T(8,128)(2,1)S(1)}, u32[]{:S(2)}, u32[]{:S(2)}) %collective-permute-start.5) | collective-permute-done | bytes 65568 | tf_op jit(solution)/shard_map/ppermute | solution.py:304
  13.4 0.0 collective-permute-done.6
  13.4 1.6 %collective-permute-start.7 = (bf16[64,1024]{1,0:T(8,128)(2,1)S(1)}, bf16[64,1024]{1,0:T(8,128)(2,1)S(1)}, u32[]{:S(2)}, u32[]{:S(2)}) collective-permute-start(bf16[64,1024]{1,0:T(8,128)(2,1)S(1)} %pad_maximum_fusion), channel_id=1, source_target_pairs={{0,4},{2,6},{4,0},{6,2},{8,12},{10,14},{12,8},{14,10},{16,20},{18,... | collective-permute-start | bytes 393224 | tf_op jit(solution)/shard_map/ppermute | solution.py:304
  15.0 1.6 %collective-permute-start.8 = (bf16[64,1024]{1,0:T(8,128)(2,1)S(1)}, bf16[64,1024]{1,0:T(8,128)(2,1)S(1)}, u32[]{:S(2)}, u32[]{:S(2)}) collective-permute-start(bf16[64,1024]{1,0:T(8,128)(2,1)S(1)} %pad_maximum_fusion.1), channel_id=1, source_target_pairs={{0,1},{1,0},{2,3},{3,2},{4,5},{5,4},{6,7},{7,6},{8,9},{9,8},{10,11... | collective-permute-start | bytes 393224 | tf_op jit(solution)/shard_map/ppermute | solution.py:304
  16.6 2.2 %collective-permute-done.7 = bf16[64,1024]{1,0:T(8,128)(2,1)S(1)} collective-permute-done((bf16[64,1024]{1,0:T(8,128)(2,1)S(1)}, bf16[64,1024]{1,0:T(8,128)(2,1)S(1)}, u32[]{:S(2)}, u32[]{:S(2)}) %collective-permute-start.7) | collective-permute-done | bytes 131104 | tf_op jit(solution)/shard_map/ppermute | solution.py:304
  18.8 1.3 %collective-permute-done.8 = bf16[64,1024]{1,0:T(8,128)(2,1)S(1)} collective-permute-done((bf16[64,1024]{1,0:T(8,128)(2,1)S(1)}, bf16[64,1024]{1,0:T(8,128)(2,1)S(1)}, u32[]{:S(2)}, u32[]{:S(2)}) %collective-permute-start.8) | collective-permute-done | bytes 131104 | tf_op jit(solution)/shard_map/ppermute | solution.py:304
  20.1 1.6 %collective-permute-start.9 = (bf16[128,1024]{1,0:T(8,128)(2,1)S(1)}, bf16[128,1024]{1,0:T(8,128)(2,1)S(1)}, u32[]{:S(2)}, u32[]{:S(2)}) collective-permute-start(bf16[128,1024]{1,0:T(8,128)(2,1)S(1)} %constant_dynamic-update-slice_fusion.refs_0_), channel_id=1, source_target_pairs={{0,1},{1,0},{2,3},{3,2},{4,5},{5,4},{6,7},{7,6},{8,9},{9,8},{10,11... | collective-permute-start | bytes 786440 | tf_op jit(solution)/shard_map/ppermute | solution.py:304
  21.7 0.6 %collective-permute-start.10 = (bf16[128,1024]{1,0:T(8,128)(2,1)S(1)}, bf16[128,1024]{1,0:T(8,128)(2,1)S(1)}, u32[]{:S(2)}, u32[]{:S(2)}) collective-permute-start(bf16[128,1024]{1,0:T(8,128)(2,1)S(1)} %constant_dynamic-update-slice_fusion.5.refs_1_.refs_0_), channel_id=1, source_target_pairs={{0,4},{2,6},{4,0},{6,2},{8,12},{10,14},{12,8},{14,10},{16,20},{18,... | collective-permute-start | bytes 786440 | tf_op jit(solution)/shard_map/ppermute | solution.py:304
  22.3 3.2 %shard_map.76 = (bf16[256,4096]{1,0:T(8,128)(2,1)}, bf16[256,4096]{1,0:T(8,128)(2,1)}, bf16[256,2048]{1,0:T(8,128)(2,1)S(1)}, f32[128,1024]{1,0:T(8,128)S(1)}) custom-call(bf16[256,4096]{1,0:T(8,128)(2,1)} %q_ref.8, bf16[256,4096]{1,0:T(8,128)(2,1)} %g_ref.8, bf16[256,2048]{1,0:T(8,128)(2,1)S(1)} %collective-permute-done.2.sq_ref, ...), custom_call_target="tpu_custom_call" | custom-call | flops 402653184 | bytes 2097152 | tf_op jit(solution)/shard_map/pallas_call | solution.py:183
  25.5 1.6 %collective-permute-done.9.refs_0_ = bf16[128,1024]{1,0:T(8,128)(2,1)S(1)} collective-permute-done((bf16[128,1024]{1,0:T(8,128)(2,1)S(1)}, bf16[128,1024]{1,0:T(8,128)(2,1)S(1)}, u32[]{:S(2)}, u32[]{:S(2)}) %collective-permute-start.9) | collective-permute-done | bytes 262176 | tf_op jit(solution)/shard_map/ppermute | solution.py:304
  27.0 1.3 %collective-permute-done.10.refs_2_.refs_1_ = bf16[128,1024]{1,0:T(8,128)(2,1)S(1)} collective-permute-done((bf16[128,1024]{1,0:T(8,128)(2,1)S(1)}, bf16[128,1024]{1,0:T(8,128)(2,1)S(1)}, u32[]{:S(2)}, u32[]{:S(2)}) %collective-permute-start.10) | collective-permute-done | bytes 262176 | tf_op jit(solution)/shard_map/ppermute | solution.py:304
  28.4 4.5 %shard_map.77 = (bf16[128,1024]{1,0:T(8,128)(2,1)S(1)}, bf16[128,1024]{1,0:T(8,128)(2,1)S(1)}) custom-call(bf16[256,4096]{1,0:T(8,128)(2,1)} %q_ref.8, bf16[256,4096]{1,0:T(8,128)(2,1)} %g_ref.8, bf16[256,2048]{1,0:T(8,128)(2,1)S(1)} %collective-permute-done.2.sq_ref, bf16[256,2048]{1,0:T(8,128)(2,1)S(1)} %collective-permute-done.3.sg_ref, ...), custom_call_target="tpu_custom_call" | custom-call | flops 1207959552 | bytes 6291456 | tf_op jit(solution)/shard_map/pallas_call | solution.py:183
  32.9 0.6 %collective-permute-start.11 = (bf16[128,1024]{1,0:T(8,128)(2,1)S(1)}, bf16[128,1024]{1,0:T(8,128)(2,1)S(1)}, u32[]{:S(2)}, u32[]{:S(2)}) collective-permute-start(bf16[128,1024]{1,0:T(8,128)(2,1)S(1)} %get-tuple-element.52), channel_id=1, source_target_pairs={{0,1},{1,0},{2,3},{3,2},{4,5},{5,4},{6,7},{7,6},{8,9},{9,8},{10,11... | collective-permute-start | bytes 786440 | tf_op jit(solution)/shard_map/ppermute | solution.py:304
  33.5 0.5 collective-permute-start.12
  34.0 4.8 %shard_map.78 = (bf16[256,4096]{1,0:T(8,128)(2,1)}, bf16[256,4096]{1,0:T(8,128)(2,1)}, bf16[256,2048]{1,0:T(8,128)(2,1)S(1)}, f32[128,1024]{1,0:T(8,128)S(1)}) custom-call(bf16[256,4096]{1,0:T(8,128)(2,1)} %q_ref.8, bf16[256,4096]{1,0:T(8,128)(2,1)} %g_ref.8, ...), custom_call_target="tpu_custom_call", output_to_operand_aliasing={{0}: (6, {}), {1}: (7, {})} | custom-call | flops 805306368 | bytes 4194304 | tf_op jit(solution)/shard_map/pallas_call | solution.py:183
  38.8 0.5 collective-permute-done.11
  39.3 0.1 convert_add_fusion.1
  39.4 0.5 collective-permute-done.12
  39.9 0.1 convert_add_fusion
  39.9 0.1 collective-permute-start.15
  40.0 0.6 %collective-permute-start.13 = (bf16[64,1024]{1,0:T(8,128)(2,1)S(1)}, bf16[64,1024]{1,0:T(8,128)(2,1)S(1)}, u32[]{:S(2)}, u32[]{:S(2)}) collective-permute-start(bf16[64,1024]{1,0:T(8,128)(2,1)S(1)} %slice.136), channel_id=1, source_target_pairs={{0,4},{2,6},{4,0},{6,2},{8,12},{10,14},{12,8},{14,10},{16,20},{18,... | collective-permute-start | bytes 393224 | tf_op jit(solution)/shard_map/ppermute | solution.py:304
  40.6 1.6 %collective-permute-start.14 = (bf16[64,1024]{1,0:T(8,128)(2,1)S(1)}, bf16[64,1024]{1,0:T(8,128)(2,1)S(1)}, u32[]{:S(2)}, u32[]{:S(2)}) collective-permute-start(bf16[64,1024]{1,0:T(8,128)(2,1)S(1)} %slice.135), channel_id=1, source_target_pairs={{0,1},{1,0},{2,3},{3,2},{4,5},{5,4},{6,7},{7,6},{8,9},{9,8},{10,11... | collective-permute-start | bytes 393224 | tf_op jit(solution)/shard_map/ppermute | solution.py:304
  42.2 3.1 %shard_map.79 = (bf16[256,4096]{1,0:T(8,128)(2,1)}, bf16[256,4096]{1,0:T(8,128)(2,1)}, bf16[256,2048]{1,0:T(8,128)(2,1)S(1)}) custom-call(bf16[256,4096]{1,0:T(8,128)(2,1)} %q_ref.8, bf16[256,4096]{1,0:T(8,128)(2,1)} %g_ref.8, bf16[256,2048]{1,0:T(8,128)(2,1)S(1)} %collective-permute-done.2.sq_ref, ...), custom_call_target="tpu_custom_call", output_to_operand_aliasing={{0}: (5, {}), {1}: (6, {}), {2}: (7, {})} | custom-call | flops 402653184 | bytes 2097152 | tf_op jit(solution)/shard_map/pallas_call | solution.py:183
  45.4 0.1 collective-permute-start.19
  45.4 0.5 collective-permute-done.13
  46.0 0.3 collective-permute-done.14
  46.5 2.4 %collective-permute-start.16 = (bf16[16,2048]{1,0:T(8,128)(2,1)S(1)}, bf16[16,2048]{1,0:T(8,128)(2,1)S(1)}, u32[]{:S(2)}, u32[]{:S(2)}) collective-permute-start(bf16[16,2048]{1,0:T(8,128)(2,1)S(1)} %get-tuple-element.82), channel_id=1, source_target_pairs={{0,24},{2,26},{4,28},{6,30},{8,16},{10,18},{12,20},{14,22},{16,8},... | collective-permute-start | bytes 196616 | tf_op jit(solution)/shard_map/ppermute | solution.py:304
  48.8 0.1 collective-permute-start.17
  48.9 2.0 %collective-permute-start.18 = (bf16[16,2048]{1,0:T(8,128)(2,1)S(1)}, bf16[16,2048]{1,0:T(8,128)(2,1)S(1)}, u32[]{:S(2)}, u32[]{:S(2)}) collective-permute-start(bf16[16,2048]{1,0:T(8,128)(2,1)S(1)} %get-tuple-element.80), channel_id=1, source_target_pairs={{0,8},{2,10},{4,12},{6,14},{8,0},{10,2},{12,4},{14,6},{16,24},{18,... | collective-permute-start | bytes 196616 | tf_op jit(solution)/shard_map/ppermute | solution.py:304
  50.9 0.0 collective-permute-done.19.refs_0_
  50.9 1.4 %shard_map.80 = (bf16[256,4096]{1,0:T(8,128)(2,1)}, bf16[256,4096]{1,0:T(8,128)(2,1)}) custom-call(bf16[256,2048]{1,0:T(8,128)(2,1)S(1)} %collective-permute-done.19.refs_0_, bf16[256,2048]{1,0:T(8,128)(2,1)S(1)} %collective-permute-done.15.refs_1_, bf16[256,4096]{1,0:T(8,128)(2,1)} %get-tuple-element.69.refs_2_, ...), custom_call_target="tpu_custom_call", output_to_operand_aliasing={{0}: (2, {}), {1}: (3, {})} | custom-call | tf_op jit(solution)/shard_map/pallas_call | solution.py:287
  52.3 0.5 collective-permute-done.16
  52.8 2.5 %collective-permute-done.17 = bf16[16,2048]{1,0:T(8,128)(2,1)S(1)} collective-permute-done((bf16[16,2048]{1,0:T(8,128)(2,1)S(1)}, bf16[16,2048]{1,0:T(8,128)(2,1)S(1)}, u32[]{:S(2)}, u32[]{:S(2)}) %collective-permute-start.17) | collective-permute-done | bytes 65568 | tf_op jit(solution)/shard_map/ppermute | solution.py:304
  55.4 0.0 collective-permute-done.18
  55.4 0.1 collective-permute-start.20
  55.5 1.2 %collective-permute-done.20.other_ref = bf16[8,2048]{1,0:T(8,128)(2,1)S(1)} collective-permute-done((bf16[8,2048]{1,0:T(8,128)(2,1)S(1)}, bf16[8,2048]{1,0:T(8,128)(2,1)S(1)}, u32[]{:S(2)}, u32[]{:S(2)}) %collective-permute-start.20) | collective-permute-done | bytes 32800 | tf_op jit(solution)/shard_map/ppermute | solution.py:304
  56.7 0.7 %shard_map.81 = (bf16[8,2048]{1,0:T(8,128)(2,1)}, bf16[8,2048]{1,0:T(8,128)(2,1)}) custom-call(bf16[8,2048]{1,0:T(8,128)(2,1)S(1)} %get-tuple-element.84.mine_ref, bf16[8,2048]{1,0:T(8,128)(2,1)S(1)} %collective-permute-done.20.other_ref), custom_call_target="tpu_custom_call" | custom-call | tf_op jit(solution)/shard_map/pallas_call | solution.py:254
  (25 shorter events, 0.3 us)
Async XLA Ops:
  0.6 1.6 %collective-permute-start.1 = (bf16[8,2048]{1,0:T(8,128)(2,1)}, bf16[8,2048]{1,0:T(8,128)(2,1)S(1)}, u32[]{:S(2)}, u32[]{:S(2)}) collective-permute-start(bf16[8,2048]{1,0:T(8,128)(2,1)} %param.6), channel_id=1, source_target_pairs={{0,2},{2,0},{4,6},{6,4},{8,10},{10,8},{12,14},{14,12},{16,18},{18,... | collective-permute-start | bytes 98312 | tf_op jit(solution)/shard_map/ppermute | solution.py:304
  1.1 1.4 %collective-permute-start = (bf16[8,2048]{1,0:T(8,128)(2,1)}, bf16[8,2048]{1,0:T(8,128)(2,1)S(1)}, u32[]{:S(2)}, u32[]{:S(2)}) collective-permute-start(bf16[8,2048]{1,0:T(8,128)(2,1)} %param.5), channel_id=1, source_target_pairs={{0,2},{2,0},{4,6},{6,4},{8,10},{10,8},{12,14},{14,12},{16,18},{18,... | collective-permute-start | bytes 98312 | tf_op jit(solution)/shard_map/ppermute | solution.py:304
  2.6 7.7 %collective-permute-start.4 = (bf16[16,2048]{1,0:T(8,128)(2,1)S(1)}, bf16[16,2048]{1,0:T(8,128)(2,1)S(1)}, u32[]{:S(2)}, u32[]{:S(2)}) collective-permute-start(bf16[16,2048]{1,0:T(8,128)(2,1)S(1)} %maximum_maximum_fusion), channel_id=1, source_target_pairs={{0,24},{2,26},{4,28},{6,30},{8,16},{10,18},{12,20},{14,22},{16,8},... | collective-permute-start | bytes 196616 | tf_op jit(solution)/shard_map/ppermute | solution.py:304
  7.4 6.0 %collective-permute-start.5 = (bf16[16,2048]{1,0:T(8,128)(2,1)S(1)}, bf16[16,2048]{1,0:T(8,128)(2,1)S(1)}, u32[]{:S(2)}, u32[]{:S(2)}) collective-permute-start(bf16[16,2048]{1,0:T(8,128)(2,1)S(1)} %maximum_maximum_fusion), channel_id=1, source_target_pairs={{0,16},{2,18},{4,20},{6,22},{8,24},{10,26},{12,28},{14,30},{16,0},... | collective-permute-start | bytes 196616 | tf_op jit(solution)/shard_map/ppermute | solution.py:304
  7.5 5.9 %collective-permute-start.6 = (bf16[16,2048]{1,0:T(8,128)(2,1)S(1)}, bf16[16,2048]{1,0:T(8,128)(2,1)S(1)}, u32[]{:S(2)}, u32[]{:S(2)}) collective-permute-start(bf16[16,2048]{1,0:T(8,128)(2,1)S(1)} %maximum_maximum_fusion), channel_id=1, source_target_pairs={{0,8},{2,10},{4,12},{6,14},{8,0},{10,2},{12,4},{14,6},{16,24},{18,... | collective-permute-start | bytes 196616 | tf_op jit(solution)/shard_map/ppermute | solution.py:304
  9.7 12.6 %collective-permute-start.2 = (bf16[256,2048]{1,0:T(8,128)(2,1)S(1)}, bf16[256,2048]{1,0:T(8,128)(2,1)S(1)}, u32[]{:S(2)}, u32[]{:S(2)}) collective-permute-start(bf16[256,2048]{1,0:T(8,128)(2,1)S(1)} %get-tuple-element.44), channel_id=1, source_target_pairs={{0,2},{2,0},{4,6},{6,4},{8,10},{10,8},{12,14},{14,12},{16,18},{18,... | collective-permute-start | bytes 3145736 | tf_op jit(solution)/shard_map/ppermute | solution.py:304
  9.7 12.5 %collective-permute-start.3 = (bf16[256,2048]{1,0:T(8,128)(2,1)S(1)}, bf16[256,2048]{1,0:T(8,128)(2,1)S(1)}, u32[]{:S(2)}, u32[]{:S(2)}) collective-permute-start(bf16[256,2048]{1,0:T(8,128)(2,1)S(1)} %get-tuple-element.45), channel_id=1, source_target_pairs={{0,2},{2,0},{4,6},{6,4},{8,10},{10,8},{12,14},{14,12},{16,18},{18,... | collective-permute-start | bytes 3145736 | tf_op jit(solution)/shard_map/ppermute | solution.py:304
  13.4 5.3 %collective-permute-start.7 = (bf16[64,1024]{1,0:T(8,128)(2,1)S(1)}, bf16[64,1024]{1,0:T(8,128)(2,1)S(1)}, u32[]{:S(2)}, u32[]{:S(2)}) collective-permute-start(bf16[64,1024]{1,0:T(8,128)(2,1)S(1)} %pad_maximum_fusion), channel_id=1, source_target_pairs={{0,4},{2,6},{4,0},{6,2},{8,12},{10,14},{12,8},{14,10},{16,20},{18,... | collective-permute-start | bytes 393224 | tf_op jit(solution)/shard_map/ppermute | solution.py:304
  15.0 5.0 %collective-permute-start.8 = (bf16[64,1024]{1,0:T(8,128)(2,1)S(1)}, bf16[64,1024]{1,0:T(8,128)(2,1)S(1)}, u32[]{:S(2)}, u32[]{:S(2)}) collective-permute-start(bf16[64,1024]{1,0:T(8,128)(2,1)S(1)} %pad_maximum_fusion.1), channel_id=1, source_target_pairs={{0,1},{1,0},{2,3},{3,2},{4,5},{5,4},{6,7},{7,6},{8,9},{9,8},{10,11... | collective-permute-start | bytes 393224 | tf_op jit(solution)/shard_map/ppermute | solution.py:304
  20.1 7.0 %collective-permute-start.9 = (bf16[128,1024]{1,0:T(8,128)(2,1)S(1)}, bf16[128,1024]{1,0:T(8,128)(2,1)S(1)}, u32[]{:S(2)}, u32[]{:S(2)}) collective-permute-start(bf16[128,1024]{1,0:T(8,128)(2,1)S(1)} %constant_dynamic-update-slice_fusion.refs_0_), channel_id=1, source_target_pairs={{0,1},{1,0},{2,3},{3,2},{4,5},{5,4},{6,7},{7,6},{8,9},{9,8},{10,11... | collective-permute-start | bytes 786440 | tf_op jit(solution)/shard_map/ppermute | solution.py:304
  21.7 6.7 %collective-permute-start.10 = (bf16[128,1024]{1,0:T(8,128)(2,1)S(1)}, bf16[128,1024]{1,0:T(8,128)(2,1)S(1)}, u32[]{:S(2)}, u32[]{:S(2)}) collective-permute-start(bf16[128,1024]{1,0:T(8,128)(2,1)S(1)} %constant_dynamic-update-slice_fusion.5.refs_1_.refs_0_), channel_id=1, source_target_pairs={{0,4},{2,6},{4,0},{6,2},{8,12},{10,14},{12,8},{14,10},{16,20},{18,... | collective-permute-start | bytes 786440 | tf_op jit(solution)/shard_map/ppermute | solution.py:304
  32.9 6.4 %collective-permute-start.11 = (bf16[128,1024]{1,0:T(8,128)(2,1)S(1)}, bf16[128,1024]{1,0:T(8,128)(2,1)S(1)}, u32[]{:S(2)}, u32[]{:S(2)}) collective-permute-start(bf16[128,1024]{1,0:T(8,128)(2,1)S(1)} %get-tuple-element.52), channel_id=1, source_target_pairs={{0,1},{1,0},{2,3},{3,2},{4,5},{5,4},{6,7},{7,6},{8,9},{9,8},{10,11... | collective-permute-start | bytes 786440 | tf_op jit(solution)/shard_map/ppermute | solution.py:304
  33.5 6.4 %collective-permute-start.12 = (bf16[128,1024]{1,0:T(8,128)(2,1)S(1)}, bf16[128,1024]{1,0:T(8,128)(2,1)S(1)}, u32[]{:S(2)}, u32[]{:S(2)}) collective-permute-start(bf16[128,1024]{1,0:T(8,128)(2,1)S(1)} %get-tuple-element.56), channel_id=1, source_target_pairs={{0,4},{2,6},{4,0},{6,2},{8,12},{10,14},{12,8},{14,10},{16,20},{18,... | collective-permute-start | bytes 786440 | tf_op jit(solution)/shard_map/ppermute | solution.py:304
  39.9 6.4 %collective-permute-start.15 = (bf16[256,2048]{1,0:T(8,128)(2,1)S(1)}, bf16[256,2048]{1,0:T(8,128)(2,1)S(1)}, u32[]{:S(2)}, u32[]{:S(2)}) collective-permute-start(bf16[256,2048]{1,0:T(8,128)(2,1)S(1)} %get-tuple-element.60), channel_id=1, source_target_pairs={{0,2},{2,0},{4,6},{6,4},{8,10},{10,8},{12,14},{14,12},{16,18},{18,... | collective-permute-start | bytes 3145736 | tf_op jit(solution)/shard_map/ppermute | solution.py:304
  40.0 6.0 %collective-permute-start.13 = (bf16[64,1024]{1,0:T(8,128)(2,1)S(1)}, bf16[64,1024]{1,0:T(8,128)(2,1)S(1)}, u32[]{:S(2)}, u32[]{:S(2)}) collective-permute-start(bf16[64,1024]{1,0:T(8,128)(2,1)S(1)} %slice.136), channel_id=1, source_target_pairs={{0,4},{2,6},{4,0},{6,2},{8,12},{10,14},{12,8},{14,10},{16,20},{18,... | collective-permute-start | bytes 393224 | tf_op jit(solution)/shard_map/ppermute | solution.py:304
  40.6 5.7 %collective-permute-start.14 = (bf16[64,1024]{1,0:T(8,128)(2,1)S(1)}, bf16[64,1024]{1,0:T(8,128)(2,1)S(1)}, u32[]{:S(2)}, u32[]{:S(2)}) collective-permute-start(bf16[64,1024]{1,0:T(8,128)(2,1)S(1)} %slice.135), channel_id=1, source_target_pairs={{0,1},{1,0},{2,3},{3,2},{4,5},{5,4},{6,7},{7,6},{8,9},{9,8},{10,11... | collective-permute-start | bytes 393224 | tf_op jit(solution)/shard_map/ppermute | solution.py:304
  45.4 5.6 %collective-permute-start.19 = (bf16[256,2048]{1,0:T(8,128)(2,1)S(1)}, bf16[256,2048]{1,0:T(8,128)(2,1)S(1)}, u32[]{:S(2)}, u32[]{:S(2)}) collective-permute-start(bf16[256,2048]{1,0:T(8,128)(2,1)S(1)} %get-tuple-element.67), channel_id=1, source_target_pairs={{0,2},{2,0},{4,6},{6,4},{8,10},{10,8},{12,14},{14,12},{16,18},{18,... | collective-permute-start | bytes 3145736 | tf_op jit(solution)/shard_map/ppermute | solution.py:304
  46.5 6.4 %collective-permute-start.16 = (bf16[16,2048]{1,0:T(8,128)(2,1)S(1)}, bf16[16,2048]{1,0:T(8,128)(2,1)S(1)}, u32[]{:S(2)}, u32[]{:S(2)}) collective-permute-start(bf16[16,2048]{1,0:T(8,128)(2,1)S(1)} %get-tuple-element.82), channel_id=1, source_target_pairs={{0,24},{2,26},{4,28},{6,30},{8,16},{10,18},{12,20},{14,22},{16,8},... | collective-permute-start | bytes 196616 | tf_op jit(solution)/shard_map/ppermute | solution.py:304
  48.8 6.6 %collective-permute-start.17 = (bf16[16,2048]{1,0:T(8,128)(2,1)S(1)}, bf16[16,2048]{1,0:T(8,128)(2,1)S(1)}, u32[]{:S(2)}, u32[]{:S(2)}) collective-permute-start(bf16[16,2048]{1,0:T(8,128)(2,1)S(1)} %get-tuple-element.81), channel_id=1, source_target_pairs={{0,16},{2,18},{4,20},{6,22},{8,24},{10,26},{12,28},{14,30},{16,0},... | collective-permute-start | bytes 196616 | tf_op jit(solution)/shard_map/ppermute | solution.py:304
  48.9 6.5 %collective-permute-start.18 = (bf16[16,2048]{1,0:T(8,128)(2,1)S(1)}, bf16[16,2048]{1,0:T(8,128)(2,1)S(1)}, u32[]{:S(2)}, u32[]{:S(2)}) collective-permute-start(bf16[16,2048]{1,0:T(8,128)(2,1)S(1)} %get-tuple-element.80), channel_id=1, source_target_pairs={{0,8},{2,10},{4,12},{6,14},{8,0},{10,2},{12,4},{14,6},{16,24},{18,... | collective-permute-start | bytes 196616 | tf_op jit(solution)/shard_map/ppermute | solution.py:304
  55.4 1.3 %collective-permute-start.20 = (bf16[8,2048]{1,0:T(8,128)(2,1)S(1)}, bf16[8,2048]{1,0:T(8,128)(2,1)S(1)}, u32[]{:S(2)}, u32[]{:S(2)}) collective-permute-start(bf16[8,2048]{1,0:T(8,128)(2,1)S(1)} %get-tuple-element.83), channel_id=1, source_target_pairs={{0,2},{2,0},{4,6},{6,4},{8,10},{10,8},{12,14},{14,12},{16,18},{18,... | collective-permute-start | bytes 98312 | tf_op jit(solution)/shard_map/ppermute | solution.py:304
